TPU v7x, 32 devices: a whole 2x2x4 slice. The times are simulated.
32 devices in a mesh: wide: 8 (over y, x, core), narrow: 4 (over z).
Axes of the slice: x: 2, y: 2, z: 4, core: 2. Of those that a mesh axis runs over, the one named last changes fastest.
Arguments:
- amplitudes: bfloat16 [256, 4, 4096], P('wide', None, 'narrow'), may hold values from -6 to 6
- amp_tiles: int32 [8, 4], replicated, may hold values from 0 to 7, all different within a row
- integrals: bfloat16 [8, 2, 4096, 4096], P('wide', None, None, 'narrow'), may hold values from -0.09375 to 0.09375
- cd_tiles: int32 [8, 2], replicated, may hold values from 0 to 7, all different within a row
- q_owner: int32 [8], replicated, may hold values from 0 to 7, each once
Outputs:
- residual: bfloat16 [256, 8, 4096], P('wide', None, 'narrow')
Inputs may be any that keep to these rules, and one draw needn't show every extreme that they name: `amp_tiles`: within a row, the 4 tiles are different. `cd_tiles`: within a row, the 2 tiles are different; every tile is named by some row. `q_owner`: each owner index appears once.
All inputs are finite; a program needn't handle non-finite values.
Results may differ from a plain program's by a relative error of at most 0.017.
Values may be sent and summed in bfloat16 or wider, within the bound.
No kernel may reach another device: no remote copies, remote signals or barrier semaphores. Data moves between devices by JAX's collectives and lax.ppermute only.
A program may use at most 64 MiB of HBM per device.

v0:
```python
import functools

import jax
import jax.numpy as jnp
from jax import lax
from jax.experimental import pallas as pl
from jax.experimental.pallas import tpu as pltpu
from jax.sharding import PartitionSpec as P

PART = 512
AHEAD = 3
COST = 1
LIMIT = 30 << 20
FIRST = 40 << 20


def pick_kernel(peers, wants, tables_from, amps, *refs):
    outs, (tables, held, slots, sem) = refs[:peers], refs[peers:]
    fetch = pltpu.make_async_copy(tables_from, tables, sem)
    fetch.start()
    width = amps.shape[1]
    for t in range(width):
        held[t] = amps[:, t, :]
    held[width] = jnp.zeros_like(held[width])
    fetch.wait()
    me = lax.axis_index("wide")

    def look(q, carry):
        peer = tables[width + wants, q] ^ me
        for k in range(wants):
            slot = jnp.int32(width)
            for t in range(width):
                slot = jnp.where(tables[t, me] == tables[width + k, q], t, slot)
            slots[peer, k] = slot
        return carry

    lax.fori_loop(0, peers, look, 0)
    for j in range(peers):
        for k in range(wants):
            outs[j][k] = held[slots[j, k]]


def pick(amplitudes, amp_tiles, cd_tiles, q_owner):
    rows, width, depth = amplitudes.shape
    peers, wants = cd_tiles.shape
    tables = jnp.concatenate([amp_tiles.T, cd_tiles.T, q_owner[None]], axis=0)
    vmem = pl.BlockSpec(memory_space=pltpu.VMEM)
    return pl.pallas_call(
        functools.partial(pick_kernel, peers, wants),
        out_shape=[jax.ShapeDtypeStruct((wants, rows, depth), jnp.bfloat16)] * peers,
        in_specs=[pl.BlockSpec(memory_space=pl.ANY), vmem],
        out_specs=[vmem] * peers,
        scratch_shapes=[
            pltpu.SMEM(tables.shape, jnp.int32),
            pltpu.VMEM((width + 1, rows, depth), jnp.bfloat16),
            pltpu.SMEM((peers, wants), jnp.int32),
            pltpu.SemaphoreType.DMA,
        ],
        compiler_params=pltpu.CompilerParams(vmem_limit_bytes=LIMIT),
        name="pick",
    )(tables, amplitudes)


def product_kernel(plan, *refs):
    refs = list(refs[plan["after"] :])
    picked = [refs.pop(0) for _ in range(plan["count"])]
    held = refs.pop(0) if plan["held"] else None
    ints = refs.pop(0) if plan["fetch"] else None
    del refs[: plan["passed"]]
    outs = [refs.pop(0) for _ in range(plan["chunks"])]
    brought = refs.pop(0) if plan["fetch"] else None
    left, sems = refs[-2:]
    source = held if plan["held"] else brought
    _, wants, share, depth = source.shape
    part = min(PART, share)
    blocks = [(s, i) for s in range(len(plan["fetch"])) for i in range(share // part)]

    def copies(n):
        s, i = blocks[n]
        start = pl.multiple_of((lax.axis_index("narrow") ^ plan["fetch"][s]) * share, share) + i * part
        return [
            pltpu.make_async_copy(
                ints.at[0, k, pl.ds(start, part), :], brought.at[s, k, pl.ds(i * part, part), :], sems.at[n, k]
            )
            for k in range(wants)
        ]

    def start(n):
        if n < len(blocks):
            for copy in copies(n):
                copy.start()

    def wait(n):
        for copy in copies(n):
            copy.wait()

    ahead = len(blocks) if plan["held"] else AHEAD
    for n in range(ahead):
        start(n)
    rows = picked[0].shape[1]
    for i, ref in enumerate(picked):
        for k in range(wants):
            left[k, i * rows : (i + 1) * rows, :] = ref[k]

    each = len(picked) * rows // len(outs)

    def block(o, s, i):
        at = slice(i * part, (i + 1) * part)
        total = None
        for k in range(wants):
            term = lax.dot_general(
                left[k], source[s, k, at, :], (((1,), (1,)), ((), ())), preferred_element_type=jnp.float32
            )
            total = term if total is None else total + term
        total = total.astype(jnp.bfloat16)
        for c, out in enumerate(outs):
            out[o, :, at] = total[c * each : (c + 1) * each]

    if plan["held"]:

        @pl.loop(0, len(plan["use"]))
        def _(o):
            for i in range(share // part):
                block(o, plan["use"][0] + o, i)

        for n in range(len(blocks)):
            wait(n)
    else:
        for n, (s, i) in enumerate(blocks):
            wait(n)
            start(n + ahead)
            block(s, s, i)


def product(picked, chunks, use, held, ints, fetch, passed, after, limit):
    _, wants, pairs, depth = ints.shape
    rows = picked[0].shape[1]
    share = pairs // lax.axis_size("narrow")
    count, shares = len(picked), len(use)
    plan = dict(
        count=count,
        chunks=chunks,
        use=use,
        held=held is not None,
        fetch=fetch,
        passed=len(passed),
        after=len(after),
    )
    vmem, any_space = pl.BlockSpec(memory_space=pltpu.VMEM), pl.BlockSpec(memory_space=pl.ANY)
    resident = ([held] if held is not None else []) + ([ints] if fetch else [])
    first_passed = len(after) + count + len(resident)
    outs = pl.pallas_call(
        functools.partial(product_kernel, plan),
        out_shape=[jax.ShapeDtypeStruct((shares, count * rows // chunks, share), jnp.bfloat16)] * chunks
        + [jax.ShapeDtypeStruct((len(fetch), wants, share, depth), jnp.bfloat16)] * bool(fetch)
        + [jax.ShapeDtypeStruct(p.shape, p.dtype) for p in passed],
        in_specs=[any_space] * len(after)
        + [vmem] * (count + (held is not None))
        + [any_space] * (bool(fetch) + len(passed)),
        out_specs=[vmem] * (chunks + bool(fetch)) + [any_space] * len(passed),
        input_output_aliases={first_passed + i: chunks + bool(fetch) + i for i in range(len(passed))},
        scratch_shapes=[
            pltpu.VMEM((wants, count * rows, depth), jnp.bfloat16),
            pltpu.SemaphoreType.DMA((max(1, len(fetch) * max(1, share // PART)), wants)),
        ],
        compiler_params=pltpu.CompilerParams(vmem_limit_bytes=limit),
        cost_estimate=pl.CostEstimate(
            flops=2 * 256 * wants * depth * share * shares // COST,
            bytes_accessed=2 * wants * depth * share * shares // COST,
            transcendentals=0,
        ),
        name="product",
    )(*after, *picked, *resident, *passed)
    return outs[:chunks], outs[chunks : chunks + bool(fetch)], outs[chunks + bool(fetch) :]


def total_kernel(places, halves, *refs):
    outs = refs[len(refs) - (2 if halves else 1) :]
    at = 0
    for o, own_places in enumerate(places):
        total = None
        for place in own_places:
            term = refs[at][place].astype(jnp.float32)
            total = term if total is None else total + term
            at += 1
        total = total.astype(jnp.bfloat16)
        if halves:
            rows = outs[0].shape[0]
            outs[0][...], outs[1][...] = total[:rows], total[rows:]
        else:
            outs[0][o] = total


def totals(lists, after, halves=False):
    terms = [term for terms in lists for term in terms]
    _, rows, share = terms[0][0].shape
    vmem, any_space = pl.BlockSpec(memory_space=pltpu.VMEM), pl.BlockSpec(memory_space=pl.ANY)
    shape = [(rows // 2, share)] * 2 if halves else [(len(lists), rows, share)]
    return pl.pallas_call(
        functools.partial(total_kernel, [[place for _, place in terms] for terms in lists], halves),
        out_shape=[jax.ShapeDtypeStruct(one, jnp.bfloat16) for one in shape],
        in_specs=[vmem] * len(terms) + [any_space] * len(after),
        out_specs=[vmem] * len(shape),
        compiler_params=pltpu.CompilerParams(vmem_limit_bytes=LIMIT),
        name="totals",
    )(*[array for array, _ in terms], *after)


def place_kernel(peers, q_owner, after, place):
    size = place.shape[0]
    me = lax.axis_index("wide")
    row = lax.broadcasted_iota(jnp.int32, (size, size), 0)
    column = lax.broadcasted_iota(jnp.int32, (size, size), 1)
    source = row // peers
    for q in range(peers):
        source += jnp.where(row % peers == q, (q_owner[q] ^ me) * (size // peers), 0)
    place[...] = (source == column).astype(jnp.bfloat16)


def place_of(q_owner, size, after):
    return pl.pallas_call(
        functools.partial(place_kernel, q_owner.shape[0]),
        out_shape=jax.ShapeDtypeStruct((size, size), jnp.bfloat16),
        in_specs=[pl.BlockSpec(memory_space=pltpu.SMEM), pl.BlockSpec(memory_space=pl.ANY)],
        out_specs=pl.BlockSpec(memory_space=pltpu.VMEM),
        compiler_params=pltpu.CompilerParams(vmem_limit_bytes=LIMIT),
        name="place",
    )(q_owner, after)


def order_kernel(peers, halves, *refs):
    shares, (place, out, held) = refs[:-3], refs[-3:]
    rows = held.shape[0] // len(peers)
    for j, half, share in zip(peers, halves, shares):
        held[j * rows : (j + 1) * rows, :] = share[...] if half is None else share[half]
    out[...] = jnp.dot(place[...], held[...], preferred_element_type=jnp.float32).astype(jnp.bfloat16)


def order(place, shares):
    size, share = place.shape[0], shares[0][1].shape[-1]
    peers, shares, halves = zip(*shares)
    vmem = pl.BlockSpec(memory_space=pltpu.VMEM)
    return pl.pallas_call(
        functools.partial(order_kernel, peers, halves),
        out_shape=jax.ShapeDtypeStruct((size, share), jnp.bfloat16),
        in_specs=[vmem] * (1 + len(shares)),
        out_specs=vmem,
        scratch_shapes=[pltpu.VMEM((size, share), jnp.bfloat16)],
        compiler_params=pltpu.CompilerParams(vmem_limit_bytes=LIMIT),
        name="order",
    )(*shares, place)


def on_device(amplitudes, amp_tiles, integrals, cd_tiles, q_owner):
    peers = lax.axis_size("wide")
    devices = lax.axis_size("narrow")
    rows = amplitudes.shape[0]

    odd, even = tuple(range(1, devices, 2)), tuple(range(0, devices, 2))
    middle = even[1:]

    def swap(value, j):
        return lax.ppermute(value, "wide", [(w, w ^ j) for w in range(peers)])

    def swap_line(value, mask):
        return lax.ppermute(value, "narrow", [(n, n ^ mask) for n in range(devices)])

    def first_step(message):
        return swap_line(message, 1)

    def later_steps(kept, come, after=()):
        terms = {0: [(come, 0)]}
        for i, r in enumerate(middle):
            terms[r] = [(kept, i), (come, odd.index(r ^ 1))]
        messages = []
        step = 1
        while 1 << step < devices:
            names = [r for r in sorted(terms) if r >> step & 1]
            messages += totals([terms.pop(r) for r in names], list(after))
            come = swap_line(messages[-1], 1 << step)
            for i, r in enumerate(names):
                terms[r ^ (1 << step)].append((come, i))
            step += 1
        return messages[0], terms[0]

    chips = peers // 2
    near = [g for g in range(1, chips) if g & (g - 1) == 0]
    far = [g for g in range(1, chips) if g & (g - 1)]

    def of(groups):
        return [j for g in groups for j in (2 * g, 2 * g + 1)]

    def multiply(groups, use, held=None, fetch=(), passed=(), after=(), limit=LIMIT):
        chosen = [lot[j] for j in of(groups)]
        outs, brought, passed = product(
            chosen, len(groups), use, held, integrals, fetch, list(passed), list(after), limit
        )
        return dict(zip(groups, outs)), *brought, passed

    lot = dict(enumerate(pick(amplitudes, amp_tiles, cd_tiles, q_owner)))
    for j in [1] + of(near):
        lot[j] = swap(lot[j], j)

    come, ready, sums = {}, {}, {}
    first, others = near[0], near[1:]
    all_odd, all_middle = tuple(range(len(odd))), tuple(range(len(middle)))
    away, odd_ints, _ = multiply([0], all_odd, fetch=odd, limit=FIRST)
    come[0] = first_step(away[0])
    outs, middle_ints, passed = multiply(
        near, all_odd, odd_ints, middle, [lot[j] for j in of(far)], [away[0]]
    )
    lot.update((j, swap(value, j)) for j, value in zip(of(far), passed))
    away.update(outs)
    come.update((g, first_step(away[g])) for g in near)
    kept, _ = multiply([0] + near, all_middle, middle_ints, after=[come[0]])
    ready[first], sums[first] = later_steps(kept[first], come[first])
    outs, home_ints, _ = multiply(far, all_odd, odd_ints, (0,), after=[ready[first]])
    away.update(outs)
    come.update((g, first_step(away[g])) for g in far)
    last = away[far[0]]
    for g in others:
        ready[g], sums[g] = later_steps(kept[g], come[g], [last])
        last = ready[g]
    outs, _ = multiply(far, all_middle, middle_ints, after=[last, sums[first][-1][0]])
    kept.update(outs)
    own, _ = multiply(range(chips), (0,), home_ints, after=[kept[far[0]]])
    place = place_of(q_owner, peers * rows, own[0])

    shares = {}

    def close(g, after):
        terms = [[(own[g], 0)] + sums[g]]
        if g in far:
            whole, = totals(terms, after)
            got = swap(whole.reshape(2, rows, -1), 2 * g)
            shares[2 * g], shares[2 * g + 1] = (got, 0), (swap(got[1], 1), None)
            return whole
        halves = totals(terms, after, halves=True)
        for j, value in zip((2 * g, 2 * g + 1), halves):
            shares[j] = (swap(value, j) if j else value, None)
        return halves[1]

    last = close(first, [place])
    for g in far + [0]:
        ready[g], sums[g] = later_steps(kept[g], come[g], [last])
        last = ready[g]
    for g in others:
        last = close(g, [last])
    for g in far:
        last = close(g, [last] + [shares[j][0] for j in of(near)])
    close(0, [last])
    return order(place, [(j, *shares[j]) for j in of(far + near + [0])]).reshape(rows, peers, -1)


def solution(mesh):
    placed = (P("wide", None, "narrow"), P(), P("wide", None, None, "narrow"), P(), P())
    return jax.shard_map(
        on_device, mesh=mesh, in_specs=placed, out_specs=P("wide", None, "narrow"), check_vma=False
    )
```

profile of v0, /device:TPU:0, one launch (start us, length us, event | category | flops | bytes accessed | tf_op | source)
XLA Modules:
  0.0 62.8 jit_solution(4127960775996672774)
XLA Ops:
  0.0 0.7 %pad_add_fusion.tables_from = s32[7,8]{1,0:T(8,128)S(1)} fusion(s32[1,8]{1,0:T(1,128)} %bitcast.8, s32[2,8]{1,0:T(2,128)} %bitcast.10, s32[4,8]{1,0:T(4,128)} %bitcast.9), kind=kLoop, calls=%fused_computation.1 | loop fusion | flops 112 | bytes 448 | tf_op jit(solution)/shard_map/concatenate | solution.py:46
  0.7 0.9 %copy-done = bf16[32,4,1024]{2,1,0:T(4,128)(2,1)S(1)} copy-done((bf16[32,4,1024]{2,1,0:T(4,128)(2,1)S(1)}, bf16[32,4,1024]{2,1,0:T(4,128)(2,1)}, u32[]{:S(2)}) %copy-start) | copy-done | bytes 262168
  1.7 0.8 %pick.1 = (bf16[2,32,1024]{2,1,0:T(8,128)(2,1)S(1)}, bf16[2,32,1024]{2,1,0:T(8,128)(2,1)S(1)}, bf16[2,32,1024]{2,1,0:T(8,128)(2,1)S(1)}, bf16[2,32,1024]{2,1,0:T...) custom-call(s32[7,8]{1,0:T(8,128)S(1)} %pad_add_fusion.tables_from, ...), custom_call_target="tpu_custom_call" | custom-call | tf_op jit(solution)/shard_map/pick/pallas_call | solution.py:48
  2.5 0.5 collective-permute-start
  3.0 2.6 %collective-permute-start.2 = (bf16[2,32,1024]{2,1,0:T(8,128)(2,1)S(1)}, bf16[2,32,1024]{2,1,0:T(8,128)(2,1)S(1)}, u32[]{:S(2)}, u32[]{:S(2)}) collective-permute-start(bf16[2,32,1024]{2,1,0:T(8,128)(2,1)S(1)} %get-tuple-element.38), channel_id=1, source_target_pairs={{0,8},{4,12},{8,0},{12,4},{16,24},{20,28},{24,16},{28,20},{1,9},{5... | collective-permute-start | bytes 393224 | tf_op jit(solution)/shard_map/ppermute | solution.py:263
  5.6 0.1 collective-permute-start.3
  5.7 1.8 %collective-permute-start.4 = (bf16[2,32,1024]{2,1,0:T(8,128)(2,1)S(1)}, bf16[2,32,1024]{2,1,0:T(8,128)(2,1)S(1)}, u32[]{:S(2)}, u32[]{:S(2)}) collective-permute-start(bf16[2,32,1024]{2,1,0:T(8,128)(2,1)S(1)} %get-tuple-element.40), channel_id=1, source_target_pairs={{0,16},{4,20},{8,24},{12,28},{16,0},{20,4},{24,8},{28,12},{1,17},{... | collective-permute-start | bytes 393224 | tf_op jit(solution)/shard_map/ppermute | solution.py:263
  7.4 0.0 collective-permute-start.5
  7.4 0.0 collective-permute-done.refs_1_.refs_2_
  7.4 4.7 %product.6 = (bf16[2,64,1024]{2,1,0:T(8,128)(2,1)S(1)}, bf16[2,2,1024,1024]{3,2,1,0:T(8,128)(2,1)S(1)}) custom-call(bf16[2,32,1024]{2,1,0:T(8,128)(2,1)S(1)} %get-tuple-element.35.refs_0_.refs_1_, bf16[2,32,1024]{2,1,0:T(8,128)(2,1)S(1)} %collective-permute-done.refs_1_.refs_2_, bf16[1,2,4096,1024]{3,2,1,0:T(8,128)(2,1)} %refs_4_.1), custom_call_target="tpu_custom_call" | custom-call | flops 2147483648 | bytes 8388608 | tf_op jit(solution)/shard_map/product/pallas_call | solution.py:152
  12.1 1.8 %collective-permute-start.1 = (bf16[2,64,1024]{2,1,0:T(8,128)(2,1)S(1)}, bf16[2,64,1024]{2,1,0:T(8,128)(2,1)S(1)}, u32[]{:S(2)}, u32[]{:S(2)}) collective-permute-start(bf16[2,64,1024]{2,1,0:T(8,128)(2,1)S(1)} %get-tuple-element.37.refs_0_), channel_id=1, source_target_pairs={{0,1},{1,0},{2,3},{3,2},{4,5},{5,4},{6,7},{7,6},{8,9},{9,8},{10,11... | collective-permute-start | bytes 786440 | tf_op jit(solution)/shard_map/ppermute | solution.py:266
  13.9 0.0 collective-permute-done.2.refs_1_.refs_3_
  13.9 0.0 collective-permute-done.3.refs_2_.refs_4_
  13.9 3.1 %product.7 = (bf16[2,64,1024]{2,1,0:T(8,128)(2,1)S(1)}, bf16[2,64,1024]{2,1,0:T(8,128)(2,1)S(1)}, bf16[1,2,1024,1024]{3,2,1,0:T(8,128)(2,1)S(1)}, bf16[2,32,1024...) custom-call(bf16[2,64,1024]{2,1,0:T(8,128)(2,1)S(1)} %get-tuple-element.37.refs_0_, ...), custom_call_target="tpu_custom_call", output_to_operand_aliasing={{3}: (7, {}), {4}: (8, {})} | custom-call | flops 2147483648 | bytes 8388608 | tf_op jit(solution)/shard_map/product/pallas_call | solution.py:152
  17.0 1.6 %collective-permute-start.7 = (bf16[2,64,1024]{2,1,0:T(8,128)(2,1)S(1)}, bf16[2,64,1024]{2,1,0:T(8,128)(2,1)S(1)}, u32[]{:S(2)}, u32[]{:S(2)}) collective-permute-start(bf16[2,64,1024]{2,1,0:T(8,128)(2,1)S(1)} %get-tuple-element.49), channel_id=1, source_target_pairs={{0,1},{1,0},{2,3},{3,2},{4,5},{5,4},{6,7},{7,6},{8,9},{9,8},{10,11... | collective-permute-start | bytes 786440 | tf_op jit(solution)/shard_map/ppermute | solution.py:266
  18.7 2.4 %collective-permute-start.8 = (bf16[2,32,1024]{2,1,0:T(8,128)(2,1)S(1)}, bf16[2,32,1024]{2,1,0:T(8,128)(2,1)S(1)}, u32[]{:S(2)}, u32[]{:S(2)}) collective-permute-start(bf16[2,32,1024]{2,1,0:T(8,128)(2,1)S(1)} %get-tuple-element.50), channel_id=1, source_target_pairs={{0,24},{4,28},{8,16},{12,20},{16,8},{20,12},{24,0},{28,4},{1,25},{... | collective-permute-start | bytes 393224 | tf_op jit(solution)/shard_map/ppermute | solution.py:263
  21.1 0.5 collective-permute-start.6
  21.6 1.5 %product.8 = (bf16[1,64,1024]{2,1,0:T(8,128)(2,1)S(1)}, bf16[1,64,1024]{2,1,0:T(8,128)(2,1)S(1)}, bf16[1,64,1024]{2,1,0:T(8,128)(2,1)S(1)}) custom-call(bf16[2,64,1024]{2,1,0:T(8,128)(2,1)S(1)} %collective-permute-done.1.refs_0_.refs_1_, bf16[2,32,1024]{2,1,0:T(8,128)(2,1)S(1)} %get-tuple-element.35.refs_0_.refs_1_, ...), custom_call_target="tpu_custom_call" | custom-call | flops 1073741824 | bytes 4194304 | tf_op jit(solution)/shard_map/product/pallas_call | solution.py:152
  23.1 3.8 %collective-permute-done.7.refs_1_ = bf16[2,64,1024]{2,1,0:T(8,128)(2,1)S(1)} collective-permute-done((bf16[2,64,1024]{2,1,0:T(8,128)(2,1)S(1)}, bf16[2,64,1024]{2,1,0:T(8,128)(2,1)S(1)}, u32[]{:S(2)}, u32[]{:S(2)}) %collective-permute-start.7) | collective-permute-done | bytes 262176 | tf_op jit(solution)/shard_map/ppermute | solution.py:266
  26.9 2.8 %collective-permute-start.10 = (bf16[1,64,1024]{2,1,0:T(8,128)(2,1)S(1)}, bf16[1,64,1024]{2,1,0:T(8,128)(2,1)S(1)}, u32[]{:S(2)}, u32[]{:S(2)}) collective-permute-start(bf16[1,64,1024]{2,1,0:T(8,128)(2,1)S(1)} %totals.8.refs_0_), channel_id=1, source_target_pairs={{0,2},{1,3},{2,0},{3,1},{4,6},{5,7},{6,4},{7,5},{8,10},{9,11},{10,... | collective-permute-start | bytes 393224 | tf_op jit(solution)/shard_map/ppermute | solution.py:266
  29.7 2.8 %product.9 = (bf16[2,64,1024]{2,1,0:T(8,128)(2,1)S(1)}, bf16[1,2,1024,1024]{3,2,1,0:T(8,128)(2,1)S(1)}) custom-call(bf16[1,64,1024]{2,1,0:T(8,128)(2,1)S(1)} %totals.8.refs_0_, bf16[2,32,1024]{2,1,0:T(8,128)(2,1)S(1)} %collective-permute-done.8.refs_1_.refs_2_.refs_7_, bf16[2,32,1024]{2,1,0:T(8,128)(2,1)S(1)} %collective-permute-done.9.refs_2_.refs_3_.refs_8_, ...), custom_call_target="tpu_custom_call" | custom-call | flops 2147483648 | bytes 8388608 | tf_op jit(solution)/shard_map/product/pallas_call | solution.py:152
  32.6 0.0 copy-start.1
  32.6 1.6 %collective-permute-start.11 = (bf16[2,64,1024]{2,1,0:T(8,128)(2,1)S(1)}, bf16[2,64,1024]{2,1,0:T(8,128)(2,1)S(1)}, u32[]{:S(2)}, u32[]{:S(2)}) collective-permute-start(bf16[2,64,1024]{2,1,0:T(8,128)(2,1)S(1)} %get-tuple-element.52.refs_2_), channel_id=1, source_target_pairs={{0,1},{1,0},{2,3},{3,2},{4,5},{5,4},{6,7},{7,6},{8,9},{9,8},{10,11... | collective-permute-start | bytes 786440 | tf_op jit(solution)/shard_map/ppermute | solution.py:266
  34.3 1.1 %collective-permute-done.6.refs_1_ = bf16[2,64,1024]{2,1,0:T(8,128)(2,1)S(1)} collective-permute-done((bf16[2,64,1024]{2,1,0:T(8,128)(2,1)S(1)}, bf16[2,64,1024]{2,1,0:T(8,128)(2,1)S(1)}, u32[]{:S(2)}, u32[]{:S(2)}) %collective-permute-start.6) | collective-permute-done | bytes 262176 | tf_op jit(solution)/shard_map/ppermute | solution.py:266
  35.4 1.1 %collective-permute-start.13 = (bf16[1,64,1024]{2,1,0:T(8,128)(2,1)S(1)}, bf16[1,64,1024]{2,1,0:T(8,128)(2,1)S(1)}, u32[]{:S(2)}, u32[]{:S(2)}) collective-permute-start(bf16[1,64,1024]{2,1,0:T(8,128)(2,1)S(1)} %totals.9.refs_0_), channel_id=1, source_target_pairs={{0,2},{1,3},{2,0},{3,1},{4,6},{5,7},{6,4},{7,5},{8,10},{9,11},{10,... | collective-permute-start | bytes 393224 | tf_op jit(solution)/shard_map/ppermute | solution.py:266
  36.5 1.4 %product.10.refs_0_ = bf16[1,64,1024]{2,1,0:T(8,128)(2,1)S(1)} custom-call(bf16[1,64,1024]{2,1,0:T(8,128)(2,1)S(1)} %totals.9.refs_0_, bf16[1,64,1024]{2,1,0:T(8,128)(2,1)S(1)} %collective-permute-done.10.refs_1_.refs_2_, bf16[2,32,1024]{2,1,0:T(8,128)(2,1)S(1)} %collective-permute-done.8.refs_1_.refs_2_.refs_7_, ...), custom_call_target="tpu_custom_call" | custom-call | flops 1073741824 | bytes 4194304 | tf_op jit(solution)/shard_map/product/pallas_call | solution.py:152
  37.9 1.3 %product.11 = (bf16[1,64,1024]{2,1,0:T(8,128)(2,1)S(1)}, bf16[1,64,1024]{2,1,0:T(8,128)(2,1)S(1)}, bf16[1,64,1024]{2,1,0:T(8,128)(2,1)S(1)}, bf16[1,64,1024]{2,1,0:T(8,128)(2,1)S(1)}) custom-call(bf16[1,64,1024]{2,1,0:T(8,128)(2,1)S(1)} %product.10.refs_0_, bf16[2,32,1024]{2,1,0:T(8,128)(2,1)S(1)} %get-tuple-element.35.refs_0_.refs_1_, ...), custom_call_target="tpu_custom_call" | custom-call | flops 1073741824 | bytes 4194304 | tf_op jit(solution)/shard_map/product/pallas_call | solution.py:152
  39.2 0.7 %place.1.refs_3_.refs_8_ = bf16[256,256]{1,0:T(8,128)(2,1)S(1)} custom-call(s32[8]{0:T(128)S(1)} %copy-done.1, bf16[1,64,1024]{2,1,0:T(8,128)(2,1)S(1)} %get-tuple-element.56.after.refs_0_), custom_call_target="tpu_custom_call" | custom-call | tf_op jit(solution)/shard_map/place/pallas_call | solution.py:221
  39.9 0.1 totals.10
  40.0 3.3 %collective-permute-done.11.refs_1_ = bf16[2,64,1024]{2,1,0:T(8,128)(2,1)S(1)} collective-permute-done((bf16[2,64,1024]{2,1,0:T(8,128)(2,1)S(1)}, bf16[2,64,1024]{2,1,0:T(8,128)(2,1)S(1)}, u32[]{:S(2)}, u32[]{:S(2)}) %collective-permute-start.11) | collective-permute-done | bytes 262176 | tf_op jit(solution)/shard_map/ppermute | solution.py:266
  43.3 1.8 %collective-permute-start.12 = (bf16[1,64,1024]{2,1,0:T(8,128)(2,1)S(1)}, bf16[1,64,1024]{2,1,0:T(8,128)(2,1)S(1)}, u32[]{:S(2)}, u32[]{:S(2)}) collective-permute-start(bf16[1,64,1024]{2,1,0:T(8,128)(2,1)S(1)} %totals.11.refs_2_), channel_id=1, source_target_pairs={{0,2},{1,3},{2,0},{3,1},{4,6},{5,7},{6,4},{7,5},{8,10},{9,11},{10,... | collective-permute-start | bytes 393224 | tf_op jit(solution)/shard_map/ppermute | solution.py:266
  45.2 0.5 collective-permute-start.15
  45.7 1.0 %collective-permute-start.14 = (bf16[32,1024]{1,0:T(8,128)(2,1)S(1)}, bf16[32,1024]{1,0:T(8,128)(2,1)S(1)}, u32[]{:S(2)}, u32[]{:S(2)}) collective-permute-start(bf16[32,1024]{1,0:T(8,128)(2,1)S(1)} %get-tuple-element.61), channel_id=1, source_target_pairs={{0,8},{4,12},{8,0},{12,4},{16,24},{20,28},{24,16},{28,20},{1,9},{5... | collective-permute-start | bytes 196616 | tf_op jit(solution)/shard_map/ppermute | solution.py:263
  46.7 0.1 totals.13
  46.8 1.6 %collective-permute-start.16 = (bf16[32,1024]{1,0:T(8,128)(2,1)S(1)}, bf16[32,1024]{1,0:T(8,128)(2,1)S(1)}, u32[]{:S(2)}, u32[]{:S(2)}) collective-permute-start(bf16[32,1024]{1,0:T(8,128)(2,1)S(1)} %get-tuple-element.62), channel_id=1, source_target_pairs={{0,16},{4,20},{8,24},{12,28},{16,0},{20,4},{24,8},{28,12},{1,17},{... | collective-permute-start | bytes 196616 | tf_op jit(solution)/shard_map/ppermute | solution.py:263
  48.4 0.2 collective-permute-start.17
  48.5 2.4 %collective-permute-done.14.refs_4_.refs_2_ = bf16[32,1024]{1,0:T(8,128)(2,1)S(1)} collective-permute-done((bf16[32,1024]{1,0:T(8,128)(2,1)S(1)}, bf16[32,1024]{1,0:T(8,128)(2,1)S(1)}, u32[]{:S(2)}, u32[]{:S(2)}) %collective-permute-start.14) | collective-permute-done | bytes 65568 | tf_op jit(solution)/shard_map/ppermute | solution.py:263
  51.0 1.1 %collective-permute-start.20 = (bf16[1,64,1024]{2,1,0:T(8,128)(2,1)S(1)}, bf16[1,64,1024]{2,1,0:T(8,128)(2,1)S(1)}, u32[]{:S(2)}, u32[]{:S(2)}) collective-permute-start(bf16[1,64,1024]{2,1,0:T(8,128)(2,1)S(1)} %totals.12.refs_3_), channel_id=1, source_target_pairs={{0,2},{1,3},{2,0},{3,1},{4,6},{5,7},{6,4},{7,5},{8,10},{9,11},{10,... | collective-permute-start | bytes 393224 | tf_op jit(solution)/shard_map/ppermute | solution.py:266
  52.1 0.4 collective-permute-done.17.refs_7_.refs_5_
  52.5 0.1 totals.14.refs_3_
  52.6 2.5 %collective-permute-start.18 = (bf16[2,32,1024]{2,1,0:T(8,128)(2,1)S(1)}, bf16[2,32,1024]{2,1,0:T(8,128)(2,1)S(1)}, u32[]{:S(2)}, u32[]{:S(2)}) collective-permute-start(bf16[2,32,1024]{2,1,0:T(8,128)(2,1)S(1)} %bitcast.7), channel_id=1, source_target_pairs={{0,24},{4,28},{8,16},{12,20},{16,8},{20,12},{24,0},{28,4},{1,25},{... | collective-permute-start | bytes 393224 | tf_op jit(solution)/shard_map/ppermute | solution.py:263
  55.0 5.1 %collective-permute-done.20.refs_2_ = bf16[1,64,1024]{2,1,0:T(8,128)(2,1)S(1)} collective-permute-done((bf16[1,64,1024]{2,1,0:T(8,128)(2,1)S(1)}, bf16[1,64,1024]{2,1,0:T(8,128)(2,1)S(1)}, u32[]{:S(2)}, u32[]{:S(2)}) %collective-permute-start.20) | collective-permute-done | bytes 131104 | tf_op jit(solution)/shard_map/ppermute | solution.py:266
  60.1 0.1 totals.15
  60.2 0.1 collective-permute-start.21
  60.3 0.5 collective-permute-start.19
  60.8 0.7 %collective-permute-done.21.refs_7_ = bf16[32,1024]{1,0:T(8,128)(2,1)S(1)} collective-permute-done((bf16[32,1024]{1,0:T(8,128)(2,1)S(1)}, bf16[32,1024]{1,0:T(8,128)(2,1)S(1)}, u32[]{:S(2)}, u32[]{:S(2)}) %collective-permute-start.21) | collective-permute-done | bytes 65568 | tf_op jit(solution)/shard_map/ppermute | solution.py:263
  61.5 0.2 collective-permute-done.19.refs_1_
  61.7 1.1 %order.1 = bf16[256,1024]{1,0:T(8,128)(2,1)} custom-call(bf16[2,32,1024]{2,1,0:T(8,128)(2,1)S(1)} %collective-permute-done.18.refs_0_, bf16[32,1024]{1,0:T(8,128)(2,1)S(1)} %collective-permute-done.19.refs_1_, bf16[32,1024]{1,0:T(8,128)(2,1)S(1)} %collective-permute-done.14.refs_4_.refs_2_, bf16[32,1024]{1,0:T(8,128)(2,1)S(1)} %collective-permute-done.15.refs_5_.refs_3_, ...), custom_call_target="tpu_custom_call" | custom-call | tf_op jit(solution)/shard_map/order/pallas_call | solution.py:243
  (19 shorter events, 0.2 us)
Async XLA Ops:
  0.7 0.9 %copy-start = (bf16[32,4,1024]{2,1,0:T(4,128)(2,1)S(1)}, bf16[32,4,1024]{2,1,0:T(4,128)(2,1)}, u32[]{:S(2)}) copy-start(bf16[32,4,1024]{2,1,0:T(4,128)(2,1)} %amps.1) | copy-start | bytes 786436
  2.5 4.9 %collective-permute-start = (bf16[2,32,1024]{2,1,0:T(8,128)(2,1)S(1)}, bf16[2,32,1024]{2,1,0:T(8,128)(2,1)S(1)}, u32[]{:S(2)}, u32[]{:S(2)}) collective-permute-start(bf16[2,32,1024]{2,1,0:T(8,128)(2,1)S(1)} %get-tuple-element.36), channel_id=1, source_target_pairs={{0,4},{4,0},{8,12},{12,8},{16,20},{20,16},{24,28},{28,24},{1,5},{5... | collective-permute-start | bytes 393224 | tf_op jit(solution)/shard_map/ppermute | solution.py:263
  3.0 10.9 %collective-permute-start.2 = (bf16[2,32,1024]{2,1,0:T(8,128)(2,1)S(1)}, bf16[2,32,1024]{2,1,0:T(8,128)(2,1)S(1)}, u32[]{:S(2)}, u32[]{:S(2)}) collective-permute-start(bf16[2,32,1024]{2,1,0:T(8,128)(2,1)S(1)} %get-tuple-element.38), channel_id=1, source_target_pairs={{0,8},{4,12},{8,0},{12,4},{16,24},{20,28},{24,16},{28,20},{1,9},{5... | collective-permute-start | bytes 393224 | tf_op jit(solution)/shard_map/ppermute | solution.py:263
  5.6 8.3 %collective-permute-start.3 = (bf16[2,32,1024]{2,1,0:T(8,128)(2,1)S(1)}, bf16[2,32,1024]{2,1,0:T(8,128)(2,1)S(1)}, u32[]{:S(2)}, u32[]{:S(2)}) collective-permute-start(bf16[2,32,1024]{2,1,0:T(8,128)(2,1)S(1)} %get-tuple-element.39), channel_id=1, source_target_pairs={{0,12},{4,8},{8,4},{12,0},{16,28},{20,24},{24,20},{28,16},{1,13},{... | collective-permute-start | bytes 393224 | tf_op jit(solution)/shard_map/ppermute | solution.py:263
  5.7 8.2 %collective-permute-start.4 = (bf16[2,32,1024]{2,1,0:T(8,128)(2,1)S(1)}, bf16[2,32,1024]{2,1,0:T(8,128)(2,1)S(1)}, u32[]{:S(2)}, u32[]{:S(2)}) collective-permute-start(bf16[2,32,1024]{2,1,0:T(8,128)(2,1)S(1)} %get-tuple-element.40), channel_id=1, source_target_pairs={{0,16},{4,20},{8,24},{12,28},{16,0},{20,4},{24,8},{28,12},{1,17},{... | collective-permute-start | bytes 393224 | tf_op jit(solution)/shard_map/ppermute | solution.py:263
  7.4 6.5 %collective-permute-start.5 = (bf16[2,32,1024]{2,1,0:T(8,128)(2,1)S(1)}, bf16[2,32,1024]{2,1,0:T(8,128)(2,1)S(1)}, u32[]{:S(2)}, u32[]{:S(2)}) collective-permute-start(bf16[2,32,1024]{2,1,0:T(8,128)(2,1)S(1)} %get-tuple-element.41), channel_id=1, source_target_pairs={{0,20},{4,16},{8,28},{12,24},{16,4},{20,0},{24,12},{28,8},{1,21},{... | collective-permute-start | bytes 393224 | tf_op jit(solution)/shard_map/ppermute | solution.py:263
  12.1 9.5 %collective-permute-start.1 = (bf16[2,64,1024]{2,1,0:T(8,128)(2,1)S(1)}, bf16[2,64,1024]{2,1,0:T(8,128)(2,1)S(1)}, u32[]{:S(2)}, u32[]{:S(2)}) collective-permute-start(bf16[2,64,1024]{2,1,0:T(8,128)(2,1)S(1)} %get-tuple-element.37.refs_0_), channel_id=1, source_target_pairs={{0,1},{1,0},{2,3},{3,2},{4,5},{5,4},{6,7},{7,6},{8,9},{9,8},{10,11... | collective-permute-start | bytes 786440 | tf_op jit(solution)/shard_map/ppermute | solution.py:266
  17.0 9.9 %collective-permute-start.7 = (bf16[2,64,1024]{2,1,0:T(8,128)(2,1)S(1)}, bf16[2,64,1024]{2,1,0:T(8,128)(2,1)S(1)}, u32[]{:S(2)}, u32[]{:S(2)}) collective-permute-start(bf16[2,64,1024]{2,1,0:T(8,128)(2,1)S(1)} %get-tuple-element.49), channel_id=1, source_target_pairs={{0,1},{1,0},{2,3},{3,2},{4,5},{5,4},{6,7},{7,6},{8,9},{9,8},{10,11... | collective-permute-start | bytes 786440 | tf_op jit(solution)/shard_map/ppermute | solution.py:266
  18.7 11.1 %collective-permute-start.8 = (bf16[2,32,1024]{2,1,0:T(8,128)(2,1)S(1)}, bf16[2,32,1024]{2,1,0:T(8,128)(2,1)S(1)}, u32[]{:S(2)}, u32[]{:S(2)}) collective-permute-start(bf16[2,32,1024]{2,1,0:T(8,128)(2,1)S(1)} %get-tuple-element.50), channel_id=1, source_target_pairs={{0,24},{4,28},{8,16},{12,20},{16,8},{20,12},{24,0},{28,4},{1,25},{... | collective-permute-start | bytes 393224 | tf_op jit(solution)/shard_map/ppermute | solution.py:263
  21.1 8.6 %collective-permute-start.9 = (bf16[2,32,1024]{2,1,0:T(8,128)(2,1)S(1)}, bf16[2,32,1024]{2,1,0:T(8,128)(2,1)S(1)}, u32[]{:S(2)}, u32[]{:S(2)}) collective-permute-start(bf16[2,32,1024]{2,1,0:T(8,128)(2,1)S(1)} %get-tuple-element.51), channel_id=1, source_target_pairs={{0,28},{4,24},{8,20},{12,16},{16,12},{20,8},{24,4},{28,0},{1,29},{... | collective-permute-start | bytes 393224 | tf_op jit(solution)/shard_map/ppermute | solution.py:263
  21.1 14.2 %collective-permute-start.6 = (bf16[2,64,1024]{2,1,0:T(8,128)(2,1)S(1)}, bf16[2,64,1024]{2,1,0:T(8,128)(2,1)S(1)}, u32[]{:S(2)}, u32[]{:S(2)}) collective-permute-start(bf16[2,64,1024]{2,1,0:T(8,128)(2,1)S(1)} %get-tuple-element.47), channel_id=1, source_target_pairs={{0,1},{1,0},{2,3},{3,2},{4,5},{5,4},{6,7},{7,6},{8,9},{9,8},{10,11... | collective-permute-start | bytes 786440 | tf_op jit(solution)/shard_map/ppermute | solution.py:266
  26.9 9.6 %collective-permute-start.10 = (bf16[1,64,1024]{2,1,0:T(8,128)(2,1)S(1)}, bf16[1,64,1024]{2,1,0:T(8,128)(2,1)S(1)}, u32[]{:S(2)}, u32[]{:S(2)}) collective-permute-start(bf16[1,64,1024]{2,1,0:T(8,128)(2,1)S(1)} %totals.8.refs_0_), channel_id=1, source_target_pairs={{0,2},{1,3},{2,0},{3,1},{4,6},{5,7},{6,4},{7,5},{8,10},{9,11},{10,... | collective-permute-start | bytes 393224 | tf_op jit(solution)/shard_map/ppermute | solution.py:266
  32.6 6.6 %copy-start.1 = (s32[8]{0:T(128)S(1)}, s32[8]{0:T(128)}, u32[]{:S(2)}) copy-start(s32[8]{0:T(128)} %q_owner.1) | copy-start | bytes 100
  32.6 10.7 %collective-permute-start.11 = (bf16[2,64,1024]{2,1,0:T(8,128)(2,1)S(1)}, bf16[2,64,1024]{2,1,0:T(8,128)(2,1)S(1)}, u32[]{:S(2)}, u32[]{:S(2)}) collective-permute-start(bf16[2,64,1024]{2,1,0:T(8,128)(2,1)S(1)} %get-tuple-element.52.refs_2_), channel_id=1, source_target_pairs={{0,1},{1,0},{2,3},{3,2},{4,5},{5,4},{6,7},{7,6},{8,9},{9,8},{10,11... | collective-permute-start | bytes 786440 | tf_op jit(solution)/shard_map/ppermute | solution.py:266
  35.4 11.4 %collective-permute-start.13 = (bf16[1,64,1024]{2,1,0:T(8,128)(2,1)S(1)}, bf16[1,64,1024]{2,1,0:T(8,128)(2,1)S(1)}, u32[]{:S(2)}, u32[]{:S(2)}) collective-permute-start(bf16[1,64,1024]{2,1,0:T(8,128)(2,1)S(1)} %totals.9.refs_0_), channel_id=1, source_target_pairs={{0,2},{1,3},{2,0},{3,1},{4,6},{5,7},{6,4},{7,5},{8,10},{9,11},{10,... | collective-permute-start | bytes 393224 | tf_op jit(solution)/shard_map/ppermute | solution.py:266
  43.3 9.2 %collective-permute-start.12 = (bf16[1,64,1024]{2,1,0:T(8,128)(2,1)S(1)}, bf16[1,64,1024]{2,1,0:T(8,128)(2,1)S(1)}, u32[]{:S(2)}, u32[]{:S(2)}) collective-permute-start(bf16[1,64,1024]{2,1,0:T(8,128)(2,1)S(1)} %totals.11.refs_2_), channel_id=1, source_target_pairs={{0,2},{1,3},{2,0},{3,1},{4,6},{5,7},{6,4},{7,5},{8,10},{9,11},{10,... | collective-permute-start | bytes 393224 | tf_op jit(solution)/shard_map/ppermute | solution.py:266
  45.2 7.0 %collective-permute-start.15 = (bf16[32,1024]{1,0:T(8,128)(2,1)S(1)}, bf16[32,1024]{1,0:T(8,128)(2,1)S(1)}, u32[]{:S(2)}, u32[]{:S(2)}) collective-permute-start(bf16[32,1024]{1,0:T(8,128)(2,1)S(1)} %get-tuple-element.57.refs_2_), channel_id=1, source_target_pairs={{0,12},{4,8},{8,4},{12,0},{16,28},{20,24},{24,20},{28,16},{1,13},{... | collective-permute-start | bytes 196616 | tf_op jit(solution)/shard_map/ppermute | solution.py:263
  45.7 5.3 %collective-permute-start.14 = (bf16[32,1024]{1,0:T(8,128)(2,1)S(1)}, bf16[32,1024]{1,0:T(8,128)(2,1)S(1)}, u32[]{:S(2)}, u32[]{:S(2)}) collective-permute-start(bf16[32,1024]{1,0:T(8,128)(2,1)S(1)} %get-tuple-element.61), channel_id=1, source_target_pairs={{0,8},{4,12},{8,0},{12,4},{16,24},{20,28},{24,16},{28,20},{1,9},{5... | collective-permute-start | bytes 196616 | tf_op jit(solution)/shard_map/ppermute | solution.py:263
  46.8 5.3 %collective-permute-start.16 = (bf16[32,1024]{1,0:T(8,128)(2,1)S(1)}, bf16[32,1024]{1,0:T(8,128)(2,1)S(1)}, u32[]{:S(2)}, u32[]{:S(2)}) collective-permute-start(bf16[32,1024]{1,0:T(8,128)(2,1)S(1)} %get-tuple-element.62), channel_id=1, source_target_pairs={{0,16},{4,20},{8,24},{12,28},{16,0},{20,4},{24,8},{28,12},{1,17},{... | collective-permute-start | bytes 196616 | tf_op jit(solution)/shard_map/ppermute | solution.py:263
  48.4 4.1 %collective-permute-start.17 = (bf16[32,1024]{1,0:T(8,128)(2,1)S(1)}, bf16[32,1024]{1,0:T(8,128)(2,1)S(1)}, u32[]{:S(2)}, u32[]{:S(2)}) collective-permute-start(bf16[32,1024]{1,0:T(8,128)(2,1)S(1)} %get-tuple-element.60.refs_3_), channel_id=1, source_target_pairs={{0,20},{4,16},{8,28},{12,24},{16,4},{20,0},{24,12},{28,8},{1,21},{... | collective-permute-start | bytes 196616 | tf_op jit(solution)/shard_map/ppermute | solution.py:263
  51.0 9.2 %collective-permute-start.20 = (bf16[1,64,1024]{2,1,0:T(8,128)(2,1)S(1)}, bf16[1,64,1024]{2,1,0:T(8,128)(2,1)S(1)}, u32[]{:S(2)}, u32[]{:S(2)}) collective-permute-start(bf16[1,64,1024]{2,1,0:T(8,128)(2,1)S(1)} %totals.12.refs_3_), channel_id=1, source_target_pairs={{0,2},{1,3},{2,0},{3,1},{4,6},{5,7},{6,4},{7,5},{8,10},{9,11},{10,... | collective-permute-start | bytes 393224 | tf_op jit(solution)/shard_map/ppermute | solution.py:266
  52.6 7.7 %collective-permute-start.18 = (bf16[2,32,1024]{2,1,0:T(8,128)(2,1)S(1)}, bf16[2,32,1024]{2,1,0:T(8,128)(2,1)S(1)}, u32[]{:S(2)}, u32[]{:S(2)}) collective-permute-start(bf16[2,32,1024]{2,1,0:T(8,128)(2,1)S(1)} %bitcast.7), channel_id=1, source_target_pairs={{0,24},{4,28},{8,16},{12,20},{16,8},{20,12},{24,0},{28,4},{1,25},{... | collective-permute-start | bytes 393224 | tf_op jit(solution)/shard_map/ppermute | solution.py:263
  60.2 1.3 %collective-permute-start.21 = (bf16[32,1024]{1,0:T(8,128)(2,1)S(1)}, bf16[32,1024]{1,0:T(8,128)(2,1)S(1)}, u32[]{:S(2)}, u32[]{:S(2)}) collective-permute-start(bf16[32,1024]{1,0:T(8,128)(2,1)S(1)} %get-tuple-element.64), channel_id=1, source_target_pairs={{0,4},{4,0},{8,12},{12,8},{16,20},{20,16},{24,28},{28,24},{1,5},{5... | collective-permute-start | bytes 196616 | tf_op jit(solution)/shard_map/ppermute | solution.py:263
  60.3 1.5 %collective-permute-start.19 = (bf16[32,1024]{1,0:T(8,128)(2,1)S(1)}, bf16[32,1024]{1,0:T(8,128)(2,1)S(1)}, u32[]{:S(2)}, u32[]{:S(2)}) collective-permute-start(bf16[32,1024]{1,0:T(8,128)(2,1)S(1)} %slice_bitcast_fusion), channel_id=1, source_target_pairs={{0,4},{4,0},{8,12},{12,8},{16,20},{20,16},{24,28},{28,24},{1,5},{5... | collective-permute-start | bytes 196616 | tf_op jit(solution)/shard_map/ppermute | solution.py:263
where the time goes:
time: 63 us; the launch traced here: 62.8 us
  starting transfers between devices  26.2 us (42%)
  Pallas kernels  17.8 us (28%)
  waiting for transfers between devices  17 us (27%)
  local copies, waits for them, and re-layouts  0.96 us (2%)
  other arithmetic  0.72 us (1%)
    pallas_call x6, Pallas kernels, product(): pl.pallas_call(functools.partial(product_kernel, plan), out_shape=[jax.Sh...  14.9 us
    ppermute x14, starting transfers between devices, swap(): return lax.ppermute(value, 'wide', [(w, w ^ j) for w in range(peers)])  13.7 us
    ppermute x8, waiting for transfers between devices, swap_line(): lax.ppermute(value, 'narrow', [(n, n ^ mask) for n in range(devices)])  13.3 us
    ppermute x8, starting transfers between devices, swap_line(): lax.ppermute(value, 'narrow', [(n, n ^ mask) for n in range(devices)])  12.4 us
    ppermute x14, waiting for transfers between devices, swap(): return lax.ppermute(value, 'wide', [(w, w ^ j) for w in range(peers)])  3.74 us
  transfers between devices with their start and end apart: 22, of which 8 were waited for; matrix products, arithmetic and copies ran while one was open for 0% of the time, Pallas kernels for 25%

commit v1 on v0

--- a/solution.py
+++ b/solution.py
@@ -316,13 +316,15 @@
     ready[first], sums[first] = later_steps(kept[first], come[first])
     outs, home_ints, _ = multiply(far, all_odd, odd_ints, (0,), after=[ready[first]])
     away.update(outs)
-    come.update((g, first_step(away[g])) for g in far)
     last = away[far[0]]
     for g in others:
         ready[g], sums[g] = later_steps(kept[g], come[g], [last])
         last = ready[g]
     outs, _ = multiply(far, all_middle, middle_ints, after=[last, sums[first][-1][0]])
     kept.update(outs)
+    for g in far:
+        sums[g] = [(swap_line(away[g][i : i + 1], r), 0) for i, r in enumerate(odd)]
+        sums[g] += [(swap_line(kept[g][i : i + 1], r), 0) for i, r in enumerate(middle)]
     own, _ = multiply(range(chips), (0,), home_ints, after=[kept[far[0]]])
     place = place_of(q_owner, peers * rows, own[0])
 
@@ -341,9 +343,8 @@
         return halves[1]
 
     last = close(first, [place])
-    for g in far + [0]:
-        ready[g], sums[g] = later_steps(kept[g], come[g], [last])
-        last = ready[g]
+    ready[0], sums[0] = later_steps(kept[0], come[0], [last])
+    last = ready[0]
     for g in others:
         last = close(g, [last])
     for g in far:

time: 63 us -> 67.6 us (1.073)
  waiting for transfers between devices: 17 us -> 22.4 us
  starting transfers between devices: 26.2 us -> 25.4 us
    ppermute x8 -> x9, waiting for transfers between devices: 13.3 us -> 16.6 us  [swap_line(): lax.ppermute(value, 'narrow', [(n, n ^ mask) for n in range(devices)])]
    ppermute x14, waiting for transfers between devices: 3.74 us -> 5.87 us  [swap(): return lax.ppermute(value, 'wide', [(w, w ^ j) for w in range(peers)])]
    ppermute x8 -> x9, starting transfers between devices: 12.4 us -> 11.6 us  [swap_line(): lax.ppermute(value, 'narrow', [(n, n ^ mask) for n in range(devices)])]
  transfers between devices with their start and end apart: 22 -> 23, of which waited for: 8 -> 11; matrix products, arithmetic and copies ran while one was open for 0% -> 0% of each run, Pallas kernels for 25% -> 24%
where the time goes in v1:
time: 67.6 us; the launch traced here: 67.5 us
  starting transfers between devices  25.4 us (38%)
  waiting for transfers between devices  22.4 us (33%)
  Pallas kernels  17.8 us (26%)
  local copies, waits for them, and re-layouts  0.98 us (1%)
  other arithmetic  0.72 us (1%)
    ppermute x9, waiting for transfers between devices, swap_line(): lax.ppermute(value, 'narrow', [(n, n ^ mask) for n in range(devices)])  16.6 us
    pallas_call x6, Pallas kernels, product(): pl.pallas_call(functools.partial(product_kernel, plan), out_shape=[jax.Sh...  14.9 us
    ppermute x14, starting transfers between devices, swap(): return lax.ppermute(value, 'wide', [(w, w ^ j) for w in range(peers)])  13.7 us
    ppermute x9, starting transfers between devices, swap_line(): lax.ppermute(value, 'narrow', [(n, n ^ mask) for n in range(devices)])  11.6 us
    ppermute x14, waiting for transfers between devices, swap(): return lax.ppermute(value, 'wide', [(w, w ^ j) for w in range(peers)])  5.87 us
  transfers between devices with their start and end apart: 23, of which 11 were waited for; matrix products, arithmetic and copies ran while one was open for 0% of the time, Pallas kernels for 24%

profile of v1, /device:TPU:0, one launch (start us, length us, event | category | flops | bytes accessed | tf_op | source)
XLA Modules:
  0.0 67.5 jit_solution(2104023249451720979)
XLA Ops:
  0.0 0.7 %pad_add_fusion.tables_from = s32[7,8]{1,0:T(8,128)S(1)} fusion(s32[1,8]{1,0:T(1,128)} %bitcast.8, s32[2,8]{1,0:T(2,128)} %bitcast.10, s32[4,8]{1,0:T(4,128)} %bitcast.9), kind=kLoop, calls=%fused_computation.1 | loop fusion | flops 112 | bytes 448 | tf_op jit(solution)/shard_map/concatenate | solution.py:46
  0.7 0.9 %copy-done = bf16[32,4,1024]{2,1,0:T(4,128)(2,1)S(1)} copy-done((bf16[32,4,1024]{2,1,0:T(4,128)(2,1)S(1)}, bf16[32,4,1024]{2,1,0:T(4,128)(2,1)}, u32[]{:S(2)}) %copy-start) | copy-done | bytes 262168
  1.7 0.8 %pick.1 = (bf16[2,32,1024]{2,1,0:T(8,128)(2,1)S(1)}, bf16[2,32,1024]{2,1,0:T(8,128)(2,1)S(1)}, bf16[2,32,1024]{2,1,0:T(8,128)(2,1)S(1)}, bf16[2,32,1024]{2,1,0:T...) custom-call(s32[7,8]{1,0:T(8,128)S(1)} %pad_add_fusion.tables_from, ...), custom_call_target="tpu_custom_call" | custom-call | tf_op jit(solution)/shard_map/pick/pallas_call | solution.py:48
  2.5 0.5 collective-permute-start
  3.0 2.6 %collective-permute-start.2 = (bf16[2,32,1024]{2,1,0:T(8,128)(2,1)S(1)}, bf16[2,32,1024]{2,1,0:T(8,128)(2,1)S(1)}, u32[]{:S(2)}, u32[]{:S(2)}) collective-permute-start(bf16[2,32,1024]{2,1,0:T(8,128)(2,1)S(1)} %get-tuple-element.38), channel_id=1, source_target_pairs={{0,8},{4,12},{8,0},{12,4},{16,24},{20,28},{24,16},{28,20},{1,9},{5... | collective-permute-start | bytes 393224 | tf_op jit(solution)/shard_map/ppermute | solution.py:263
  5.6 0.1 collective-permute-start.3
  5.7 1.8 %collective-permute-start.4 = (bf16[2,32,1024]{2,1,0:T(8,128)(2,1)S(1)}, bf16[2,32,1024]{2,1,0:T(8,128)(2,1)S(1)}, u32[]{:S(2)}, u32[]{:S(2)}) collective-permute-start(bf16[2,32,1024]{2,1,0:T(8,128)(2,1)S(1)} %get-tuple-element.40), channel_id=1, source_target_pairs={{0,16},{4,20},{8,24},{12,28},{16,0},{20,4},{24,8},{28,12},{1,17},{... | collective-permute-start | bytes 393224 | tf_op jit(solution)/shard_map/ppermute | solution.py:263
  7.4 0.0 collective-permute-done.refs_1_.refs_2_
  7.4 4.7 %product.6 = (bf16[2,64,1024]{2,1,0:T(8,128)(2,1)S(1)}, bf16[2,2,1024,1024]{3,2,1,0:T(8,128)(2,1)S(1)}) custom-call(bf16[2,32,1024]{2,1,0:T(8,128)(2,1)S(1)} %get-tuple-element.35.refs_0_.refs_1_, bf16[2,32,1024]{2,1,0:T(8,128)(2,1)S(1)} %collective-permute-done.refs_1_.refs_2_, bf16[1,2,4096,1024]{3,2,1,0:T(8,128)(2,1)} %refs_4_.1), custom_call_target="tpu_custom_call" | custom-call | flops 2147483648 | bytes 8388608 | tf_op jit(solution)/shard_map/product/pallas_call | solution.py:152
  12.1 1.8 %collective-permute-start.1 = (bf16[2,64,1024]{2,1,0:T(8,128)(2,1)S(1)}, bf16[2,64,1024]{2,1,0:T(8,128)(2,1)S(1)}, u32[]{:S(2)}, u32[]{:S(2)}) collective-permute-start(bf16[2,64,1024]{2,1,0:T(8,128)(2,1)S(1)} %get-tuple-element.37.refs_0_), channel_id=1, source_target_pairs={{0,1},{1,0},{2,3},{3,2},{4,5},{5,4},{6,7},{7,6},{8,9},{9,8},{10,11... | collective-permute-start | bytes 786440 | tf_op jit(solution)/shard_map/ppermute | solution.py:266
  13.9 0.0 collective-permute-done.3.refs_2_.refs_4_
  13.9 0.0 collective-permute-done.4.refs_3_.refs_5_
  13.9 3.1 %product.7 = (bf16[2,64,1024]{2,1,0:T(8,128)(2,1)S(1)}, bf16[2,64,1024]{2,1,0:T(8,128)(2,1)S(1)}, bf16[1,2,1024,1024]{3,2,1,0:T(8,128)(2,1)S(1)}, bf16[2,32,1024...) custom-call(bf16[2,64,1024]{2,1,0:T(8,128)(2,1)S(1)} %get-tuple-element.37.refs_0_, ...), custom_call_target="tpu_custom_call", output_to_operand_aliasing={{3}: (7, {}), {4}: (8, {})} | custom-call | flops 2147483648 | bytes 8388608 | tf_op jit(solution)/shard_map/product/pallas_call | solution.py:152
  17.0 1.6 %collective-permute-start.7 = (bf16[2,64,1024]{2,1,0:T(8,128)(2,1)S(1)}, bf16[2,64,1024]{2,1,0:T(8,128)(2,1)S(1)}, u32[]{:S(2)}, u32[]{:S(2)}) collective-permute-start(bf16[2,64,1024]{2,1,0:T(8,128)(2,1)S(1)} %get-tuple-element.49), channel_id=1, source_target_pairs={{0,1},{1,0},{2,3},{3,2},{4,5},{5,4},{6,7},{7,6},{8,9},{9,8},{10,11... | collective-permute-start | bytes 786440 | tf_op jit(solution)/shard_map/ppermute | solution.py:266
  18.7 2.4 %collective-permute-start.8 = (bf16[2,32,1024]{2,1,0:T(8,128)(2,1)S(1)}, bf16[2,32,1024]{2,1,0:T(8,128)(2,1)S(1)}, u32[]{:S(2)}, u32[]{:S(2)}) collective-permute-start(bf16[2,32,1024]{2,1,0:T(8,128)(2,1)S(1)} %get-tuple-element.50), channel_id=1, source_target_pairs={{0,24},{4,28},{8,16},{12,20},{16,8},{20,12},{24,0},{28,4},{1,25},{... | collective-permute-start | bytes 393224 | tf_op jit(solution)/shard_map/ppermute | solution.py:263
  21.1 0.5 collective-permute-start.6
  21.6 1.5 %product.8 = (bf16[1,64,1024]{2,1,0:T(8,128)(2,1)S(1)}, bf16[1,64,1024]{2,1,0:T(8,128)(2,1)S(1)}, bf16[1,64,1024]{2,1,0:T(8,128)(2,1)S(1)}) custom-call(bf16[2,64,1024]{2,1,0:T(8,128)(2,1)S(1)} %collective-permute-done.1.refs_0_.refs_1_, bf16[2,32,1024]{2,1,0:T(8,128)(2,1)S(1)} %get-tuple-element.35.refs_0_.refs_1_, ...), custom_call_target="tpu_custom_call" | custom-call | flops 1073741824 | bytes 4194304 | tf_op jit(solution)/shard_map/product/pallas_call | solution.py:152
  23.1 3.8 %collective-permute-done.7.refs_1_ = bf16[2,64,1024]{2,1,0:T(8,128)(2,1)S(1)} collective-permute-done((bf16[2,64,1024]{2,1,0:T(8,128)(2,1)S(1)}, bf16[2,64,1024]{2,1,0:T(8,128)(2,1)S(1)}, u32[]{:S(2)}, u32[]{:S(2)}) %collective-permute-start.7) | collective-permute-done | bytes 262176 | tf_op jit(solution)/shard_map/ppermute | solution.py:266
  26.9 2.8 %collective-permute-start.10 = (bf16[1,64,1024]{2,1,0:T(8,128)(2,1)S(1)}, bf16[1,64,1024]{2,1,0:T(8,128)(2,1)S(1)}, u32[]{:S(2)}, u32[]{:S(2)}) collective-permute-start(bf16[1,64,1024]{2,1,0:T(8,128)(2,1)S(1)} %totals.7.refs_0_), channel_id=1, source_target_pairs={{0,2},{1,3},{2,0},{3,1},{4,6},{5,7},{6,4},{7,5},{8,10},{9,11},{10,... | collective-permute-start | bytes 393224 | tf_op jit(solution)/shard_map/ppermute | solution.py:266
  29.7 2.8 %product.9 = (bf16[2,64,1024]{2,1,0:T(8,128)(2,1)S(1)}, bf16[1,2,1024,1024]{3,2,1,0:T(8,128)(2,1)S(1)}) custom-call(bf16[1,64,1024]{2,1,0:T(8,128)(2,1)S(1)} %totals.7.refs_0_, bf16[2,32,1024]{2,1,0:T(8,128)(2,1)S(1)} %collective-permute-done.8.refs_1_.refs_2_.refs_7_, bf16[2,32,1024]{2,1,0:T(8,128)(2,1)S(1)} %collective-permute-done.9.refs_2_.refs_3_.refs_8_, ...), custom_call_target="tpu_custom_call" | custom-call | flops 2147483648 | bytes 8388608 | tf_op jit(solution)/shard_map/product/pallas_call | solution.py:152
  32.6 0.0 copy-start.1
  32.6 1.4 %collective-permute-start.12 = (bf16[1,64,1024]{2,1,0:T(8,128)(2,1)S(1)}, bf16[1,64,1024]{2,1,0:T(8,128)(2,1)S(1)}, u32[]{:S(2)}, u32[]{:S(2)}) collective-permute-start(bf16[1,64,1024]{2,1,0:T(8,128)(2,1)S(1)} %get-tuple-element.65), channel_id=1, source_target_pairs={{0,3},{1,2},{2,1},{3,0},{4,7},{5,6},{6,5},{7,4},{8,11},{9,10},{10,... | collective-permute-start | bytes 393224 | tf_op jit(solution)/shard_map/ppermute | solution.py:266
  34.0 0.3 collective-permute-start.11
  34.4 0.5 collective-permute-done.6.refs_1_
  34.9 2.3 %collective-permute-start.14 = (bf16[1,64,1024]{2,1,0:T(8,128)(2,1)S(1)}, bf16[1,64,1024]{2,1,0:T(8,128)(2,1)S(1)}, u32[]{:S(2)}, u32[]{:S(2)}) collective-permute-start(bf16[1,64,1024]{2,1,0:T(8,128)(2,1)S(1)} %totals.8.refs_0_), channel_id=1, source_target_pairs={{0,2},{1,3},{2,0},{3,1},{4,6},{5,7},{6,4},{7,5},{8,10},{9,11},{10,... | collective-permute-start | bytes 393224 | tf_op jit(solution)/shard_map/ppermute | solution.py:266
  37.2 1.4 %product.10.refs_0_ = bf16[1,64,1024]{2,1,0:T(8,128)(2,1)S(1)} custom-call(bf16[1,64,1024]{2,1,0:T(8,128)(2,1)S(1)} %totals.8.refs_0_, bf16[1,64,1024]{2,1,0:T(8,128)(2,1)S(1)} %collective-permute-done.10.refs_1_.refs_2_, bf16[2,32,1024]{2,1,0:T(8,128)(2,1)S(1)} %collective-permute-done.8.refs_1_.refs_2_.refs_7_, ...), custom_call_target="tpu_custom_call" | custom-call | flops 1073741824 | bytes 4194304 | tf_op jit(solution)/shard_map/product/pallas_call | solution.py:152
  38.6 0.9 %collective-permute-start.13 = (bf16[1,64,1024]{2,1,0:T(8,128)(2,1)S(1)}, bf16[1,64,1024]{2,1,0:T(8,128)(2,1)S(1)}, u32[]{:S(2)}, u32[]{:S(2)}) collective-permute-start(bf16[1,64,1024]{2,1,0:T(8,128)(2,1)S(1)} %product.10.refs_0_), channel_id=1, source_target_pairs={{0,2},{1,3},{2,0},{3,1},{4,6},{5,7},{6,4},{7,5},{8,10},{9,11},{10,... | collective-permute-start | bytes 393224 | tf_op jit(solution)/shard_map/ppermute | solution.py:266
  39.5 1.3 %product.11 = (bf16[1,64,1024]{2,1,0:T(8,128)(2,1)S(1)}, bf16[1,64,1024]{2,1,0:T(8,128)(2,1)S(1)}, bf16[1,64,1024]{2,1,0:T(8,128)(2,1)S(1)}, bf16[1,64,1024]{2,1,0:T(8,128)(2,1)S(1)}) custom-call(bf16[1,64,1024]{2,1,0:T(8,128)(2,1)S(1)} %product.10.refs_0_, bf16[2,32,1024]{2,1,0:T(8,128)(2,1)S(1)} %get-tuple-element.35.refs_0_.refs_1_, ...), custom_call_target="tpu_custom_call" | custom-call | flops 1073741824 | bytes 4194304 | tf_op jit(solution)/shard_map/product/pallas_call | solution.py:152
  40.8 0.7 %place.1.refs_3_.refs_8_ = bf16[256,256]{1,0:T(8,128)(2,1)S(1)} custom-call(s32[8]{0:T(128)S(1)} %copy-done.1, bf16[1,64,1024]{2,1,0:T(8,128)(2,1)S(1)} %get-tuple-element.58.after.refs_0_), custom_call_target="tpu_custom_call" | custom-call | tf_op jit(solution)/shard_map/place/pallas_call | solution.py:221
  41.5 0.1 totals.9
  41.6 9.5 %collective-permute-done.14.refs_2_ = bf16[1,64,1024]{2,1,0:T(8,128)(2,1)S(1)} collective-permute-done((bf16[1,64,1024]{2,1,0:T(8,128)(2,1)S(1)}, bf16[1,64,1024]{2,1,0:T(8,128)(2,1)S(1)}, u32[]{:S(2)}, u32[]{:S(2)}) %collective-permute-start.14) | collective-permute-done | bytes 131104 | tf_op jit(solution)/shard_map/ppermute | solution.py:266
  51.2 0.1 totals.11
  51.2 1.6 %collective-permute-start.17 = (bf16[32,1024]{1,0:T(8,128)(2,1)S(1)}, bf16[32,1024]{1,0:T(8,128)(2,1)S(1)}, u32[]{:S(2)}, u32[]{:S(2)}) collective-permute-start(bf16[32,1024]{1,0:T(8,128)(2,1)S(1)} %get-tuple-element.62), channel_id=1, source_target_pairs={{0,16},{4,20},{8,24},{12,28},{16,0},{20,4},{24,8},{28,12},{1,17},{... | collective-permute-start | bytes 196616 | tf_op jit(solution)/shard_map/ppermute | solution.py:263
  52.8 1.5 %collective-permute-start.15 = (bf16[32,1024]{1,0:T(8,128)(2,1)S(1)}, bf16[32,1024]{1,0:T(8,128)(2,1)S(1)}, u32[]{:S(2)}, u32[]{:S(2)}) collective-permute-start(bf16[32,1024]{1,0:T(8,128)(2,1)S(1)} %get-tuple-element.61), channel_id=1, source_target_pairs={{0,8},{4,12},{8,0},{12,4},{16,24},{20,28},{24,16},{28,20},{1,9},{5... | collective-permute-start | bytes 196616 | tf_op jit(solution)/shard_map/ppermute | solution.py:263
  54.3 0.5 collective-permute-start.16
  54.8 0.8 %collective-permute-done.17.refs_7_.refs_4_ = bf16[32,1024]{1,0:T(8,128)(2,1)S(1)} collective-permute-done((bf16[32,1024]{1,0:T(8,128)(2,1)S(1)}, bf16[32,1024]{1,0:T(8,128)(2,1)S(1)}, u32[]{:S(2)}, u32[]{:S(2)}) %collective-permute-start.17) | collective-permute-done | bytes 65568 | tf_op jit(solution)/shard_map/ppermute | solution.py:263
  55.6 1.5 %collective-permute-done.18.refs_8_.refs_5_ = bf16[32,1024]{1,0:T(8,128)(2,1)S(1)} collective-permute-done((bf16[32,1024]{1,0:T(8,128)(2,1)S(1)}, bf16[32,1024]{1,0:T(8,128)(2,1)S(1)}, u32[]{:S(2)}, u32[]{:S(2)}) %collective-permute-start.18) | collective-permute-done | bytes 65568 | tf_op jit(solution)/shard_map/ppermute | solution.py:263
  57.0 0.5 collective-permute-done.15.refs_5_.refs_2_
  57.6 0.9 %collective-permute-done.16.refs_6_.refs_3_ = bf16[32,1024]{1,0:T(8,128)(2,1)S(1)} collective-permute-done((bf16[32,1024]{1,0:T(8,128)(2,1)S(1)}, bf16[32,1024]{1,0:T(8,128)(2,1)S(1)}, u32[]{:S(2)}, u32[]{:S(2)}) %collective-permute-start.16) | collective-permute-done | bytes 65568 | tf_op jit(solution)/shard_map/ppermute | solution.py:263
  58.5 0.1 totals.12.refs_3_
  58.6 2.7 %collective-permute-start.19 = (bf16[2,32,1024]{2,1,0:T(8,128)(2,1)S(1)}, bf16[2,32,1024]{2,1,0:T(8,128)(2,1)S(1)}, u32[]{:S(2)}, u32[]{:S(2)}) collective-permute-start(bf16[2,32,1024]{2,1,0:T(8,128)(2,1)S(1)} %bitcast.7), channel_id=1, source_target_pairs={{0,24},{4,28},{8,16},{12,20},{16,8},{20,12},{24,0},{28,4},{1,25},{... | collective-permute-start | bytes 393224 | tf_op jit(solution)/shard_map/ppermute | solution.py:263
  61.3 2.8 %collective-permute-done.21.refs_2_ = bf16[1,64,1024]{2,1,0:T(8,128)(2,1)S(1)} collective-permute-done((bf16[1,64,1024]{2,1,0:T(8,128)(2,1)S(1)}, bf16[1,64,1024]{2,1,0:T(8,128)(2,1)S(1)}, u32[]{:S(2)}, u32[]{:S(2)}) %collective-permute-start.21) | collective-permute-done | bytes 131104 | tf_op jit(solution)/shard_map/ppermute | solution.py:266
  64.1 0.1 totals.13
  64.1 0.1 collective-permute-start.22
  64.2 0.9 %collective-permute-done.19.refs_0_ = bf16[2,32,1024]{2,1,0:T(8,128)(2,1)S(1)} collective-permute-done((bf16[2,32,1024]{2,1,0:T(8,128)(2,1)S(1)}, bf16[2,32,1024]{2,1,0:T(8,128)(2,1)S(1)}, u32[]{:S(2)}, u32[]{:S(2)}) %collective-permute-start.19) | collective-permute-done | bytes 131104 | tf_op jit(solution)/shard_map/ppermute | solution.py:263
  65.1 0.3 collective-permute-done.22.refs_7_
  65.5 0.9 %collective-permute-done.20.refs_1_ = bf16[32,1024]{1,0:T(8,128)(2,1)S(1)} collective-permute-done((bf16[32,1024]{1,0:T(8,128)(2,1)S(1)}, bf16[32,1024]{1,0:T(8,128)(2,1)S(1)}, u32[]{:S(2)}, u32[]{:S(2)}) %collective-permute-start.20) | collective-permute-done | bytes 65568 | tf_op jit(solution)/shard_map/ppermute | solution.py:263
  66.4 1.1 %order.1 = bf16[256,1024]{1,0:T(8,128)(2,1)} custom-call(bf16[2,32,1024]{2,1,0:T(8,128)(2,1)S(1)} %collective-permute-done.19.refs_0_, bf16[32,1024]{1,0:T(8,128)(2,1)S(1)} %collective-permute-done.20.refs_1_, bf16[32,1024]{1,0:T(8,128)(2,1)S(1)} %collective-permute-done.15.refs_5_.refs_2_, bf16[32,1024]{1,0:T(8,128)(2,1)S(1)} %collective-permute-done.16.refs_6_.refs_3_, ...), custom_call_target="tpu_custom_call" | custom-call | tf_op jit(solution)/shard_map/order/pallas_call | solution.py:243
  (21 shorter events, 0.2 us)
Async XLA Ops:
  0.7 0.9 %copy-start = (bf16[32,4,1024]{2,1,0:T(4,128)(2,1)S(1)}, bf16[32,4,1024]{2,1,0:T(4,128)(2,1)}, u32[]{:S(2)}) copy-start(bf16[32,4,1024]{2,1,0:T(4,128)(2,1)} %amps.1) | copy-start | bytes 786436
  2.5 4.9 %collective-permute-start = (bf16[2,32,1024]{2,1,0:T(8,128)(2,1)S(1)}, bf16[2,32,1024]{2,1,0:T(8,128)(2,1)S(1)}, u32[]{:S(2)}, u32[]{:S(2)}) collective-permute-start(bf16[2,32,1024]{2,1,0:T(8,128)(2,1)S(1)} %get-tuple-element.36), channel_id=1, source_target_pairs={{0,4},{4,0},{8,12},{12,8},{16,20},{20,16},{24,28},{28,24},{1,5},{5... | collective-permute-start | bytes 393224 | tf_op jit(solution)/shard_map/ppermute | solution.py:263
  3.0 10.9 %collective-permute-start.2 = (bf16[2,32,1024]{2,1,0:T(8,128)(2,1)S(1)}, bf16[2,32,1024]{2,1,0:T(8,128)(2,1)S(1)}, u32[]{:S(2)}, u32[]{:S(2)}) collective-permute-start(bf16[2,32,1024]{2,1,0:T(8,128)(2,1)S(1)} %get-tuple-element.38), channel_id=1, source_target_pairs={{0,8},{4,12},{8,0},{12,4},{16,24},{20,28},{24,16},{28,20},{1,9},{5... | collective-permute-start | bytes 393224 | tf_op jit(solution)/shard_map/ppermute | solution.py:263
  5.6 8.3 %collective-permute-start.3 = (bf16[2,32,1024]{2,1,0:T(8,128)(2,1)S(1)}, bf16[2,32,1024]{2,1,0:T(8,128)(2,1)S(1)}, u32[]{:S(2)}, u32[]{:S(2)}) collective-permute-start(bf16[2,32,1024]{2,1,0:T(8,128)(2,1)S(1)} %get-tuple-element.39), channel_id=1, source_target_pairs={{0,12},{4,8},{8,4},{12,0},{16,28},{20,24},{24,20},{28,16},{1,13},{... | collective-permute-start | bytes 393224 | tf_op jit(solution)/shard_map/ppermute | solution.py:263
  5.7 8.2 %collective-permute-start.4 = (bf16[2,32,1024]{2,1,0:T(8,128)(2,1)S(1)}, bf16[2,32,1024]{2,1,0:T(8,128)(2,1)S(1)}, u32[]{:S(2)}, u32[]{:S(2)}) collective-permute-start(bf16[2,32,1024]{2,1,0:T(8,128)(2,1)S(1)} %get-tuple-element.40), channel_id=1, source_target_pairs={{0,16},{4,20},{8,24},{12,28},{16,0},{20,4},{24,8},{28,12},{1,17},{... | collective-permute-start | bytes 393224 | tf_op jit(solution)/shard_map/ppermute | solution.py:263
  7.4 6.5 %collective-permute-start.5 = (bf16[2,32,1024]{2,1,0:T(8,128)(2,1)S(1)}, bf16[2,32,1024]{2,1,0:T(8,128)(2,1)S(1)}, u32[]{:S(2)}, u32[]{:S(2)}) collective-permute-start(bf16[2,32,1024]{2,1,0:T(8,128)(2,1)S(1)} %get-tuple-element.41), channel_id=1, source_target_pairs={{0,20},{4,16},{8,28},{12,24},{16,4},{20,0},{24,12},{28,8},{1,21},{... | collective-permute-start | bytes 393224 | tf_op jit(solution)/shard_map/ppermute | solution.py:263
  12.1 9.5 %collective-permute-start.1 = (bf16[2,64,1024]{2,1,0:T(8,128)(2,1)S(1)}, bf16[2,64,1024]{2,1,0:T(8,128)(2,1)S(1)}, u32[]{:S(2)}, u32[]{:S(2)}) collective-permute-start(bf16[2,64,1024]{2,1,0:T(8,128)(2,1)S(1)} %get-tuple-element.37.refs_0_), channel_id=1, source_target_pairs={{0,1},{1,0},{2,3},{3,2},{4,5},{5,4},{6,7},{7,6},{8,9},{9,8},{10,11... | collective-permute-start | bytes 786440 | tf_op jit(solution)/shard_map/ppermute | solution.py:266
  17.0 9.9 %collective-permute-start.7 = (bf16[2,64,1024]{2,1,0:T(8,128)(2,1)S(1)}, bf16[2,64,1024]{2,1,0:T(8,128)(2,1)S(1)}, u32[]{:S(2)}, u32[]{:S(2)}) collective-permute-start(bf16[2,64,1024]{2,1,0:T(8,128)(2,1)S(1)} %get-tuple-element.49), channel_id=1, source_target_pairs={{0,1},{1,0},{2,3},{3,2},{4,5},{5,4},{6,7},{7,6},{8,9},{9,8},{10,11... | collective-permute-start | bytes 786440 | tf_op jit(solution)/shard_map/ppermute | solution.py:266
  18.7 11.1 %collective-permute-start.8 = (bf16[2,32,1024]{2,1,0:T(8,128)(2,1)S(1)}, bf16[2,32,1024]{2,1,0:T(8,128)(2,1)S(1)}, u32[]{:S(2)}, u32[]{:S(2)}) collective-permute-start(bf16[2,32,1024]{2,1,0:T(8,128)(2,1)S(1)} %get-tuple-element.50), channel_id=1, source_target_pairs={{0,24},{4,28},{8,16},{12,20},{16,8},{20,12},{24,0},{28,4},{1,25},{... | collective-permute-start | bytes 393224 | tf_op jit(solution)/shard_map/ppermute | solution.py:263
  21.1 8.6 %collective-permute-start.9 = (bf16[2,32,1024]{2,1,0:T(8,128)(2,1)S(1)}, bf16[2,32,1024]{2,1,0:T(8,128)(2,1)S(1)}, u32[]{:S(2)}, u32[]{:S(2)}) collective-permute-start(bf16[2,32,1024]{2,1,0:T(8,128)(2,1)S(1)} %get-tuple-element.51), channel_id=1, source_target_pairs={{0,28},{4,24},{8,20},{12,16},{16,12},{20,8},{24,4},{28,0},{1,29},{... | collective-permute-start | bytes 393224 | tf_op jit(solution)/shard_map/ppermute | solution.py:263
  21.1 13.7 %collective-permute-start.6 = (bf16[2,64,1024]{2,1,0:T(8,128)(2,1)S(1)}, bf16[2,64,1024]{2,1,0:T(8,128)(2,1)S(1)}, u32[]{:S(2)}, u32[]{:S(2)}) collective-permute-start(bf16[2,64,1024]{2,1,0:T(8,128)(2,1)S(1)} %get-tuple-element.47), channel_id=1, source_target_pairs={{0,1},{1,0},{2,3},{3,2},{4,5},{5,4},{6,7},{7,6},{8,9},{9,8},{10,11... | collective-permute-start | bytes 786440 | tf_op jit(solution)/shard_map/ppermute | solution.py:266
  26.9 10.3 %collective-permute-start.10 = (bf16[1,64,1024]{2,1,0:T(8,128)(2,1)S(1)}, bf16[1,64,1024]{2,1,0:T(8,128)(2,1)S(1)}, u32[]{:S(2)}, u32[]{:S(2)}) collective-permute-start(bf16[1,64,1024]{2,1,0:T(8,128)(2,1)S(1)} %totals.7.refs_0_), channel_id=1, source_target_pairs={{0,2},{1,3},{2,0},{3,1},{4,6},{5,7},{6,4},{7,5},{8,10},{9,11},{10,... | collective-permute-start | bytes 393224 | tf_op jit(solution)/shard_map/ppermute | solution.py:266
  32.6 8.2 %copy-start.1 = (s32[8]{0:T(128)S(1)}, s32[8]{0:T(128)}, u32[]{:S(2)}) copy-start(s32[8]{0:T(128)} %q_owner.1) | copy-start | bytes 100
  32.6 20.2 %collective-permute-start.12 = (bf16[1,64,1024]{2,1,0:T(8,128)(2,1)S(1)}, bf16[1,64,1024]{2,1,0:T(8,128)(2,1)S(1)}, u32[]{:S(2)}, u32[]{:S(2)}) collective-permute-start(bf16[1,64,1024]{2,1,0:T(8,128)(2,1)S(1)} %get-tuple-element.65), channel_id=1, source_target_pairs={{0,3},{1,2},{2,1},{3,0},{4,7},{5,6},{6,5},{7,4},{8,11},{9,10},{10,... | collective-permute-start | bytes 393224 | tf_op jit(solution)/shard_map/ppermute | solution.py:266
  34.0 20.3 %collective-permute-start.11 = (bf16[1,64,1024]{2,1,0:T(8,128)(2,1)S(1)}, bf16[1,64,1024]{2,1,0:T(8,128)(2,1)S(1)}, u32[]{:S(2)}, u32[]{:S(2)}) collective-permute-start(bf16[1,64,1024]{2,1,0:T(8,128)(2,1)S(1)} %get-tuple-element.66), channel_id=1, source_target_pairs={{0,1},{1,0},{2,3},{3,2},{4,5},{5,4},{6,7},{7,6},{8,9},{9,8},{10,11... | collective-permute-start | bytes 393224 | tf_op jit(solution)/shard_map/ppermute | solution.py:266
  34.9 16.3 %collective-permute-start.14 = (bf16[1,64,1024]{2,1,0:T(8,128)(2,1)S(1)}, bf16[1,64,1024]{2,1,0:T(8,128)(2,1)S(1)}, u32[]{:S(2)}, u32[]{:S(2)}) collective-permute-start(bf16[1,64,1024]{2,1,0:T(8,128)(2,1)S(1)} %totals.8.refs_0_), channel_id=1, source_target_pairs={{0,2},{1,3},{2,0},{3,1},{4,6},{5,7},{6,4},{7,5},{8,10},{9,11},{10,... | collective-permute-start | bytes 393224 | tf_op jit(solution)/shard_map/ppermute | solution.py:266
  38.6 19.9 %collective-permute-start.13 = (bf16[1,64,1024]{2,1,0:T(8,128)(2,1)S(1)}, bf16[1,64,1024]{2,1,0:T(8,128)(2,1)S(1)}, u32[]{:S(2)}, u32[]{:S(2)}) collective-permute-start(bf16[1,64,1024]{2,1,0:T(8,128)(2,1)S(1)} %product.10.refs_0_), channel_id=1, source_target_pairs={{0,2},{1,3},{2,0},{3,1},{4,6},{5,7},{6,4},{7,5},{8,10},{9,11},{10,... | collective-permute-start | bytes 393224 | tf_op jit(solution)/shard_map/ppermute | solution.py:266
  51.2 4.3 %collective-permute-start.17 = (bf16[32,1024]{1,0:T(8,128)(2,1)S(1)}, bf16[32,1024]{1,0:T(8,128)(2,1)S(1)}, u32[]{:S(2)}, u32[]{:S(2)}) collective-permute-start(bf16[32,1024]{1,0:T(8,128)(2,1)S(1)} %get-tuple-element.62), channel_id=1, source_target_pairs={{0,16},{4,20},{8,24},{12,28},{16,0},{20,4},{24,8},{28,12},{1,17},{... | collective-permute-start | bytes 196616 | tf_op jit(solution)/shard_map/ppermute | solution.py:263
  52.8 4.2 %collective-permute-start.18 = (bf16[32,1024]{1,0:T(8,128)(2,1)S(1)}, bf16[32,1024]{1,0:T(8,128)(2,1)S(1)}, u32[]{:S(2)}, u32[]{:S(2)}) collective-permute-start(bf16[32,1024]{1,0:T(8,128)(2,1)S(1)} %get-tuple-element.60.refs_4_), channel_id=1, source_target_pairs={{0,20},{4,16},{8,28},{12,24},{16,4},{20,0},{24,12},{28,8},{1,21},{... | collective-permute-start | bytes 196616 | tf_op jit(solution)/shard_map/ppermute | solution.py:263
  52.8 4.7 %collective-permute-start.15 = (bf16[32,1024]{1,0:T(8,128)(2,1)S(1)}, bf16[32,1024]{1,0:T(8,128)(2,1)S(1)}, u32[]{:S(2)}, u32[]{:S(2)}) collective-permute-start(bf16[32,1024]{1,0:T(8,128)(2,1)S(1)} %get-tuple-element.61), channel_id=1, source_target_pairs={{0,8},{4,12},{8,0},{12,4},{16,24},{20,28},{24,16},{28,20},{1,9},{5... | collective-permute-start | bytes 196616 | tf_op jit(solution)/shard_map/ppermute | solution.py:263
  54.3 4.2 %collective-permute-start.16 = (bf16[32,1024]{1,0:T(8,128)(2,1)S(1)}, bf16[32,1024]{1,0:T(8,128)(2,1)S(1)}, u32[]{:S(2)}, u32[]{:S(2)}) collective-permute-start(bf16[32,1024]{1,0:T(8,128)(2,1)S(1)} %get-tuple-element.59.refs_2_), channel_id=1, source_target_pairs={{0,12},{4,8},{8,4},{12,0},{16,28},{20,24},{24,20},{28,16},{1,13},{... | collective-permute-start | bytes 196616 | tf_op jit(solution)/shard_map/ppermute | solution.py:263
  55.6 8.5 %collective-permute-start.21 = (bf16[1,64,1024]{2,1,0:T(8,128)(2,1)S(1)}, bf16[1,64,1024]{2,1,0:T(8,128)(2,1)S(1)}, u32[]{:S(2)}, u32[]{:S(2)}) collective-permute-start(bf16[1,64,1024]{2,1,0:T(8,128)(2,1)S(1)} %totals.10.refs_3_), channel_id=1, source_target_pairs={{0,2},{1,3},{2,0},{3,1},{4,6},{5,7},{6,4},{7,5},{8,10},{9,11},{10,... | collective-permute-start | bytes 393224 | tf_op jit(solution)/shard_map/ppermute | solution.py:266
  58.6 6.5 %collective-permute-start.19 = (bf16[2,32,1024]{2,1,0:T(8,128)(2,1)S(1)}, bf16[2,32,1024]{2,1,0:T(8,128)(2,1)S(1)}, u32[]{:S(2)}, u32[]{:S(2)}) collective-permute-start(bf16[2,32,1024]{2,1,0:T(8,128)(2,1)S(1)} %bitcast.7), channel_id=1, source_target_pairs={{0,24},{4,28},{8,16},{12,20},{16,8},{20,12},{24,0},{28,4},{1,25},{... | collective-permute-start | bytes 393224 | tf_op jit(solution)/shard_map/ppermute | solution.py:263
  64.1 1.3 %collective-permute-start.22 = (bf16[32,1024]{1,0:T(8,128)(2,1)S(1)}, bf16[32,1024]{1,0:T(8,128)(2,1)S(1)}, u32[]{:S(2)}, u32[]{:S(2)}) collective-permute-start(bf16[32,1024]{1,0:T(8,128)(2,1)S(1)} %get-tuple-element.64), channel_id=1, source_target_pairs={{0,4},{4,0},{8,12},{12,8},{16,20},{20,16},{24,28},{28,24},{1,5},{5... | collective-permute-start | bytes 196616 | tf_op jit(solution)/shard_map/ppermute | solution.py:263
  65.1 1.3 %collective-permute-start.20 = (bf16[32,1024]{1,0:T(8,128)(2,1)S(1)}, bf16[32,1024]{1,0:T(8,128)(2,1)S(1)}, u32[]{:S(2)}, u32[]{:S(2)}) collective-permute-start(bf16[32,1024]{1,0:T(8,128)(2,1)S(1)} %slice_bitcast_fusion), channel_id=1, source_target_pairs={{0,4},{4,0},{8,12},{12,8},{16,20},{20,16},{24,28},{28,24},{1,5},{5... | collective-permute-start | bytes 196616 | tf_op jit(solution)/shard_map/ppermute | solution.py:263

commit v2 on v1

--- a/solution.py
+++ b/solution.py
@@ -314,13 +314,13 @@
     come.update((g, first_step(away[g])) for g in near)
     kept, _ = multiply([0] + near, all_middle, middle_ints, after=[come[0]])
     ready[first], sums[first] = later_steps(kept[first], come[first])
-    outs, home_ints, _ = multiply(far, all_odd, odd_ints, (0,), after=[ready[first]])
-    away.update(outs)
-    last = away[far[0]]
+    last = ready[first]
     for g in others:
         ready[g], sums[g] = later_steps(kept[g], come[g], [last])
         last = ready[g]
-    outs, _ = multiply(far, all_middle, middle_ints, after=[last, sums[first][-1][0]])
+    outs, home_ints, _ = multiply(far, all_odd, odd_ints, (0,), after=[last])
+    away.update(outs)
+    outs, _ = multiply(far, all_middle, middle_ints, after=[away[far[0]], sums[first][-1][0]])
     kept.update(outs)
     for g in far:
         sums[g] = [(swap_line(away[g][i : i + 1], r), 0) for i, r in enumerate(odd)]

time: 67.6 us -> 65.1 us (0.963)
  waiting for transfers between devices: 22.4 us -> 15.1 us
  starting transfers between devices: 25.4 us -> 29.8 us
    ppermute x14, waiting for transfers between devices: 5.87 us -> 1.7 us  [swap(): return lax.ppermute(value, 'wide', [(w, w ^ j) for w in range(peers)])]
    ppermute x9, starting transfers between devices: 11.6 us -> 15.5 us  [swap_line(): lax.ppermute(value, 'narrow', [(n, n ^ mask) for n in range(devices)])]
    ppermute x9, waiting for transfers between devices: 16.6 us -> 13.4 us  [swap_line(): lax.ppermute(value, 'narrow', [(n, n ^ mask) for n in range(devices)])]
  transfers between devices with their start and end apart: 23 -> 23, of which waited for: 11 -> 8; matrix products, arithmetic and copies ran while one was open for 0% -> 0% of each run, Pallas kernels for 24% -> 25%
where the time goes in v2:
time: 65.1 us; the launch traced here: 64.6 us
  starting transfers between devices  29.8 us (46%)
  Pallas kernels  17.8 us (27%)
  waiting for transfers between devices  15.1 us (23%)
  local copies, waits for them, and re-layouts  0.98 us (2%)
  other arithmetic  0.72 us (1%)
    ppermute x9, starting transfers between devices, swap_line(): lax.ppermute(value, 'narrow', [(n, n ^ mask) for n in range(devices)])  15.5 us
    pallas_call x6, Pallas kernels, product(): pl.pallas_call(functools.partial(product_kernel, plan), out_shape=[jax.Sh...  14.9 us
    ppermute x14, starting transfers between devices, swap(): return lax.ppermute(value, 'wide', [(w, w ^ j) for w in range(peers)])  14.2 us
    ppermute x9, waiting for transfers between devices, swap_line(): lax.ppermute(value, 'narrow', [(n, n ^ mask) for n in range(devices)])  13.4 us
    ppermute x14, waiting for transfers between devices, swap(): return lax.ppermute(value, 'wide', [(w, w ^ j) for w in range(peers)])  1.7 us
  transfers between devices with their start and end apart: 23, of which 8 were waited for; matrix products, arithmetic and copies ran while one was open for 0% of the time, Pallas kernels for 25%

profile of v2, /device:TPU:0, one launch (start us, length us, event | category | flops | bytes accessed | tf_op | source)
XLA Modules:
  0.0 64.6 jit_solution(14538107746654381552)
XLA Ops:
  0.0 0.7 %pad_add_fusion.tables_from = s32[7,8]{1,0:T(8,128)S(1)} fusion(s32[1,8]{1,0:T(1,128)} %bitcast.8, s32[2,8]{1,0:T(2,128)} %bitcast.10, s32[4,8]{1,0:T(4,128)} %bitcast.9), kind=kLoop, calls=%fused_computation.1 | loop fusion | flops 112 | bytes 448 | tf_op jit(solution)/shard_map/concatenate | solution.py:46
  0.7 0.9 %copy-done = bf16[32,4,1024]{2,1,0:T(4,128)(2,1)S(1)} copy-done((bf16[32,4,1024]{2,1,0:T(4,128)(2,1)S(1)}, bf16[32,4,1024]{2,1,0:T(4,128)(2,1)}, u32[]{:S(2)}) %copy-start) | copy-done | bytes 262168
  1.7 0.8 %pick.1 = (bf16[2,32,1024]{2,1,0:T(8,128)(2,1)S(1)}, bf16[2,32,1024]{2,1,0:T(8,128)(2,1)S(1)}, bf16[2,32,1024]{2,1,0:T(8,128)(2,1)S(1)}, bf16[2,32,1024]{2,1,0:T...) custom-call(s32[7,8]{1,0:T(8,128)S(1)} %pad_add_fusion.tables_from, ...), custom_call_target="tpu_custom_call" | custom-call | tf_op jit(solution)/shard_map/pick/pallas_call | solution.py:48
  2.5 0.5 collective-permute-start
  3.0 2.6 %collective-permute-start.2 = (bf16[2,32,1024]{2,1,0:T(8,128)(2,1)S(1)}, bf16[2,32,1024]{2,1,0:T(8,128)(2,1)S(1)}, u32[]{:S(2)}, u32[]{:S(2)}) collective-permute-start(bf16[2,32,1024]{2,1,0:T(8,128)(2,1)S(1)} %get-tuple-element.38), channel_id=1, source_target_pairs={{0,8},{4,12},{8,0},{12,4},{16,24},{20,28},{24,16},{28,20},{1,9},{5... | collective-permute-start | bytes 393224 | tf_op jit(solution)/shard_map/ppermute | solution.py:263
  5.6 0.1 collective-permute-start.3
  5.7 1.8 %collective-permute-start.4 = (bf16[2,32,1024]{2,1,0:T(8,128)(2,1)S(1)}, bf16[2,32,1024]{2,1,0:T(8,128)(2,1)S(1)}, u32[]{:S(2)}, u32[]{:S(2)}) collective-permute-start(bf16[2,32,1024]{2,1,0:T(8,128)(2,1)S(1)} %get-tuple-element.40), channel_id=1, source_target_pairs={{0,16},{4,20},{8,24},{12,28},{16,0},{20,4},{24,8},{28,12},{1,17},{... | collective-permute-start | bytes 393224 | tf_op jit(solution)/shard_map/ppermute | solution.py:263
  7.4 0.0 collective-permute-start.5
  7.4 0.0 collective-permute-done.refs_1_.refs_2_
  7.4 4.7 %product.6 = (bf16[2,64,1024]{2,1,0:T(8,128)(2,1)S(1)}, bf16[2,2,1024,1024]{3,2,1,0:T(8,128)(2,1)S(1)}) custom-call(bf16[2,32,1024]{2,1,0:T(8,128)(2,1)S(1)} %get-tuple-element.35.refs_0_.refs_1_, bf16[2,32,1024]{2,1,0:T(8,128)(2,1)S(1)} %collective-permute-done.refs_1_.refs_2_, bf16[1,2,4096,1024]{3,2,1,0:T(8,128)(2,1)} %refs_4_.1), custom_call_target="tpu_custom_call" | custom-call | flops 2147483648 | bytes 8388608 | tf_op jit(solution)/shard_map/product/pallas_call | solution.py:152
  12.1 1.8 %collective-permute-start.1 = (bf16[2,64,1024]{2,1,0:T(8,128)(2,1)S(1)}, bf16[2,64,1024]{2,1,0:T(8,128)(2,1)S(1)}, u32[]{:S(2)}, u32[]{:S(2)}) collective-permute-start(bf16[2,64,1024]{2,1,0:T(8,128)(2,1)S(1)} %get-tuple-element.37.refs_0_), channel_id=1, source_target_pairs={{0,1},{1,0},{2,3},{3,2},{4,5},{5,4},{6,7},{7,6},{8,9},{9,8},{10,11... | collective-permute-start | bytes 786440 | tf_op jit(solution)/shard_map/ppermute | solution.py:266
  13.9 0.0 collective-permute-done.2.refs_1_.refs_3_
  13.9 0.0 collective-permute-done.3.refs_2_.refs_4_
  13.9 3.1 %product.7 = (bf16[2,64,1024]{2,1,0:T(8,128)(2,1)S(1)}, bf16[2,64,1024]{2,1,0:T(8,128)(2,1)S(1)}, bf16[1,2,1024,1024]{3,2,1,0:T(8,128)(2,1)S(1)}, bf16[2,32,1024...) custom-call(bf16[2,64,1024]{2,1,0:T(8,128)(2,1)S(1)} %get-tuple-element.37.refs_0_, ...), custom_call_target="tpu_custom_call", output_to_operand_aliasing={{3}: (7, {}), {4}: (8, {})} | custom-call | flops 2147483648 | bytes 8388608 | tf_op jit(solution)/shard_map/product/pallas_call | solution.py:152
  17.0 1.6 %collective-permute-start.7 = (bf16[2,64,1024]{2,1,0:T(8,128)(2,1)S(1)}, bf16[2,64,1024]{2,1,0:T(8,128)(2,1)S(1)}, u32[]{:S(2)}, u32[]{:S(2)}) collective-permute-start(bf16[2,64,1024]{2,1,0:T(8,128)(2,1)S(1)} %get-tuple-element.49), channel_id=1, source_target_pairs={{0,1},{1,0},{2,3},{3,2},{4,5},{5,4},{6,7},{7,6},{8,9},{9,8},{10,11... | collective-permute-start | bytes 786440 | tf_op jit(solution)/shard_map/ppermute | solution.py:266
  18.7 0.5 collective-permute-start.6
  19.1 2.5 %collective-permute-start.8 = (bf16[2,32,1024]{2,1,0:T(8,128)(2,1)S(1)}, bf16[2,32,1024]{2,1,0:T(8,128)(2,1)S(1)}, u32[]{:S(2)}, u32[]{:S(2)}) collective-permute-start(bf16[2,32,1024]{2,1,0:T(8,128)(2,1)S(1)} %get-tuple-element.50), channel_id=1, source_target_pairs={{0,24},{4,28},{8,16},{12,20},{16,8},{20,12},{24,0},{28,4},{1,25},{... | collective-permute-start | bytes 393224 | tf_op jit(solution)/shard_map/ppermute | solution.py:263
  21.6 1.5 %product.8 = (bf16[1,64,1024]{2,1,0:T(8,128)(2,1)S(1)}, bf16[1,64,1024]{2,1,0:T(8,128)(2,1)S(1)}, bf16[1,64,1024]{2,1,0:T(8,128)(2,1)S(1)}) custom-call(bf16[2,64,1024]{2,1,0:T(8,128)(2,1)S(1)} %collective-permute-done.1.refs_0_.refs_1_, bf16[2,32,1024]{2,1,0:T(8,128)(2,1)S(1)} %get-tuple-element.35.refs_0_.refs_1_, ...), custom_call_target="tpu_custom_call" | custom-call | flops 1073741824 | bytes 4194304 | tf_op jit(solution)/shard_map/product/pallas_call | solution.py:152
  23.1 3.8 %collective-permute-done.7.refs_1_ = bf16[2,64,1024]{2,1,0:T(8,128)(2,1)S(1)} collective-permute-done((bf16[2,64,1024]{2,1,0:T(8,128)(2,1)S(1)}, bf16[2,64,1024]{2,1,0:T(8,128)(2,1)S(1)}, u32[]{:S(2)}, u32[]{:S(2)}) %collective-permute-start.7) | collective-permute-done | bytes 262176 | tf_op jit(solution)/shard_map/ppermute | solution.py:266
  26.9 2.8 %collective-permute-start.10 = (bf16[1,64,1024]{2,1,0:T(8,128)(2,1)S(1)}, bf16[1,64,1024]{2,1,0:T(8,128)(2,1)S(1)}, u32[]{:S(2)}, u32[]{:S(2)}) collective-permute-start(bf16[1,64,1024]{2,1,0:T(8,128)(2,1)S(1)} %totals.7.refs_2_), channel_id=1, source_target_pairs={{0,2},{1,3},{2,0},{3,1},{4,6},{5,7},{6,4},{7,5},{8,10},{9,11},{10,... | collective-permute-start | bytes 393224 | tf_op jit(solution)/shard_map/ppermute | solution.py:266
  29.7 5.1 %collective-permute-done.6.refs_1_ = bf16[2,64,1024]{2,1,0:T(8,128)(2,1)S(1)} collective-permute-done((bf16[2,64,1024]{2,1,0:T(8,128)(2,1)S(1)}, bf16[2,64,1024]{2,1,0:T(8,128)(2,1)S(1)}, u32[]{:S(2)}, u32[]{:S(2)}) %collective-permute-start.6) | collective-permute-done | bytes 262176 | tf_op jit(solution)/shard_map/ppermute | solution.py:266
  34.9 1.0 %collective-permute-start.14 = (bf16[1,64,1024]{2,1,0:T(8,128)(2,1)S(1)}, bf16[1,64,1024]{2,1,0:T(8,128)(2,1)S(1)}, u32[]{:S(2)}, u32[]{:S(2)}) collective-permute-start(bf16[1,64,1024]{2,1,0:T(8,128)(2,1)S(1)} %totals.8.refs_0_), channel_id=1, source_target_pairs={{0,2},{1,3},{2,0},{3,1},{4,6},{5,7},{6,4},{7,5},{8,10},{9,11},{10,... | collective-permute-start | bytes 393224 | tf_op jit(solution)/shard_map/ppermute | solution.py:266
  35.9 2.8 %product.9 = (bf16[2,64,1024]{2,1,0:T(8,128)(2,1)S(1)}, bf16[1,2,1024,1024]{3,2,1,0:T(8,128)(2,1)S(1)}) custom-call(bf16[1,64,1024]{2,1,0:T(8,128)(2,1)S(1)} %totals.8.refs_0_, bf16[2,32,1024]{2,1,0:T(8,128)(2,1)S(1)} %collective-permute-done.8.refs_1_.refs_2_.refs_7_, bf16[2,32,1024]{2,1,0:T(8,128)(2,1)S(1)} %collective-permute-done.9.refs_2_.refs_3_.refs_8_, ...), custom_call_target="tpu_custom_call" | custom-call | flops 2147483648 | bytes 8388608 | tf_op jit(solution)/shard_map/product/pallas_call | solution.py:152
  38.8 0.0 copy-start.1
  38.8 2.0 %collective-permute-start.12 = (bf16[1,64,1024]{2,1,0:T(8,128)(2,1)S(1)}, bf16[1,64,1024]{2,1,0:T(8,128)(2,1)S(1)}, u32[]{:S(2)}, u32[]{:S(2)}) collective-permute-start(bf16[1,64,1024]{2,1,0:T(8,128)(2,1)S(1)} %get-tuple-element.65), channel_id=1, source_target_pairs={{0,3},{1,2},{2,1},{3,0},{4,7},{5,6},{6,5},{7,4},{8,11},{9,10},{10,... | collective-permute-start | bytes 393224 | tf_op jit(solution)/shard_map/ppermute | solution.py:266
  40.8 0.6 collective-permute-start.11
  41.4 1.4 %product.10.refs_0_ = bf16[1,64,1024]{2,1,0:T(8,128)(2,1)S(1)} custom-call(bf16[2,64,1024]{2,1,0:T(8,128)(2,1)S(1)} %get-tuple-element.52.refs_0_, bf16[1,64,1024]{2,1,0:T(8,128)(2,1)S(1)} %collective-permute-done.10.refs_1_.refs_2_, bf16[2,32,1024]{2,1,0:T(8,128)(2,1)S(1)} %collective-permute-done.8.refs_1_.refs_2_.refs_7_, ...), custom_call_target="tpu_custom_call" | custom-call | flops 1073741824 | bytes 4194304 | tf_op jit(solution)/shard_map/product/pallas_call | solution.py:152
  42.8 1.9 %collective-permute-start.13 = (bf16[1,64,1024]{2,1,0:T(8,128)(2,1)S(1)}, bf16[1,64,1024]{2,1,0:T(8,128)(2,1)S(1)}, u32[]{:S(2)}, u32[]{:S(2)}) collective-permute-start(bf16[1,64,1024]{2,1,0:T(8,128)(2,1)S(1)} %product.10.refs_0_), channel_id=1, source_target_pairs={{0,2},{1,3},{2,0},{3,1},{4,6},{5,7},{6,4},{7,5},{8,10},{9,11},{10,... | collective-permute-start | bytes 393224 | tf_op jit(solution)/shard_map/ppermute | solution.py:266
  44.7 1.3 %product.11 = (bf16[1,64,1024]{2,1,0:T(8,128)(2,1)S(1)}, bf16[1,64,1024]{2,1,0:T(8,128)(2,1)S(1)}, bf16[1,64,1024]{2,1,0:T(8,128)(2,1)S(1)}, bf16[1,64,1024]{2,1,0:T(8,128)(2,1)S(1)}) custom-call(bf16[1,64,1024]{2,1,0:T(8,128)(2,1)S(1)} %product.10.refs_0_, bf16[2,32,1024]{2,1,0:T(8,128)(2,1)S(1)} %get-tuple-element.35.refs_0_.refs_1_, ...), custom_call_target="tpu_custom_call" | custom-call | flops 1073741824 | bytes 4194304 | tf_op jit(solution)/shard_map/product/pallas_call | solution.py:152
  46.1 0.7 %place.1.refs_3_.refs_8_ = bf16[256,256]{1,0:T(8,128)(2,1)S(1)} custom-call(s32[8]{0:T(128)S(1)} %copy-done.1, bf16[1,64,1024]{2,1,0:T(8,128)(2,1)S(1)} %get-tuple-element.58.after.refs_0_), custom_call_target="tpu_custom_call" | custom-call | tf_op jit(solution)/shard_map/place/pallas_call | solution.py:221
  46.8 0.1 totals.9
  46.9 0.3 collective-permute-done.14.refs_2_
  47.1 0.1 totals.11
  47.2 1.3 %collective-permute-start.17 = (bf16[32,1024]{1,0:T(8,128)(2,1)S(1)}, bf16[32,1024]{1,0:T(8,128)(2,1)S(1)}, u32[]{:S(2)}, u32[]{:S(2)}) collective-permute-start(bf16[32,1024]{1,0:T(8,128)(2,1)S(1)} %get-tuple-element.62), channel_id=1, source_target_pairs={{0,16},{4,20},{8,24},{12,28},{16,0},{20,4},{24,8},{28,12},{1,17},{... | collective-permute-start | bytes 196616 | tf_op jit(solution)/shard_map/ppermute | solution.py:263
  48.5 1.7 %collective-permute-start.15 = (bf16[32,1024]{1,0:T(8,128)(2,1)S(1)}, bf16[32,1024]{1,0:T(8,128)(2,1)S(1)}, u32[]{:S(2)}, u32[]{:S(2)}) collective-permute-start(bf16[32,1024]{1,0:T(8,128)(2,1)S(1)} %get-tuple-element.61), channel_id=1, source_target_pairs={{0,8},{4,12},{8,0},{12,4},{16,24},{20,28},{24,16},{28,20},{1,9},{5... | collective-permute-start | bytes 196616 | tf_op jit(solution)/shard_map/ppermute | solution.py:263
  50.3 0.5 collective-permute-start.16
  50.7 0.8 %collective-permute-done.17.refs_7_.refs_4_ = bf16[32,1024]{1,0:T(8,128)(2,1)S(1)} collective-permute-done((bf16[32,1024]{1,0:T(8,128)(2,1)S(1)}, bf16[32,1024]{1,0:T(8,128)(2,1)S(1)}, u32[]{:S(2)}, u32[]{:S(2)}) %collective-permute-start.17) | collective-permute-done | bytes 65568 | tf_op jit(solution)/shard_map/ppermute | solution.py:263
  51.5 3.3 %collective-permute-start.21 = (bf16[1,64,1024]{2,1,0:T(8,128)(2,1)S(1)}, bf16[1,64,1024]{2,1,0:T(8,128)(2,1)S(1)}, u32[]{:S(2)}, u32[]{:S(2)}) collective-permute-start(bf16[1,64,1024]{2,1,0:T(8,128)(2,1)S(1)} %totals.10.refs_3_), channel_id=1, source_target_pairs={{0,2},{1,3},{2,0},{3,1},{4,6},{5,7},{6,4},{7,5},{8,10},{9,11},{10,... | collective-permute-start | bytes 393224 | tf_op jit(solution)/shard_map/ppermute | solution.py:266
  54.8 0.1 collective-permute-done.13.refs_3_
  55.0 0.1 totals.12.refs_3_
  55.1 2.7 %collective-permute-start.19 = (bf16[2,32,1024]{2,1,0:T(8,128)(2,1)S(1)}, bf16[2,32,1024]{2,1,0:T(8,128)(2,1)S(1)}, u32[]{:S(2)}, u32[]{:S(2)}) collective-permute-start(bf16[2,32,1024]{2,1,0:T(8,128)(2,1)S(1)} %bitcast.7), channel_id=1, source_target_pairs={{0,24},{4,28},{8,16},{12,20},{16,8},{20,12},{24,0},{28,4},{1,25},{... | collective-permute-start | bytes 393224 | tf_op jit(solution)/shard_map/ppermute | solution.py:263
  57.7 4.1 %collective-permute-done.21.refs_2_ = bf16[1,64,1024]{2,1,0:T(8,128)(2,1)S(1)} collective-permute-done((bf16[1,64,1024]{2,1,0:T(8,128)(2,1)S(1)}, bf16[1,64,1024]{2,1,0:T(8,128)(2,1)S(1)}, u32[]{:S(2)}, u32[]{:S(2)}) %collective-permute-start.21) | collective-permute-done | bytes 131104 | tf_op jit(solution)/shard_map/ppermute | solution.py:266
  61.8 0.1 totals.13
  61.9 0.1 collective-permute-start.22
  62.0 0.5 collective-permute-start.20
  62.6 0.7 %collective-permute-done.22.refs_7_ = bf16[32,1024]{1,0:T(8,128)(2,1)S(1)} collective-permute-done((bf16[32,1024]{1,0:T(8,128)(2,1)S(1)}, bf16[32,1024]{1,0:T(8,128)(2,1)S(1)}, u32[]{:S(2)}, u32[]{:S(2)}) %collective-permute-start.22) | collective-permute-done | bytes 65568 | tf_op jit(solution)/shard_map/ppermute | solution.py:263
  63.2 0.2 collective-permute-done.20.refs_1_
  63.5 1.1 %order.1 = bf16[256,1024]{1,0:T(8,128)(2,1)} custom-call(bf16[2,32,1024]{2,1,0:T(8,128)(2,1)S(1)} %collective-permute-done.19.refs_0_, bf16[32,1024]{1,0:T(8,128)(2,1)S(1)} %collective-permute-done.20.refs_1_, bf16[32,1024]{1,0:T(8,128)(2,1)S(1)} %collective-permute-done.15.refs_5_.refs_2_, bf16[32,1024]{1,0:T(8,128)(2,1)S(1)} %collective-permute-done.16.refs_6_.refs_3_, ...), custom_call_target="tpu_custom_call" | custom-call | tf_op jit(solution)/shard_map/order/pallas_call | solution.py:243
  (21 shorter events, 0.2 us)
Async XLA Ops:
  0.7 0.9 %copy-start = (bf16[32,4,1024]{2,1,0:T(4,128)(2,1)S(1)}, bf16[32,4,1024]{2,1,0:T(4,128)(2,1)}, u32[]{:S(2)}) copy-start(bf16[32,4,1024]{2,1,0:T(4,128)(2,1)} %amps.1) | copy-start | bytes 786436
  2.5 4.9 %collective-permute-start = (bf16[2,32,1024]{2,1,0:T(8,128)(2,1)S(1)}, bf16[2,32,1024]{2,1,0:T(8,128)(2,1)S(1)}, u32[]{:S(2)}, u32[]{:S(2)}) collective-permute-start(bf16[2,32,1024]{2,1,0:T(8,128)(2,1)S(1)} %get-tuple-element.36), channel_id=1, source_target_pairs={{0,4},{4,0},{8,12},{12,8},{16,20},{20,16},{24,28},{28,24},{1,5},{5... | collective-permute-start | bytes 393224 | tf_op jit(solution)/shard_map/ppermute | solution.py:263
  3.0 10.9 %collective-permute-start.2 = (bf16[2,32,1024]{2,1,0:T(8,128)(2,1)S(1)}, bf16[2,32,1024]{2,1,0:T(8,128)(2,1)S(1)}, u32[]{:S(2)}, u32[]{:S(2)}) collective-permute-start(bf16[2,32,1024]{2,1,0:T(8,128)(2,1)S(1)} %get-tuple-element.38), channel_id=1, source_target_pairs={{0,8},{4,12},{8,0},{12,4},{16,24},{20,28},{24,16},{28,20},{1,9},{5... | collective-permute-start | bytes 393224 | tf_op jit(solution)/shard_map/ppermute | solution.py:263
  5.6 8.3 %collective-permute-start.3 = (bf16[2,32,1024]{2,1,0:T(8,128)(2,1)S(1)}, bf16[2,32,1024]{2,1,0:T(8,128)(2,1)S(1)}, u32[]{:S(2)}, u32[]{:S(2)}) collective-permute-start(bf16[2,32,1024]{2,1,0:T(8,128)(2,1)S(1)} %get-tuple-element.39), channel_id=1, source_target_pairs={{0,12},{4,8},{8,4},{12,0},{16,28},{20,24},{24,20},{28,16},{1,13},{... | collective-permute-start | bytes 393224 | tf_op jit(solution)/shard_map/ppermute | solution.py:263
  5.7 8.2 %collective-permute-start.4 = (bf16[2,32,1024]{2,1,0:T(8,128)(2,1)S(1)}, bf16[2,32,1024]{2,1,0:T(8,128)(2,1)S(1)}, u32[]{:S(2)}, u32[]{:S(2)}) collective-permute-start(bf16[2,32,1024]{2,1,0:T(8,128)(2,1)S(1)} %get-tuple-element.40), channel_id=1, source_target_pairs={{0,16},{4,20},{8,24},{12,28},{16,0},{20,4},{24,8},{28,12},{1,17},{... | collective-permute-start | bytes 393224 | tf_op jit(solution)/shard_map/ppermute | solution.py:263
  7.4 6.5 %collective-permute-start.5 = (bf16[2,32,1024]{2,1,0:T(8,128)(2,1)S(1)}, bf16[2,32,1024]{2,1,0:T(8,128)(2,1)S(1)}, u32[]{:S(2)}, u32[]{:S(2)}) collective-permute-start(bf16[2,32,1024]{2,1,0:T(8,128)(2,1)S(1)} %get-tuple-element.41), channel_id=1, source_target_pairs={{0,20},{4,16},{8,28},{12,24},{16,4},{20,0},{24,12},{28,8},{1,21},{... | collective-permute-start | bytes 393224 | tf_op jit(solution)/shard_map/ppermute | solution.py:263
  12.1 9.5 %collective-permute-start.1 = (bf16[2,64,1024]{2,1,0:T(8,128)(2,1)S(1)}, bf16[2,64,1024]{2,1,0:T(8,128)(2,1)S(1)}, u32[]{:S(2)}, u32[]{:S(2)}) collective-permute-start(bf16[2,64,1024]{2,1,0:T(8,128)(2,1)S(1)} %get-tuple-element.37.refs_0_), channel_id=1, source_target_pairs={{0,1},{1,0},{2,3},{3,2},{4,5},{5,4},{6,7},{7,6},{8,9},{9,8},{10,11... | collective-permute-start | bytes 786440 | tf_op jit(solution)/shard_map/ppermute | solution.py:266
  17.0 9.9 %collective-permute-start.7 = (bf16[2,64,1024]{2,1,0:T(8,128)(2,1)S(1)}, bf16[2,64,1024]{2,1,0:T(8,128)(2,1)S(1)}, u32[]{:S(2)}, u32[]{:S(2)}) collective-permute-start(bf16[2,64,1024]{2,1,0:T(8,128)(2,1)S(1)} %get-tuple-element.49), channel_id=1, source_target_pairs={{0,1},{1,0},{2,3},{3,2},{4,5},{5,4},{6,7},{7,6},{8,9},{9,8},{10,11... | collective-permute-start | bytes 786440 | tf_op jit(solution)/shard_map/ppermute | solution.py:266
  18.7 16.2 %collective-permute-start.6 = (bf16[2,64,1024]{2,1,0:T(8,128)(2,1)S(1)}, bf16[2,64,1024]{2,1,0:T(8,128)(2,1)S(1)}, u32[]{:S(2)}, u32[]{:S(2)}) collective-permute-start(bf16[2,64,1024]{2,1,0:T(8,128)(2,1)S(1)} %get-tuple-element.47), channel_id=1, source_target_pairs={{0,1},{1,0},{2,3},{3,2},{4,5},{5,4},{6,7},{7,6},{8,9},{9,8},{10,11... | collective-permute-start | bytes 786440 | tf_op jit(solution)/shard_map/ppermute | solution.py:266
  19.1 16.8 %collective-permute-start.8 = (bf16[2,32,1024]{2,1,0:T(8,128)(2,1)S(1)}, bf16[2,32,1024]{2,1,0:T(8,128)(2,1)S(1)}, u32[]{:S(2)}, u32[]{:S(2)}) collective-permute-start(bf16[2,32,1024]{2,1,0:T(8,128)(2,1)S(1)} %get-tuple-element.50), channel_id=1, source_target_pairs={{0,24},{4,28},{8,16},{12,20},{16,8},{20,12},{24,0},{28,4},{1,25},{... | collective-permute-start | bytes 393224 | tf_op jit(solution)/shard_map/ppermute | solution.py:263
  21.6 14.3 %collective-permute-start.9 = (bf16[2,32,1024]{2,1,0:T(8,128)(2,1)S(1)}, bf16[2,32,1024]{2,1,0:T(8,128)(2,1)S(1)}, u32[]{:S(2)}, u32[]{:S(2)}) collective-permute-start(bf16[2,32,1024]{2,1,0:T(8,128)(2,1)S(1)} %get-tuple-element.51), channel_id=1, source_target_pairs={{0,28},{4,24},{8,20},{12,16},{16,12},{20,8},{24,4},{28,0},{1,29},{... | collective-permute-start | bytes 393224 | tf_op jit(solution)/shard_map/ppermute | solution.py:263
  26.9 14.5 %collective-permute-start.10 = (bf16[1,64,1024]{2,1,0:T(8,128)(2,1)S(1)}, bf16[1,64,1024]{2,1,0:T(8,128)(2,1)S(1)}, u32[]{:S(2)}, u32[]{:S(2)}) collective-permute-start(bf16[1,64,1024]{2,1,0:T(8,128)(2,1)S(1)} %totals.7.refs_2_), channel_id=1, source_target_pairs={{0,2},{1,3},{2,0},{3,1},{4,6},{5,7},{6,4},{7,5},{8,10},{9,11},{10,... | collective-permute-start | bytes 393224 | tf_op jit(solution)/shard_map/ppermute | solution.py:266
  34.9 12.2 %collective-permute-start.14 = (bf16[1,64,1024]{2,1,0:T(8,128)(2,1)S(1)}, bf16[1,64,1024]{2,1,0:T(8,128)(2,1)S(1)}, u32[]{:S(2)}, u32[]{:S(2)}) collective-permute-start(bf16[1,64,1024]{2,1,0:T(8,128)(2,1)S(1)} %totals.8.refs_0_), channel_id=1, source_target_pairs={{0,2},{1,3},{2,0},{3,1},{4,6},{5,7},{6,4},{7,5},{8,10},{9,11},{10,... | collective-permute-start | bytes 393224 | tf_op jit(solution)/shard_map/ppermute | solution.py:266
  38.8 7.3 %copy-start.1 = (s32[8]{0:T(128)S(1)}, s32[8]{0:T(128)}, u32[]{:S(2)}) copy-start(s32[8]{0:T(128)} %q_owner.1) | copy-start | bytes 100
  38.8 9.7 %collective-permute-start.12 = (bf16[1,64,1024]{2,1,0:T(8,128)(2,1)S(1)}, bf16[1,64,1024]{2,1,0:T(8,128)(2,1)S(1)}, u32[]{:S(2)}, u32[]{:S(2)}) collective-permute-start(bf16[1,64,1024]{2,1,0:T(8,128)(2,1)S(1)} %get-tuple-element.65), channel_id=1, source_target_pairs={{0,3},{1,2},{2,1},{3,0},{4,7},{5,6},{6,5},{7,4},{8,11},{9,10},{10,... | collective-permute-start | bytes 393224 | tf_op jit(solution)/shard_map/ppermute | solution.py:266
  40.8 9.5 %collective-permute-start.11 = (bf16[1,64,1024]{2,1,0:T(8,128)(2,1)S(1)}, bf16[1,64,1024]{2,1,0:T(8,128)(2,1)S(1)}, u32[]{:S(2)}, u32[]{:S(2)}) collective-permute-start(bf16[1,64,1024]{2,1,0:T(8,128)(2,1)S(1)} %get-tuple-element.66), channel_id=1, source_target_pairs={{0,1},{1,0},{2,3},{3,2},{4,5},{5,4},{6,7},{7,6},{8,9},{9,8},{10,11... | collective-permute-start | bytes 393224 | tf_op jit(solution)/shard_map/ppermute | solution.py:266
  42.8 12.1 %collective-permute-start.13 = (bf16[1,64,1024]{2,1,0:T(8,128)(2,1)S(1)}, bf16[1,64,1024]{2,1,0:T(8,128)(2,1)S(1)}, u32[]{:S(2)}, u32[]{:S(2)}) collective-permute-start(bf16[1,64,1024]{2,1,0:T(8,128)(2,1)S(1)} %product.10.refs_0_), channel_id=1, source_target_pairs={{0,2},{1,3},{2,0},{3,1},{4,6},{5,7},{6,4},{7,5},{8,10},{9,11},{10,... | collective-permute-start | bytes 393224 | tf_op jit(solution)/shard_map/ppermute | solution.py:266
  47.2 4.3 %collective-permute-start.17 = (bf16[32,1024]{1,0:T(8,128)(2,1)S(1)}, bf16[32,1024]{1,0:T(8,128)(2,1)S(1)}, u32[]{:S(2)}, u32[]{:S(2)}) collective-permute-start(bf16[32,1024]{1,0:T(8,128)(2,1)S(1)} %get-tuple-element.62), channel_id=1, source_target_pairs={{0,16},{4,20},{8,24},{12,28},{16,0},{20,4},{24,8},{28,12},{1,17},{... | collective-permute-start | bytes 196616 | tf_op jit(solution)/shard_map/ppermute | solution.py:263
  48.5 6.3 %collective-permute-start.18 = (bf16[32,1024]{1,0:T(8,128)(2,1)S(1)}, bf16[32,1024]{1,0:T(8,128)(2,1)S(1)}, u32[]{:S(2)}, u32[]{:S(2)}) collective-permute-start(bf16[32,1024]{1,0:T(8,128)(2,1)S(1)} %get-tuple-element.60.refs_4_), channel_id=1, source_target_pairs={{0,20},{4,16},{8,28},{12,24},{16,4},{20,0},{24,12},{28,8},{1,21},{... | collective-permute-start | bytes 196616 | tf_op jit(solution)/shard_map/ppermute | solution.py:263
  48.5 6.3 %collective-permute-start.15 = (bf16[32,1024]{1,0:T(8,128)(2,1)S(1)}, bf16[32,1024]{1,0:T(8,128)(2,1)S(1)}, u32[]{:S(2)}, u32[]{:S(2)}) collective-permute-start(bf16[32,1024]{1,0:T(8,128)(2,1)S(1)} %get-tuple-element.61), channel_id=1, source_target_pairs={{0,8},{4,12},{8,0},{12,4},{16,24},{20,28},{24,16},{28,20},{1,9},{5... | collective-permute-start | bytes 196616 | tf_op jit(solution)/shard_map/ppermute | solution.py:263
  50.3 4.6 %collective-permute-start.16 = (bf16[32,1024]{1,0:T(8,128)(2,1)S(1)}, bf16[32,1024]{1,0:T(8,128)(2,1)S(1)}, u32[]{:S(2)}, u32[]{:S(2)}) collective-permute-start(bf16[32,1024]{1,0:T(8,128)(2,1)S(1)} %get-tuple-element.59.refs_2_), channel_id=1, source_target_pairs={{0,12},{4,8},{8,4},{12,0},{16,28},{20,24},{24,20},{28,16},{1,13},{... | collective-permute-start | bytes 196616 | tf_op jit(solution)/shard_map/ppermute | solution.py:263
  51.5 10.3 %collective-permute-start.21 = (bf16[1,64,1024]{2,1,0:T(8,128)(2,1)S(1)}, bf16[1,64,1024]{2,1,0:T(8,128)(2,1)S(1)}, u32[]{:S(2)}, u32[]{:S(2)}) collective-permute-start(bf16[1,64,1024]{2,1,0:T(8,128)(2,1)S(1)} %totals.10.refs_3_), channel_id=1, source_target_pairs={{0,2},{1,3},{2,0},{3,1},{4,6},{5,7},{6,4},{7,5},{8,10},{9,11},{10,... | collective-permute-start | bytes 393224 | tf_op jit(solution)/shard_map/ppermute | solution.py:266
  55.1 6.9 %collective-permute-start.19 = (bf16[2,32,1024]{2,1,0:T(8,128)(2,1)S(1)}, bf16[2,32,1024]{2,1,0:T(8,128)(2,1)S(1)}, u32[]{:S(2)}, u32[]{:S(2)}) collective-permute-start(bf16[2,32,1024]{2,1,0:T(8,128)(2,1)S(1)} %bitcast.7), channel_id=1, source_target_pairs={{0,24},{4,28},{8,16},{12,20},{16,8},{20,12},{24,0},{28,4},{1,25},{... | collective-permute-start | bytes 393224 | tf_op jit(solution)/shard_map/ppermute | solution.py:263
  61.9 1.3 %collective-permute-start.22 = (bf16[32,1024]{1,0:T(8,128)(2,1)S(1)}, bf16[32,1024]{1,0:T(8,128)(2,1)S(1)}, u32[]{:S(2)}, u32[]{:S(2)}) collective-permute-start(bf16[32,1024]{1,0:T(8,128)(2,1)S(1)} %get-tuple-element.64), channel_id=1, source_target_pairs={{0,4},{4,0},{8,12},{12,8},{16,20},{20,16},{24,28},{28,24},{1,5},{5... | collective-permute-start | bytes 196616 | tf_op jit(solution)/shard_map/ppermute | solution.py:263
  62.0 1.5 %collective-permute-start.20 = (bf16[32,1024]{1,0:T(8,128)(2,1)S(1)}, bf16[32,1024]{1,0:T(8,128)(2,1)S(1)}, u32[]{:S(2)}, u32[]{:S(2)}) collective-permute-start(bf16[32,1024]{1,0:T(8,128)(2,1)S(1)} %slice_bitcast_fusion), channel_id=1, source_target_pairs={{0,4},{4,0},{8,12},{12,8},{16,20},{20,16},{24,28},{28,24},{1,5},{5... | collective-permute-start | bytes 196616 | tf_op jit(solution)/shard_map/ppermute | solution.py:263

commit v3 on v0

--- a/solution.py
+++ b/solution.py
@@ -330,14 +330,13 @@
 
     def close(g, after):
         terms = [[(own[g], 0)] + sums[g]]
-        if g in far:
+        if g:
             whole, = totals(terms, after)
             got = swap(whole.reshape(2, rows, -1), 2 * g)
             shares[2 * g], shares[2 * g + 1] = (got, 0), (swap(got[1], 1), None)
             return whole
         halves = totals(terms, after, halves=True)
-        for j, value in zip((2 * g, 2 * g + 1), halves):
-            shares[j] = (swap(value, j) if j else value, None)
+        shares[0], shares[1] = (halves[0], None), (swap(halves[1], 1), None)
         return halves[1]
 
     last = close(first, [place])
@@ -347,7 +346,7 @@
     for g in others:
         last = close(g, [last])
     for g in far:
-        last = close(g, [last] + [shares[j][0] for j in of(near)])
+        last = close(g, [last])
     close(0, [last])
     return order(place, [(j, *shares[j]) for j in of(far + near + [0])]).reshape(rows, peers, -1)
 

time: 63 us -> 64.5 us (1.024)
  waiting for transfers between devices: 17 us -> 18.2 us
    ppermute x8, waiting for transfers between devices: 13.3 us -> 14.2 us  [swap_line(): lax.ppermute(value, 'narrow', [(n, n ^ mask) for n in range(devices)])]
  transfers between devices with their start and end apart: 22 -> 22, of which waited for: 8 -> 6; matrix products, arithmetic and copies ran while one was open for 0% -> 0% of each run, Pallas kernels for 25% -> 25%
where the time goes in v3:
time: 64.5 us; the launch traced here: 64.3 us
  starting transfers between devices  26.4 us (41%)
  waiting for transfers between devices  18.2 us (28%)
  Pallas kernels  17.8 us (28%)
  local copies, waits for them, and re-layouts  0.97 us (2%)
  other arithmetic  0.72 us (1%)
    pallas_call x6, Pallas kernels, product(): pl.pallas_call(functools.partial(product_kernel, plan), out_shape=[jax.Sh...  14.9 us
    ppermute x8, waiting for transfers between devices, swap_line(): lax.ppermute(value, 'narrow', [(n, n ^ mask) for n in range(devices)])  14.2 us
    ppermute x14, starting transfers between devices, swap(): return lax.ppermute(value, 'wide', [(w, w ^ j) for w in range(peers)])  13.9 us
    ppermute x8, starting transfers between devices, swap_line(): lax.ppermute(value, 'narrow', [(n, n ^ mask) for n in range(devices)])  12.5 us
    ppermute x14, waiting for transfers between devices, swap(): return lax.ppermute(value, 'wide', [(w, w ^ j) for w in range(peers)])  3.93 us
  transfers between devices with their start and end apart: 22, of which 6 were waited for; matrix products, arithmetic and copies ran while one was open for 0% of the time, Pallas kernels for 25%

profile of v3, /device:TPU:0, one launch (start us, length us, event | category | flops | bytes accessed | tf_op | source)
XLA Modules:
  0.0 64.3 jit_solution(7374479551782254408)
XLA Ops:
  0.0 0.7 %pad_add_fusion.tables_from = s32[7,8]{1,0:T(8,128)S(1)} fusion(s32[1,8]{1,0:T(1,128)} %bitcast.16, s32[2,8]{1,0:T(2,128)} %bitcast.18, s32[4,8]{1,0:T(4,128)} %bitcast.17), kind=kLoop, calls=%fused_computation.3 | loop fusion | flops 112 | bytes 448 | tf_op jit(solution)/shard_map/concatenate | solution.py:46
  0.7 0.9 %copy-done = bf16[32,4,1024]{2,1,0:T(4,128)(2,1)S(1)} copy-done((bf16[32,4,1024]{2,1,0:T(4,128)(2,1)S(1)}, bf16[32,4,1024]{2,1,0:T(4,128)(2,1)}, u32[]{:S(2)}) %copy-start) | copy-done | bytes 262168
  1.7 0.8 %pick.1 = (bf16[2,32,1024]{2,1,0:T(8,128)(2,1)S(1)}, bf16[2,32,1024]{2,1,0:T(8,128)(2,1)S(1)}, bf16[2,32,1024]{2,1,0:T(8,128)(2,1)S(1)}, bf16[2,32,1024]{2,1,0:T...) custom-call(s32[7,8]{1,0:T(8,128)S(1)} %pad_add_fusion.tables_from, ...), custom_call_target="tpu_custom_call" | custom-call | tf_op jit(solution)/shard_map/pick/pallas_call | solution.py:48
  2.5 0.5 collective-permute-start
  3.0 2.6 %collective-permute-start.2 = (bf16[2,32,1024]{2,1,0:T(8,128)(2,1)S(1)}, bf16[2,32,1024]{2,1,0:T(8,128)(2,1)S(1)}, u32[]{:S(2)}, u32[]{:S(2)}) collective-permute-start(bf16[2,32,1024]{2,1,0:T(8,128)(2,1)S(1)} %get-tuple-element.34), channel_id=1, source_target_pairs={{0,8},{4,12},{8,0},{12,4},{16,24},{20,28},{24,16},{28,20},{1,9},{5... | collective-permute-start | bytes 393224 | tf_op jit(solution)/shard_map/ppermute | solution.py:263
  5.6 0.1 collective-permute-start.3
  5.7 1.8 %collective-permute-start.4 = (bf16[2,32,1024]{2,1,0:T(8,128)(2,1)S(1)}, bf16[2,32,1024]{2,1,0:T(8,128)(2,1)S(1)}, u32[]{:S(2)}, u32[]{:S(2)}) collective-permute-start(bf16[2,32,1024]{2,1,0:T(8,128)(2,1)S(1)} %get-tuple-element.36), channel_id=1, source_target_pairs={{0,16},{4,20},{8,24},{12,28},{16,0},{20,4},{24,8},{28,12},{1,17},{... | collective-permute-start | bytes 393224 | tf_op jit(solution)/shard_map/ppermute | solution.py:263
  7.4 0.0 collective-permute-start.5
  7.4 0.0 collective-permute-done.refs_1_.refs_2_
  7.4 4.7 %product.6 = (bf16[2,64,1024]{2,1,0:T(8,128)(2,1)S(1)}, bf16[2,2,1024,1024]{3,2,1,0:T(8,128)(2,1)S(1)}) custom-call(bf16[2,32,1024]{2,1,0:T(8,128)(2,1)S(1)} %get-tuple-element.31.refs_0_.refs_1_, bf16[2,32,1024]{2,1,0:T(8,128)(2,1)S(1)} %collective-permute-done.refs_1_.refs_2_, bf16[1,2,4096,1024]{3,2,1,0:T(8,128)(2,1)} %refs_4_.1), custom_call_target="tpu_custom_call" | custom-call | flops 2147483648 | bytes 8388608 | tf_op jit(solution)/shard_map/product/pallas_call | solution.py:152
  12.1 1.8 %collective-permute-start.1 = (bf16[2,64,1024]{2,1,0:T(8,128)(2,1)S(1)}, bf16[2,64,1024]{2,1,0:T(8,128)(2,1)S(1)}, u32[]{:S(2)}, u32[]{:S(2)}) collective-permute-start(bf16[2,64,1024]{2,1,0:T(8,128)(2,1)S(1)} %get-tuple-element.33.refs_0_), channel_id=1, source_target_pairs={{0,1},{1,0},{2,3},{3,2},{4,5},{5,4},{6,7},{7,6},{8,9},{9,8},{10,11... | collective-permute-start | bytes 786440 | tf_op jit(solution)/shard_map/ppermute | solution.py:266
  13.9 0.0 collective-permute-done.2.refs_1_.refs_3_
  13.9 0.0 collective-permute-done.3.refs_2_.refs_4_
  13.9 0.0 collective-permute-done.4.refs_3_.refs_5_
  13.9 3.1 %product.7 = (bf16[2,64,1024]{2,1,0:T(8,128)(2,1)S(1)}, bf16[2,64,1024]{2,1,0:T(8,128)(2,1)S(1)}, bf16[1,2,1024,1024]{3,2,1,0:T(8,128)(2,1)S(1)}, bf16[2,32,1024...) custom-call(bf16[2,64,1024]{2,1,0:T(8,128)(2,1)S(1)} %get-tuple-element.33.refs_0_, ...), custom_call_target="tpu_custom_call", output_to_operand_aliasing={{3}: (7, {}), {4}: (8, {})} | custom-call | flops 2147483648 | bytes 8388608 | tf_op jit(solution)/shard_map/product/pallas_call | solution.py:152
  17.0 1.6 %collective-permute-start.7 = (bf16[2,64,1024]{2,1,0:T(8,128)(2,1)S(1)}, bf16[2,64,1024]{2,1,0:T(8,128)(2,1)S(1)}, u32[]{:S(2)}, u32[]{:S(2)}) collective-permute-start(bf16[2,64,1024]{2,1,0:T(8,128)(2,1)S(1)} %get-tuple-element.45), channel_id=1, source_target_pairs={{0,1},{1,0},{2,3},{3,2},{4,5},{5,4},{6,7},{7,6},{8,9},{9,8},{10,11... | collective-permute-start | bytes 786440 | tf_op jit(solution)/shard_map/ppermute | solution.py:266
  18.7 2.4 %collective-permute-start.8 = (bf16[2,32,1024]{2,1,0:T(8,128)(2,1)S(1)}, bf16[2,32,1024]{2,1,0:T(8,128)(2,1)S(1)}, u32[]{:S(2)}, u32[]{:S(2)}) collective-permute-start(bf16[2,32,1024]{2,1,0:T(8,128)(2,1)S(1)} %get-tuple-element.46), channel_id=1, source_target_pairs={{0,24},{4,28},{8,16},{12,20},{16,8},{20,12},{24,0},{28,4},{1,25},{... | collective-permute-start | bytes 393224 | tf_op jit(solution)/shard_map/ppermute | solution.py:263
  21.1 0.0 collective-permute-start.9
  21.1 0.5 collective-permute-start.6
  21.6 0.0 collective-permute-done.1.refs_0_.refs_1_
  21.6 1.5 %product.8 = (bf16[1,64,1024]{2,1,0:T(8,128)(2,1)S(1)}, bf16[1,64,1024]{2,1,0:T(8,128)(2,1)S(1)}, bf16[1,64,1024]{2,1,0:T(8,128)(2,1)S(1)}) custom-call(bf16[2,64,1024]{2,1,0:T(8,128)(2,1)S(1)} %collective-permute-done.1.refs_0_.refs_1_, bf16[2,32,1024]{2,1,0:T(8,128)(2,1)S(1)} %get-tuple-element.31.refs_0_.refs_1_, ...), custom_call_target="tpu_custom_call" | custom-call | flops 1073741824 | bytes 4194304 | tf_op jit(solution)/shard_map/product/pallas_call | solution.py:152
  23.1 3.8 %collective-permute-done.7.refs_1_ = bf16[2,64,1024]{2,1,0:T(8,128)(2,1)S(1)} collective-permute-done((bf16[2,64,1024]{2,1,0:T(8,128)(2,1)S(1)}, bf16[2,64,1024]{2,1,0:T(8,128)(2,1)S(1)}, u32[]{:S(2)}, u32[]{:S(2)}) %collective-permute-start.7) | collective-permute-done | bytes 262176 | tf_op jit(solution)/shard_map/ppermute | solution.py:266
  26.9 2.8 %collective-permute-start.10 = (bf16[1,64,1024]{2,1,0:T(8,128)(2,1)S(1)}, bf16[1,64,1024]{2,1,0:T(8,128)(2,1)S(1)}, u32[]{:S(2)}, u32[]{:S(2)}) collective-permute-start(bf16[1,64,1024]{2,1,0:T(8,128)(2,1)S(1)} %totals.8.refs_0_), channel_id=1, source_target_pairs={{0,2},{1,3},{2,0},{3,1},{4,6},{5,7},{6,4},{7,5},{8,10},{9,11},{10,... | collective-permute-start | bytes 393224 | tf_op jit(solution)/shard_map/ppermute | solution.py:266
  29.7 2.8 %product.9 = (bf16[2,64,1024]{2,1,0:T(8,128)(2,1)S(1)}, bf16[1,2,1024,1024]{3,2,1,0:T(8,128)(2,1)S(1)}) custom-call(bf16[1,64,1024]{2,1,0:T(8,128)(2,1)S(1)} %totals.8.refs_0_, bf16[2,32,1024]{2,1,0:T(8,128)(2,1)S(1)} %collective-permute-done.8.refs_1_.refs_2_.refs_7_, bf16[2,32,1024]{2,1,0:T(8,128)(2,1)S(1)} %collective-permute-done.9.refs_2_.refs_3_.refs_8_, ...), custom_call_target="tpu_custom_call" | custom-call | flops 2147483648 | bytes 8388608 | tf_op jit(solution)/shard_map/product/pallas_call | solution.py:152
  32.6 0.0 copy-start.1
  32.6 1.6 %collective-permute-start.11 = (bf16[2,64,1024]{2,1,0:T(8,128)(2,1)S(1)}, bf16[2,64,1024]{2,1,0:T(8,128)(2,1)S(1)}, u32[]{:S(2)}, u32[]{:S(2)}) collective-permute-start(bf16[2,64,1024]{2,1,0:T(8,128)(2,1)S(1)} %get-tuple-element.48.refs_2_), channel_id=1, source_target_pairs={{0,1},{1,0},{2,3},{3,2},{4,5},{5,4},{6,7},{7,6},{8,9},{9,8},{10,11... | collective-permute-start | bytes 786440 | tf_op jit(solution)/shard_map/ppermute | solution.py:266
  34.3 1.1 %collective-permute-done.6.refs_1_ = bf16[2,64,1024]{2,1,0:T(8,128)(2,1)S(1)} collective-permute-done((bf16[2,64,1024]{2,1,0:T(8,128)(2,1)S(1)}, bf16[2,64,1024]{2,1,0:T(8,128)(2,1)S(1)}, u32[]{:S(2)}, u32[]{:S(2)}) %collective-permute-start.6) | collective-permute-done | bytes 262176 | tf_op jit(solution)/shard_map/ppermute | solution.py:266
  35.4 1.1 %collective-permute-start.13 = (bf16[1,64,1024]{2,1,0:T(8,128)(2,1)S(1)}, bf16[1,64,1024]{2,1,0:T(8,128)(2,1)S(1)}, u32[]{:S(2)}, u32[]{:S(2)}) collective-permute-start(bf16[1,64,1024]{2,1,0:T(8,128)(2,1)S(1)} %totals.9.refs_0_), channel_id=1, source_target_pairs={{0,2},{1,3},{2,0},{3,1},{4,6},{5,7},{6,4},{7,5},{8,10},{9,11},{10,... | collective-permute-start | bytes 393224 | tf_op jit(solution)/shard_map/ppermute | solution.py:266
  36.5 1.4 %product.10.refs_0_ = bf16[1,64,1024]{2,1,0:T(8,128)(2,1)S(1)} custom-call(bf16[1,64,1024]{2,1,0:T(8,128)(2,1)S(1)} %totals.9.refs_0_, bf16[1,64,1024]{2,1,0:T(8,128)(2,1)S(1)} %collective-permute-done.10.refs_1_.refs_2_, bf16[2,32,1024]{2,1,0:T(8,128)(2,1)S(1)} %collective-permute-done.8.refs_1_.refs_2_.refs_7_, ...), custom_call_target="tpu_custom_call" | custom-call | flops 1073741824 | bytes 4194304 | tf_op jit(solution)/shard_map/product/pallas_call | solution.py:152
  37.9 1.3 %product.11 = (bf16[1,64,1024]{2,1,0:T(8,128)(2,1)S(1)}, bf16[1,64,1024]{2,1,0:T(8,128)(2,1)S(1)}, bf16[1,64,1024]{2,1,0:T(8,128)(2,1)S(1)}, bf16[1,64,1024]{2,1,0:T(8,128)(2,1)S(1)}) custom-call(bf16[1,64,1024]{2,1,0:T(8,128)(2,1)S(1)} %product.10.refs_0_, bf16[2,32,1024]{2,1,0:T(8,128)(2,1)S(1)} %get-tuple-element.31.refs_0_.refs_1_, ...), custom_call_target="tpu_custom_call" | custom-call | flops 1073741824 | bytes 4194304 | tf_op jit(solution)/shard_map/product/pallas_call | solution.py:152
  39.2 0.7 %place.1.refs_3_.refs_8_ = bf16[256,256]{1,0:T(8,128)(2,1)S(1)} custom-call(s32[8]{0:T(128)S(1)} %copy-done.1, bf16[1,64,1024]{2,1,0:T(8,128)(2,1)S(1)} %get-tuple-element.52.after.refs_0_), custom_call_target="tpu_custom_call" | custom-call | tf_op jit(solution)/shard_map/place/pallas_call | solution.py:221
  39.9 0.1 totals.10.refs_2_
  40.0 1.6 %collective-permute-start.16 = (bf16[2,32,1024]{2,1,0:T(8,128)(2,1)S(1)}, bf16[2,32,1024]{2,1,0:T(8,128)(2,1)S(1)}, u32[]{:S(2)}, u32[]{:S(2)}) collective-permute-start(bf16[2,32,1024]{2,1,0:T(8,128)(2,1)S(1)} %bitcast.13), channel_id=1, source_target_pairs={{0,8},{4,12},{8,0},{12,4},{16,24},{20,28},{24,16},{28,20},{1,9},{5... | collective-permute-start | bytes 393224 | tf_op jit(solution)/shard_map/ppermute | solution.py:263
  41.6 1.7 %collective-permute-done.11.refs_1_ = bf16[2,64,1024]{2,1,0:T(8,128)(2,1)S(1)} collective-permute-done((bf16[2,64,1024]{2,1,0:T(8,128)(2,1)S(1)}, bf16[2,64,1024]{2,1,0:T(8,128)(2,1)S(1)}, u32[]{:S(2)}, u32[]{:S(2)}) %collective-permute-start.11) | collective-permute-done | bytes 262176 | tf_op jit(solution)/shard_map/ppermute | solution.py:266
  43.3 1.8 %collective-permute-start.12 = (bf16[1,64,1024]{2,1,0:T(8,128)(2,1)S(1)}, bf16[1,64,1024]{2,1,0:T(8,128)(2,1)S(1)}, u32[]{:S(2)}, u32[]{:S(2)}) collective-permute-start(bf16[1,64,1024]{2,1,0:T(8,128)(2,1)S(1)} %totals.11.refs_2_), channel_id=1, source_target_pairs={{0,2},{1,3},{2,0},{3,1},{4,6},{5,7},{6,4},{7,5},{8,10},{9,11},{10,... | collective-permute-start | bytes 393224 | tf_op jit(solution)/shard_map/ppermute | solution.py:266
  45.2 1.2 %collective-permute-start.20 = (bf16[1,64,1024]{2,1,0:T(8,128)(2,1)S(1)}, bf16[1,64,1024]{2,1,0:T(8,128)(2,1)S(1)}, u32[]{:S(2)}, u32[]{:S(2)}) collective-permute-start(bf16[1,64,1024]{2,1,0:T(8,128)(2,1)S(1)} %totals.12.refs_3_), channel_id=1, source_target_pairs={{0,2},{1,3},{2,0},{3,1},{4,6},{5,7},{6,4},{7,5},{8,10},{9,11},{10,... | collective-permute-start | bytes 393224 | tf_op jit(solution)/shard_map/ppermute | solution.py:266
  46.4 0.1 totals.13.refs_3_
  46.5 1.8 %collective-permute-start.18 = (bf16[2,32,1024]{2,1,0:T(8,128)(2,1)S(1)}, bf16[2,32,1024]{2,1,0:T(8,128)(2,1)S(1)}, u32[]{:S(2)}, u32[]{:S(2)}) collective-permute-start(bf16[2,32,1024]{2,1,0:T(8,128)(2,1)S(1)} %bitcast.15), channel_id=1, source_target_pairs={{0,16},{4,20},{8,24},{12,28},{16,0},{20,4},{24,8},{28,12},{1,17},{... | collective-permute-start | bytes 393224 | tf_op jit(solution)/shard_map/ppermute | solution.py:263
  48.2 0.1 collective-permute-start.17
  48.3 7.7 %collective-permute-done.12.refs_2_ = bf16[1,64,1024]{2,1,0:T(8,128)(2,1)S(1)} collective-permute-done((bf16[1,64,1024]{2,1,0:T(8,128)(2,1)S(1)}, bf16[1,64,1024]{2,1,0:T(8,128)(2,1)S(1)}, u32[]{:S(2)}, u32[]{:S(2)}) %collective-permute-start.12) | collective-permute-done | bytes 131104 | tf_op jit(solution)/shard_map/ppermute | solution.py:266
  56.0 0.1 totals.14.refs_3_
  56.0 2.5 %collective-permute-start.14 = (bf16[2,32,1024]{2,1,0:T(8,128)(2,1)S(1)}, bf16[2,32,1024]{2,1,0:T(8,128)(2,1)S(1)}, u32[]{:S(2)}, u32[]{:S(2)}) collective-permute-start(bf16[2,32,1024]{2,1,0:T(8,128)(2,1)S(1)} %bitcast.14), channel_id=1, source_target_pairs={{0,24},{4,28},{8,16},{12,20},{16,8},{20,12},{24,0},{28,4},{1,25},{... | collective-permute-start | bytes 393224 | tf_op jit(solution)/shard_map/ppermute | solution.py:263
  58.6 0.1 collective-permute-start.19
  58.7 0.1 totals.15
  58.7 0.5 collective-permute-start.21
  59.3 2.7 %collective-permute-done.14.refs_0_ = bf16[2,32,1024]{2,1,0:T(8,128)(2,1)S(1)} collective-permute-done((bf16[2,32,1024]{2,1,0:T(8,128)(2,1)S(1)}, bf16[2,32,1024]{2,1,0:T(8,128)(2,1)S(1)}, u32[]{:S(2)}, u32[]{:S(2)}) %collective-permute-start.14) | collective-permute-done | bytes 131104 | tf_op jit(solution)/shard_map/ppermute | solution.py:263
  62.0 1.2 %collective-permute-done.15.refs_1_ = bf16[32,1024]{1,0:T(8,128)(2,1)S(1)} collective-permute-done((bf16[32,1024]{1,0:T(8,128)(2,1)S(1)}, bf16[32,1024]{1,0:T(8,128)(2,1)S(1)}, u32[]{:S(2)}, u32[]{:S(2)}) %collective-permute-start.15) | collective-permute-done | bytes 65568 | tf_op jit(solution)/shard_map/ppermute | solution.py:263
  63.2 1.1 %order.1 = bf16[256,1024]{1,0:T(8,128)(2,1)} custom-call(bf16[2,32,1024]{2,1,0:T(8,128)(2,1)S(1)} %collective-permute-done.14.refs_0_, bf16[32,1024]{1,0:T(8,128)(2,1)S(1)} %collective-permute-done.15.refs_1_, bf16[2,32,1024]{2,1,0:T(8,128)(2,1)S(1)} %collective-permute-done.16.refs_2_, bf16[32,1024]{1,0:T(8,128)(2,1)S(1)} %collective-permute-done.17.refs_3_, ...), custom_call_target="tpu_custom_call" | custom-call | tf_op jit(solution)/shard_map/order/pallas_call | solution.py:243
  (21 shorter events, 0.2 us)
Async XLA Ops:
  0.7 0.9 %copy-start = (bf16[32,4,1024]{2,1,0:T(4,128)(2,1)S(1)}, bf16[32,4,1024]{2,1,0:T(4,128)(2,1)}, u32[]{:S(2)}) copy-start(bf16[32,4,1024]{2,1,0:T(4,128)(2,1)} %amps.1) | copy-start | bytes 786436
  2.5 4.9 %collective-permute-start = (bf16[2,32,1024]{2,1,0:T(8,128)(2,1)S(1)}, bf16[2,32,1024]{2,1,0:T(8,128)(2,1)S(1)}, u32[]{:S(2)}, u32[]{:S(2)}) collective-permute-start(bf16[2,32,1024]{2,1,0:T(8,128)(2,1)S(1)} %get-tuple-element.32), channel_id=1, source_target_pairs={{0,4},{4,0},{8,12},{12,8},{16,20},{20,16},{24,28},{28,24},{1,5},{5... | collective-permute-start | bytes 393224 | tf_op jit(solution)/shard_map/ppermute | solution.py:263
  3.0 10.9 %collective-permute-start.2 = (bf16[2,32,1024]{2,1,0:T(8,128)(2,1)S(1)}, bf16[2,32,1024]{2,1,0:T(8,128)(2,1)S(1)}, u32[]{:S(2)}, u32[]{:S(2)}) collective-permute-start(bf16[2,32,1024]{2,1,0:T(8,128)(2,1)S(1)} %get-tuple-element.34), channel_id=1, source_target_pairs={{0,8},{4,12},{8,0},{12,4},{16,24},{20,28},{24,16},{28,20},{1,9},{5... | collective-permute-start | bytes 393224 | tf_op jit(solution)/shard_map/ppermute | solution.py:263
  5.6 8.3 %collective-permute-start.3 = (bf16[2,32,1024]{2,1,0:T(8,128)(2,1)S(1)}, bf16[2,32,1024]{2,1,0:T(8,128)(2,1)S(1)}, u32[]{:S(2)}, u32[]{:S(2)}) collective-permute-start(bf16[2,32,1024]{2,1,0:T(8,128)(2,1)S(1)} %get-tuple-element.35), channel_id=1, source_target_pairs={{0,12},{4,8},{8,4},{12,0},{16,28},{20,24},{24,20},{28,16},{1,13},{... | collective-permute-start | bytes 393224 | tf_op jit(solution)/shard_map/ppermute | solution.py:263
  5.7 8.2 %collective-permute-start.4 = (bf16[2,32,1024]{2,1,0:T(8,128)(2,1)S(1)}, bf16[2,32,1024]{2,1,0:T(8,128)(2,1)S(1)}, u32[]{:S(2)}, u32[]{:S(2)}) collective-permute-start(bf16[2,32,1024]{2,1,0:T(8,128)(2,1)S(1)} %get-tuple-element.36), channel_id=1, source_target_pairs={{0,16},{4,20},{8,24},{12,28},{16,0},{20,4},{24,8},{28,12},{1,17},{... | collective-permute-start | bytes 393224 | tf_op jit(solution)/shard_map/ppermute | solution.py:263
  7.4 6.5 %collective-permute-start.5 = (bf16[2,32,1024]{2,1,0:T(8,128)(2,1)S(1)}, bf16[2,32,1024]{2,1,0:T(8,128)(2,1)S(1)}, u32[]{:S(2)}, u32[]{:S(2)}) collective-permute-start(bf16[2,32,1024]{2,1,0:T(8,128)(2,1)S(1)} %get-tuple-element.37), channel_id=1, source_target_pairs={{0,20},{4,16},{8,28},{12,24},{16,4},{20,0},{24,12},{28,8},{1,21},{... | collective-permute-start | bytes 393224 | tf_op jit(solution)/shard_map/ppermute | solution.py:263
  12.1 9.5 %collective-permute-start.1 = (bf16[2,64,1024]{2,1,0:T(8,128)(2,1)S(1)}, bf16[2,64,1024]{2,1,0:T(8,128)(2,1)S(1)}, u32[]{:S(2)}, u32[]{:S(2)}) collective-permute-start(bf16[2,64,1024]{2,1,0:T(8,128)(2,1)S(1)} %get-tuple-element.33.refs_0_), channel_id=1, source_target_pairs={{0,1},{1,0},{2,3},{3,2},{4,5},{5,4},{6,7},{7,6},{8,9},{9,8},{10,11... | collective-permute-start | bytes 786440 | tf_op jit(solution)/shard_map/ppermute | solution.py:266
  17.0 9.9 %collective-permute-start.7 = (bf16[2,64,1024]{2,1,0:T(8,128)(2,1)S(1)}, bf16[2,64,1024]{2,1,0:T(8,128)(2,1)S(1)}, u32[]{:S(2)}, u32[]{:S(2)}) collective-permute-start(bf16[2,64,1024]{2,1,0:T(8,128)(2,1)S(1)} %get-tuple-element.45), channel_id=1, source_target_pairs={{0,1},{1,0},{2,3},{3,2},{4,5},{5,4},{6,7},{7,6},{8,9},{9,8},{10,11... | collective-permute-start | bytes 786440 | tf_op jit(solution)/shard_map/ppermute | solution.py:266
  18.7 11.1 %collective-permute-start.8 = (bf16[2,32,1024]{2,1,0:T(8,128)(2,1)S(1)}, bf16[2,32,1024]{2,1,0:T(8,128)(2,1)S(1)}, u32[]{:S(2)}, u32[]{:S(2)}) collective-permute-start(bf16[2,32,1024]{2,1,0:T(8,128)(2,1)S(1)} %get-tuple-element.46), channel_id=1, source_target_pairs={{0,24},{4,28},{8,16},{12,20},{16,8},{20,12},{24,0},{28,4},{1,25},{... | collective-permute-start | bytes 393224 | tf_op jit(solution)/shard_map/ppermute | solution.py:263
  21.1 8.6 %collective-permute-start.9 = (bf16[2,32,1024]{2,1,0:T(8,128)(2,1)S(1)}, bf16[2,32,1024]{2,1,0:T(8,128)(2,1)S(1)}, u32[]{:S(2)}, u32[]{:S(2)}) collective-permute-start(bf16[2,32,1024]{2,1,0:T(8,128)(2,1)S(1)} %get-tuple-element.47), channel_id=1, source_target_pairs={{0,28},{4,24},{8,20},{12,16},{16,12},{20,8},{24,4},{28,0},{1,29},{... | collective-permute-start | bytes 393224 | tf_op jit(solution)/shard_map/ppermute | solution.py:263
  21.1 14.2 %collective-permute-start.6 = (bf16[2,64,1024]{2,1,0:T(8,128)(2,1)S(1)}, bf16[2,64,1024]{2,1,0:T(8,128)(2,1)S(1)}, u32[]{:S(2)}, u32[]{:S(2)}) collective-permute-start(bf16[2,64,1024]{2,1,0:T(8,128)(2,1)S(1)} %get-tuple-element.43), channel_id=1, source_target_pairs={{0,1},{1,0},{2,3},{3,2},{4,5},{5,4},{6,7},{7,6},{8,9},{9,8},{10,11... | collective-permute-start | bytes 786440 | tf_op jit(solution)/shard_map/ppermute | solution.py:266
  26.9 9.6 %collective-permute-start.10 = (bf16[1,64,1024]{2,1,0:T(8,128)(2,1)S(1)}, bf16[1,64,1024]{2,1,0:T(8,128)(2,1)S(1)}, u32[]{:S(2)}, u32[]{:S(2)}) collective-permute-start(bf16[1,64,1024]{2,1,0:T(8,128)(2,1)S(1)} %totals.8.refs_0_), channel_id=1, source_target_pairs={{0,2},{1,3},{2,0},{3,1},{4,6},{5,7},{6,4},{7,5},{8,10},{9,11},{10,... | collective-permute-start | bytes 393224 | tf_op jit(solution)/shard_map/ppermute | solution.py:266
  32.6 6.6 %copy-start.1 = (s32[8]{0:T(128)S(1)}, s32[8]{0:T(128)}, u32[]{:S(2)}) copy-start(s32[8]{0:T(128)} %q_owner.1) | copy-start | bytes 100
  32.6 10.7 %collective-permute-start.11 = (bf16[2,64,1024]{2,1,0:T(8,128)(2,1)S(1)}, bf16[2,64,1024]{2,1,0:T(8,128)(2,1)S(1)}, u32[]{:S(2)}, u32[]{:S(2)}) collective-permute-start(bf16[2,64,1024]{2,1,0:T(8,128)(2,1)S(1)} %get-tuple-element.48.refs_2_), channel_id=1, source_target_pairs={{0,1},{1,0},{2,3},{3,2},{4,5},{5,4},{6,7},{7,6},{8,9},{9,8},{10,11... | collective-permute-start | bytes 786440 | tf_op jit(solution)/shard_map/ppermute | solution.py:266
  35.4 11.0 %collective-permute-start.13 = (bf16[1,64,1024]{2,1,0:T(8,128)(2,1)S(1)}, bf16[1,64,1024]{2,1,0:T(8,128)(2,1)S(1)}, u32[]{:S(2)}, u32[]{:S(2)}) collective-permute-start(bf16[1,64,1024]{2,1,0:T(8,128)(2,1)S(1)} %totals.9.refs_0_), channel_id=1, source_target_pairs={{0,2},{1,3},{2,0},{3,1},{4,6},{5,7},{6,4},{7,5},{8,10},{9,11},{10,... | collective-permute-start | bytes 393224 | tf_op jit(solution)/shard_map/ppermute | solution.py:266
  40.0 8.2 %collective-permute-start.16 = (bf16[2,32,1024]{2,1,0:T(8,128)(2,1)S(1)}, bf16[2,32,1024]{2,1,0:T(8,128)(2,1)S(1)}, u32[]{:S(2)}, u32[]{:S(2)}) collective-permute-start(bf16[2,32,1024]{2,1,0:T(8,128)(2,1)S(1)} %bitcast.13), channel_id=1, source_target_pairs={{0,8},{4,12},{8,0},{12,4},{16,24},{20,28},{24,16},{28,20},{1,9},{5... | collective-permute-start | bytes 393224 | tf_op jit(solution)/shard_map/ppermute | solution.py:263
  43.3 12.7 %collective-permute-start.12 = (bf16[1,64,1024]{2,1,0:T(8,128)(2,1)S(1)}, bf16[1,64,1024]{2,1,0:T(8,128)(2,1)S(1)}, u32[]{:S(2)}, u32[]{:S(2)}) collective-permute-start(bf16[1,64,1024]{2,1,0:T(8,128)(2,1)S(1)} %totals.11.refs_2_), channel_id=1, source_target_pairs={{0,2},{1,3},{2,0},{3,1},{4,6},{5,7},{6,4},{7,5},{8,10},{9,11},{10,... | collective-permute-start | bytes 393224 | tf_op jit(solution)/shard_map/ppermute | solution.py:266
  45.2 13.5 %collective-permute-start.20 = (bf16[1,64,1024]{2,1,0:T(8,128)(2,1)S(1)}, bf16[1,64,1024]{2,1,0:T(8,128)(2,1)S(1)}, u32[]{:S(2)}, u32[]{:S(2)}) collective-permute-start(bf16[1,64,1024]{2,1,0:T(8,128)(2,1)S(1)} %totals.12.refs_3_), channel_id=1, source_target_pairs={{0,2},{1,3},{2,0},{3,1},{4,6},{5,7},{6,4},{7,5},{8,10},{9,11},{10,... | collective-permute-start | bytes 393224 | tf_op jit(solution)/shard_map/ppermute | solution.py:266
  46.5 12.1 %collective-permute-start.18 = (bf16[2,32,1024]{2,1,0:T(8,128)(2,1)S(1)}, bf16[2,32,1024]{2,1,0:T(8,128)(2,1)S(1)}, u32[]{:S(2)}, u32[]{:S(2)}) collective-permute-start(bf16[2,32,1024]{2,1,0:T(8,128)(2,1)S(1)} %bitcast.15), channel_id=1, source_target_pairs={{0,16},{4,20},{8,24},{12,28},{16,0},{20,4},{24,8},{28,12},{1,17},{... | collective-permute-start | bytes 393224 | tf_op jit(solution)/shard_map/ppermute | solution.py:263
  48.2 13.7 %collective-permute-start.17 = (bf16[32,1024]{1,0:T(8,128)(2,1)S(1)}, bf16[32,1024]{1,0:T(8,128)(2,1)S(1)}, u32[]{:S(2)}, u32[]{:S(2)}) collective-permute-start(bf16[32,1024]{1,0:T(8,128)(2,1)S(1)} %slice_bitcast_fusion.1), channel_id=1, source_target_pairs={{0,4},{4,0},{8,12},{12,8},{16,20},{20,16},{24,28},{28,24},{1,5},{5... | collective-permute-start | bytes 196616 | tf_op jit(solution)/shard_map/ppermute | solution.py:263
  56.0 5.9 %collective-permute-start.14 = (bf16[2,32,1024]{2,1,0:T(8,128)(2,1)S(1)}, bf16[2,32,1024]{2,1,0:T(8,128)(2,1)S(1)}, u32[]{:S(2)}, u32[]{:S(2)}) collective-permute-start(bf16[2,32,1024]{2,1,0:T(8,128)(2,1)S(1)} %bitcast.14), channel_id=1, source_target_pairs={{0,24},{4,28},{8,16},{12,20},{16,8},{20,12},{24,0},{28,4},{1,25},{... | collective-permute-start | bytes 393224 | tf_op jit(solution)/shard_map/ppermute | solution.py:263
  58.6 3.4 %collective-permute-start.19 = (bf16[32,1024]{1,0:T(8,128)(2,1)S(1)}, bf16[32,1024]{1,0:T(8,128)(2,1)S(1)}, u32[]{:S(2)}, u32[]{:S(2)}) collective-permute-start(bf16[32,1024]{1,0:T(8,128)(2,1)S(1)} %slice_bitcast_fusion), channel_id=1, source_target_pairs={{0,4},{4,0},{8,12},{12,8},{16,20},{20,16},{24,28},{28,24},{1,5},{5... | collective-permute-start | bytes 196616 | tf_op jit(solution)/shard_map/ppermute | solution.py:263
  58.7 3.3 %collective-permute-start.21 = (bf16[32,1024]{1,0:T(8,128)(2,1)S(1)}, bf16[32,1024]{1,0:T(8,128)(2,1)S(1)}, u32[]{:S(2)}, u32[]{:S(2)}) collective-permute-start(bf16[32,1024]{1,0:T(8,128)(2,1)S(1)} %get-tuple-element.56), channel_id=1, source_target_pairs={{0,4},{4,0},{8,12},{12,8},{16,20},{20,16},{24,28},{28,24},{1,5},{5... | collective-permute-start | bytes 196616 | tf_op jit(solution)/shard_map/ppermute | solution.py:263
  62.0 1.3 %collective-permute-start.15 = (bf16[32,1024]{1,0:T(8,128)(2,1)S(1)}, bf16[32,1024]{1,0:T(8,128)(2,1)S(1)}, u32[]{:S(2)}, u32[]{:S(2)}) collective-permute-start(bf16[32,1024]{1,0:T(8,128)(2,1)S(1)} %slice_bitcast_fusion.2), channel_id=1, source_target_pairs={{0,4},{4,0},{8,12},{12,8},{16,20},{20,16},{24,28},{28,24},{1,5},{5... | collective-permute-start | bytes 196616 | tf_op jit(solution)/shard_map/ppermute | solution.py:263

commit v4 on v3

--- a/solution.py
+++ b/solution.py
@@ -284,71 +284,71 @@
         return messages[0], terms[0]
 
     chips = peers // 2
-    near = [g for g in range(1, chips) if g & (g - 1) == 0]
-    far = [g for g in range(1, chips) if g & (g - 1)]
-
-    def of(groups):
-        return [j for g in groups for j in (2 * g, 2 * g + 1)]
-
-    def multiply(groups, use, held=None, fetch=(), passed=(), after=(), limit=LIMIT):
-        chosen = [lot[j] for j in of(groups)]
+    mine = (0, 1)
+    near = [(2 * g, 2 * g + 1) for g in range(1, chips) if g & (g - 1) == 0]
+    far = [(j,) for g in range(1, chips) if g & (g - 1) for j in (2 * g, 2 * g + 1)]
+
+    def multiply(units, use, held=None, fetch=(), passed=(), after=(), limit=LIMIT):
+        chosen = [lot[j] for unit in units for j in unit]
         outs, brought, passed = product(
-            chosen, len(groups), use, held, integrals, fetch, list(passed), list(after), limit
+            chosen, len(units), use, held, integrals, fetch, list(passed), list(after), limit
         )
-        return dict(zip(groups, outs)), *brought, passed
+        return dict(zip(units, outs)), *brought, passed
 
     lot = dict(enumerate(pick(amplitudes, amp_tiles, cd_tiles, q_owner)))
-    for j in [1] + of(near):
+    for j in [1] + [j for unit in near for j in unit]:
         lot[j] = swap(lot[j], j)
 
     come, ready, sums = {}, {}, {}
     first, others = near[0], near[1:]
     all_odd, all_middle = tuple(range(len(odd))), tuple(range(len(middle)))
-    away, odd_ints, _ = multiply([0], all_odd, fetch=odd, limit=FIRST)
-    come[0] = first_step(away[0])
+    away, odd_ints, _ = multiply([mine], all_odd, fetch=odd, limit=FIRST)
+    come[mine] = first_step(away[mine])
     outs, middle_ints, passed = multiply(
-        near, all_odd, odd_ints, middle, [lot[j] for j in of(far)], [away[0]]
+        near, all_odd, odd_ints, middle, [lot[j] for j, in far], [away[mine]]
     )
-    lot.update((j, swap(value, j)) for j, value in zip(of(far), passed))
+    lot.update((j, swap(value, j)) for (j,), value in zip(far, passed))
     away.update(outs)
-    come.update((g, first_step(away[g])) for g in near)
-    kept, _ = multiply([0] + near, all_middle, middle_ints, after=[come[0]])
+    come.update((u, first_step(away[u])) for u in near)
+    kept, _ = multiply([mine] + near, all_middle, middle_ints, after=[come[mine]])
     ready[first], sums[first] = later_steps(kept[first], come[first])
     outs, home_ints, _ = multiply(far, all_odd, odd_ints, (0,), after=[ready[first]])
     away.update(outs)
-    come.update((g, first_step(away[g])) for g in far)
+    come.update((u, first_step(away[u])) for u in far)
     last = away[far[0]]
-    for g in others:
-        ready[g], sums[g] = later_steps(kept[g], come[g], [last])
-        last = ready[g]
+    for u in others:
+        ready[u], sums[u] = later_steps(kept[u], come[u], [last])
+        last = ready[u]
     outs, _ = multiply(far, all_middle, middle_ints, after=[last, sums[first][-1][0]])
     kept.update(outs)
-    own, _ = multiply(range(chips), (0,), home_ints, after=[kept[far[0]]])
-    place = place_of(q_owner, peers * rows, own[0])
+    own, _ = multiply([mine] + near, (0,), home_ints, after=[kept[far[0]]])
+    outs, _ = multiply(far, (0,), home_ints, after=[own[mine]])
+    own.update(outs)
+    place = place_of(q_owner, peers * rows, own[far[0]])
 
     shares = {}
 
-    def close(g, after):
-        terms = [[(own[g], 0)] + sums[g]]
-        if g:
-            whole, = totals(terms, after)
-            got = swap(whole.reshape(2, rows, -1), 2 * g)
-            shares[2 * g], shares[2 * g + 1] = (got, 0), (swap(got[1], 1), None)
-            return whole
-        halves = totals(terms, after, halves=True)
-        shares[0], shares[1] = (halves[0], None), (swap(halves[1], 1), None)
-        return halves[1]
+    def close(u, after):
+        terms = [[(own[u], 0)] + sums[u]]
+        if u == mine:
+            halves = totals(terms, after, halves=True)
+            shares[0], shares[1] = (halves[0], None), (swap(halves[1], 1), None)
+            return halves[1]
+        whole, = totals(terms, after)
+        j = u[0]
+        got = swap(whole.reshape(len(u), rows, -1), j)
+        shares[j] = got, 0
+        if len(u) == 2:
+            shares[j + 1] = swap(got[1], 1), None
+        return whole
 
     last = close(first, [place])
-    for g in far + [0]:
-        ready[g], sums[g] = later_steps(kept[g], come[g], [last])
-        last = ready[g]
-    for g in others:
-        last = close(g, [last])
-    for g in far:
-        last = close(g, [last])
-    close(0, [last])
-    return order(place, [(j, *shares[j]) for j in of(far + near + [0])]).reshape(rows, peers, -1)
+    for u in far + [mine]:
+        ready[u], sums[u] = later_steps(kept[u], come[u], [last])
+        last = ready[u]
+    for u in others + far + [mine]:
+        last = close(u, [last])
+    return order(place, [(j, *shares[j]) for u in far + near + [mine] for j in u]).reshape(rows, peers, -1)
 
 
 def solution(mesh):

time: 64.5 us -> 63.4 us (0.983)
  waiting for transfers between devices: 18.2 us -> 12.4 us
  starting transfers between devices: 26.4 us -> 29.5 us
  Pallas kernels: 17.8 us -> 19.5 us
    ppermute x8 -> x10, waiting for transfers between devices: 14.2 us -> 9.68 us  [swap_line(): lax.ppermute(value, 'narrow', [(n, n ^ mask) for n in range(devices)])]
    ppermute x8 -> x10, starting transfers between devices: 12.5 us -> 15.1 us  [swap_line(): lax.ppermute(value, 'narrow', [(n, n ^ mask) for n in range(devices)])]
    pallas_call x6 -> x7, Pallas kernels: 14.9 us -> 16.5 us  [product(): pl.pallas_call(functools.partial(product_kernel, plan), out_shape=[jax.Sh...]
    ppermute x14, waiting for transfers between devices: 3.93 us -> 2.67 us  [swap(): return lax.ppermute(value, 'wide', [(w, w ^ j) for w in range(peers)])]
  transfers between devices with their start and end apart: 22 -> 24, of which waited for: 6 -> 4; matrix products, arithmetic and copies ran while one was open for 0% -> 0% of each run, Pallas kernels for 25% -> 28%
where the time goes in v4:
time: 63.4 us; the launch traced here: 63.2 us
  starting transfers between devices  29.5 us (47%)
  Pallas kernels  19.5 us (31%)
  waiting for transfers between devices  12.4 us (20%)
  local copies, waits for them, and re-layouts  0.97 us (2%)
  other arithmetic  0.72 us (1%)
    pallas_call x7, Pallas kernels, product(): pl.pallas_call(functools.partial(product_kernel, plan), out_shape=[jax.Sh...  16.5 us
    ppermute x10, starting transfers between devices, swap_line(): lax.ppermute(value, 'narrow', [(n, n ^ mask) for n in range(devices)])  15.1 us
    ppermute x14, starting transfers between devices, swap(): return lax.ppermute(value, 'wide', [(w, w ^ j) for w in range(peers)])  14.4 us
    ppermute x10, waiting for transfers between devices, swap_line(): lax.ppermute(value, 'narrow', [(n, n ^ mask) for n in range(devices)])  9.68 us
    ppermute x14, waiting for transfers between devices, swap(): return lax.ppermute(value, 'wide', [(w, w ^ j) for w in range(peers)])  2.67 us
  transfers between devices with their start and end apart: 24, of which 4 were waited for; matrix products, arithmetic and copies ran while one was open for 0% of the time, Pallas kernels for 28%

profile of v4, /device:TPU:0, one launch (start us, length us, event | category | flops | bytes accessed | tf_op | source)
XLA Modules:
  0.0 63.2 jit_solution(10360643530558227427)
XLA Ops:
  0.0 0.7 %pad_add_fusion.tables_from = s32[7,8]{1,0:T(8,128)S(1)} fusion(s32[1,8]{1,0:T(1,128)} %bitcast.12, s32[2,8]{1,0:T(2,128)} %bitcast.14, s32[4,8]{1,0:T(4,128)} %bitcast.13), kind=kLoop, calls=%fused_computation.2 | loop fusion | flops 112 | bytes 448 | tf_op jit(solution)/shard_map/concatenate | solution.py:46
  0.7 0.9 %copy-done = bf16[32,4,1024]{2,1,0:T(4,128)(2,1)S(1)} copy-done((bf16[32,4,1024]{2,1,0:T(4,128)(2,1)S(1)}, bf16[32,4,1024]{2,1,0:T(4,128)(2,1)}, u32[]{:S(2)}) %copy-start) | copy-done | bytes 262168
  1.7 0.8 %pick.1 = (bf16[2,32,1024]{2,1,0:T(8,128)(2,1)S(1)}, bf16[2,32,1024]{2,1,0:T(8,128)(2,1)S(1)}, bf16[2,32,1024]{2,1,0:T(8,128)(2,1)S(1)}, bf16[2,32,1024]{2,1,0:T...) custom-call(s32[7,8]{1,0:T(8,128)S(1)} %pad_add_fusion.tables_from, ...), custom_call_target="tpu_custom_call" | custom-call | tf_op jit(solution)/shard_map/pick/pallas_call | solution.py:48
  2.5 0.5 collective-permute-start
  3.0 2.6 %collective-permute-start.2 = (bf16[2,32,1024]{2,1,0:T(8,128)(2,1)S(1)}, bf16[2,32,1024]{2,1,0:T(8,128)(2,1)S(1)}, u32[]{:S(2)}, u32[]{:S(2)}) collective-permute-start(bf16[2,32,1024]{2,1,0:T(8,128)(2,1)S(1)} %get-tuple-element.38), channel_id=1, source_target_pairs={{0,8},{4,12},{8,0},{12,4},{16,24},{20,28},{24,16},{28,20},{1,9},{5... | collective-permute-start | bytes 393224 | tf_op jit(solution)/shard_map/ppermute | solution.py:263
  5.6 0.1 collective-permute-start.3
  5.7 1.8 %collective-permute-start.4 = (bf16[2,32,1024]{2,1,0:T(8,128)(2,1)S(1)}, bf16[2,32,1024]{2,1,0:T(8,128)(2,1)S(1)}, u32[]{:S(2)}, u32[]{:S(2)}) collective-permute-start(bf16[2,32,1024]{2,1,0:T(8,128)(2,1)S(1)} %get-tuple-element.40), channel_id=1, source_target_pairs={{0,16},{4,20},{8,24},{12,28},{16,0},{20,4},{24,8},{28,12},{1,17},{... | collective-permute-start | bytes 393224 | tf_op jit(solution)/shard_map/ppermute | solution.py:263
  7.4 0.0 collective-permute-start.5
  7.4 0.0 collective-permute-done.refs_1_.refs_2_
  7.4 4.7 %product.7 = (bf16[2,64,1024]{2,1,0:T(8,128)(2,1)S(1)}, bf16[2,2,1024,1024]{3,2,1,0:T(8,128)(2,1)S(1)}) custom-call(bf16[2,32,1024]{2,1,0:T(8,128)(2,1)S(1)} %get-tuple-element.35.refs_0_.refs_1_, bf16[2,32,1024]{2,1,0:T(8,128)(2,1)S(1)} %collective-permute-done.refs_1_.refs_2_, bf16[1,2,4096,1024]{3,2,1,0:T(8,128)(2,1)} %refs_4_.1), custom_call_target="tpu_custom_call" | custom-call | flops 2147483648 | bytes 8388608 | tf_op jit(solution)/shard_map/product/pallas_call | solution.py:152
  12.1 1.8 %collective-permute-start.1 = (bf16[2,64,1024]{2,1,0:T(8,128)(2,1)S(1)}, bf16[2,64,1024]{2,1,0:T(8,128)(2,1)S(1)}, u32[]{:S(2)}, u32[]{:S(2)}) collective-permute-start(bf16[2,64,1024]{2,1,0:T(8,128)(2,1)S(1)} %get-tuple-element.37.refs_0_), channel_id=1, source_target_pairs={{0,1},{1,0},{2,3},{3,2},{4,5},{5,4},{6,7},{7,6},{8,9},{9,8},{10,11... | collective-permute-start | bytes 786440 | tf_op jit(solution)/shard_map/ppermute | solution.py:266
  13.9 0.0 collective-permute-done.2.refs_1_.refs_3_
  13.9 0.0 collective-permute-done.3.refs_2_.refs_4_
  13.9 0.0 collective-permute-done.4.refs_3_.refs_5_
  13.9 3.1 %product.8 = (bf16[2,64,1024]{2,1,0:T(8,128)(2,1)S(1)}, bf16[2,64,1024]{2,1,0:T(8,128)(2,1)S(1)}, bf16[1,2,1024,1024]{3,2,1,0:T(8,128)(2,1)S(1)}, bf16[2,32,1024...) custom-call(bf16[2,64,1024]{2,1,0:T(8,128)(2,1)S(1)} %get-tuple-element.37.refs_0_, ...), custom_call_target="tpu_custom_call", output_to_operand_aliasing={{3}: (7, {}), {4}: (8, {})} | custom-call | flops 2147483648 | bytes 8388608 | tf_op jit(solution)/shard_map/product/pallas_call | solution.py:152
  17.0 1.6 %collective-permute-start.7 = (bf16[2,64,1024]{2,1,0:T(8,128)(2,1)S(1)}, bf16[2,64,1024]{2,1,0:T(8,128)(2,1)S(1)}, u32[]{:S(2)}, u32[]{:S(2)}) collective-permute-start(bf16[2,64,1024]{2,1,0:T(8,128)(2,1)S(1)} %get-tuple-element.49), channel_id=1, source_target_pairs={{0,1},{1,0},{2,3},{3,2},{4,5},{5,4},{6,7},{7,6},{8,9},{9,8},{10,11... | collective-permute-start | bytes 786440 | tf_op jit(solution)/shard_map/ppermute | solution.py:266
  18.7 2.4 %collective-permute-start.8 = (bf16[2,32,1024]{2,1,0:T(8,128)(2,1)S(1)}, bf16[2,32,1024]{2,1,0:T(8,128)(2,1)S(1)}, u32[]{:S(2)}, u32[]{:S(2)}) collective-permute-start(bf16[2,32,1024]{2,1,0:T(8,128)(2,1)S(1)} %get-tuple-element.50), channel_id=1, source_target_pairs={{0,24},{4,28},{8,16},{12,20},{16,8},{20,12},{24,0},{28,4},{1,25},{... | collective-permute-start | bytes 393224 | tf_op jit(solution)/shard_map/ppermute | solution.py:263
  21.1 0.0 collective-permute-start.9
  21.1 0.5 collective-permute-start.6
  21.6 1.5 %product.9 = (bf16[1,64,1024]{2,1,0:T(8,128)(2,1)S(1)}, bf16[1,64,1024]{2,1,0:T(8,128)(2,1)S(1)}, bf16[1,64,1024]{2,1,0:T(8,128)(2,1)S(1)}) custom-call(bf16[2,64,1024]{2,1,0:T(8,128)(2,1)S(1)} %collective-permute-done.1.refs_0_.refs_1_, bf16[2,32,1024]{2,1,0:T(8,128)(2,1)S(1)} %get-tuple-element.35.refs_0_.refs_1_, ...), custom_call_target="tpu_custom_call" | custom-call | flops 1073741824 | bytes 4194304 | tf_op jit(solution)/shard_map/product/pallas_call | solution.py:152
  23.1 3.8 %collective-permute-done.7.refs_1_ = bf16[2,64,1024]{2,1,0:T(8,128)(2,1)S(1)} collective-permute-done((bf16[2,64,1024]{2,1,0:T(8,128)(2,1)S(1)}, bf16[2,64,1024]{2,1,0:T(8,128)(2,1)S(1)}, u32[]{:S(2)}, u32[]{:S(2)}) %collective-permute-start.7) | collective-permute-done | bytes 262176 | tf_op jit(solution)/shard_map/ppermute | solution.py:266
  26.9 2.8 %collective-permute-start.10 = (bf16[1,64,1024]{2,1,0:T(8,128)(2,1)S(1)}, bf16[1,64,1024]{2,1,0:T(8,128)(2,1)S(1)}, u32[]{:S(2)}, u32[]{:S(2)}) collective-permute-start(bf16[1,64,1024]{2,1,0:T(8,128)(2,1)S(1)} %totals.10.refs_0_), channel_id=1, source_target_pairs={{0,2},{1,3},{2,0},{3,1},{4,6},{5,7},{6,4},{7,5},{8,10},{9,11},{10,... | collective-permute-start | bytes 393224 | tf_op jit(solution)/shard_map/ppermute | solution.py:266
  29.7 2.8 %product.10 = (bf16[2,32,1024]{2,1,0:T(8,128)(2,1)S(1)}, bf16[2,32,1024]{2,1,0:T(8,128)(2,1)S(1)}, bf16[1,2,1024,1024]{3,2,1,0:T(8,128)(2,1)S(1)}) custom-call(bf16[1,64,1024]{2,1,0:T(8,128)(2,1)S(1)} %totals.10.refs_0_, bf16[2,32,1024]{2,1,0:T(8,128)(2,1)S(1)} %collective-permute-done.8.refs_1_.refs_2_, ...), custom_call_target="tpu_custom_call" | custom-call | flops 2147483648 | bytes 8388608 | tf_op jit(solution)/shard_map/product/pallas_call | solution.py:152
  32.6 0.0 copy-start.1
  32.6 1.6 %collective-permute-start.11 = (bf16[2,32,1024]{2,1,0:T(8,128)(2,1)S(1)}, bf16[2,32,1024]{2,1,0:T(8,128)(2,1)S(1)}, u32[]{:S(2)}, u32[]{:S(2)}) collective-permute-start(bf16[2,32,1024]{2,1,0:T(8,128)(2,1)S(1)} %get-tuple-element.52.refs_2_), channel_id=1, source_target_pairs={{0,1},{1,0},{2,3},{3,2},{4,5},{5,4},{6,7},{7,6},{8,9},{9,8},{10,11... | collective-permute-start | bytes 393224 | tf_op jit(solution)/shard_map/ppermute | solution.py:266
  34.3 1.1 %collective-permute-done.6.refs_1_ = bf16[2,64,1024]{2,1,0:T(8,128)(2,1)S(1)} collective-permute-done((bf16[2,64,1024]{2,1,0:T(8,128)(2,1)S(1)}, bf16[2,64,1024]{2,1,0:T(8,128)(2,1)S(1)}, u32[]{:S(2)}, u32[]{:S(2)}) %collective-permute-start.6) | collective-permute-done | bytes 262176 | tf_op jit(solution)/shard_map/ppermute | solution.py:266
  35.4 1.1 %collective-permute-start.13 = (bf16[1,64,1024]{2,1,0:T(8,128)(2,1)S(1)}, bf16[1,64,1024]{2,1,0:T(8,128)(2,1)S(1)}, u32[]{:S(2)}, u32[]{:S(2)}) collective-permute-start(bf16[1,64,1024]{2,1,0:T(8,128)(2,1)S(1)} %totals.11.refs_0_), channel_id=1, source_target_pairs={{0,2},{1,3},{2,0},{3,1},{4,6},{5,7},{6,4},{7,5},{8,10},{9,11},{10,... | collective-permute-start | bytes 393224 | tf_op jit(solution)/shard_map/ppermute | solution.py:266
  36.5 2.4 %collective-permute-start.14 = (bf16[2,32,1024]{2,1,0:T(8,128)(2,1)S(1)}, bf16[2,32,1024]{2,1,0:T(8,128)(2,1)S(1)}, u32[]{:S(2)}, u32[]{:S(2)}) collective-permute-start(bf16[2,32,1024]{2,1,0:T(8,128)(2,1)S(1)} %get-tuple-element.61), channel_id=1, source_target_pairs={{0,1},{1,0},{2,3},{3,2},{4,5},{5,4},{6,7},{7,6},{8,9},{9,8},{10,11... | collective-permute-start | bytes 393224 | tf_op jit(solution)/shard_map/ppermute | solution.py:266
  38.9 1.4 %product.11 = (bf16[1,32,1024]{2,1,0:T(8,128)(2,1)S(1)}, bf16[1,32,1024]{2,1,0:T(8,128)(2,1)S(1)}) custom-call(bf16[1,64,1024]{2,1,0:T(8,128)(2,1)S(1)} %totals.11.refs_0_, bf16[1,64,1024]{2,1,0:T(8,128)(2,1)S(1)} %collective-permute-done.10.refs_1_.refs_2_, bf16[2,32,1024]{2,1,0:T(8,128)(2,1)S(1)} %collective-permute-done.8.refs_1_.refs_2_, ...), custom_call_target="tpu_custom_call" | custom-call | flops 1073741824 | bytes 4194304 | tf_op jit(solution)/shard_map/product/pallas_call | solution.py:152
  40.3 1.5 %product.12 = (bf16[1,64,1024]{2,1,0:T(8,128)(2,1)S(1)}, bf16[1,64,1024]{2,1,0:T(8,128)(2,1)S(1)}, bf16[1,64,1024]{2,1,0:T(8,128)(2,1)S(1)}) custom-call(bf16[1,32,1024]{2,1,0:T(8,128)(2,1)S(1)} %get-tuple-element.53.refs_0_, bf16[2,32,1024]{2,1,0:T(8,128)(2,1)S(1)} %get-tuple-element.35.refs_0_.refs_1_, ...), custom_call_target="tpu_custom_call" | custom-call | flops 1073741824 | bytes 4194304 | tf_op jit(solution)/shard_map/product/pallas_call | solution.py:152
  41.9 1.4 %product.13 = (bf16[1,32,1024]{2,1,0:T(8,128)(2,1)S(1)}, bf16[1,32,1024]{2,1,0:T(8,128)(2,1)S(1)}) custom-call(bf16[1,64,1024]{2,1,0:T(8,128)(2,1)S(1)} %get-tuple-element.55.refs_0_, bf16[2,32,1024]{2,1,0:T(8,128)(2,1)S(1)} %collective-permute-done.8.refs_1_.refs_2_, bf16[2,32,1024]{2,1,0:T(8,128)(2,1)S(1)} %collective-permute-done.9.refs_2_.refs_3_, ...), custom_call_target="tpu_custom_call" | custom-call | flops 1073741824 | bytes 4194304 | tf_op jit(solution)/shard_map/product/pallas_call | solution.py:152
  43.3 0.7 %place.1.refs_3_.refs_8_ = bf16[256,256]{1,0:T(8,128)(2,1)S(1)} custom-call(s32[8]{0:T(128)S(1)} %copy-done.1, bf16[1,32,1024]{2,1,0:T(8,128)(2,1)S(1)} %get-tuple-element.56.after.refs_0_), custom_call_target="tpu_custom_call" | custom-call | tf_op jit(solution)/shard_map/place/pallas_call | solution.py:221
  44.0 0.1 totals.12.refs_2_
  44.1 1.5 %collective-permute-start.18 = (bf16[2,32,1024]{2,1,0:T(8,128)(2,1)S(1)}, bf16[2,32,1024]{2,1,0:T(8,128)(2,1)S(1)}, u32[]{:S(2)}, u32[]{:S(2)}) collective-permute-start(bf16[2,32,1024]{2,1,0:T(8,128)(2,1)S(1)} %bitcast.10), channel_id=1, source_target_pairs={{0,8},{4,12},{8,0},{12,4},{16,24},{20,28},{24,16},{28,20},{1,9},{5... | collective-permute-start | bytes 393224 | tf_op jit(solution)/shard_map/ppermute | solution.py:263
  45.7 0.1 collective-permute-start.12
  45.8 2.9 %collective-permute-start.16 = (bf16[1,32,1024]{2,1,0:T(8,128)(2,1)S(1)}, bf16[1,32,1024]{2,1,0:T(8,128)(2,1)S(1)}, u32[]{:S(2)}, u32[]{:S(2)}) collective-permute-start(bf16[1,32,1024]{2,1,0:T(8,128)(2,1)S(1)} %totals.14.refs_2_), channel_id=1, source_target_pairs={{0,2},{1,3},{2,0},{3,1},{4,6},{5,7},{6,4},{7,5},{8,10},{9,11},{10,... | collective-permute-start | bytes 196616 | tf_op jit(solution)/shard_map/ppermute | solution.py:266
  48.8 0.1 collective-permute-start.22
  48.9 0.1 totals.16.refs_3_
  49.0 1.6 %collective-permute-start.20 = (bf16[2,32,1024]{2,1,0:T(8,128)(2,1)S(1)}, bf16[2,32,1024]{2,1,0:T(8,128)(2,1)S(1)}, u32[]{:S(2)}, u32[]{:S(2)}) collective-permute-start(bf16[2,32,1024]{2,1,0:T(8,128)(2,1)S(1)} %bitcast.11), channel_id=1, source_target_pairs={{0,16},{4,20},{8,24},{12,28},{16,0},{20,4},{24,8},{28,12},{1,17},{... | collective-permute-start | bytes 393224 | tf_op jit(solution)/shard_map/ppermute | solution.py:263
  50.6 4.8 %collective-permute-done.12.refs_2_ = bf16[1,32,1024]{2,1,0:T(8,128)(2,1)S(1)} collective-permute-done((bf16[1,32,1024]{2,1,0:T(8,128)(2,1)S(1)}, bf16[1,32,1024]{2,1,0:T(8,128)(2,1)S(1)}, u32[]{:S(2)}, u32[]{:S(2)}) %collective-permute-start.12) | collective-permute-done | bytes 65568 | tf_op jit(solution)/shard_map/ppermute | solution.py:266
  55.4 1.5 %collective-permute-start.15 = (bf16[1,32,1024]{2,1,0:T(8,128)(2,1)S(1)}, bf16[1,32,1024]{2,1,0:T(8,128)(2,1)S(1)}, u32[]{:S(2)}, u32[]{:S(2)}) collective-permute-start(bf16[1,32,1024]{2,1,0:T(8,128)(2,1)S(1)} %totals.17.refs_3_), channel_id=1, source_target_pairs={{0,24},{4,28},{8,16},{12,20},{16,8},{20,12},{24,0},{28,4},{1,25},{... | collective-permute-start | bytes 196616 | tf_op jit(solution)/shard_map/ppermute | solution.py:263
  56.9 0.1 collective-permute-start.17
  57.0 1.7 %collective-permute-start.19 = (bf16[32,1024]{1,0:T(8,128)(2,1)S(1)}, bf16[32,1024]{1,0:T(8,128)(2,1)S(1)}, u32[]{:S(2)}, u32[]{:S(2)}) collective-permute-start(bf16[32,1024]{1,0:T(8,128)(2,1)S(1)} %slice_bitcast_fusion.1), channel_id=1, source_target_pairs={{0,4},{4,0},{8,12},{12,8},{16,20},{20,16},{24,28},{28,24},{1,5},{5... | collective-permute-start | bytes 196616 | tf_op jit(solution)/shard_map/ppermute | solution.py:263
  58.7 0.1 collective-permute-start.21
  58.8 0.1 totals.19
  58.9 0.5 collective-permute-start.23
  59.4 2.6 %collective-permute-done.17.refs_1_ = bf16[1,32,1024]{2,1,0:T(8,128)(2,1)S(1)} collective-permute-done((bf16[1,32,1024]{2,1,0:T(8,128)(2,1)S(1)}, bf16[1,32,1024]{2,1,0:T(8,128)(2,1)S(1)}, u32[]{:S(2)}, u32[]{:S(2)}) %collective-permute-start.17) | collective-permute-done | bytes 65568 | tf_op jit(solution)/shard_map/ppermute | solution.py:263
  62.1 1.1 %order.1 = bf16[256,1024]{1,0:T(8,128)(2,1)} custom-call(bf16[1,32,1024]{2,1,0:T(8,128)(2,1)S(1)} %collective-permute-done.15.refs_0_, bf16[1,32,1024]{2,1,0:T(8,128)(2,1)S(1)} %collective-permute-done.17.refs_1_, bf16[2,32,1024]{2,1,0:T(8,128)(2,1)S(1)} %collective-permute-done.18.refs_2_, bf16[32,1024]{1,0:T(8,128)(2,1)S(1)} %collective-permute-done.19.refs_3_, ...), custom_call_target="tpu_custom_call" | custom-call | tf_op jit(solution)/shard_map/order/pallas_call | solution.py:243
  (27 shorter events, 0.2 us)
Async XLA Ops:
  0.7 0.9 %copy-start = (bf16[32,4,1024]{2,1,0:T(4,128)(2,1)S(1)}, bf16[32,4,1024]{2,1,0:T(4,128)(2,1)}, u32[]{:S(2)}) copy-start(bf16[32,4,1024]{2,1,0:T(4,128)(2,1)} %amps.1) | copy-start | bytes 786436
  2.5 4.9 %collective-permute-start = (bf16[2,32,1024]{2,1,0:T(8,128)(2,1)S(1)}, bf16[2,32,1024]{2,1,0:T(8,128)(2,1)S(1)}, u32[]{:S(2)}, u32[]{:S(2)}) collective-permute-start(bf16[2,32,1024]{2,1,0:T(8,128)(2,1)S(1)} %get-tuple-element.36), channel_id=1, source_target_pairs={{0,4},{4,0},{8,12},{12,8},{16,20},{20,16},{24,28},{28,24},{1,5},{5... | collective-permute-start | bytes 393224 | tf_op jit(solution)/shard_map/ppermute | solution.py:263
  3.0 10.9 %collective-permute-start.2 = (bf16[2,32,1024]{2,1,0:T(8,128)(2,1)S(1)}, bf16[2,32,1024]{2,1,0:T(8,128)(2,1)S(1)}, u32[]{:S(2)}, u32[]{:S(2)}) collective-permute-start(bf16[2,32,1024]{2,1,0:T(8,128)(2,1)S(1)} %get-tuple-element.38), channel_id=1, source_target_pairs={{0,8},{4,12},{8,0},{12,4},{16,24},{20,28},{24,16},{28,20},{1,9},{5... | collective-permute-start | bytes 393224 | tf_op jit(solution)/shard_map/ppermute | solution.py:263
  5.6 8.3 %collective-permute-start.3 = (bf16[2,32,1024]{2,1,0:T(8,128)(2,1)S(1)}, bf16[2,32,1024]{2,1,0:T(8,128)(2,1)S(1)}, u32[]{:S(2)}, u32[]{:S(2)}) collective-permute-start(bf16[2,32,1024]{2,1,0:T(8,128)(2,1)S(1)} %get-tuple-element.39), channel_id=1, source_target_pairs={{0,12},{4,8},{8,4},{12,0},{16,28},{20,24},{24,20},{28,16},{1,13},{... | collective-permute-start | bytes 393224 | tf_op jit(solution)/shard_map/ppermute | solution.py:263
  5.7 8.2 %collective-permute-start.4 = (bf16[2,32,1024]{2,1,0:T(8,128)(2,1)S(1)}, bf16[2,32,1024]{2,1,0:T(8,128)(2,1)S(1)}, u32[]{:S(2)}, u32[]{:S(2)}) collective-permute-start(bf16[2,32,1024]{2,1,0:T(8,128)(2,1)S(1)} %get-tuple-element.40), channel_id=1, source_target_pairs={{0,16},{4,20},{8,24},{12,28},{16,0},{20,4},{24,8},{28,12},{1,17},{... | collective-permute-start | bytes 393224 | tf_op jit(solution)/shard_map/ppermute | solution.py:263
  7.4 6.5 %collective-permute-start.5 = (bf16[2,32,1024]{2,1,0:T(8,128)(2,1)S(1)}, bf16[2,32,1024]{2,1,0:T(8,128)(2,1)S(1)}, u32[]{:S(2)}, u32[]{:S(2)}) collective-permute-start(bf16[2,32,1024]{2,1,0:T(8,128)(2,1)S(1)} %get-tuple-element.41), channel_id=1, source_target_pairs={{0,20},{4,16},{8,28},{12,24},{16,4},{20,0},{24,12},{28,8},{1,21},{... | collective-permute-start | bytes 393224 | tf_op jit(solution)/shard_map/ppermute | solution.py:263
  12.1 9.5 %collective-permute-start.1 = (bf16[2,64,1024]{2,1,0:T(8,128)(2,1)S(1)}, bf16[2,64,1024]{2,1,0:T(8,128)(2,1)S(1)}, u32[]{:S(2)}, u32[]{:S(2)}) collective-permute-start(bf16[2,64,1024]{2,1,0:T(8,128)(2,1)S(1)} %get-tuple-element.37.refs_0_), channel_id=1, source_target_pairs={{0,1},{1,0},{2,3},{3,2},{4,5},{5,4},{6,7},{7,6},{8,9},{9,8},{10,11... | collective-permute-start | bytes 786440 | tf_op jit(solution)/shard_map/ppermute | solution.py:266
  17.0 9.9 %collective-permute-start.7 = (bf16[2,64,1024]{2,1,0:T(8,128)(2,1)S(1)}, bf16[2,64,1024]{2,1,0:T(8,128)(2,1)S(1)}, u32[]{:S(2)}, u32[]{:S(2)}) collective-permute-start(bf16[2,64,1024]{2,1,0:T(8,128)(2,1)S(1)} %get-tuple-element.49), channel_id=1, source_target_pairs={{0,1},{1,0},{2,3},{3,2},{4,5},{5,4},{6,7},{7,6},{8,9},{9,8},{10,11... | collective-permute-start | bytes 786440 | tf_op jit(solution)/shard_map/ppermute | solution.py:266
  18.7 11.1 %collective-permute-start.8 = (bf16[2,32,1024]{2,1,0:T(8,128)(2,1)S(1)}, bf16[2,32,1024]{2,1,0:T(8,128)(2,1)S(1)}, u32[]{:S(2)}, u32[]{:S(2)}) collective-permute-start(bf16[2,32,1024]{2,1,0:T(8,128)(2,1)S(1)} %get-tuple-element.50), channel_id=1, source_target_pairs={{0,24},{4,28},{8,16},{12,20},{16,8},{20,12},{24,0},{28,4},{1,25},{... | collective-permute-start | bytes 393224 | tf_op jit(solution)/shard_map/ppermute | solution.py:263
  21.1 8.6 %collective-permute-start.9 = (bf16[2,32,1024]{2,1,0:T(8,128)(2,1)S(1)}, bf16[2,32,1024]{2,1,0:T(8,128)(2,1)S(1)}, u32[]{:S(2)}, u32[]{:S(2)}) collective-permute-start(bf16[2,32,1024]{2,1,0:T(8,128)(2,1)S(1)} %get-tuple-element.51), channel_id=1, source_target_pairs={{0,28},{4,24},{8,20},{12,16},{16,12},{20,8},{24,4},{28,0},{1,29},{... | collective-permute-start | bytes 393224 | tf_op jit(solution)/shard_map/ppermute | solution.py:263
  21.1 14.2 %collective-permute-start.6 = (bf16[2,64,1024]{2,1,0:T(8,128)(2,1)S(1)}, bf16[2,64,1024]{2,1,0:T(8,128)(2,1)S(1)}, u32[]{:S(2)}, u32[]{:S(2)}) collective-permute-start(bf16[2,64,1024]{2,1,0:T(8,128)(2,1)S(1)} %get-tuple-element.47), channel_id=1, source_target_pairs={{0,1},{1,0},{2,3},{3,2},{4,5},{5,4},{6,7},{7,6},{8,9},{9,8},{10,11... | collective-permute-start | bytes 786440 | tf_op jit(solution)/shard_map/ppermute | solution.py:266
  26.9 12.0 %collective-permute-start.10 = (bf16[1,64,1024]{2,1,0:T(8,128)(2,1)S(1)}, bf16[1,64,1024]{2,1,0:T(8,128)(2,1)S(1)}, u32[]{:S(2)}, u32[]{:S(2)}) collective-permute-start(bf16[1,64,1024]{2,1,0:T(8,128)(2,1)S(1)} %totals.10.refs_0_), channel_id=1, source_target_pairs={{0,2},{1,3},{2,0},{3,1},{4,6},{5,7},{6,4},{7,5},{8,10},{9,11},{10,... | collective-permute-start | bytes 393224 | tf_op jit(solution)/shard_map/ppermute | solution.py:266
  32.6 10.7 %copy-start.1 = (s32[8]{0:T(128)S(1)}, s32[8]{0:T(128)}, u32[]{:S(2)}) copy-start(s32[8]{0:T(128)} %q_owner.1) | copy-start | bytes 100
  32.6 13.0 %collective-permute-start.11 = (bf16[2,32,1024]{2,1,0:T(8,128)(2,1)S(1)}, bf16[2,32,1024]{2,1,0:T(8,128)(2,1)S(1)}, u32[]{:S(2)}, u32[]{:S(2)}) collective-permute-start(bf16[2,32,1024]{2,1,0:T(8,128)(2,1)S(1)} %get-tuple-element.52.refs_2_), channel_id=1, source_target_pairs={{0,1},{1,0},{2,3},{3,2},{4,5},{5,4},{6,7},{7,6},{8,9},{9,8},{10,11... | collective-permute-start | bytes 393224 | tf_op jit(solution)/shard_map/ppermute | solution.py:266
  35.4 13.5 %collective-permute-start.13 = (bf16[1,64,1024]{2,1,0:T(8,128)(2,1)S(1)}, bf16[1,64,1024]{2,1,0:T(8,128)(2,1)S(1)}, u32[]{:S(2)}, u32[]{:S(2)}) collective-permute-start(bf16[1,64,1024]{2,1,0:T(8,128)(2,1)S(1)} %totals.11.refs_0_), channel_id=1, source_target_pairs={{0,2},{1,3},{2,0},{3,1},{4,6},{5,7},{6,4},{7,5},{8,10},{9,11},{10,... | collective-permute-start | bytes 393224 | tf_op jit(solution)/shard_map/ppermute | solution.py:266
  36.5 9.3 %collective-permute-start.14 = (bf16[2,32,1024]{2,1,0:T(8,128)(2,1)S(1)}, bf16[2,32,1024]{2,1,0:T(8,128)(2,1)S(1)}, u32[]{:S(2)}, u32[]{:S(2)}) collective-permute-start(bf16[2,32,1024]{2,1,0:T(8,128)(2,1)S(1)} %get-tuple-element.61), channel_id=1, source_target_pairs={{0,1},{1,0},{2,3},{3,2},{4,5},{5,4},{6,7},{7,6},{8,9},{9,8},{10,11... | collective-permute-start | bytes 393224 | tf_op jit(solution)/shard_map/ppermute | solution.py:266
  44.1 12.9 %collective-permute-start.18 = (bf16[2,32,1024]{2,1,0:T(8,128)(2,1)S(1)}, bf16[2,32,1024]{2,1,0:T(8,128)(2,1)S(1)}, u32[]{:S(2)}, u32[]{:S(2)}) collective-permute-start(bf16[2,32,1024]{2,1,0:T(8,128)(2,1)S(1)} %bitcast.10), channel_id=1, source_target_pairs={{0,8},{4,12},{8,0},{12,4},{16,24},{20,28},{24,16},{28,20},{1,9},{5... | collective-permute-start | bytes 393224 | tf_op jit(solution)/shard_map/ppermute | solution.py:263
  45.7 9.7 %collective-permute-start.12 = (bf16[1,32,1024]{2,1,0:T(8,128)(2,1)S(1)}, bf16[1,32,1024]{2,1,0:T(8,128)(2,1)S(1)}, u32[]{:S(2)}, u32[]{:S(2)}) collective-permute-start(bf16[1,32,1024]{2,1,0:T(8,128)(2,1)S(1)} %totals.13.refs_2_), channel_id=1, source_target_pairs={{0,2},{1,3},{2,0},{3,1},{4,6},{5,7},{6,4},{7,5},{8,10},{9,11},{10,... | collective-permute-start | bytes 196616 | tf_op jit(solution)/shard_map/ppermute | solution.py:266
  45.8 11.1 %collective-permute-start.16 = (bf16[1,32,1024]{2,1,0:T(8,128)(2,1)S(1)}, bf16[1,32,1024]{2,1,0:T(8,128)(2,1)S(1)}, u32[]{:S(2)}, u32[]{:S(2)}) collective-permute-start(bf16[1,32,1024]{2,1,0:T(8,128)(2,1)S(1)} %totals.14.refs_2_), channel_id=1, source_target_pairs={{0,2},{1,3},{2,0},{3,1},{4,6},{5,7},{6,4},{7,5},{8,10},{9,11},{10,... | collective-permute-start | bytes 196616 | tf_op jit(solution)/shard_map/ppermute | solution.py:266
  48.8 10.0 %collective-permute-start.22 = (bf16[1,64,1024]{2,1,0:T(8,128)(2,1)S(1)}, bf16[1,64,1024]{2,1,0:T(8,128)(2,1)S(1)}, u32[]{:S(2)}, u32[]{:S(2)}) collective-permute-start(bf16[1,64,1024]{2,1,0:T(8,128)(2,1)S(1)} %totals.15.refs_3_), channel_id=1, source_target_pairs={{0,2},{1,3},{2,0},{3,1},{4,6},{5,7},{6,4},{7,5},{8,10},{9,11},{10,... | collective-permute-start | bytes 393224 | tf_op jit(solution)/shard_map/ppermute | solution.py:266
  49.0 9.7 %collective-permute-start.20 = (bf16[2,32,1024]{2,1,0:T(8,128)(2,1)S(1)}, bf16[2,32,1024]{2,1,0:T(8,128)(2,1)S(1)}, u32[]{:S(2)}, u32[]{:S(2)}) collective-permute-start(bf16[2,32,1024]{2,1,0:T(8,128)(2,1)S(1)} %bitcast.11), channel_id=1, source_target_pairs={{0,16},{4,20},{8,24},{12,28},{16,0},{20,4},{24,8},{28,12},{1,17},{... | collective-permute-start | bytes 393224 | tf_op jit(solution)/shard_map/ppermute | solution.py:263
  55.4 6.6 %collective-permute-start.15 = (bf16[1,32,1024]{2,1,0:T(8,128)(2,1)S(1)}, bf16[1,32,1024]{2,1,0:T(8,128)(2,1)S(1)}, u32[]{:S(2)}, u32[]{:S(2)}) collective-permute-start(bf16[1,32,1024]{2,1,0:T(8,128)(2,1)S(1)} %totals.17.refs_3_), channel_id=1, source_target_pairs={{0,24},{4,28},{8,16},{12,20},{16,8},{20,12},{24,0},{28,4},{1,25},{... | collective-permute-start | bytes 196616 | tf_op jit(solution)/shard_map/ppermute | solution.py:263
  56.9 5.1 %collective-permute-start.17 = (bf16[1,32,1024]{2,1,0:T(8,128)(2,1)S(1)}, bf16[1,32,1024]{2,1,0:T(8,128)(2,1)S(1)}, u32[]{:S(2)}, u32[]{:S(2)}) collective-permute-start(bf16[1,32,1024]{2,1,0:T(8,128)(2,1)S(1)} %totals.18.refs_3_), channel_id=1, source_target_pairs={{0,28},{4,24},{8,20},{12,16},{16,12},{20,8},{24,4},{28,0},{1,29},{... | collective-permute-start | bytes 196616 | tf_op jit(solution)/shard_map/ppermute | solution.py:263
  57.0 5.0 %collective-permute-start.19 = (bf16[32,1024]{1,0:T(8,128)(2,1)S(1)}, bf16[32,1024]{1,0:T(8,128)(2,1)S(1)}, u32[]{:S(2)}, u32[]{:S(2)}) collective-permute-start(bf16[32,1024]{1,0:T(8,128)(2,1)S(1)} %slice_bitcast_fusion.1), channel_id=1, source_target_pairs={{0,4},{4,0},{8,12},{12,8},{16,20},{20,16},{24,28},{28,24},{1,5},{5... | collective-permute-start | bytes 196616 | tf_op jit(solution)/shard_map/ppermute | solution.py:263
  58.7 3.3 %collective-permute-start.21 = (bf16[32,1024]{1,0:T(8,128)(2,1)S(1)}, bf16[32,1024]{1,0:T(8,128)(2,1)S(1)}, u32[]{:S(2)}, u32[]{:S(2)}) collective-permute-start(bf16[32,1024]{1,0:T(8,128)(2,1)S(1)} %slice_bitcast_fusion), channel_id=1, source_target_pairs={{0,4},{4,0},{8,12},{12,8},{16,20},{20,16},{24,28},{28,24},{1,5},{5... | collective-permute-start | bytes 196616 | tf_op jit(solution)/shard_map/ppermute | solution.py:263
  58.9 3.2 %collective-permute-start.23 = (bf16[32,1024]{1,0:T(8,128)(2,1)S(1)}, bf16[32,1024]{1,0:T(8,128)(2,1)S(1)}, u32[]{:S(2)}, u32[]{:S(2)}) collective-permute-start(bf16[32,1024]{1,0:T(8,128)(2,1)S(1)} %get-tuple-element.64), channel_id=1, source_target_pairs={{0,4},{4,0},{8,12},{12,8},{16,20},{20,16},{24,28},{28,24},{1,5},{5... | collective-permute-start | bytes 196616 | tf_op jit(solution)/shard_map/ppermute | solution.py:263

commit v5 on v4

--- a/solution.py
+++ b/solution.py
@@ -271,7 +271,7 @@
     def later_steps(kept, come, after=()):
         terms = {0: [(come, 0)]}
         for i, r in enumerate(middle):
-            terms[r] = [(kept, i), (come, odd.index(r ^ 1))]
+            terms[r] = [(kept, i + 1), (come, odd.index(r ^ 1))]
         messages = []
         step = 1
         while 1 << step < devices:
@@ -301,35 +301,30 @@
 
     come, ready, sums = {}, {}, {}
     first, others = near[0], near[1:]
-    all_odd, all_middle = tuple(range(len(odd))), tuple(range(len(middle)))
+    all_odd, all_even = tuple(range(len(odd))), tuple(range(len(even)))
     away, odd_ints, _ = multiply([mine], all_odd, fetch=odd, limit=FIRST)
     come[mine] = first_step(away[mine])
-    outs, middle_ints, passed = multiply(
-        near, all_odd, odd_ints, middle, [lot[j] for j, in far], [away[mine]]
-    )
+    outs, even_ints, passed = multiply(near, all_odd, odd_ints, even, [lot[j] for j, in far], [away[mine]])
     lot.update((j, swap(value, j)) for (j,), value in zip(far, passed))
     away.update(outs)
     come.update((u, first_step(away[u])) for u in near)
-    kept, _ = multiply([mine] + near, all_middle, middle_ints, after=[come[mine]])
-    ready[first], sums[first] = later_steps(kept[first], come[first])
-    outs, home_ints, _ = multiply(far, all_odd, odd_ints, (0,), after=[ready[first]])
+    kept, _ = multiply([mine] + near, all_even, even_ints, after=[come[mine]])
+    place = place_of(q_owner, peers * rows, kept[mine])
+    ready[first], sums[first] = later_steps(kept[first], come[first], [place])
+    outs, _ = multiply(far, all_odd, odd_ints, after=[ready[first]])
     away.update(outs)
     come.update((u, first_step(away[u])) for u in far)
     last = away[far[0]]
     for u in others:
         ready[u], sums[u] = later_steps(kept[u], come[u], [last])
         last = ready[u]
-    outs, _ = multiply(far, all_middle, middle_ints, after=[last, sums[first][-1][0]])
+    outs, _ = multiply(far, all_even, even_ints, after=[last, sums[first][-1][0]])
     kept.update(outs)
-    own, _ = multiply([mine] + near, (0,), home_ints, after=[kept[far[0]]])
-    outs, _ = multiply(far, (0,), home_ints, after=[own[mine]])
-    own.update(outs)
-    place = place_of(q_owner, peers * rows, own[far[0]])
 
     shares = {}
 
     def close(u, after):
-        terms = [[(own[u], 0)] + sums[u]]
+        terms = [[(kept[u], 0)] + sums[u]]
         if u == mine:
             halves = totals(terms, after, halves=True)
             shares[0], shares[1] = (halves[0], None), (swap(halves[1], 1), None)
@@ -342,12 +337,13 @@
             shares[j + 1] = swap(got[1], 1), None
         return whole
 
-    last = close(first, [place])
+    last = close(first, [kept[far[0]]])
     for u in far + [mine]:
         ready[u], sums[u] = later_steps(kept[u], come[u], [last])
         last = ready[u]
-    for u in others + far + [mine]:
+    for u in others + far:
         last = close(u, [last])
+    close(mine, [last] + [shares[j][0] for j in first])
     return order(place, [(j, *shares[j]) for u in far + near + [mine] for j in u]).reshape(rows, peers, -1)
 
 

time: 63.4 us -> 60.9 us (0.961)
  waiting for transfers between devices: 12.4 us -> 9.47 us
    ppermute x10, waiting for transfers between devices: 9.68 us -> 7.26 us  [swap_line(): lax.ppermute(value, 'narrow', [(n, n ^ mask) for n in range(devices)])]
    pallas_call x7 -> x5, Pallas kernels: 16.5 us -> 16.9 us  [product(): pl.pallas_call(functools.partial(product_kernel, plan), out_shape=[jax.Sh...]
  transfers between devices with their start and end apart: 24 -> 24, of which waited for: 4 -> 6; matrix products, arithmetic and copies ran while one was open for 0% -> 0% of each run, Pallas kernels for 28% -> 30%
where the time goes in v5:
time: 60.9 us; the launch traced here: 60.8 us
  starting transfers between devices  29.6 us (49%)
  Pallas kernels  19.9 us (33%)
  waiting for transfers between devices  9.47 us (16%)
  local copies, waits for them, and re-layouts  0.97 us (2%)
  other arithmetic  0.72 us (1%)
    pallas_call x5, Pallas kernels, product(): pl.pallas_call(functools.partial(product_kernel, plan), out_shape=[jax.Sh...  16.9 us
    ppermute x10, starting transfers between devices, swap_line(): lax.ppermute(value, 'narrow', [(n, n ^ mask) for n in range(devices)])  15.2 us
    ppermute x14, starting transfers between devices, swap(): return lax.ppermute(value, 'wide', [(w, w ^ j) for w in range(peers)])  14.4 us
    ppermute x10, waiting for transfers between devices, swap_line(): lax.ppermute(value, 'narrow', [(n, n ^ mask) for n in range(devices)])  7.26 us
    ppermute x14, waiting for transfers between devices, swap(): return lax.ppermute(value, 'wide', [(w, w ^ j) for w in range(peers)])  2.21 us
  transfers between devices with their start and end apart: 24, of which 6 were waited for; matrix products, arithmetic and copies ran while one was open for 0% of the time, Pallas kernels for 30%

profile of v5, /device:TPU:0, one launch (start us, length us, event | category | flops | bytes accessed | tf_op | source)
XLA Modules:
  0.0 60.8 jit_solution(1988879525757734115)
XLA Ops:
  0.0 0.7 %pad_add_fusion.tables_from = s32[7,8]{1,0:T(8,128)S(1)} fusion(s32[1,8]{1,0:T(1,128)} %bitcast.12, s32[2,8]{1,0:T(2,128)} %bitcast.14, s32[4,8]{1,0:T(4,128)} %bitcast.13), kind=kLoop, calls=%fused_computation.2 | loop fusion | flops 112 | bytes 448 | tf_op jit(solution)/shard_map/concatenate | solution.py:46
  0.7 0.9 %copy-done = bf16[32,4,1024]{2,1,0:T(4,128)(2,1)S(1)} copy-done((bf16[32,4,1024]{2,1,0:T(4,128)(2,1)S(1)}, bf16[32,4,1024]{2,1,0:T(4,128)(2,1)}, u32[]{:S(2)}) %copy-start) | copy-done | bytes 262168
  1.7 0.8 %pick.1 = (bf16[2,32,1024]{2,1,0:T(8,128)(2,1)S(1)}, bf16[2,32,1024]{2,1,0:T(8,128)(2,1)S(1)}, bf16[2,32,1024]{2,1,0:T(8,128)(2,1)S(1)}, bf16[2,32,1024]{2,1,0:T...) custom-call(s32[7,8]{1,0:T(8,128)S(1)} %pad_add_fusion.tables_from, ...), custom_call_target="tpu_custom_call" | custom-call | tf_op jit(solution)/shard_map/pick/pallas_call | solution.py:48
  2.5 0.5 collective-permute-start
  3.0 2.6 %collective-permute-start.2 = (bf16[2,32,1024]{2,1,0:T(8,128)(2,1)S(1)}, bf16[2,32,1024]{2,1,0:T(8,128)(2,1)S(1)}, u32[]{:S(2)}, u32[]{:S(2)}) collective-permute-start(bf16[2,32,1024]{2,1,0:T(8,128)(2,1)S(1)} %get-tuple-element.32), channel_id=1, source_target_pairs={{0,8},{4,12},{8,0},{12,4},{16,24},{20,28},{24,16},{28,20},{1,9},{5... | collective-permute-start | bytes 393224 | tf_op jit(solution)/shard_map/ppermute | solution.py:263
  5.6 0.1 collective-permute-start.3
  5.7 1.8 %collective-permute-start.4 = (bf16[2,32,1024]{2,1,0:T(8,128)(2,1)S(1)}, bf16[2,32,1024]{2,1,0:T(8,128)(2,1)S(1)}, u32[]{:S(2)}, u32[]{:S(2)}) collective-permute-start(bf16[2,32,1024]{2,1,0:T(8,128)(2,1)S(1)} %get-tuple-element.34), channel_id=1, source_target_pairs={{0,16},{4,20},{8,24},{12,28},{16,0},{20,4},{24,8},{28,12},{1,17},{... | collective-permute-start | bytes 393224 | tf_op jit(solution)/shard_map/ppermute | solution.py:263
  7.4 0.0 collective-permute-done.refs_1_.refs_2_
  7.4 4.7 %product.5 = (bf16[2,64,1024]{2,1,0:T(8,128)(2,1)S(1)}, bf16[2,2,1024,1024]{3,2,1,0:T(8,128)(2,1)S(1)}) custom-call(bf16[2,32,1024]{2,1,0:T(8,128)(2,1)S(1)} %get-tuple-element.29.refs_0_.refs_1_, bf16[2,32,1024]{2,1,0:T(8,128)(2,1)S(1)} %collective-permute-done.refs_1_.refs_2_, bf16[1,2,4096,1024]{3,2,1,0:T(8,128)(2,1)} %refs_6_.1), custom_call_target="tpu_custom_call" | custom-call | flops 2147483648 | bytes 8388608 | tf_op jit(solution)/shard_map/product/pallas_call | solution.py:152
  12.1 1.8 %collective-permute-start.1 = (bf16[2,64,1024]{2,1,0:T(8,128)(2,1)S(1)}, bf16[2,64,1024]{2,1,0:T(8,128)(2,1)S(1)}, u32[]{:S(2)}, u32[]{:S(2)}) collective-permute-start(bf16[2,64,1024]{2,1,0:T(8,128)(2,1)S(1)} %get-tuple-element.31.refs_0_), channel_id=1, source_target_pairs={{0,1},{1,0},{2,3},{3,2},{4,5},{5,4},{6,7},{7,6},{8,9},{9,8},{10,11... | collective-permute-start | bytes 786440 | tf_op jit(solution)/shard_map/ppermute | solution.py:266
  13.9 0.0 collective-permute-done.3.refs_2_.refs_4_
  13.9 0.0 collective-permute-done.4.refs_3_.refs_5_
  13.9 3.5 %product.6 = (bf16[2,64,1024]{2,1,0:T(8,128)(2,1)S(1)}, bf16[2,64,1024]{2,1,0:T(8,128)(2,1)S(1)}, bf16[2,2,1024,1024]{3,2,1,0:T(8,128)(2,1)S(1)}, bf16[2,32,1024...) custom-call(bf16[2,64,1024]{2,1,0:T(8,128)(2,1)S(1)} %get-tuple-element.31.refs_0_, ...), custom_call_target="tpu_custom_call", output_to_operand_aliasing={{3}: (7, {}), {4}: (8, {})} | custom-call | flops 2147483648 | bytes 8388608 | tf_op jit(solution)/shard_map/product/pallas_call | solution.py:152
  17.4 0.0 copy-start.1
  17.4 1.6 %collective-permute-start.7 = (bf16[2,64,1024]{2,1,0:T(8,128)(2,1)S(1)}, bf16[2,64,1024]{2,1,0:T(8,128)(2,1)S(1)}, u32[]{:S(2)}, u32[]{:S(2)}) collective-permute-start(bf16[2,64,1024]{2,1,0:T(8,128)(2,1)S(1)} %get-tuple-element.43), channel_id=1, source_target_pairs={{0,1},{1,0},{2,3},{3,2},{4,5},{5,4},{6,7},{7,6},{8,9},{9,8},{10,11... | collective-permute-start | bytes 786440 | tf_op jit(solution)/shard_map/ppermute | solution.py:266
  19.1 2.4 %collective-permute-start.8 = (bf16[2,32,1024]{2,1,0:T(8,128)(2,1)S(1)}, bf16[2,32,1024]{2,1,0:T(8,128)(2,1)S(1)}, u32[]{:S(2)}, u32[]{:S(2)}) collective-permute-start(bf16[2,32,1024]{2,1,0:T(8,128)(2,1)S(1)} %get-tuple-element.45), channel_id=1, source_target_pairs={{0,24},{4,28},{8,16},{12,20},{16,8},{20,12},{24,0},{28,4},{1,25},{... | collective-permute-start | bytes 393224 | tf_op jit(solution)/shard_map/ppermute | solution.py:263
  21.5 0.0 collective-permute-start.9
  21.5 0.5 collective-permute-start.6
  22.0 3.1 %product.7 = (bf16[2,64,1024]{2,1,0:T(8,128)(2,1)S(1)}, bf16[2,64,1024]{2,1,0:T(8,128)(2,1)S(1)}, bf16[2,64,1024]{2,1,0:T(8,128)(2,1)S(1)}) custom-call(bf16[2,64,1024]{2,1,0:T(8,128)(2,1)S(1)} %collective-permute-done.1.refs_0_.refs_1_, bf16[2,32,1024]{2,1,0:T(8,128)(2,1)S(1)} %get-tuple-element.29.refs_0_.refs_1_, ...), custom_call_target="tpu_custom_call" | custom-call | flops 2147483648 | bytes 8388608 | tf_op jit(solution)/shard_map/product/pallas_call | solution.py:152
  25.1 0.7 %place.1.refs_2_.refs_8_ = bf16[256,256]{1,0:T(8,128)(2,1)S(1)} custom-call(s32[8]{0:T(128)S(1)} %copy-done.1, bf16[2,64,1024]{2,1,0:T(8,128)(2,1)S(1)} %get-tuple-element.44.after.refs_0_), custom_call_target="tpu_custom_call" | custom-call | tf_op jit(solution)/shard_map/place/pallas_call | solution.py:221
  25.8 1.1 %collective-permute-done.7.refs_1_ = bf16[2,64,1024]{2,1,0:T(8,128)(2,1)S(1)} collective-permute-done((bf16[2,64,1024]{2,1,0:T(8,128)(2,1)S(1)}, bf16[2,64,1024]{2,1,0:T(8,128)(2,1)S(1)}, u32[]{:S(2)}, u32[]{:S(2)}) %collective-permute-start.7) | collective-permute-done | bytes 262176 | tf_op jit(solution)/shard_map/ppermute | solution.py:266
  26.9 2.8 %collective-permute-start.10 = (bf16[1,64,1024]{2,1,0:T(8,128)(2,1)S(1)}, bf16[1,64,1024]{2,1,0:T(8,128)(2,1)S(1)}, u32[]{:S(2)}, u32[]{:S(2)}) collective-permute-start(bf16[1,64,1024]{2,1,0:T(8,128)(2,1)S(1)} %totals.10.refs_0_), channel_id=1, source_target_pairs={{0,2},{1,3},{2,0},{3,1},{4,6},{5,7},{6,4},{7,5},{8,10},{9,11},{10,... | collective-permute-start | bytes 393224 | tf_op jit(solution)/shard_map/ppermute | solution.py:266
  29.7 0.0 collective-permute-done.8.refs_1_.refs_2_
  29.7 2.8 %product.8 = (bf16[2,32,1024]{2,1,0:T(8,128)(2,1)S(1)}, bf16[2,32,1024]{2,1,0:T(8,128)(2,1)S(1)}) custom-call(bf16[1,64,1024]{2,1,0:T(8,128)(2,1)S(1)} %totals.10.refs_0_, bf16[2,32,1024]{2,1,0:T(8,128)(2,1)S(1)} %collective-permute-done.8.refs_1_.refs_2_, bf16[2,32,1024]{2,1,0:T(8,128)(2,1)S(1)} %collective-permute-done.9.refs_2_.refs_3_, ...), custom_call_target="tpu_custom_call" | custom-call | flops 2147483648 | bytes 8388608 | tf_op jit(solution)/shard_map/product/pallas_call | solution.py:152
  32.6 1.6 %collective-permute-start.11 = (bf16[2,32,1024]{2,1,0:T(8,128)(2,1)S(1)}, bf16[2,32,1024]{2,1,0:T(8,128)(2,1)S(1)}, u32[]{:S(2)}, u32[]{:S(2)}) collective-permute-start(bf16[2,32,1024]{2,1,0:T(8,128)(2,1)S(1)} %get-tuple-element.47.refs_2_), channel_id=1, source_target_pairs={{0,1},{1,0},{2,3},{3,2},{4,5},{5,4},{6,7},{7,6},{8,9},{9,8},{10,11... | collective-permute-start | bytes 393224 | tf_op jit(solution)/shard_map/ppermute | solution.py:266
  34.2 1.1 %collective-permute-done.6.refs_1_ = bf16[2,64,1024]{2,1,0:T(8,128)(2,1)S(1)} collective-permute-done((bf16[2,64,1024]{2,1,0:T(8,128)(2,1)S(1)}, bf16[2,64,1024]{2,1,0:T(8,128)(2,1)S(1)}, u32[]{:S(2)}, u32[]{:S(2)}) %collective-permute-start.6) | collective-permute-done | bytes 262176 | tf_op jit(solution)/shard_map/ppermute | solution.py:266
  35.4 1.1 %collective-permute-start.13 = (bf16[1,64,1024]{2,1,0:T(8,128)(2,1)S(1)}, bf16[1,64,1024]{2,1,0:T(8,128)(2,1)S(1)}, u32[]{:S(2)}, u32[]{:S(2)}) collective-permute-start(bf16[1,64,1024]{2,1,0:T(8,128)(2,1)S(1)} %totals.11.refs_0_), channel_id=1, source_target_pairs={{0,2},{1,3},{2,0},{3,1},{4,6},{5,7},{6,4},{7,5},{8,10},{9,11},{10,... | collective-permute-start | bytes 393224 | tf_op jit(solution)/shard_map/ppermute | solution.py:266
  36.5 2.4 %collective-permute-start.14 = (bf16[2,32,1024]{2,1,0:T(8,128)(2,1)S(1)}, bf16[2,32,1024]{2,1,0:T(8,128)(2,1)S(1)}, u32[]{:S(2)}, u32[]{:S(2)}) collective-permute-start(bf16[2,32,1024]{2,1,0:T(8,128)(2,1)S(1)} %get-tuple-element.50), channel_id=1, source_target_pairs={{0,1},{1,0},{2,3},{3,2},{4,5},{5,4},{6,7},{7,6},{8,9},{9,8},{10,11... | collective-permute-start | bytes 393224 | tf_op jit(solution)/shard_map/ppermute | solution.py:266
  38.9 0.0 collective-permute-done.10.refs_1_.refs_2_
  38.9 2.8 %product.9 = (bf16[2,32,1024]{2,1,0:T(8,128)(2,1)S(1)}, bf16[2,32,1024]{2,1,0:T(8,128)(2,1)S(1)}) custom-call(bf16[1,64,1024]{2,1,0:T(8,128)(2,1)S(1)} %totals.11.refs_0_, bf16[1,64,1024]{2,1,0:T(8,128)(2,1)S(1)} %collective-permute-done.10.refs_1_.refs_2_, bf16[2,32,1024]{2,1,0:T(8,128)(2,1)S(1)} %collective-permute-done.8.refs_1_.refs_2_, ...), custom_call_target="tpu_custom_call" | custom-call | flops 2147483648 | bytes 8388608 | tf_op jit(solution)/shard_map/product/pallas_call | solution.py:152
  41.8 0.1 totals.12.refs_2_
  41.8 1.5 %collective-permute-start.18 = (bf16[2,32,1024]{2,1,0:T(8,128)(2,1)S(1)}, bf16[2,32,1024]{2,1,0:T(8,128)(2,1)S(1)}, u32[]{:S(2)}, u32[]{:S(2)}) collective-permute-start(bf16[2,32,1024]{2,1,0:T(8,128)(2,1)S(1)} %bitcast.10), channel_id=1, source_target_pairs={{0,8},{4,12},{8,0},{12,4},{16,24},{20,28},{24,16},{28,20},{1,9},{5... | collective-permute-start | bytes 393224 | tf_op jit(solution)/shard_map/ppermute | solution.py:263
  43.4 0.1 collective-permute-start.12
  43.6 3.1 %collective-permute-start.16 = (bf16[1,32,1024]{2,1,0:T(8,128)(2,1)S(1)}, bf16[1,32,1024]{2,1,0:T(8,128)(2,1)S(1)}, u32[]{:S(2)}, u32[]{:S(2)}) collective-permute-start(bf16[1,32,1024]{2,1,0:T(8,128)(2,1)S(1)} %totals.14.refs_2_), channel_id=1, source_target_pairs={{0,2},{1,3},{2,0},{3,1},{4,6},{5,7},{6,4},{7,5},{8,10},{9,11},{10,... | collective-permute-start | bytes 196616 | tf_op jit(solution)/shard_map/ppermute | solution.py:266
  46.7 0.1 collective-permute-start.22
  46.7 0.1 totals.16.refs_3_
  46.8 1.6 %collective-permute-start.20 = (bf16[2,32,1024]{2,1,0:T(8,128)(2,1)S(1)}, bf16[2,32,1024]{2,1,0:T(8,128)(2,1)S(1)}, u32[]{:S(2)}, u32[]{:S(2)}) collective-permute-start(bf16[2,32,1024]{2,1,0:T(8,128)(2,1)S(1)} %bitcast.11), channel_id=1, source_target_pairs={{0,16},{4,20},{8,24},{12,28},{16,0},{20,4},{24,8},{28,12},{1,17},{... | collective-permute-start | bytes 393224 | tf_op jit(solution)/shard_map/ppermute | solution.py:263
  48.4 2.1 %collective-permute-done.12.refs_2_ = bf16[1,32,1024]{2,1,0:T(8,128)(2,1)S(1)} collective-permute-done((bf16[1,32,1024]{2,1,0:T(8,128)(2,1)S(1)}, bf16[1,32,1024]{2,1,0:T(8,128)(2,1)S(1)}, u32[]{:S(2)}, u32[]{:S(2)}) %collective-permute-start.12) | collective-permute-done | bytes 65568 | tf_op jit(solution)/shard_map/ppermute | solution.py:266
  50.5 1.3 %collective-permute-start.15 = (bf16[1,32,1024]{2,1,0:T(8,128)(2,1)S(1)}, bf16[1,32,1024]{2,1,0:T(8,128)(2,1)S(1)}, u32[]{:S(2)}, u32[]{:S(2)}) collective-permute-start(bf16[1,32,1024]{2,1,0:T(8,128)(2,1)S(1)} %totals.17.refs_3_), channel_id=1, source_target_pairs={{0,24},{4,28},{8,16},{12,20},{16,8},{20,12},{24,0},{28,4},{1,25},{... | collective-permute-start | bytes 196616 | tf_op jit(solution)/shard_map/ppermute | solution.py:263
  51.8 2.9 %collective-permute-done.16.refs_2_ = bf16[1,32,1024]{2,1,0:T(8,128)(2,1)S(1)} collective-permute-done((bf16[1,32,1024]{2,1,0:T(8,128)(2,1)S(1)}, bf16[1,32,1024]{2,1,0:T(8,128)(2,1)S(1)}, u32[]{:S(2)}, u32[]{:S(2)}) %collective-permute-start.16) | collective-permute-done | bytes 65568 | tf_op jit(solution)/shard_map/ppermute | solution.py:266
  54.7 0.1 collective-permute-start.17
  54.8 2.0 %collective-permute-start.19 = (bf16[32,1024]{1,0:T(8,128)(2,1)S(1)}, bf16[32,1024]{1,0:T(8,128)(2,1)S(1)}, u32[]{:S(2)}, u32[]{:S(2)}) collective-permute-start(bf16[32,1024]{1,0:T(8,128)(2,1)S(1)} %slice_bitcast_fusion.1), channel_id=1, source_target_pairs={{0,4},{4,0},{8,12},{12,8},{16,20},{20,16},{24,28},{28,24},{1,5},{5... | collective-permute-start | bytes 196616 | tf_op jit(solution)/shard_map/ppermute | solution.py:263
  56.9 0.1 collective-permute-start.21
  57.0 0.8 %collective-permute-done.19.refs_5_.refs_3_ = bf16[32,1024]{1,0:T(8,128)(2,1)S(1)} collective-permute-done((bf16[32,1024]{1,0:T(8,128)(2,1)S(1)}, bf16[32,1024]{1,0:T(8,128)(2,1)S(1)}, u32[]{:S(2)}, u32[]{:S(2)}) %collective-permute-start.19) | collective-permute-done | bytes 65568 | tf_op jit(solution)/shard_map/ppermute | solution.py:263
  57.8 0.1 totals.19
  57.8 0.4 collective-permute-start.23
  58.3 1.4 %collective-permute-done.17.refs_1_ = bf16[1,32,1024]{2,1,0:T(8,128)(2,1)S(1)} collective-permute-done((bf16[1,32,1024]{2,1,0:T(8,128)(2,1)S(1)}, bf16[1,32,1024]{2,1,0:T(8,128)(2,1)S(1)}, u32[]{:S(2)}, u32[]{:S(2)}) %collective-permute-start.17) | collective-permute-done | bytes 65568 | tf_op jit(solution)/shard_map/ppermute | solution.py:263
  59.7 1.1 %order.1 = bf16[256,1024]{1,0:T(8,128)(2,1)} custom-call(bf16[1,32,1024]{2,1,0:T(8,128)(2,1)S(1)} %collective-permute-done.15.refs_0_, bf16[1,32,1024]{2,1,0:T(8,128)(2,1)S(1)} %collective-permute-done.17.refs_1_, bf16[2,32,1024]{2,1,0:T(8,128)(2,1)S(1)} %collective-permute-done.18.refs_4_.refs_2_, ...), custom_call_target="tpu_custom_call" | custom-call | tf_op jit(solution)/shard_map/order/pallas_call | solution.py:243
  (25 shorter events, 0.2 us)
Async XLA Ops:
  0.7 0.9 %copy-start = (bf16[32,4,1024]{2,1,0:T(4,128)(2,1)S(1)}, bf16[32,4,1024]{2,1,0:T(4,128)(2,1)}, u32[]{:S(2)}) copy-start(bf16[32,4,1024]{2,1,0:T(4,128)(2,1)} %amps.1) | copy-start | bytes 786436
  2.5 4.9 %collective-permute-start = (bf16[2,32,1024]{2,1,0:T(8,128)(2,1)S(1)}, bf16[2,32,1024]{2,1,0:T(8,128)(2,1)S(1)}, u32[]{:S(2)}, u32[]{:S(2)}) collective-permute-start(bf16[2,32,1024]{2,1,0:T(8,128)(2,1)S(1)} %get-tuple-element.30), channel_id=1, source_target_pairs={{0,4},{4,0},{8,12},{12,8},{16,20},{20,16},{24,28},{28,24},{1,5},{5... | collective-permute-start | bytes 393224 | tf_op jit(solution)/shard_map/ppermute | solution.py:263
  3.0 10.9 %collective-permute-start.2 = (bf16[2,32,1024]{2,1,0:T(8,128)(2,1)S(1)}, bf16[2,32,1024]{2,1,0:T(8,128)(2,1)S(1)}, u32[]{:S(2)}, u32[]{:S(2)}) collective-permute-start(bf16[2,32,1024]{2,1,0:T(8,128)(2,1)S(1)} %get-tuple-element.32), channel_id=1, source_target_pairs={{0,8},{4,12},{8,0},{12,4},{16,24},{20,28},{24,16},{28,20},{1,9},{5... | collective-permute-start | bytes 393224 | tf_op jit(solution)/shard_map/ppermute | solution.py:263
  5.6 8.3 %collective-permute-start.3 = (bf16[2,32,1024]{2,1,0:T(8,128)(2,1)S(1)}, bf16[2,32,1024]{2,1,0:T(8,128)(2,1)S(1)}, u32[]{:S(2)}, u32[]{:S(2)}) collective-permute-start(bf16[2,32,1024]{2,1,0:T(8,128)(2,1)S(1)} %get-tuple-element.33), channel_id=1, source_target_pairs={{0,12},{4,8},{8,4},{12,0},{16,28},{20,24},{24,20},{28,16},{1,13},{... | collective-permute-start | bytes 393224 | tf_op jit(solution)/shard_map/ppermute | solution.py:263
  5.7 8.2 %collective-permute-start.4 = (bf16[2,32,1024]{2,1,0:T(8,128)(2,1)S(1)}, bf16[2,32,1024]{2,1,0:T(8,128)(2,1)S(1)}, u32[]{:S(2)}, u32[]{:S(2)}) collective-permute-start(bf16[2,32,1024]{2,1,0:T(8,128)(2,1)S(1)} %get-tuple-element.34), channel_id=1, source_target_pairs={{0,16},{4,20},{8,24},{12,28},{16,0},{20,4},{24,8},{28,12},{1,17},{... | collective-permute-start | bytes 393224 | tf_op jit(solution)/shard_map/ppermute | solution.py:263
  7.4 6.5 %collective-permute-start.5 = (bf16[2,32,1024]{2,1,0:T(8,128)(2,1)S(1)}, bf16[2,32,1024]{2,1,0:T(8,128)(2,1)S(1)}, u32[]{:S(2)}, u32[]{:S(2)}) collective-permute-start(bf16[2,32,1024]{2,1,0:T(8,128)(2,1)S(1)} %get-tuple-element.35), channel_id=1, source_target_pairs={{0,20},{4,16},{8,28},{12,24},{16,4},{20,0},{24,12},{28,8},{1,21},{... | collective-permute-start | bytes 393224 | tf_op jit(solution)/shard_map/ppermute | solution.py:263
  12.1 9.9 %collective-permute-start.1 = (bf16[2,64,1024]{2,1,0:T(8,128)(2,1)S(1)}, bf16[2,64,1024]{2,1,0:T(8,128)(2,1)S(1)}, u32[]{:S(2)}, u32[]{:S(2)}) collective-permute-start(bf16[2,64,1024]{2,1,0:T(8,128)(2,1)S(1)} %get-tuple-element.31.refs_0_), channel_id=1, source_target_pairs={{0,1},{1,0},{2,3},{3,2},{4,5},{5,4},{6,7},{7,6},{8,9},{9,8},{10,11... | collective-permute-start | bytes 786440 | tf_op jit(solution)/shard_map/ppermute | solution.py:266
  17.4 7.7 %copy-start.1 = (s32[8]{0:T(128)S(1)}, s32[8]{0:T(128)}, u32[]{:S(2)}) copy-start(s32[8]{0:T(128)} %q_owner.1) | copy-start | bytes 100
  17.4 9.5 %collective-permute-start.7 = (bf16[2,64,1024]{2,1,0:T(8,128)(2,1)S(1)}, bf16[2,64,1024]{2,1,0:T(8,128)(2,1)S(1)}, u32[]{:S(2)}, u32[]{:S(2)}) collective-permute-start(bf16[2,64,1024]{2,1,0:T(8,128)(2,1)S(1)} %get-tuple-element.43), channel_id=1, source_target_pairs={{0,1},{1,0},{2,3},{3,2},{4,5},{5,4},{6,7},{7,6},{8,9},{9,8},{10,11... | collective-permute-start | bytes 786440 | tf_op jit(solution)/shard_map/ppermute | solution.py:266
  19.1 10.7 %collective-permute-start.8 = (bf16[2,32,1024]{2,1,0:T(8,128)(2,1)S(1)}, bf16[2,32,1024]{2,1,0:T(8,128)(2,1)S(1)}, u32[]{:S(2)}, u32[]{:S(2)}) collective-permute-start(bf16[2,32,1024]{2,1,0:T(8,128)(2,1)S(1)} %get-tuple-element.45), channel_id=1, source_target_pairs={{0,24},{4,28},{8,16},{12,20},{16,8},{20,12},{24,0},{28,4},{1,25},{... | collective-permute-start | bytes 393224 | tf_op jit(solution)/shard_map/ppermute | solution.py:263
  21.5 8.2 %collective-permute-start.9 = (bf16[2,32,1024]{2,1,0:T(8,128)(2,1)S(1)}, bf16[2,32,1024]{2,1,0:T(8,128)(2,1)S(1)}, u32[]{:S(2)}, u32[]{:S(2)}) collective-permute-start(bf16[2,32,1024]{2,1,0:T(8,128)(2,1)S(1)} %get-tuple-element.46), channel_id=1, source_target_pairs={{0,28},{4,24},{8,20},{12,16},{16,12},{20,8},{24,4},{28,0},{1,29},{... | collective-permute-start | bytes 393224 | tf_op jit(solution)/shard_map/ppermute | solution.py:263
  21.5 13.8 %collective-permute-start.6 = (bf16[2,64,1024]{2,1,0:T(8,128)(2,1)S(1)}, bf16[2,64,1024]{2,1,0:T(8,128)(2,1)S(1)}, u32[]{:S(2)}, u32[]{:S(2)}) collective-permute-start(bf16[2,64,1024]{2,1,0:T(8,128)(2,1)S(1)} %get-tuple-element.41), channel_id=1, source_target_pairs={{0,1},{1,0},{2,3},{3,2},{4,5},{5,4},{6,7},{7,6},{8,9},{9,8},{10,11... | collective-permute-start | bytes 786440 | tf_op jit(solution)/shard_map/ppermute | solution.py:266
  26.9 12.0 %collective-permute-start.10 = (bf16[1,64,1024]{2,1,0:T(8,128)(2,1)S(1)}, bf16[1,64,1024]{2,1,0:T(8,128)(2,1)S(1)}, u32[]{:S(2)}, u32[]{:S(2)}) collective-permute-start(bf16[1,64,1024]{2,1,0:T(8,128)(2,1)S(1)} %totals.10.refs_0_), channel_id=1, source_target_pairs={{0,2},{1,3},{2,0},{3,1},{4,6},{5,7},{6,4},{7,5},{8,10},{9,11},{10,... | collective-permute-start | bytes 393224 | tf_op jit(solution)/shard_map/ppermute | solution.py:266
  32.6 10.8 %collective-permute-start.11 = (bf16[2,32,1024]{2,1,0:T(8,128)(2,1)S(1)}, bf16[2,32,1024]{2,1,0:T(8,128)(2,1)S(1)}, u32[]{:S(2)}, u32[]{:S(2)}) collective-permute-start(bf16[2,32,1024]{2,1,0:T(8,128)(2,1)S(1)} %get-tuple-element.47.refs_2_), channel_id=1, source_target_pairs={{0,1},{1,0},{2,3},{3,2},{4,5},{5,4},{6,7},{7,6},{8,9},{9,8},{10,11... | collective-permute-start | bytes 393224 | tf_op jit(solution)/shard_map/ppermute | solution.py:266
  35.4 11.4 %collective-permute-start.13 = (bf16[1,64,1024]{2,1,0:T(8,128)(2,1)S(1)}, bf16[1,64,1024]{2,1,0:T(8,128)(2,1)S(1)}, u32[]{:S(2)}, u32[]{:S(2)}) collective-permute-start(bf16[1,64,1024]{2,1,0:T(8,128)(2,1)S(1)} %totals.11.refs_0_), channel_id=1, source_target_pairs={{0,2},{1,3},{2,0},{3,1},{4,6},{5,7},{6,4},{7,5},{8,10},{9,11},{10,... | collective-permute-start | bytes 393224 | tf_op jit(solution)/shard_map/ppermute | solution.py:266
  36.5 7.0 %collective-permute-start.14 = (bf16[2,32,1024]{2,1,0:T(8,128)(2,1)S(1)}, bf16[2,32,1024]{2,1,0:T(8,128)(2,1)S(1)}, u32[]{:S(2)}, u32[]{:S(2)}) collective-permute-start(bf16[2,32,1024]{2,1,0:T(8,128)(2,1)S(1)} %get-tuple-element.50), channel_id=1, source_target_pairs={{0,1},{1,0},{2,3},{3,2},{4,5},{5,4},{6,7},{7,6},{8,9},{9,8},{10,11... | collective-permute-start | bytes 393224 | tf_op jit(solution)/shard_map/ppermute | solution.py:266
  41.8 13.0 %collective-permute-start.18 = (bf16[2,32,1024]{2,1,0:T(8,128)(2,1)S(1)}, bf16[2,32,1024]{2,1,0:T(8,128)(2,1)S(1)}, u32[]{:S(2)}, u32[]{:S(2)}) collective-permute-start(bf16[2,32,1024]{2,1,0:T(8,128)(2,1)S(1)} %bitcast.10), channel_id=1, source_target_pairs={{0,8},{4,12},{8,0},{12,4},{16,24},{20,28},{24,16},{28,20},{1,9},{5... | collective-permute-start | bytes 393224 | tf_op jit(solution)/shard_map/ppermute | solution.py:263
  43.4 7.1 %collective-permute-start.12 = (bf16[1,32,1024]{2,1,0:T(8,128)(2,1)S(1)}, bf16[1,32,1024]{2,1,0:T(8,128)(2,1)S(1)}, u32[]{:S(2)}, u32[]{:S(2)}) collective-permute-start(bf16[1,32,1024]{2,1,0:T(8,128)(2,1)S(1)} %totals.13.refs_2_), channel_id=1, source_target_pairs={{0,2},{1,3},{2,0},{3,1},{4,6},{5,7},{6,4},{7,5},{8,10},{9,11},{10,... | collective-permute-start | bytes 196616 | tf_op jit(solution)/shard_map/ppermute | solution.py:266
  43.6 11.1 %collective-permute-start.16 = (bf16[1,32,1024]{2,1,0:T(8,128)(2,1)S(1)}, bf16[1,32,1024]{2,1,0:T(8,128)(2,1)S(1)}, u32[]{:S(2)}, u32[]{:S(2)}) collective-permute-start(bf16[1,32,1024]{2,1,0:T(8,128)(2,1)S(1)} %totals.14.refs_2_), channel_id=1, source_target_pairs={{0,2},{1,3},{2,0},{3,1},{4,6},{5,7},{6,4},{7,5},{8,10},{9,11},{10,... | collective-permute-start | bytes 196616 | tf_op jit(solution)/shard_map/ppermute | solution.py:266
  46.7 10.3 %collective-permute-start.22 = (bf16[1,64,1024]{2,1,0:T(8,128)(2,1)S(1)}, bf16[1,64,1024]{2,1,0:T(8,128)(2,1)S(1)}, u32[]{:S(2)}, u32[]{:S(2)}) collective-permute-start(bf16[1,64,1024]{2,1,0:T(8,128)(2,1)S(1)} %totals.15.refs_3_), channel_id=1, source_target_pairs={{0,2},{1,3},{2,0},{3,1},{4,6},{5,7},{6,4},{7,5},{8,10},{9,11},{10,... | collective-permute-start | bytes 393224 | tf_op jit(solution)/shard_map/ppermute | solution.py:266
  46.8 10.1 %collective-permute-start.20 = (bf16[2,32,1024]{2,1,0:T(8,128)(2,1)S(1)}, bf16[2,32,1024]{2,1,0:T(8,128)(2,1)S(1)}, u32[]{:S(2)}, u32[]{:S(2)}) collective-permute-start(bf16[2,32,1024]{2,1,0:T(8,128)(2,1)S(1)} %bitcast.11), channel_id=1, source_target_pairs={{0,16},{4,20},{8,24},{12,28},{16,0},{20,4},{24,8},{28,12},{1,17},{... | collective-permute-start | bytes 393224 | tf_op jit(solution)/shard_map/ppermute | solution.py:263
  50.5 9.1 %collective-permute-start.15 = (bf16[1,32,1024]{2,1,0:T(8,128)(2,1)S(1)}, bf16[1,32,1024]{2,1,0:T(8,128)(2,1)S(1)}, u32[]{:S(2)}, u32[]{:S(2)}) collective-permute-start(bf16[1,32,1024]{2,1,0:T(8,128)(2,1)S(1)} %totals.17.refs_3_), channel_id=1, source_target_pairs={{0,24},{4,28},{8,16},{12,20},{16,8},{20,12},{24,0},{28,4},{1,25},{... | collective-permute-start | bytes 196616 | tf_op jit(solution)/shard_map/ppermute | solution.py:263
  54.7 4.9 %collective-permute-start.17 = (bf16[1,32,1024]{2,1,0:T(8,128)(2,1)S(1)}, bf16[1,32,1024]{2,1,0:T(8,128)(2,1)S(1)}, u32[]{:S(2)}, u32[]{:S(2)}) collective-permute-start(bf16[1,32,1024]{2,1,0:T(8,128)(2,1)S(1)} %totals.18.refs_3_), channel_id=1, source_target_pairs={{0,28},{4,24},{8,20},{12,16},{16,12},{20,8},{24,4},{28,0},{1,29},{... | collective-permute-start | bytes 196616 | tf_op jit(solution)/shard_map/ppermute | solution.py:263
  54.8 2.9 %collective-permute-start.19 = (bf16[32,1024]{1,0:T(8,128)(2,1)S(1)}, bf16[32,1024]{1,0:T(8,128)(2,1)S(1)}, u32[]{:S(2)}, u32[]{:S(2)}) collective-permute-start(bf16[32,1024]{1,0:T(8,128)(2,1)S(1)} %slice_bitcast_fusion.1), channel_id=1, source_target_pairs={{0,4},{4,0},{8,12},{12,8},{16,20},{20,16},{24,28},{28,24},{1,5},{5... | collective-permute-start | bytes 196616 | tf_op jit(solution)/shard_map/ppermute | solution.py:263
  56.9 2.7 %collective-permute-start.21 = (bf16[32,1024]{1,0:T(8,128)(2,1)S(1)}, bf16[32,1024]{1,0:T(8,128)(2,1)S(1)}, u32[]{:S(2)}, u32[]{:S(2)}) collective-permute-start(bf16[32,1024]{1,0:T(8,128)(2,1)S(1)} %slice_bitcast_fusion), channel_id=1, source_target_pairs={{0,4},{4,0},{8,12},{12,8},{16,20},{20,16},{24,28},{28,24},{1,5},{5... | collective-permute-start | bytes 196616 | tf_op jit(solution)/shard_map/ppermute | solution.py:263
  57.8 1.8 %collective-permute-start.23 = (bf16[32,1024]{1,0:T(8,128)(2,1)S(1)}, bf16[32,1024]{1,0:T(8,128)(2,1)S(1)}, u32[]{:S(2)}, u32[]{:S(2)}) collective-permute-start(bf16[32,1024]{1,0:T(8,128)(2,1)S(1)} %get-tuple-element.52), channel_id=1, source_target_pairs={{0,4},{4,0},{8,12},{12,8},{16,20},{20,16},{24,28},{28,24},{1,5},{5... | collective-permute-start | bytes 196616 | tf_op jit(solution)/shard_map/ppermute | solution.py:263

commit v6 on v5

--- a/solution.py
+++ b/solution.py
@@ -73,14 +73,17 @@
     source = held if plan["held"] else brought
     _, wants, share, depth = source.shape
     part = min(PART, share)
-    blocks = [(s, i) for s in range(len(plan["fetch"])) for i in range(share // part)]
+    blocks = [(s, at, part) for s in range(len(plan["fetch"])) for at in range(0, share, part)]
+    if not plan["held"]:
+        s, at, _ = blocks.pop()
+        blocks += [(s, at, part // 2), (s, at + part // 2, part // 2)]
 
     def copies(n):
-        s, i = blocks[n]
-        start = pl.multiple_of((lax.axis_index("narrow") ^ plan["fetch"][s]) * share, share) + i * part
+        s, at, size = blocks[n]
+        start = pl.multiple_of((lax.axis_index("narrow") ^ plan["fetch"][s]) * share, share) + at
         return [
             pltpu.make_async_copy(
-                ints.at[0, k, pl.ds(start, part), :], brought.at[s, k, pl.ds(i * part, part), :], sems.at[n, k]
+                ints.at[0, k, pl.ds(start, size), :], brought.at[s, k, pl.ds(at, size), :], sems.at[n, k]
             )
             for k in range(wants)
         ]
@@ -104,8 +107,8 @@
 
     each = len(picked) * rows // len(outs)
 
-    def block(o, s, i):
-        at = slice(i * part, (i + 1) * part)
+    def block(o, s, start, size):
+        at = slice(start, start + size)
         total = None
         for k in range(wants):
             term = lax.dot_general(
@@ -120,16 +123,16 @@
 
         @pl.loop(0, len(plan["use"]))
         def _(o):
-            for i in range(share // part):
-                block(o, plan["use"][0] + o, i)
+            for at in range(0, share, part):
+                block(o, plan["use"][0] + o, at, part)
 
         for n in range(len(blocks)):
             wait(n)
     else:
-        for n, (s, i) in enumerate(blocks):
+        for n, (s, at, size) in enumerate(blocks):
             wait(n)
             start(n + ahead)
-            block(s, s, i)
+            block(s, s, at, size)
 
 
 def product(picked, chunks, use, held, ints, fetch, passed, after, limit):
@@ -161,7 +164,7 @@
         input_output_aliases={first_passed + i: chunks + bool(fetch) + i for i in range(len(passed))},
         scratch_shapes=[
             pltpu.VMEM((wants, count * rows, depth), jnp.bfloat16),
-            pltpu.SemaphoreType.DMA((max(1, len(fetch) * max(1, share // PART)), wants)),
+            pltpu.SemaphoreType.DMA((1 + len(fetch) * max(1, share // PART), wants)),
         ],
         compiler_params=pltpu.CompilerParams(vmem_limit_bytes=limit),
         cost_estimate=pl.CostEstimate(
@@ -229,11 +232,19 @@
 
 
 def order_kernel(peers, halves, *refs):
-    shares, (place, out, held) = refs[:-3], refs[-3:]
+    shares, (place, out, held, ready, sems) = refs[:-5], refs[-5:]
     rows = held.shape[0] // len(peers)
     for j, half, share in zip(peers, halves, shares):
         held[j * rows : (j + 1) * rows, :] = share[...] if half is None else share[half]
-    out[...] = jnp.dot(place[...], held[...], preferred_element_type=jnp.float32).astype(jnp.bfloat16)
+    half = held.shape[1] // 2
+    copies = []
+    for c in range(2):
+        at = slice(c * half, (c + 1) * half)
+        ready[:, at] = jnp.dot(place[...], held[:, at], preferred_element_type=jnp.float32).astype(jnp.bfloat16)
+        copies.append(pltpu.make_async_copy(ready.at[:, at], out.at[:, at], sems.at[c]))
+        copies[c].start()
+    for copy in copies:
+        copy.wait()
 
 
 def order(place, shares):
@@ -244,8 +255,12 @@
         functools.partial(order_kernel, peers, halves),
         out_shape=jax.ShapeDtypeStruct((size, share), jnp.bfloat16),
         in_specs=[vmem] * (1 + len(shares)),
-        out_specs=vmem,
-        scratch_shapes=[pltpu.VMEM((size, share), jnp.bfloat16)],
+        out_specs=pl.BlockSpec(memory_space=pl.ANY),
+        scratch_shapes=[
+            pltpu.VMEM((size, share), jnp.bfloat16),
+            pltpu.VMEM((size, share), jnp.bfloat16),
+            pltpu.SemaphoreType.DMA((2,)),
+        ],
         compiler_params=pltpu.CompilerParams(vmem_limit_bytes=LIMIT),
         name="order",
     )(*shares, place)
@@ -341,9 +356,10 @@
     for u in far + [mine]:
         ready[u], sums[u] = later_steps(kept[u], come[u], [last])
         last = ready[u]
-    for u in others + far:
+    for u in others:
+        last = close(u, [last, shares[first[0]][0]])
+    for u in far + [mine]:
         last = close(u, [last])
-    close(mine, [last] + [shares[j][0] for j in first])
     return order(place, [(j, *shares[j]) for u in far + near + [mine] for j in u]).reshape(rows, peers, -1)
 
 

time: 60.9 us -> 61.5 us (level)
  waiting for transfers between devices: 9.47 us -> 12.6 us
  starting transfers between devices: 29.6 us -> 26.5 us
    ppermute x14, starting transfers between devices: 14.4 us -> 11.2 us  [swap(): return lax.ppermute(value, 'wide', [(w, w ^ j) for w in range(peers)])]
    ppermute x10, waiting for transfers between devices: 7.26 us -> 9.97 us  [swap_line(): lax.ppermute(value, 'narrow', [(n, n ^ mask) for n in range(devices)])]
    pallas_call x5, Pallas kernels: 16.9 us -> 17.5 us  [product(): pl.pallas_call(functools.partial(product_kernel, plan), out_shape=[jax.Sh...]
  transfers between devices with their start and end apart: 24 -> 24, of which waited for: 6 -> 8; matrix products, arithmetic and copies ran while one was open for 0% -> 0% of each run, Pallas kernels for 30% -> 30%
where the time goes in v6:
time: 61.5 us; the launch traced here: 61.3 us
  starting transfers between devices  26.5 us (43%)
  Pallas kernels  20.4 us (33%)
  waiting for transfers between devices  12.6 us (20%)
  local copies, waits for them, and re-layouts  0.97 us (2%)
  other arithmetic  0.72 us (1%)
    pallas_call x5, Pallas kernels, product(): pl.pallas_call(functools.partial(product_kernel, plan), out_shape=[jax.Sh...  17.5 us
    ppermute x10, starting transfers between devices, swap_line(): lax.ppermute(value, 'narrow', [(n, n ^ mask) for n in range(devices)])  15.2 us
    ppermute x14, starting transfers between devices, swap(): return lax.ppermute(value, 'wide', [(w, w ^ j) for w in range(peers)])  11.2 us
    ppermute x10, waiting for transfers between devices, swap_line(): lax.ppermute(value, 'narrow', [(n, n ^ mask) for n in range(devices)])  9.97 us
    ppermute x14, waiting for transfers between devices, swap(): return lax.ppermute(value, 'wide', [(w, w ^ j) for w in range(peers)])  2.59 us
  transfers between devices with their start and end apart: 24, of which 8 were waited for; matrix products, arithmetic and copies ran while one was open for 0% of the time, Pallas kernels for 30%

profile of v6, /device:TPU:0, one launch (start us, length us, event | category | flops | bytes accessed | tf_op | source)
XLA Modules:
  0.0 61.3 jit_solution(15545681249543382000)
XLA Ops:
  0.0 0.7 %pad_add_fusion.tables_from = s32[7,8]{1,0:T(8,128)S(1)} fusion(s32[1,8]{1,0:T(1,128)} %bitcast.12, s32[2,8]{1,0:T(2,128)} %bitcast.14, s32[4,8]{1,0:T(4,128)} %bitcast.13), kind=kLoop, calls=%fused_computation.2 | loop fusion | flops 112 | bytes 448 | tf_op jit(solution)/shard_map/concatenate | solution.py:46
  0.7 0.9 %copy-done = bf16[32,4,1024]{2,1,0:T(4,128)(2,1)S(1)} copy-done((bf16[32,4,1024]{2,1,0:T(4,128)(2,1)S(1)}, bf16[32,4,1024]{2,1,0:T(4,128)(2,1)}, u32[]{:S(2)}) %copy-start) | copy-done | bytes 262168
  1.7 0.8 %pick.1 = (bf16[2,32,1024]{2,1,0:T(8,128)(2,1)S(1)}, bf16[2,32,1024]{2,1,0:T(8,128)(2,1)S(1)}, bf16[2,32,1024]{2,1,0:T(8,128)(2,1)S(1)}, bf16[2,32,1024]{2,1,0:T...) custom-call(s32[7,8]{1,0:T(8,128)S(1)} %pad_add_fusion.tables_from, ...), custom_call_target="tpu_custom_call" | custom-call | tf_op jit(solution)/shard_map/pick/pallas_call | solution.py:48
  2.5 0.5 collective-permute-start
  3.0 2.6 %collective-permute-start.2 = (bf16[2,32,1024]{2,1,0:T(8,128)(2,1)S(1)}, bf16[2,32,1024]{2,1,0:T(8,128)(2,1)S(1)}, u32[]{:S(2)}, u32[]{:S(2)}) collective-permute-start(bf16[2,32,1024]{2,1,0:T(8,128)(2,1)S(1)} %get-tuple-element.32), channel_id=1, source_target_pairs={{0,8},{4,12},{8,0},{12,4},{16,24},{20,28},{24,16},{28,20},{1,9},{5... | collective-permute-start | bytes 393224 | tf_op jit(solution)/shard_map/ppermute | solution.py:278
  5.6 0.1 collective-permute-start.3
  5.7 1.8 %collective-permute-start.4 = (bf16[2,32,1024]{2,1,0:T(8,128)(2,1)S(1)}, bf16[2,32,1024]{2,1,0:T(8,128)(2,1)S(1)}, u32[]{:S(2)}, u32[]{:S(2)}) collective-permute-start(bf16[2,32,1024]{2,1,0:T(8,128)(2,1)S(1)} %get-tuple-element.34), channel_id=1, source_target_pairs={{0,16},{4,20},{8,24},{12,28},{16,0},{20,4},{24,8},{28,12},{1,17},{... | collective-permute-start | bytes 393224 | tf_op jit(solution)/shard_map/ppermute | solution.py:278
  7.4 0.0 collective-permute-start.5
  7.4 0.0 collective-permute-done.refs_1_.refs_2_
  7.4 5.2 %product.5 = (bf16[2,64,1024]{2,1,0:T(8,128)(2,1)S(1)}, bf16[2,2,1024,1024]{3,2,1,0:T(8,128)(2,1)S(1)}) custom-call(bf16[2,32,1024]{2,1,0:T(8,128)(2,1)S(1)} %get-tuple-element.29.refs_0_.refs_1_, bf16[2,32,1024]{2,1,0:T(8,128)(2,1)S(1)} %collective-permute-done.refs_1_.refs_2_, bf16[1,2,4096,1024]{3,2,1,0:T(8,128)(2,1)} %refs_6_.1), custom_call_target="tpu_custom_call" | custom-call | flops 2147483648 | bytes 8388608 | tf_op jit(solution)/shard_map/product/pallas_call | solution.py:155
  12.7 1.8 %collective-permute-start.1 = (bf16[2,64,1024]{2,1,0:T(8,128)(2,1)S(1)}, bf16[2,64,1024]{2,1,0:T(8,128)(2,1)S(1)}, u32[]{:S(2)}, u32[]{:S(2)}) collective-permute-start(bf16[2,64,1024]{2,1,0:T(8,128)(2,1)S(1)} %get-tuple-element.31.refs_0_), channel_id=1, source_target_pairs={{0,1},{1,0},{2,3},{3,2},{4,5},{5,4},{6,7},{7,6},{8,9},{9,8},{10,11... | collective-permute-start | bytes 786440 | tf_op jit(solution)/shard_map/ppermute | solution.py:281
  14.5 0.0 collective-permute-done.3.refs_2_.refs_4_
  14.5 0.0 collective-permute-done.4.refs_3_.refs_5_
  14.5 3.5 %product.6 = (bf16[2,64,1024]{2,1,0:T(8,128)(2,1)S(1)}, bf16[2,64,1024]{2,1,0:T(8,128)(2,1)S(1)}, bf16[2,2,1024,1024]{3,2,1,0:T(8,128)(2,1)S(1)}, bf16[2,32,1024...) custom-call(bf16[2,64,1024]{2,1,0:T(8,128)(2,1)S(1)} %get-tuple-element.31.refs_0_, ...), custom_call_target="tpu_custom_call", output_to_operand_aliasing={{3}: (7, {}), {4}: (8, {})} | custom-call | flops 2147483648 | bytes 8388608 | tf_op jit(solution)/shard_map/product/pallas_call | solution.py:155
  18.0 0.0 copy-start.1
  18.0 1.0 %collective-permute-start.7 = (bf16[2,64,1024]{2,1,0:T(8,128)(2,1)S(1)}, bf16[2,64,1024]{2,1,0:T(8,128)(2,1)S(1)}, u32[]{:S(2)}, u32[]{:S(2)}) collective-permute-start(bf16[2,64,1024]{2,1,0:T(8,128)(2,1)S(1)} %get-tuple-element.43), channel_id=1, source_target_pairs={{0,1},{1,0},{2,3},{3,2},{4,5},{5,4},{6,7},{7,6},{8,9},{9,8},{10,11... | collective-permute-start | bytes 786440 | tf_op jit(solution)/shard_map/ppermute | solution.py:281
  19.1 2.4 %collective-permute-start.8 = (bf16[2,32,1024]{2,1,0:T(8,128)(2,1)S(1)}, bf16[2,32,1024]{2,1,0:T(8,128)(2,1)S(1)}, u32[]{:S(2)}, u32[]{:S(2)}) collective-permute-start(bf16[2,32,1024]{2,1,0:T(8,128)(2,1)S(1)} %get-tuple-element.45), channel_id=1, source_target_pairs={{0,24},{4,28},{8,16},{12,20},{16,8},{20,12},{24,0},{28,4},{1,25},{... | collective-permute-start | bytes 393224 | tf_op jit(solution)/shard_map/ppermute | solution.py:278
  21.5 0.0 collective-permute-start.9
  21.5 1.1 %collective-permute-start.6 = (bf16[2,64,1024]{2,1,0:T(8,128)(2,1)S(1)}, bf16[2,64,1024]{2,1,0:T(8,128)(2,1)S(1)}, u32[]{:S(2)}, u32[]{:S(2)}) collective-permute-start(bf16[2,64,1024]{2,1,0:T(8,128)(2,1)S(1)} %get-tuple-element.41), channel_id=1, source_target_pairs={{0,1},{1,0},{2,3},{3,2},{4,5},{5,4},{6,7},{7,6},{8,9},{9,8},{10,11... | collective-permute-start | bytes 786440 | tf_op jit(solution)/shard_map/ppermute | solution.py:281
  22.6 3.1 %product.7 = (bf16[2,64,1024]{2,1,0:T(8,128)(2,1)S(1)}, bf16[2,64,1024]{2,1,0:T(8,128)(2,1)S(1)}, bf16[2,64,1024]{2,1,0:T(8,128)(2,1)S(1)}) custom-call(bf16[2,64,1024]{2,1,0:T(8,128)(2,1)S(1)} %collective-permute-done.1.refs_0_.refs_1_, bf16[2,32,1024]{2,1,0:T(8,128)(2,1)S(1)} %get-tuple-element.29.refs_0_.refs_1_, ...), custom_call_target="tpu_custom_call" | custom-call | flops 2147483648 | bytes 8388608 | tf_op jit(solution)/shard_map/product/pallas_call | solution.py:155
  25.7 0.7 %place.1.refs_2_.refs_8_ = bf16[256,256]{1,0:T(8,128)(2,1)S(1)} custom-call(s32[8]{0:T(128)S(1)} %copy-done.1, bf16[2,64,1024]{2,1,0:T(8,128)(2,1)S(1)} %get-tuple-element.44.after.refs_0_), custom_call_target="tpu_custom_call" | custom-call | tf_op jit(solution)/shard_map/place/pallas_call | solution.py:224
  26.4 1.1 %collective-permute-done.7.refs_1_ = bf16[2,64,1024]{2,1,0:T(8,128)(2,1)S(1)} collective-permute-done((bf16[2,64,1024]{2,1,0:T(8,128)(2,1)S(1)}, bf16[2,64,1024]{2,1,0:T(8,128)(2,1)S(1)}, u32[]{:S(2)}, u32[]{:S(2)}) %collective-permute-start.7) | collective-permute-done | bytes 262176 | tf_op jit(solution)/shard_map/ppermute | solution.py:281
  27.5 2.8 %collective-permute-start.10 = (bf16[1,64,1024]{2,1,0:T(8,128)(2,1)S(1)}, bf16[1,64,1024]{2,1,0:T(8,128)(2,1)S(1)}, u32[]{:S(2)}, u32[]{:S(2)}) collective-permute-start(bf16[1,64,1024]{2,1,0:T(8,128)(2,1)S(1)} %totals.10.refs_0_), channel_id=1, source_target_pairs={{0,2},{1,3},{2,0},{3,1},{4,6},{5,7},{6,4},{7,5},{8,10},{9,11},{10,... | collective-permute-start | bytes 393224 | tf_op jit(solution)/shard_map/ppermute | solution.py:281
  30.4 2.8 %product.8 = (bf16[2,32,1024]{2,1,0:T(8,128)(2,1)S(1)}, bf16[2,32,1024]{2,1,0:T(8,128)(2,1)S(1)}) custom-call(bf16[1,64,1024]{2,1,0:T(8,128)(2,1)S(1)} %totals.10.refs_0_, bf16[2,32,1024]{2,1,0:T(8,128)(2,1)S(1)} %collective-permute-done.8.refs_1_.refs_2_, bf16[2,32,1024]{2,1,0:T(8,128)(2,1)S(1)} %collective-permute-done.9.refs_2_.refs_3_, ...), custom_call_target="tpu_custom_call" | custom-call | flops 2147483648 | bytes 8388608 | tf_op jit(solution)/shard_map/product/pallas_call | solution.py:155
  33.2 1.6 %collective-permute-start.11 = (bf16[2,32,1024]{2,1,0:T(8,128)(2,1)S(1)}, bf16[2,32,1024]{2,1,0:T(8,128)(2,1)S(1)}, u32[]{:S(2)}, u32[]{:S(2)}) collective-permute-start(bf16[2,32,1024]{2,1,0:T(8,128)(2,1)S(1)} %get-tuple-element.47.refs_2_), channel_id=1, source_target_pairs={{0,1},{1,0},{2,3},{3,2},{4,5},{5,4},{6,7},{7,6},{8,9},{9,8},{10,11... | collective-permute-start | bytes 393224 | tf_op jit(solution)/shard_map/ppermute | solution.py:281
  34.8 1.1 %collective-permute-done.6.refs_1_ = bf16[2,64,1024]{2,1,0:T(8,128)(2,1)S(1)} collective-permute-done((bf16[2,64,1024]{2,1,0:T(8,128)(2,1)S(1)}, bf16[2,64,1024]{2,1,0:T(8,128)(2,1)S(1)}, u32[]{:S(2)}, u32[]{:S(2)}) %collective-permute-start.6) | collective-permute-done | bytes 262176 | tf_op jit(solution)/shard_map/ppermute | solution.py:281
  36.0 1.1 %collective-permute-start.13 = (bf16[1,64,1024]{2,1,0:T(8,128)(2,1)S(1)}, bf16[1,64,1024]{2,1,0:T(8,128)(2,1)S(1)}, u32[]{:S(2)}, u32[]{:S(2)}) collective-permute-start(bf16[1,64,1024]{2,1,0:T(8,128)(2,1)S(1)} %totals.11.refs_0_), channel_id=1, source_target_pairs={{0,2},{1,3},{2,0},{3,1},{4,6},{5,7},{6,4},{7,5},{8,10},{9,11},{10,... | collective-permute-start | bytes 393224 | tf_op jit(solution)/shard_map/ppermute | solution.py:281
  37.1 2.5 %collective-permute-start.14 = (bf16[2,32,1024]{2,1,0:T(8,128)(2,1)S(1)}, bf16[2,32,1024]{2,1,0:T(8,128)(2,1)S(1)}, u32[]{:S(2)}, u32[]{:S(2)}) collective-permute-start(bf16[2,32,1024]{2,1,0:T(8,128)(2,1)S(1)} %get-tuple-element.50), channel_id=1, source_target_pairs={{0,1},{1,0},{2,3},{3,2},{4,5},{5,4},{6,7},{7,6},{8,9},{9,8},{10,11... | collective-permute-start | bytes 393224 | tf_op jit(solution)/shard_map/ppermute | solution.py:281
  39.6 2.8 %product.9 = (bf16[2,32,1024]{2,1,0:T(8,128)(2,1)S(1)}, bf16[2,32,1024]{2,1,0:T(8,128)(2,1)S(1)}) custom-call(bf16[1,64,1024]{2,1,0:T(8,128)(2,1)S(1)} %totals.11.refs_0_, bf16[1,64,1024]{2,1,0:T(8,128)(2,1)S(1)} %collective-permute-done.10.refs_1_.refs_2_, bf16[2,32,1024]{2,1,0:T(8,128)(2,1)S(1)} %collective-permute-done.8.refs_1_.refs_2_, ...), custom_call_target="tpu_custom_call" | custom-call | flops 2147483648 | bytes 8388608 | tf_op jit(solution)/shard_map/product/pallas_call | solution.py:155
  42.4 0.1 totals.12.refs_2_
  42.5 1.5 %collective-permute-start.15 = (bf16[2,32,1024]{2,1,0:T(8,128)(2,1)S(1)}, bf16[2,32,1024]{2,1,0:T(8,128)(2,1)S(1)}, u32[]{:S(2)}, u32[]{:S(2)}) collective-permute-start(bf16[2,32,1024]{2,1,0:T(8,128)(2,1)S(1)} %bitcast.10), channel_id=1, source_target_pairs={{0,8},{4,12},{8,0},{12,4},{16,24},{20,28},{24,16},{28,20},{1,9},{5... | collective-permute-start | bytes 393224 | tf_op jit(solution)/shard_map/ppermute | solution.py:278
  44.0 0.1 collective-permute-start.12
  44.2 3.1 %collective-permute-start.17 = (bf16[1,32,1024]{2,1,0:T(8,128)(2,1)S(1)}, bf16[1,32,1024]{2,1,0:T(8,128)(2,1)S(1)}, u32[]{:S(2)}, u32[]{:S(2)}) collective-permute-start(bf16[1,32,1024]{2,1,0:T(8,128)(2,1)S(1)} %totals.14.refs_2_), channel_id=1, source_target_pairs={{0,2},{1,3},{2,0},{3,1},{4,6},{5,7},{6,4},{7,5},{8,10},{9,11},{10,... | collective-permute-start | bytes 196616 | tf_op jit(solution)/shard_map/ppermute | solution.py:281
  47.3 0.1 collective-permute-start.22
  47.4 0.1 collective-permute-done.15.refs_4_.refs_2_
  47.5 0.1 totals.16.refs_3_
  47.5 1.6 %collective-permute-start.20 = (bf16[2,32,1024]{2,1,0:T(8,128)(2,1)S(1)}, bf16[2,32,1024]{2,1,0:T(8,128)(2,1)S(1)}, u32[]{:S(2)}, u32[]{:S(2)}) collective-permute-start(bf16[2,32,1024]{2,1,0:T(8,128)(2,1)S(1)} %bitcast.11), channel_id=1, source_target_pairs={{0,16},{4,20},{8,24},{12,28},{16,0},{20,4},{24,8},{28,12},{1,17},{... | collective-permute-start | bytes 393224 | tf_op jit(solution)/shard_map/ppermute | solution.py:278
  49.1 3.4 %collective-permute-done.12.refs_2_ = bf16[1,32,1024]{2,1,0:T(8,128)(2,1)S(1)} collective-permute-done((bf16[1,32,1024]{2,1,0:T(8,128)(2,1)S(1)}, bf16[1,32,1024]{2,1,0:T(8,128)(2,1)S(1)}, u32[]{:S(2)}, u32[]{:S(2)}) %collective-permute-start.12) | collective-permute-done | bytes 65568 | tf_op jit(solution)/shard_map/ppermute | solution.py:281
  52.5 0.1 collective-permute-start.16
  52.6 2.7 %collective-permute-done.17.refs_2_ = bf16[1,32,1024]{2,1,0:T(8,128)(2,1)S(1)} collective-permute-done((bf16[1,32,1024]{2,1,0:T(8,128)(2,1)S(1)}, bf16[1,32,1024]{2,1,0:T(8,128)(2,1)S(1)}, u32[]{:S(2)}, u32[]{:S(2)}) %collective-permute-start.17) | collective-permute-done | bytes 65568 | tf_op jit(solution)/shard_map/ppermute | solution.py:281
  55.3 0.1 collective-permute-start.18
  55.4 1.7 %collective-permute-done.22.refs_2_ = bf16[1,64,1024]{2,1,0:T(8,128)(2,1)S(1)} collective-permute-done((bf16[1,64,1024]{2,1,0:T(8,128)(2,1)S(1)}, bf16[1,64,1024]{2,1,0:T(8,128)(2,1)S(1)}, u32[]{:S(2)}, u32[]{:S(2)}) %collective-permute-start.22) | collective-permute-done | bytes 131104 | tf_op jit(solution)/shard_map/ppermute | solution.py:281
  57.1 0.1 totals.19
  57.2 0.4 collective-permute-start.23
  57.5 0.3 collective-permute-start.21
  57.8 0.7 %collective-permute-done.23.refs_7_ = bf16[32,1024]{1,0:T(8,128)(2,1)S(1)} collective-permute-done((bf16[32,1024]{1,0:T(8,128)(2,1)S(1)}, bf16[32,1024]{1,0:T(8,128)(2,1)S(1)}, u32[]{:S(2)}, u32[]{:S(2)}) %collective-permute-start.23) | collective-permute-done | bytes 65568 | tf_op jit(solution)/shard_map/ppermute | solution.py:278
  58.5 1.8 %collective-permute-done.18.refs_1_ = bf16[1,32,1024]{2,1,0:T(8,128)(2,1)S(1)} collective-permute-done((bf16[1,32,1024]{2,1,0:T(8,128)(2,1)S(1)}, bf16[1,32,1024]{2,1,0:T(8,128)(2,1)S(1)}, u32[]{:S(2)}, u32[]{:S(2)}) %collective-permute-start.18) | collective-permute-done | bytes 65568 | tf_op jit(solution)/shard_map/ppermute | solution.py:278
  60.3 1.0 %order.1 = bf16[256,1024]{1,0:T(8,128)(2,1)} custom-call(bf16[1,32,1024]{2,1,0:T(8,128)(2,1)S(1)} %collective-permute-done.16.refs_0_, bf16[1,32,1024]{2,1,0:T(8,128)(2,1)S(1)} %collective-permute-done.18.refs_1_, bf16[2,32,1024]{2,1,0:T(8,128)(2,1)S(1)} %collective-permute-done.15.refs_4_.refs_2_, bf16[32,1024]{1,0:T(8,128)(2,1)S(1)} %collective-permute-done.19.refs_3_, ...), custom_call_target="tpu_custom_call" | custom-call | tf_op jit(solution)/shard_map/order/pallas_call | solution.py:254
  (25 shorter events, 0.2 us)
Async XLA Ops:
  0.7 0.9 %copy-start = (bf16[32,4,1024]{2,1,0:T(4,128)(2,1)S(1)}, bf16[32,4,1024]{2,1,0:T(4,128)(2,1)}, u32[]{:S(2)}) copy-start(bf16[32,4,1024]{2,1,0:T(4,128)(2,1)} %amps.1) | copy-start | bytes 786436
  2.5 4.9 %collective-permute-start = (bf16[2,32,1024]{2,1,0:T(8,128)(2,1)S(1)}, bf16[2,32,1024]{2,1,0:T(8,128)(2,1)S(1)}, u32[]{:S(2)}, u32[]{:S(2)}) collective-permute-start(bf16[2,32,1024]{2,1,0:T(8,128)(2,1)S(1)} %get-tuple-element.30), channel_id=1, source_target_pairs={{0,4},{4,0},{8,12},{12,8},{16,20},{20,16},{24,28},{28,24},{1,5},{5... | collective-permute-start | bytes 393224 | tf_op jit(solution)/shard_map/ppermute | solution.py:278
  3.0 11.5 %collective-permute-start.2 = (bf16[2,32,1024]{2,1,0:T(8,128)(2,1)S(1)}, bf16[2,32,1024]{2,1,0:T(8,128)(2,1)S(1)}, u32[]{:S(2)}, u32[]{:S(2)}) collective-permute-start(bf16[2,32,1024]{2,1,0:T(8,128)(2,1)S(1)} %get-tuple-element.32), channel_id=1, source_target_pairs={{0,8},{4,12},{8,0},{12,4},{16,24},{20,28},{24,16},{28,20},{1,9},{5... | collective-permute-start | bytes 393224 | tf_op jit(solution)/shard_map/ppermute | solution.py:278
  5.6 8.9 %collective-permute-start.3 = (bf16[2,32,1024]{2,1,0:T(8,128)(2,1)S(1)}, bf16[2,32,1024]{2,1,0:T(8,128)(2,1)S(1)}, u32[]{:S(2)}, u32[]{:S(2)}) collective-permute-start(bf16[2,32,1024]{2,1,0:T(8,128)(2,1)S(1)} %get-tuple-element.33), channel_id=1, source_target_pairs={{0,12},{4,8},{8,4},{12,0},{16,28},{20,24},{24,20},{28,16},{1,13},{... | collective-permute-start | bytes 393224 | tf_op jit(solution)/shard_map/ppermute | solution.py:278
  5.7 8.8 %collective-permute-start.4 = (bf16[2,32,1024]{2,1,0:T(8,128)(2,1)S(1)}, bf16[2,32,1024]{2,1,0:T(8,128)(2,1)S(1)}, u32[]{:S(2)}, u32[]{:S(2)}) collective-permute-start(bf16[2,32,1024]{2,1,0:T(8,128)(2,1)S(1)} %get-tuple-element.34), channel_id=1, source_target_pairs={{0,16},{4,20},{8,24},{12,28},{16,0},{20,4},{24,8},{28,12},{1,17},{... | collective-permute-start | bytes 393224 | tf_op jit(solution)/shard_map/ppermute | solution.py:278
  7.4 7.1 %collective-permute-start.5 = (bf16[2,32,1024]{2,1,0:T(8,128)(2,1)S(1)}, bf16[2,32,1024]{2,1,0:T(8,128)(2,1)S(1)}, u32[]{:S(2)}, u32[]{:S(2)}) collective-permute-start(bf16[2,32,1024]{2,1,0:T(8,128)(2,1)S(1)} %get-tuple-element.35), channel_id=1, source_target_pairs={{0,20},{4,16},{8,28},{12,24},{16,4},{20,0},{24,12},{28,8},{1,21},{... | collective-permute-start | bytes 393224 | tf_op jit(solution)/shard_map/ppermute | solution.py:278
  12.7 9.9 %collective-permute-start.1 = (bf16[2,64,1024]{2,1,0:T(8,128)(2,1)S(1)}, bf16[2,64,1024]{2,1,0:T(8,128)(2,1)S(1)}, u32[]{:S(2)}, u32[]{:S(2)}) collective-permute-start(bf16[2,64,1024]{2,1,0:T(8,128)(2,1)S(1)} %get-tuple-element.31.refs_0_), channel_id=1, source_target_pairs={{0,1},{1,0},{2,3},{3,2},{4,5},{5,4},{6,7},{7,6},{8,9},{9,8},{10,11... | collective-permute-start | bytes 786440 | tf_op jit(solution)/shard_map/ppermute | solution.py:281
  18.0 7.7 %copy-start.1 = (s32[8]{0:T(128)S(1)}, s32[8]{0:T(128)}, u32[]{:S(2)}) copy-start(s32[8]{0:T(128)} %q_owner.1) | copy-start | bytes 100
  18.0 9.5 %collective-permute-start.7 = (bf16[2,64,1024]{2,1,0:T(8,128)(2,1)S(1)}, bf16[2,64,1024]{2,1,0:T(8,128)(2,1)S(1)}, u32[]{:S(2)}, u32[]{:S(2)}) collective-permute-start(bf16[2,64,1024]{2,1,0:T(8,128)(2,1)S(1)} %get-tuple-element.43), channel_id=1, source_target_pairs={{0,1},{1,0},{2,3},{3,2},{4,5},{5,4},{6,7},{7,6},{8,9},{9,8},{10,11... | collective-permute-start | bytes 786440 | tf_op jit(solution)/shard_map/ppermute | solution.py:281
  19.1 11.3 %collective-permute-start.8 = (bf16[2,32,1024]{2,1,0:T(8,128)(2,1)S(1)}, bf16[2,32,1024]{2,1,0:T(8,128)(2,1)S(1)}, u32[]{:S(2)}, u32[]{:S(2)}) collective-permute-start(bf16[2,32,1024]{2,1,0:T(8,128)(2,1)S(1)} %get-tuple-element.45), channel_id=1, source_target_pairs={{0,24},{4,28},{8,16},{12,20},{16,8},{20,12},{24,0},{28,4},{1,25},{... | collective-permute-start | bytes 393224 | tf_op jit(solution)/shard_map/ppermute | solution.py:278
  21.5 8.8 %collective-permute-start.9 = (bf16[2,32,1024]{2,1,0:T(8,128)(2,1)S(1)}, bf16[2,32,1024]{2,1,0:T(8,128)(2,1)S(1)}, u32[]{:S(2)}, u32[]{:S(2)}) collective-permute-start(bf16[2,32,1024]{2,1,0:T(8,128)(2,1)S(1)} %get-tuple-element.46), channel_id=1, source_target_pairs={{0,28},{4,24},{8,20},{12,16},{16,12},{20,8},{24,4},{28,0},{1,29},{... | collective-permute-start | bytes 393224 | tf_op jit(solution)/shard_map/ppermute | solution.py:278
  21.5 14.4 %collective-permute-start.6 = (bf16[2,64,1024]{2,1,0:T(8,128)(2,1)S(1)}, bf16[2,64,1024]{2,1,0:T(8,128)(2,1)S(1)}, u32[]{:S(2)}, u32[]{:S(2)}) collective-permute-start(bf16[2,64,1024]{2,1,0:T(8,128)(2,1)S(1)} %get-tuple-element.41), channel_id=1, source_target_pairs={{0,1},{1,0},{2,3},{3,2},{4,5},{5,4},{6,7},{7,6},{8,9},{9,8},{10,11... | collective-permute-start | bytes 786440 | tf_op jit(solution)/shard_map/ppermute | solution.py:281
  27.5 12.0 %collective-permute-start.10 = (bf16[1,64,1024]{2,1,0:T(8,128)(2,1)S(1)}, bf16[1,64,1024]{2,1,0:T(8,128)(2,1)S(1)}, u32[]{:S(2)}, u32[]{:S(2)}) collective-permute-start(bf16[1,64,1024]{2,1,0:T(8,128)(2,1)S(1)} %totals.10.refs_0_), channel_id=1, source_target_pairs={{0,2},{1,3},{2,0},{3,1},{4,6},{5,7},{6,4},{7,5},{8,10},{9,11},{10,... | collective-permute-start | bytes 393224 | tf_op jit(solution)/shard_map/ppermute | solution.py:281
  33.2 10.8 %collective-permute-start.11 = (bf16[2,32,1024]{2,1,0:T(8,128)(2,1)S(1)}, bf16[2,32,1024]{2,1,0:T(8,128)(2,1)S(1)}, u32[]{:S(2)}, u32[]{:S(2)}) collective-permute-start(bf16[2,32,1024]{2,1,0:T(8,128)(2,1)S(1)} %get-tuple-element.47.refs_2_), channel_id=1, source_target_pairs={{0,1},{1,0},{2,3},{3,2},{4,5},{5,4},{6,7},{7,6},{8,9},{9,8},{10,11... | collective-permute-start | bytes 393224 | tf_op jit(solution)/shard_map/ppermute | solution.py:281
  36.0 11.4 %collective-permute-start.13 = (bf16[1,64,1024]{2,1,0:T(8,128)(2,1)S(1)}, bf16[1,64,1024]{2,1,0:T(8,128)(2,1)S(1)}, u32[]{:S(2)}, u32[]{:S(2)}) collective-permute-start(bf16[1,64,1024]{2,1,0:T(8,128)(2,1)S(1)} %totals.11.refs_0_), channel_id=1, source_target_pairs={{0,2},{1,3},{2,0},{3,1},{4,6},{5,7},{6,4},{7,5},{8,10},{9,11},{10,... | collective-permute-start | bytes 393224 | tf_op jit(solution)/shard_map/ppermute | solution.py:281
  37.1 7.1 %collective-permute-start.14 = (bf16[2,32,1024]{2,1,0:T(8,128)(2,1)S(1)}, bf16[2,32,1024]{2,1,0:T(8,128)(2,1)S(1)}, u32[]{:S(2)}, u32[]{:S(2)}) collective-permute-start(bf16[2,32,1024]{2,1,0:T(8,128)(2,1)S(1)} %get-tuple-element.50), channel_id=1, source_target_pairs={{0,1},{1,0},{2,3},{3,2},{4,5},{5,4},{6,7},{7,6},{8,9},{9,8},{10,11... | collective-permute-start | bytes 393224 | tf_op jit(solution)/shard_map/ppermute | solution.py:281
  42.5 5.0 %collective-permute-start.15 = (bf16[2,32,1024]{2,1,0:T(8,128)(2,1)S(1)}, bf16[2,32,1024]{2,1,0:T(8,128)(2,1)S(1)}, u32[]{:S(2)}, u32[]{:S(2)}) collective-permute-start(bf16[2,32,1024]{2,1,0:T(8,128)(2,1)S(1)} %bitcast.10), channel_id=1, source_target_pairs={{0,8},{4,12},{8,0},{12,4},{16,24},{20,28},{24,16},{28,20},{1,9},{5... | collective-permute-start | bytes 393224 | tf_op jit(solution)/shard_map/ppermute | solution.py:278
  44.0 8.5 %collective-permute-start.12 = (bf16[1,32,1024]{2,1,0:T(8,128)(2,1)S(1)}, bf16[1,32,1024]{2,1,0:T(8,128)(2,1)S(1)}, u32[]{:S(2)}, u32[]{:S(2)}) collective-permute-start(bf16[1,32,1024]{2,1,0:T(8,128)(2,1)S(1)} %totals.13.refs_2_), channel_id=1, source_target_pairs={{0,2},{1,3},{2,0},{3,1},{4,6},{5,7},{6,4},{7,5},{8,10},{9,11},{10,... | collective-permute-start | bytes 196616 | tf_op jit(solution)/shard_map/ppermute | solution.py:281
  44.2 11.1 %collective-permute-start.17 = (bf16[1,32,1024]{2,1,0:T(8,128)(2,1)S(1)}, bf16[1,32,1024]{2,1,0:T(8,128)(2,1)S(1)}, u32[]{:S(2)}, u32[]{:S(2)}) collective-permute-start(bf16[1,32,1024]{2,1,0:T(8,128)(2,1)S(1)} %totals.14.refs_2_), channel_id=1, source_target_pairs={{0,2},{1,3},{2,0},{3,1},{4,6},{5,7},{6,4},{7,5},{8,10},{9,11},{10,... | collective-permute-start | bytes 196616 | tf_op jit(solution)/shard_map/ppermute | solution.py:281
  47.3 9.8 %collective-permute-start.22 = (bf16[1,64,1024]{2,1,0:T(8,128)(2,1)S(1)}, bf16[1,64,1024]{2,1,0:T(8,128)(2,1)S(1)}, u32[]{:S(2)}, u32[]{:S(2)}) collective-permute-start(bf16[1,64,1024]{2,1,0:T(8,128)(2,1)S(1)} %totals.15.refs_3_), channel_id=1, source_target_pairs={{0,2},{1,3},{2,0},{3,1},{4,6},{5,7},{6,4},{7,5},{8,10},{9,11},{10,... | collective-permute-start | bytes 393224 | tf_op jit(solution)/shard_map/ppermute | solution.py:281
  47.5 10.0 %collective-permute-start.20 = (bf16[2,32,1024]{2,1,0:T(8,128)(2,1)S(1)}, bf16[2,32,1024]{2,1,0:T(8,128)(2,1)S(1)}, u32[]{:S(2)}, u32[]{:S(2)}) collective-permute-start(bf16[2,32,1024]{2,1,0:T(8,128)(2,1)S(1)} %bitcast.11), channel_id=1, source_target_pairs={{0,16},{4,20},{8,24},{12,28},{16,0},{20,4},{24,8},{28,12},{1,17},{... | collective-permute-start | bytes 393224 | tf_op jit(solution)/shard_map/ppermute | solution.py:278
  49.1 8.7 %collective-permute-start.19 = (bf16[32,1024]{1,0:T(8,128)(2,1)S(1)}, bf16[32,1024]{1,0:T(8,128)(2,1)S(1)}, u32[]{:S(2)}, u32[]{:S(2)}) collective-permute-start(bf16[32,1024]{1,0:T(8,128)(2,1)S(1)} %slice_bitcast_fusion.1), channel_id=1, source_target_pairs={{0,4},{4,0},{8,12},{12,8},{16,20},{20,16},{24,28},{28,24},{1,5},{5... | collective-permute-start | bytes 196616 | tf_op jit(solution)/shard_map/ppermute | solution.py:278
  52.5 7.7 %collective-permute-start.16 = (bf16[1,32,1024]{2,1,0:T(8,128)(2,1)S(1)}, bf16[1,32,1024]{2,1,0:T(8,128)(2,1)S(1)}, u32[]{:S(2)}, u32[]{:S(2)}) collective-permute-start(bf16[1,32,1024]{2,1,0:T(8,128)(2,1)S(1)} %totals.17.refs_3_), channel_id=1, source_target_pairs={{0,24},{4,28},{8,16},{12,20},{16,8},{20,12},{24,0},{28,4},{1,25},{... | collective-permute-start | bytes 196616 | tf_op jit(solution)/shard_map/ppermute | solution.py:278
  55.3 4.9 %collective-permute-start.18 = (bf16[1,32,1024]{2,1,0:T(8,128)(2,1)S(1)}, bf16[1,32,1024]{2,1,0:T(8,128)(2,1)S(1)}, u32[]{:S(2)}, u32[]{:S(2)}) collective-permute-start(bf16[1,32,1024]{2,1,0:T(8,128)(2,1)S(1)} %totals.18.refs_3_), channel_id=1, source_target_pairs={{0,28},{4,24},{8,20},{12,16},{16,12},{20,8},{24,4},{28,0},{1,29},{... | collective-permute-start | bytes 196616 | tf_op jit(solution)/shard_map/ppermute | solution.py:278
  57.2 1.3 %collective-permute-start.23 = (bf16[32,1024]{1,0:T(8,128)(2,1)S(1)}, bf16[32,1024]{1,0:T(8,128)(2,1)S(1)}, u32[]{:S(2)}, u32[]{:S(2)}) collective-permute-start(bf16[32,1024]{1,0:T(8,128)(2,1)S(1)} %get-tuple-element.52), channel_id=1, source_target_pairs={{0,4},{4,0},{8,12},{12,8},{16,20},{20,16},{24,28},{28,24},{1,5},{5... | collective-permute-start | bytes 196616 | tf_op jit(solution)/shard_map/ppermute | solution.py:278
  57.5 2.7 %collective-permute-start.21 = (bf16[32,1024]{1,0:T(8,128)(2,1)S(1)}, bf16[32,1024]{1,0:T(8,128)(2,1)S(1)}, u32[]{:S(2)}, u32[]{:S(2)}) collective-permute-start(bf16[32,1024]{1,0:T(8,128)(2,1)S(1)} %slice_bitcast_fusion), channel_id=1, source_target_pairs={{0,4},{4,0},{8,12},{12,8},{16,20},{20,16},{24,28},{28,24},{1,5},{5... | collective-permute-start | bytes 196616 | tf_op jit(solution)/shard_map/ppermute | solution.py:278

commit v7 on v6

--- a/solution.py
+++ b/solution.py
@@ -74,10 +74,6 @@
     _, wants, share, depth = source.shape
     part = min(PART, share)
     blocks = [(s, at, part) for s in range(len(plan["fetch"])) for at in range(0, share, part)]
-    if not plan["held"]:
-        s, at, _ = blocks.pop()
-        blocks += [(s, at, part // 2), (s, at + part // 2, part // 2)]
-
     def copies(n):
         s, at, size = blocks[n]
         start = pl.multiple_of((lax.axis_index("narrow") ^ plan["fetch"][s]) * share, share) + at
@@ -353,12 +349,15 @@
         return whole
 
     last = close(first, [kept[far[0]]])
-    for u in far + [mine]:
+    for u in far:
         ready[u], sums[u] = later_steps(kept[u], come[u], [last])
         last = ready[u]
     for u in others:
         last = close(u, [last, shares[first[0]][0]])
-    for u in far + [mine]:
+    last = close(far[0], [last])
+    ready[mine], sums[mine] = later_steps(kept[mine], come[mine], [last])
+    last = ready[mine]
+    for u in far[1:] + [mine]:
         last = close(u, [last])
     return order(place, [(j, *shares[j]) for u in far + near + [mine] for j in u]).reshape(rows, peers, -1)
 

time: 61.5 us -> 60.8 us (0.989)
  waiting for transfers between devices: 12.6 us -> 9.77 us
  starting transfers between devices: 26.5 us -> 29.1 us
    ppermute x14, starting transfers between devices: 11.2 us -> 14 us  [swap(): return lax.ppermute(value, 'wide', [(w, w ^ j) for w in range(peers)])]
    ppermute x10, waiting for transfers between devices: 9.97 us -> 8.17 us  [swap_line(): lax.ppermute(value, 'narrow', [(n, n ^ mask) for n in range(devices)])]
    ppermute x14, waiting for transfers between devices: 2.59 us -> 1.61 us  [swap(): return lax.ppermute(value, 'wide', [(w, w ^ j) for w in range(peers)])]
where the time goes in v7:
time: 60.8 us; the launch traced here: 60.6 us
  starting transfers between devices  29.1 us (48%)
  Pallas kernels  19.9 us (33%)
  waiting for transfers between devices  9.77 us (16%)
  local copies, waits for them, and re-layouts  0.97 us (2%)
  other arithmetic  0.72 us (1%)
    pallas_call x5, Pallas kernels, product(): pl.pallas_call(functools.partial(product_kernel, plan), out_shape=[jax.Sh...  16.9 us
    ppermute x10, starting transfers between devices, swap_line(): lax.ppermute(value, 'narrow', [(n, n ^ mask) for n in range(devices)])  15.2 us
    ppermute x14, starting transfers between devices, swap(): return lax.ppermute(value, 'wide', [(w, w ^ j) for w in range(peers)])  14 us
    ppermute x10, waiting for transfers between devices, swap_line(): lax.ppermute(value, 'narrow', [(n, n ^ mask) for n in range(devices)])  8.17 us
    ppermute x14, waiting for transfers between devices, swap(): return lax.ppermute(value, 'wide', [(w, w ^ j) for w in range(peers)])  1.61 us
  transfers between devices with their start and end apart: 24, of which 8 were waited for; matrix products, arithmetic and copies ran while one was open for 0% of the time, Pallas kernels for 30%

profile of v7, /device:TPU:0, one launch (start us, length us, event | category | flops | bytes accessed | tf_op | source)
XLA Modules:
  0.0 60.6 jit_solution(2143901560475596854)
XLA Ops:
  0.0 0.7 %pad_add_fusion.tables_from = s32[7,8]{1,0:T(8,128)S(1)} fusion(s32[1,8]{1,0:T(1,128)} %bitcast.12, s32[2,8]{1,0:T(2,128)} %bitcast.14, s32[4,8]{1,0:T(4,128)} %bitcast.13), kind=kLoop, calls=%fused_computation.2 | loop fusion | flops 112 | bytes 448 | tf_op jit(solution)/shard_map/concatenate | solution.py:46
  0.7 0.9 %copy-done = bf16[32,4,1024]{2,1,0:T(4,128)(2,1)S(1)} copy-done((bf16[32,4,1024]{2,1,0:T(4,128)(2,1)S(1)}, bf16[32,4,1024]{2,1,0:T(4,128)(2,1)}, u32[]{:S(2)}) %copy-start) | copy-done | bytes 262168
  1.7 0.8 %pick.1 = (bf16[2,32,1024]{2,1,0:T(8,128)(2,1)S(1)}, bf16[2,32,1024]{2,1,0:T(8,128)(2,1)S(1)}, bf16[2,32,1024]{2,1,0:T(8,128)(2,1)S(1)}, bf16[2,32,1024]{2,1,0:T...) custom-call(s32[7,8]{1,0:T(8,128)S(1)} %pad_add_fusion.tables_from, ...), custom_call_target="tpu_custom_call" | custom-call | tf_op jit(solution)/shard_map/pick/pallas_call | solution.py:48
  2.5 0.5 collective-permute-start
  3.0 2.6 %collective-permute-start.2 = (bf16[2,32,1024]{2,1,0:T(8,128)(2,1)S(1)}, bf16[2,32,1024]{2,1,0:T(8,128)(2,1)S(1)}, u32[]{:S(2)}, u32[]{:S(2)}) collective-permute-start(bf16[2,32,1024]{2,1,0:T(8,128)(2,1)S(1)} %get-tuple-element.32), channel_id=1, source_target_pairs={{0,8},{4,12},{8,0},{12,4},{16,24},{20,28},{24,16},{28,20},{1,9},{5... | collective-permute-start | bytes 393224 | tf_op jit(solution)/shard_map/ppermute | solution.py:274
  5.6 0.1 collective-permute-start.3
  5.7 1.8 %collective-permute-start.4 = (bf16[2,32,1024]{2,1,0:T(8,128)(2,1)S(1)}, bf16[2,32,1024]{2,1,0:T(8,128)(2,1)S(1)}, u32[]{:S(2)}, u32[]{:S(2)}) collective-permute-start(bf16[2,32,1024]{2,1,0:T(8,128)(2,1)S(1)} %get-tuple-element.34), channel_id=1, source_target_pairs={{0,16},{4,20},{8,24},{12,28},{16,0},{20,4},{24,8},{28,12},{1,17},{... | collective-permute-start | bytes 393224 | tf_op jit(solution)/shard_map/ppermute | solution.py:274
  7.4 0.0 collective-permute-start.5
  7.4 0.0 collective-permute-done.refs_1_.refs_2_
  7.4 4.7 %product.5 = (bf16[2,64,1024]{2,1,0:T(8,128)(2,1)S(1)}, bf16[2,2,1024,1024]{3,2,1,0:T(8,128)(2,1)S(1)}) custom-call(bf16[2,32,1024]{2,1,0:T(8,128)(2,1)S(1)} %get-tuple-element.29.refs_0_.refs_1_, bf16[2,32,1024]{2,1,0:T(8,128)(2,1)S(1)} %collective-permute-done.refs_1_.refs_2_, bf16[1,2,4096,1024]{3,2,1,0:T(8,128)(2,1)} %refs_6_.1), custom_call_target="tpu_custom_call" | custom-call | flops 2147483648 | bytes 8388608 | tf_op jit(solution)/shard_map/product/pallas_call | solution.py:151
  12.1 1.8 %collective-permute-start.1 = (bf16[2,64,1024]{2,1,0:T(8,128)(2,1)S(1)}, bf16[2,64,1024]{2,1,0:T(8,128)(2,1)S(1)}, u32[]{:S(2)}, u32[]{:S(2)}) collective-permute-start(bf16[2,64,1024]{2,1,0:T(8,128)(2,1)S(1)} %get-tuple-element.31.refs_0_), channel_id=1, source_target_pairs={{0,1},{1,0},{2,3},{3,2},{4,5},{5,4},{6,7},{7,6},{8,9},{9,8},{10,11... | collective-permute-start | bytes 786440 | tf_op jit(solution)/shard_map/ppermute | solution.py:277
  13.9 0.0 collective-permute-done.5.refs_4_.refs_6_
  13.9 3.5 %product.6 = (bf16[2,64,1024]{2,1,0:T(8,128)(2,1)S(1)}, bf16[2,64,1024]{2,1,0:T(8,128)(2,1)S(1)}, bf16[2,2,1024,1024]{3,2,1,0:T(8,128)(2,1)S(1)}, bf16[2,32,1024...) custom-call(bf16[2,64,1024]{2,1,0:T(8,128)(2,1)S(1)} %get-tuple-element.31.refs_0_, ...), custom_call_target="tpu_custom_call", output_to_operand_aliasing={{3}: (7, {}), {4}: (8, {})} | custom-call | flops 2147483648 | bytes 8388608 | tf_op jit(solution)/shard_map/product/pallas_call | solution.py:151
  17.4 0.0 copy-start.1
  17.5 1.6 %collective-permute-start.7 = (bf16[2,64,1024]{2,1,0:T(8,128)(2,1)S(1)}, bf16[2,64,1024]{2,1,0:T(8,128)(2,1)S(1)}, u32[]{:S(2)}, u32[]{:S(2)}) collective-permute-start(bf16[2,64,1024]{2,1,0:T(8,128)(2,1)S(1)} %get-tuple-element.43), channel_id=1, source_target_pairs={{0,1},{1,0},{2,3},{3,2},{4,5},{5,4},{6,7},{7,6},{8,9},{9,8},{10,11... | collective-permute-start | bytes 786440 | tf_op jit(solution)/shard_map/ppermute | solution.py:277
  19.1 2.4 %collective-permute-start.8 = (bf16[2,32,1024]{2,1,0:T(8,128)(2,1)S(1)}, bf16[2,32,1024]{2,1,0:T(8,128)(2,1)S(1)}, u32[]{:S(2)}, u32[]{:S(2)}) collective-permute-start(bf16[2,32,1024]{2,1,0:T(8,128)(2,1)S(1)} %get-tuple-element.45), channel_id=1, source_target_pairs={{0,24},{4,28},{8,16},{12,20},{16,8},{20,12},{24,0},{28,4},{1,25},{... | collective-permute-start | bytes 393224 | tf_op jit(solution)/shard_map/ppermute | solution.py:274
  21.5 0.0 collective-permute-start.9
  21.5 0.5 collective-permute-start.6
  22.0 3.1 %product.7 = (bf16[2,64,1024]{2,1,0:T(8,128)(2,1)S(1)}, bf16[2,64,1024]{2,1,0:T(8,128)(2,1)S(1)}, bf16[2,64,1024]{2,1,0:T(8,128)(2,1)S(1)}) custom-call(bf16[2,64,1024]{2,1,0:T(8,128)(2,1)S(1)} %collective-permute-done.1.refs_0_.refs_1_, bf16[2,32,1024]{2,1,0:T(8,128)(2,1)S(1)} %get-tuple-element.29.refs_0_.refs_1_, ...), custom_call_target="tpu_custom_call" | custom-call | flops 2147483648 | bytes 8388608 | tf_op jit(solution)/shard_map/product/pallas_call | solution.py:151
  25.2 0.7 %place.1.refs_2_.refs_8_ = bf16[256,256]{1,0:T(8,128)(2,1)S(1)} custom-call(s32[8]{0:T(128)S(1)} %copy-done.1, bf16[2,64,1024]{2,1,0:T(8,128)(2,1)S(1)} %get-tuple-element.44.after.refs_0_), custom_call_target="tpu_custom_call" | custom-call | tf_op jit(solution)/shard_map/place/pallas_call | solution.py:220
  25.9 1.1 %collective-permute-done.7.refs_1_ = bf16[2,64,1024]{2,1,0:T(8,128)(2,1)S(1)} collective-permute-done((bf16[2,64,1024]{2,1,0:T(8,128)(2,1)S(1)}, bf16[2,64,1024]{2,1,0:T(8,128)(2,1)S(1)}, u32[]{:S(2)}, u32[]{:S(2)}) %collective-permute-start.7) | collective-permute-done | bytes 262176 | tf_op jit(solution)/shard_map/ppermute | solution.py:277
  27.0 2.8 %collective-permute-start.10 = (bf16[1,64,1024]{2,1,0:T(8,128)(2,1)S(1)}, bf16[1,64,1024]{2,1,0:T(8,128)(2,1)S(1)}, u32[]{:S(2)}, u32[]{:S(2)}) collective-permute-start(bf16[1,64,1024]{2,1,0:T(8,128)(2,1)S(1)} %totals.10.refs_0_), channel_id=1, source_target_pairs={{0,2},{1,3},{2,0},{3,1},{4,6},{5,7},{6,4},{7,5},{8,10},{9,11},{10,... | collective-permute-start | bytes 393224 | tf_op jit(solution)/shard_map/ppermute | solution.py:277
  29.8 0.0 collective-permute-done.8.refs_1_.refs_2_
  29.8 2.8 %product.8 = (bf16[2,32,1024]{2,1,0:T(8,128)(2,1)S(1)}, bf16[2,32,1024]{2,1,0:T(8,128)(2,1)S(1)}) custom-call(bf16[1,64,1024]{2,1,0:T(8,128)(2,1)S(1)} %totals.10.refs_0_, bf16[2,32,1024]{2,1,0:T(8,128)(2,1)S(1)} %collective-permute-done.8.refs_1_.refs_2_, bf16[2,32,1024]{2,1,0:T(8,128)(2,1)S(1)} %collective-permute-done.9.refs_2_.refs_3_, ...), custom_call_target="tpu_custom_call" | custom-call | flops 2147483648 | bytes 8388608 | tf_op jit(solution)/shard_map/product/pallas_call | solution.py:151
  32.6 1.6 %collective-permute-start.11 = (bf16[2,32,1024]{2,1,0:T(8,128)(2,1)S(1)}, bf16[2,32,1024]{2,1,0:T(8,128)(2,1)S(1)}, u32[]{:S(2)}, u32[]{:S(2)}) collective-permute-start(bf16[2,32,1024]{2,1,0:T(8,128)(2,1)S(1)} %get-tuple-element.47.refs_2_), channel_id=1, source_target_pairs={{0,1},{1,0},{2,3},{3,2},{4,5},{5,4},{6,7},{7,6},{8,9},{9,8},{10,11... | collective-permute-start | bytes 393224 | tf_op jit(solution)/shard_map/ppermute | solution.py:277
  34.2 1.1 %collective-permute-done.6.refs_1_ = bf16[2,64,1024]{2,1,0:T(8,128)(2,1)S(1)} collective-permute-done((bf16[2,64,1024]{2,1,0:T(8,128)(2,1)S(1)}, bf16[2,64,1024]{2,1,0:T(8,128)(2,1)S(1)}, u32[]{:S(2)}, u32[]{:S(2)}) %collective-permute-start.6) | collective-permute-done | bytes 262176 | tf_op jit(solution)/shard_map/ppermute | solution.py:277
  35.4 1.1 %collective-permute-start.13 = (bf16[1,64,1024]{2,1,0:T(8,128)(2,1)S(1)}, bf16[1,64,1024]{2,1,0:T(8,128)(2,1)S(1)}, u32[]{:S(2)}, u32[]{:S(2)}) collective-permute-start(bf16[1,64,1024]{2,1,0:T(8,128)(2,1)S(1)} %totals.11.refs_0_), channel_id=1, source_target_pairs={{0,2},{1,3},{2,0},{3,1},{4,6},{5,7},{6,4},{7,5},{8,10},{9,11},{10,... | collective-permute-start | bytes 393224 | tf_op jit(solution)/shard_map/ppermute | solution.py:277
  36.5 2.4 %collective-permute-start.14 = (bf16[2,32,1024]{2,1,0:T(8,128)(2,1)S(1)}, bf16[2,32,1024]{2,1,0:T(8,128)(2,1)S(1)}, u32[]{:S(2)}, u32[]{:S(2)}) collective-permute-start(bf16[2,32,1024]{2,1,0:T(8,128)(2,1)S(1)} %get-tuple-element.50), channel_id=1, source_target_pairs={{0,1},{1,0},{2,3},{3,2},{4,5},{5,4},{6,7},{7,6},{8,9},{9,8},{10,11... | collective-permute-start | bytes 393224 | tf_op jit(solution)/shard_map/ppermute | solution.py:277
  38.9 2.8 %product.9 = (bf16[2,32,1024]{2,1,0:T(8,128)(2,1)S(1)}, bf16[2,32,1024]{2,1,0:T(8,128)(2,1)S(1)}) custom-call(bf16[1,64,1024]{2,1,0:T(8,128)(2,1)S(1)} %totals.11.refs_0_, bf16[1,64,1024]{2,1,0:T(8,128)(2,1)S(1)} %collective-permute-done.10.refs_1_.refs_2_, bf16[2,32,1024]{2,1,0:T(8,128)(2,1)S(1)} %collective-permute-done.8.refs_1_.refs_2_, ...), custom_call_target="tpu_custom_call" | custom-call | flops 2147483648 | bytes 8388608 | tf_op jit(solution)/shard_map/product/pallas_call | solution.py:151
  41.8 0.1 totals.12.refs_2_
  41.8 1.5 %collective-permute-start.15 = (bf16[2,32,1024]{2,1,0:T(8,128)(2,1)S(1)}, bf16[2,32,1024]{2,1,0:T(8,128)(2,1)S(1)}, u32[]{:S(2)}, u32[]{:S(2)}) collective-permute-start(bf16[2,32,1024]{2,1,0:T(8,128)(2,1)S(1)} %bitcast.10), channel_id=1, source_target_pairs={{0,8},{4,12},{8,0},{12,4},{16,24},{20,28},{24,16},{28,20},{1,9},{5... | collective-permute-start | bytes 393224 | tf_op jit(solution)/shard_map/ppermute | solution.py:274
  43.4 0.1 collective-permute-start.12
  43.6 3.1 %collective-permute-start.17 = (bf16[1,32,1024]{2,1,0:T(8,128)(2,1)S(1)}, bf16[1,32,1024]{2,1,0:T(8,128)(2,1)S(1)}, u32[]{:S(2)}, u32[]{:S(2)}) collective-permute-start(bf16[1,32,1024]{2,1,0:T(8,128)(2,1)S(1)} %totals.14.refs_3_), channel_id=1, source_target_pairs={{0,2},{1,3},{2,0},{3,1},{4,6},{5,7},{6,4},{7,5},{8,10},{9,11},{10,... | collective-permute-start | bytes 196616 | tf_op jit(solution)/shard_map/ppermute | solution.py:277
  46.6 0.2 collective-permute-done.15.refs_4_.refs_2_
  46.9 0.1 totals.15.refs_3_
  46.9 3.3 %collective-permute-done.12.refs_2_ = bf16[1,32,1024]{2,1,0:T(8,128)(2,1)S(1)} collective-permute-done((bf16[1,32,1024]{2,1,0:T(8,128)(2,1)S(1)}, bf16[1,32,1024]{2,1,0:T(8,128)(2,1)S(1)}, u32[]{:S(2)}, u32[]{:S(2)}) %collective-permute-start.12) | collective-permute-done | bytes 65568 | tf_op jit(solution)/shard_map/ppermute | solution.py:277
  50.2 1.5 %collective-permute-start.16 = (bf16[1,32,1024]{2,1,0:T(8,128)(2,1)S(1)}, bf16[1,32,1024]{2,1,0:T(8,128)(2,1)S(1)}, u32[]{:S(2)}, u32[]{:S(2)}) collective-permute-start(bf16[1,32,1024]{2,1,0:T(8,128)(2,1)S(1)} %totals.16.refs_2_), channel_id=1, source_target_pairs={{0,24},{4,28},{8,16},{12,20},{16,8},{20,12},{24,0},{28,4},{1,25},{... | collective-permute-start | bytes 196616 | tf_op jit(solution)/shard_map/ppermute | solution.py:274
  51.8 0.1 collective-permute-start.22
  51.9 0.6 collective-permute-start.20
  52.5 2.6 %collective-permute-start.18 = (bf16[1,32,1024]{2,1,0:T(8,128)(2,1)S(1)}, bf16[1,32,1024]{2,1,0:T(8,128)(2,1)S(1)}, u32[]{:S(2)}, u32[]{:S(2)}) collective-permute-start(bf16[1,32,1024]{2,1,0:T(8,128)(2,1)S(1)} %totals.18.refs_3_), channel_id=1, source_target_pairs={{0,28},{4,24},{8,20},{12,16},{16,12},{20,8},{24,4},{28,0},{1,29},{... | collective-permute-start | bytes 196616 | tf_op jit(solution)/shard_map/ppermute | solution.py:274
  55.2 2.7 %collective-permute-done.22.refs_2_ = bf16[1,64,1024]{2,1,0:T(8,128)(2,1)S(1)} collective-permute-done((bf16[1,64,1024]{2,1,0:T(8,128)(2,1)S(1)}, bf16[1,64,1024]{2,1,0:T(8,128)(2,1)S(1)}, u32[]{:S(2)}, u32[]{:S(2)}) %collective-permute-start.22) | collective-permute-done | bytes 131104 | tf_op jit(solution)/shard_map/ppermute | solution.py:277
  57.8 0.1 totals.19
  57.9 0.1 collective-permute-start.23
  58.0 0.3 collective-permute-done.20.refs_4_
  58.3 0.2 collective-permute-start.21
  58.6 0.7 %collective-permute-done.23.refs_7_ = bf16[32,1024]{1,0:T(8,128)(2,1)S(1)} collective-permute-done((bf16[32,1024]{1,0:T(8,128)(2,1)S(1)}, bf16[32,1024]{1,0:T(8,128)(2,1)S(1)}, u32[]{:S(2)}, u32[]{:S(2)}) %collective-permute-start.23) | collective-permute-done | bytes 65568 | tf_op jit(solution)/shard_map/ppermute | solution.py:274
  59.2 0.4 collective-permute-done.21.refs_5_
  59.6 1.0 %order.1 = bf16[256,1024]{1,0:T(8,128)(2,1)} custom-call(bf16[1,32,1024]{2,1,0:T(8,128)(2,1)S(1)} %collective-permute-done.16.refs_0_, bf16[1,32,1024]{2,1,0:T(8,128)(2,1)S(1)} %collective-permute-done.18.refs_1_, bf16[2,32,1024]{2,1,0:T(8,128)(2,1)S(1)} %collective-permute-done.15.refs_4_.refs_2_, bf16[32,1024]{1,0:T(8,128)(2,1)S(1)} %collective-permute-done.19.refs_3_, ...), custom_call_target="tpu_custom_call" | custom-call | tf_op jit(solution)/shard_map/order/pallas_call | solution.py:250
  (25 shorter events, 0.2 us)
Async XLA Ops:
  0.7 0.9 %copy-start = (bf16[32,4,1024]{2,1,0:T(4,128)(2,1)S(1)}, bf16[32,4,1024]{2,1,0:T(4,128)(2,1)}, u32[]{:S(2)}) copy-start(bf16[32,4,1024]{2,1,0:T(4,128)(2,1)} %amps.1) | copy-start | bytes 786436
  2.5 4.9 %collective-permute-start = (bf16[2,32,1024]{2,1,0:T(8,128)(2,1)S(1)}, bf16[2,32,1024]{2,1,0:T(8,128)(2,1)S(1)}, u32[]{:S(2)}, u32[]{:S(2)}) collective-permute-start(bf16[2,32,1024]{2,1,0:T(8,128)(2,1)S(1)} %get-tuple-element.30), channel_id=1, source_target_pairs={{0,4},{4,0},{8,12},{12,8},{16,20},{20,16},{24,28},{28,24},{1,5},{5... | collective-permute-start | bytes 393224 | tf_op jit(solution)/shard_map/ppermute | solution.py:274
  3.0 10.9 %collective-permute-start.2 = (bf16[2,32,1024]{2,1,0:T(8,128)(2,1)S(1)}, bf16[2,32,1024]{2,1,0:T(8,128)(2,1)S(1)}, u32[]{:S(2)}, u32[]{:S(2)}) collective-permute-start(bf16[2,32,1024]{2,1,0:T(8,128)(2,1)S(1)} %get-tuple-element.32), channel_id=1, source_target_pairs={{0,8},{4,12},{8,0},{12,4},{16,24},{20,28},{24,16},{28,20},{1,9},{5... | collective-permute-start | bytes 393224 | tf_op jit(solution)/shard_map/ppermute | solution.py:274
  5.6 8.3 %collective-permute-start.3 = (bf16[2,32,1024]{2,1,0:T(8,128)(2,1)S(1)}, bf16[2,32,1024]{2,1,0:T(8,128)(2,1)S(1)}, u32[]{:S(2)}, u32[]{:S(2)}) collective-permute-start(bf16[2,32,1024]{2,1,0:T(8,128)(2,1)S(1)} %get-tuple-element.33), channel_id=1, source_target_pairs={{0,12},{4,8},{8,4},{12,0},{16,28},{20,24},{24,20},{28,16},{1,13},{... | collective-permute-start | bytes 393224 | tf_op jit(solution)/shard_map/ppermute | solution.py:274
  5.7 8.3 %collective-permute-start.4 = (bf16[2,32,1024]{2,1,0:T(8,128)(2,1)S(1)}, bf16[2,32,1024]{2,1,0:T(8,128)(2,1)S(1)}, u32[]{:S(2)}, u32[]{:S(2)}) collective-permute-start(bf16[2,32,1024]{2,1,0:T(8,128)(2,1)S(1)} %get-tuple-element.34), channel_id=1, source_target_pairs={{0,16},{4,20},{8,24},{12,28},{16,0},{20,4},{24,8},{28,12},{1,17},{... | collective-permute-start | bytes 393224 | tf_op jit(solution)/shard_map/ppermute | solution.py:274
  7.4 6.5 %collective-permute-start.5 = (bf16[2,32,1024]{2,1,0:T(8,128)(2,1)S(1)}, bf16[2,32,1024]{2,1,0:T(8,128)(2,1)S(1)}, u32[]{:S(2)}, u32[]{:S(2)}) collective-permute-start(bf16[2,32,1024]{2,1,0:T(8,128)(2,1)S(1)} %get-tuple-element.35), channel_id=1, source_target_pairs={{0,20},{4,16},{8,28},{12,24},{16,4},{20,0},{24,12},{28,8},{1,21},{... | collective-permute-start | bytes 393224 | tf_op jit(solution)/shard_map/ppermute | solution.py:274
  12.1 9.9 %collective-permute-start.1 = (bf16[2,64,1024]{2,1,0:T(8,128)(2,1)S(1)}, bf16[2,64,1024]{2,1,0:T(8,128)(2,1)S(1)}, u32[]{:S(2)}, u32[]{:S(2)}) collective-permute-start(bf16[2,64,1024]{2,1,0:T(8,128)(2,1)S(1)} %get-tuple-element.31.refs_0_), channel_id=1, source_target_pairs={{0,1},{1,0},{2,3},{3,2},{4,5},{5,4},{6,7},{7,6},{8,9},{9,8},{10,11... | collective-permute-start | bytes 786440 | tf_op jit(solution)/shard_map/ppermute | solution.py:277
  17.4 7.7 %copy-start.1 = (s32[8]{0:T(128)S(1)}, s32[8]{0:T(128)}, u32[]{:S(2)}) copy-start(s32[8]{0:T(128)} %q_owner.1) | copy-start | bytes 100
  17.5 9.5 %collective-permute-start.7 = (bf16[2,64,1024]{2,1,0:T(8,128)(2,1)S(1)}, bf16[2,64,1024]{2,1,0:T(8,128)(2,1)S(1)}, u32[]{:S(2)}, u32[]{:S(2)}) collective-permute-start(bf16[2,64,1024]{2,1,0:T(8,128)(2,1)S(1)} %get-tuple-element.43), channel_id=1, source_target_pairs={{0,1},{1,0},{2,3},{3,2},{4,5},{5,4},{6,7},{7,6},{8,9},{9,8},{10,11... | collective-permute-start | bytes 786440 | tf_op jit(solution)/shard_map/ppermute | solution.py:277
  19.1 10.7 %collective-permute-start.8 = (bf16[2,32,1024]{2,1,0:T(8,128)(2,1)S(1)}, bf16[2,32,1024]{2,1,0:T(8,128)(2,1)S(1)}, u32[]{:S(2)}, u32[]{:S(2)}) collective-permute-start(bf16[2,32,1024]{2,1,0:T(8,128)(2,1)S(1)} %get-tuple-element.45), channel_id=1, source_target_pairs={{0,24},{4,28},{8,16},{12,20},{16,8},{20,12},{24,0},{28,4},{1,25},{... | collective-permute-start | bytes 393224 | tf_op jit(solution)/shard_map/ppermute | solution.py:274
  21.5 8.2 %collective-permute-start.9 = (bf16[2,32,1024]{2,1,0:T(8,128)(2,1)S(1)}, bf16[2,32,1024]{2,1,0:T(8,128)(2,1)S(1)}, u32[]{:S(2)}, u32[]{:S(2)}) collective-permute-start(bf16[2,32,1024]{2,1,0:T(8,128)(2,1)S(1)} %get-tuple-element.46), channel_id=1, source_target_pairs={{0,28},{4,24},{8,20},{12,16},{16,12},{20,8},{24,4},{28,0},{1,29},{... | collective-permute-start | bytes 393224 | tf_op jit(solution)/shard_map/ppermute | solution.py:274
  21.5 13.8 %collective-permute-start.6 = (bf16[2,64,1024]{2,1,0:T(8,128)(2,1)S(1)}, bf16[2,64,1024]{2,1,0:T(8,128)(2,1)S(1)}, u32[]{:S(2)}, u32[]{:S(2)}) collective-permute-start(bf16[2,64,1024]{2,1,0:T(8,128)(2,1)S(1)} %get-tuple-element.41), channel_id=1, source_target_pairs={{0,1},{1,0},{2,3},{3,2},{4,5},{5,4},{6,7},{7,6},{8,9},{9,8},{10,11... | collective-permute-start | bytes 786440 | tf_op jit(solution)/shard_map/ppermute | solution.py:277
  27.0 12.0 %collective-permute-start.10 = (bf16[1,64,1024]{2,1,0:T(8,128)(2,1)S(1)}, bf16[1,64,1024]{2,1,0:T(8,128)(2,1)S(1)}, u32[]{:S(2)}, u32[]{:S(2)}) collective-permute-start(bf16[1,64,1024]{2,1,0:T(8,128)(2,1)S(1)} %totals.10.refs_0_), channel_id=1, source_target_pairs={{0,2},{1,3},{2,0},{3,1},{4,6},{5,7},{6,4},{7,5},{8,10},{9,11},{10,... | collective-permute-start | bytes 393224 | tf_op jit(solution)/shard_map/ppermute | solution.py:277
  32.6 10.8 %collective-permute-start.11 = (bf16[2,32,1024]{2,1,0:T(8,128)(2,1)S(1)}, bf16[2,32,1024]{2,1,0:T(8,128)(2,1)S(1)}, u32[]{:S(2)}, u32[]{:S(2)}) collective-permute-start(bf16[2,32,1024]{2,1,0:T(8,128)(2,1)S(1)} %get-tuple-element.47.refs_2_), channel_id=1, source_target_pairs={{0,1},{1,0},{2,3},{3,2},{4,5},{5,4},{6,7},{7,6},{8,9},{9,8},{10,11... | collective-permute-start | bytes 393224 | tf_op jit(solution)/shard_map/ppermute | solution.py:277
  35.4 11.3 %collective-permute-start.13 = (bf16[1,64,1024]{2,1,0:T(8,128)(2,1)S(1)}, bf16[1,64,1024]{2,1,0:T(8,128)(2,1)S(1)}, u32[]{:S(2)}, u32[]{:S(2)}) collective-permute-start(bf16[1,64,1024]{2,1,0:T(8,128)(2,1)S(1)} %totals.11.refs_0_), channel_id=1, source_target_pairs={{0,2},{1,3},{2,0},{3,1},{4,6},{5,7},{6,4},{7,5},{8,10},{9,11},{10,... | collective-permute-start | bytes 393224 | tf_op jit(solution)/shard_map/ppermute | solution.py:277
  36.5 7.0 %collective-permute-start.14 = (bf16[2,32,1024]{2,1,0:T(8,128)(2,1)S(1)}, bf16[2,32,1024]{2,1,0:T(8,128)(2,1)S(1)}, u32[]{:S(2)}, u32[]{:S(2)}) collective-permute-start(bf16[2,32,1024]{2,1,0:T(8,128)(2,1)S(1)} %get-tuple-element.50), channel_id=1, source_target_pairs={{0,1},{1,0},{2,3},{3,2},{4,5},{5,4},{6,7},{7,6},{8,9},{9,8},{10,11... | collective-permute-start | bytes 393224 | tf_op jit(solution)/shard_map/ppermute | solution.py:277
  41.8 5.0 %collective-permute-start.15 = (bf16[2,32,1024]{2,1,0:T(8,128)(2,1)S(1)}, bf16[2,32,1024]{2,1,0:T(8,128)(2,1)S(1)}, u32[]{:S(2)}, u32[]{:S(2)}) collective-permute-start(bf16[2,32,1024]{2,1,0:T(8,128)(2,1)S(1)} %bitcast.10), channel_id=1, source_target_pairs={{0,8},{4,12},{8,0},{12,4},{16,24},{20,28},{24,16},{28,20},{1,9},{5... | collective-permute-start | bytes 393224 | tf_op jit(solution)/shard_map/ppermute | solution.py:274
  43.4 6.8 %collective-permute-start.12 = (bf16[1,32,1024]{2,1,0:T(8,128)(2,1)S(1)}, bf16[1,32,1024]{2,1,0:T(8,128)(2,1)S(1)}, u32[]{:S(2)}, u32[]{:S(2)}) collective-permute-start(bf16[1,32,1024]{2,1,0:T(8,128)(2,1)S(1)} %totals.13.refs_2_), channel_id=1, source_target_pairs={{0,2},{1,3},{2,0},{3,1},{4,6},{5,7},{6,4},{7,5},{8,10},{9,11},{10,... | collective-permute-start | bytes 196616 | tf_op jit(solution)/shard_map/ppermute | solution.py:277
  43.6 8.9 %collective-permute-start.17 = (bf16[1,32,1024]{2,1,0:T(8,128)(2,1)S(1)}, bf16[1,32,1024]{2,1,0:T(8,128)(2,1)S(1)}, u32[]{:S(2)}, u32[]{:S(2)}) collective-permute-start(bf16[1,32,1024]{2,1,0:T(8,128)(2,1)S(1)} %totals.14.refs_3_), channel_id=1, source_target_pairs={{0,2},{1,3},{2,0},{3,1},{4,6},{5,7},{6,4},{7,5},{8,10},{9,11},{10,... | collective-permute-start | bytes 196616 | tf_op jit(solution)/shard_map/ppermute | solution.py:277
  50.2 8.3 %collective-permute-start.16 = (bf16[1,32,1024]{2,1,0:T(8,128)(2,1)S(1)}, bf16[1,32,1024]{2,1,0:T(8,128)(2,1)S(1)}, u32[]{:S(2)}, u32[]{:S(2)}) collective-permute-start(bf16[1,32,1024]{2,1,0:T(8,128)(2,1)S(1)} %totals.16.refs_2_), channel_id=1, source_target_pairs={{0,24},{4,28},{8,16},{12,20},{16,8},{20,12},{24,0},{28,4},{1,25},{... | collective-permute-start | bytes 196616 | tf_op jit(solution)/shard_map/ppermute | solution.py:274
  51.8 6.0 %collective-permute-start.22 = (bf16[1,64,1024]{2,1,0:T(8,128)(2,1)S(1)}, bf16[1,64,1024]{2,1,0:T(8,128)(2,1)S(1)}, u32[]{:S(2)}, u32[]{:S(2)}) collective-permute-start(bf16[1,64,1024]{2,1,0:T(8,128)(2,1)S(1)} %totals.17.refs_3_), channel_id=1, source_target_pairs={{0,2},{1,3},{2,0},{3,1},{4,6},{5,7},{6,4},{7,5},{8,10},{9,11},{10,... | collective-permute-start | bytes 393224 | tf_op jit(solution)/shard_map/ppermute | solution.py:277
  51.9 6.4 %collective-permute-start.20 = (bf16[2,32,1024]{2,1,0:T(8,128)(2,1)S(1)}, bf16[2,32,1024]{2,1,0:T(8,128)(2,1)S(1)}, u32[]{:S(2)}, u32[]{:S(2)}) collective-permute-start(bf16[2,32,1024]{2,1,0:T(8,128)(2,1)S(1)} %bitcast.11), channel_id=1, source_target_pairs={{0,16},{4,20},{8,24},{12,28},{16,0},{20,4},{24,8},{28,12},{1,17},{... | collective-permute-start | bytes 393224 | tf_op jit(solution)/shard_map/ppermute | solution.py:274
  52.5 6.1 %collective-permute-start.19 = (bf16[32,1024]{1,0:T(8,128)(2,1)S(1)}, bf16[32,1024]{1,0:T(8,128)(2,1)S(1)}, u32[]{:S(2)}, u32[]{:S(2)}) collective-permute-start(bf16[32,1024]{1,0:T(8,128)(2,1)S(1)} %slice_bitcast_fusion.1), channel_id=1, source_target_pairs={{0,4},{4,0},{8,12},{12,8},{16,20},{20,16},{24,28},{28,24},{1,5},{5... | collective-permute-start | bytes 196616 | tf_op jit(solution)/shard_map/ppermute | solution.py:274
  52.5 6.0 %collective-permute-start.18 = (bf16[1,32,1024]{2,1,0:T(8,128)(2,1)S(1)}, bf16[1,32,1024]{2,1,0:T(8,128)(2,1)S(1)}, u32[]{:S(2)}, u32[]{:S(2)}) collective-permute-start(bf16[1,32,1024]{2,1,0:T(8,128)(2,1)S(1)} %totals.18.refs_3_), channel_id=1, source_target_pairs={{0,28},{4,24},{8,20},{12,16},{16,12},{20,8},{24,4},{28,0},{1,29},{... | collective-permute-start | bytes 196616 | tf_op jit(solution)/shard_map/ppermute | solution.py:274
  57.9 1.3 %collective-permute-start.23 = (bf16[32,1024]{1,0:T(8,128)(2,1)S(1)}, bf16[32,1024]{1,0:T(8,128)(2,1)S(1)}, u32[]{:S(2)}, u32[]{:S(2)}) collective-permute-start(bf16[32,1024]{1,0:T(8,128)(2,1)S(1)} %get-tuple-element.52), channel_id=1, source_target_pairs={{0,4},{4,0},{8,12},{12,8},{16,20},{20,16},{24,28},{28,24},{1,5},{5... | collective-permute-start | bytes 196616 | tf_op jit(solution)/shard_map/ppermute | solution.py:274
  58.3 1.3 %collective-permute-start.21 = (bf16[32,1024]{1,0:T(8,128)(2,1)S(1)}, bf16[32,1024]{1,0:T(8,128)(2,1)S(1)}, u32[]{:S(2)}, u32[]{:S(2)}) collective-permute-start(bf16[32,1024]{1,0:T(8,128)(2,1)S(1)} %slice_bitcast_fusion), channel_id=1, source_target_pairs={{0,4},{4,0},{8,12},{12,8},{16,20},{20,16},{24,28},{28,24},{1,5},{5... | collective-permute-start | bytes 196616 | tf_op jit(solution)/shard_map/ppermute | solution.py:274

commit v8 on v7

--- a/solution.py
+++ b/solution.py
@@ -325,12 +325,12 @@
     outs, _ = multiply(far, all_odd, odd_ints, after=[ready[first]])
     away.update(outs)
     come.update((u, first_step(away[u])) for u in far)
-    last = away[far[0]]
+    outs, _ = multiply(far, all_even, even_ints, after=[away[far[0]]])
+    kept.update(outs)
+    last = kept[far[0]]
     for u in others:
-        ready[u], sums[u] = later_steps(kept[u], come[u], [last])
+        ready[u], sums[u] = later_steps(kept[u], come[u], [last, sums[first][-1][0]])
         last = ready[u]
-    outs, _ = multiply(far, all_even, even_ints, after=[last, sums[first][-1][0]])
-    kept.update(outs)
 
     shares = {}
 
@@ -348,16 +348,16 @@
             shares[j + 1] = swap(got[1], 1), None
         return whole
 
-    last = close(first, [kept[far[0]]])
-    for u in far:
+    last = close(first, [last])
+    for u in far[::-1]:
         ready[u], sums[u] = later_steps(kept[u], come[u], [last])
         last = ready[u]
     for u in others:
         last = close(u, [last, shares[first[0]][0]])
-    last = close(far[0], [last])
+    last = close(far[-1], [last])
     ready[mine], sums[mine] = later_steps(kept[mine], come[mine], [last])
     last = ready[mine]
-    for u in far[1:] + [mine]:
+    for u in far[:-1] + [mine]:
         last = close(u, [last])
     return order(place, [(j, *shares[j]) for u in far + near + [mine] for j in u]).reshape(rows, peers, -1)
 

time: 60.8 us -> 63.3 us (1.041)
  waiting for transfers between devices: 9.77 us -> 13.8 us
  starting transfers between devices: 29.1 us -> 27.6 us
    ppermute x10, waiting for transfers between devices: 8.17 us -> 12.8 us  [swap_line(): lax.ppermute(value, 'narrow', [(n, n ^ mask) for n in range(devices)])]
    ppermute x10, starting transfers between devices: 15.2 us -> 13.6 us  [swap_line(): lax.ppermute(value, 'narrow', [(n, n ^ mask) for n in range(devices)])]
    ppermute x14, waiting for transfers between devices: 1.61 us -> 0.92 us  [swap(): return lax.ppermute(value, 'wide', [(w, w ^ j) for w in range(peers)])]
  transfers between devices with their start and end apart: 24 -> 24, of which waited for: 8 -> 6; matrix products, arithmetic and copies ran while one was open for 0% -> 0% of each run, Pallas kernels for 30% -> 29%
where the time goes in v8:
time: 63.3 us; the launch traced here: 63.1 us
  starting transfers between devices  27.6 us (44%)
  Pallas kernels  19.9 us (31%)
  waiting for transfers between devices  13.8 us (22%)
  local copies, waits for them, and re-layouts  0.97 us (2%)
  other arithmetic  0.72 us (1%)
    pallas_call x5, Pallas kernels, product(): pl.pallas_call(functools.partial(product_kernel, plan), out_shape=[jax.Sh...  17 us
    ppermute x14, starting transfers between devices, swap(): return lax.ppermute(value, 'wide', [(w, w ^ j) for w in range(peers)])  14 us
    ppermute x10, starting transfers between devices, swap_line(): lax.ppermute(value, 'narrow', [(n, n ^ mask) for n in range(devices)])  13.6 us
    ppermute x10, waiting for transfers between devices, swap_line(): lax.ppermute(value, 'narrow', [(n, n ^ mask) for n in range(devices)])  12.8 us
  transfers between devices with their start and end apart: 24, of which 6 were waited for; matrix products, arithmetic and copies ran while one was open for 0% of the time, Pallas kernels for 29%

profile of v8, /device:TPU:0, one launch (start us, length us, event | category | flops | bytes accessed | tf_op | source)
XLA Modules:
  0.0 63.1 jit_solution(18335647191753959791)
XLA Ops:
  0.0 0.7 %pad_add_fusion.tables_from = s32[7,8]{1,0:T(8,128)S(1)} fusion(s32[1,8]{1,0:T(1,128)} %bitcast.12, s32[2,8]{1,0:T(2,128)} %bitcast.14, s32[4,8]{1,0:T(4,128)} %bitcast.13), kind=kLoop, calls=%fused_computation.2 | loop fusion | flops 112 | bytes 448 | tf_op jit(solution)/shard_map/concatenate | solution.py:46
  0.7 0.9 %copy-done = bf16[32,4,1024]{2,1,0:T(4,128)(2,1)S(1)} copy-done((bf16[32,4,1024]{2,1,0:T(4,128)(2,1)S(1)}, bf16[32,4,1024]{2,1,0:T(4,128)(2,1)}, u32[]{:S(2)}) %copy-start) | copy-done | bytes 262168
  1.7 0.8 %pick.1 = (bf16[2,32,1024]{2,1,0:T(8,128)(2,1)S(1)}, bf16[2,32,1024]{2,1,0:T(8,128)(2,1)S(1)}, bf16[2,32,1024]{2,1,0:T(8,128)(2,1)S(1)}, bf16[2,32,1024]{2,1,0:T...) custom-call(s32[7,8]{1,0:T(8,128)S(1)} %pad_add_fusion.tables_from, ...), custom_call_target="tpu_custom_call" | custom-call | tf_op jit(solution)/shard_map/pick/pallas_call | solution.py:48
  2.5 0.5 collective-permute-start
  3.0 2.6 %collective-permute-start.2 = (bf16[2,32,1024]{2,1,0:T(8,128)(2,1)S(1)}, bf16[2,32,1024]{2,1,0:T(8,128)(2,1)S(1)}, u32[]{:S(2)}, u32[]{:S(2)}) collective-permute-start(bf16[2,32,1024]{2,1,0:T(8,128)(2,1)S(1)} %get-tuple-element.32), channel_id=1, source_target_pairs={{0,8},{4,12},{8,0},{12,4},{16,24},{20,28},{24,16},{28,20},{1,9},{5... | collective-permute-start | bytes 393224 | tf_op jit(solution)/shard_map/ppermute | solution.py:274
  5.6 0.1 collective-permute-start.3
  5.7 1.8 %collective-permute-start.4 = (bf16[2,32,1024]{2,1,0:T(8,128)(2,1)S(1)}, bf16[2,32,1024]{2,1,0:T(8,128)(2,1)S(1)}, u32[]{:S(2)}, u32[]{:S(2)}) collective-permute-start(bf16[2,32,1024]{2,1,0:T(8,128)(2,1)S(1)} %get-tuple-element.34), channel_id=1, source_target_pairs={{0,16},{4,20},{8,24},{12,28},{16,0},{20,4},{24,8},{28,12},{1,17},{... | collective-permute-start | bytes 393224 | tf_op jit(solution)/shard_map/ppermute | solution.py:274
  7.4 0.0 collective-permute-start.5
  7.4 4.7 %product.5 = (bf16[2,64,1024]{2,1,0:T(8,128)(2,1)S(1)}, bf16[2,2,1024,1024]{3,2,1,0:T(8,128)(2,1)S(1)}) custom-call(bf16[2,32,1024]{2,1,0:T(8,128)(2,1)S(1)} %get-tuple-element.29.refs_0_.refs_1_, bf16[2,32,1024]{2,1,0:T(8,128)(2,1)S(1)} %collective-permute-done.refs_1_.refs_2_, bf16[1,2,4096,1024]{3,2,1,0:T(8,128)(2,1)} %refs_6_.1), custom_call_target="tpu_custom_call" | custom-call | flops 2147483648 | bytes 8388608 | tf_op jit(solution)/shard_map/product/pallas_call | solution.py:151
  12.1 1.8 %collective-permute-start.1 = (bf16[2,64,1024]{2,1,0:T(8,128)(2,1)S(1)}, bf16[2,64,1024]{2,1,0:T(8,128)(2,1)S(1)}, u32[]{:S(2)}, u32[]{:S(2)}) collective-permute-start(bf16[2,64,1024]{2,1,0:T(8,128)(2,1)S(1)} %get-tuple-element.31.refs_0_), channel_id=1, source_target_pairs={{0,1},{1,0},{2,3},{3,2},{4,5},{5,4},{6,7},{7,6},{8,9},{9,8},{10,11... | collective-permute-start | bytes 786440 | tf_op jit(solution)/shard_map/ppermute | solution.py:277
  13.9 0.0 collective-permute-done.4.refs_3_.refs_5_
  13.9 0.0 collective-permute-done.5.refs_4_.refs_6_
  13.9 3.5 %product.6 = (bf16[2,64,1024]{2,1,0:T(8,128)(2,1)S(1)}, bf16[2,64,1024]{2,1,0:T(8,128)(2,1)S(1)}, bf16[2,2,1024,1024]{3,2,1,0:T(8,128)(2,1)S(1)}, bf16[2,32,1024...) custom-call(bf16[2,64,1024]{2,1,0:T(8,128)(2,1)S(1)} %get-tuple-element.31.refs_0_, ...), custom_call_target="tpu_custom_call", output_to_operand_aliasing={{3}: (7, {}), {4}: (8, {})} | custom-call | flops 2147483648 | bytes 8388608 | tf_op jit(solution)/shard_map/product/pallas_call | solution.py:151
  17.4 0.0 copy-start.1
  17.5 1.6 %collective-permute-start.6 = (bf16[2,64,1024]{2,1,0:T(8,128)(2,1)S(1)}, bf16[2,64,1024]{2,1,0:T(8,128)(2,1)S(1)}, u32[]{:S(2)}, u32[]{:S(2)}) collective-permute-start(bf16[2,64,1024]{2,1,0:T(8,128)(2,1)S(1)} %get-tuple-element.41), channel_id=1, source_target_pairs={{0,1},{1,0},{2,3},{3,2},{4,5},{5,4},{6,7},{7,6},{8,9},{9,8},{10,11... | collective-permute-start | bytes 786440 | tf_op jit(solution)/shard_map/ppermute | solution.py:277
  19.1 2.4 %collective-permute-start.7 = (bf16[2,32,1024]{2,1,0:T(8,128)(2,1)S(1)}, bf16[2,32,1024]{2,1,0:T(8,128)(2,1)S(1)}, u32[]{:S(2)}, u32[]{:S(2)}) collective-permute-start(bf16[2,32,1024]{2,1,0:T(8,128)(2,1)S(1)} %get-tuple-element.43), channel_id=1, source_target_pairs={{0,24},{4,28},{8,16},{12,20},{16,8},{20,12},{24,0},{28,4},{1,25},{... | collective-permute-start | bytes 393224 | tf_op jit(solution)/shard_map/ppermute | solution.py:274
  21.5 0.0 collective-permute-start.8
  21.5 0.5 collective-permute-start.12
  22.0 3.1 %product.7 = (bf16[2,64,1024]{2,1,0:T(8,128)(2,1)S(1)}, bf16[2,64,1024]{2,1,0:T(8,128)(2,1)S(1)}, bf16[2,64,1024]{2,1,0:T(8,128)(2,1)S(1)}) custom-call(bf16[2,64,1024]{2,1,0:T(8,128)(2,1)S(1)} %collective-permute-done.1.refs_0_.refs_1_, bf16[2,32,1024]{2,1,0:T(8,128)(2,1)S(1)} %get-tuple-element.29.refs_0_.refs_1_, ...), custom_call_target="tpu_custom_call" | custom-call | flops 2147483648 | bytes 8388608 | tf_op jit(solution)/shard_map/product/pallas_call | solution.py:151
  25.2 0.7 %place.1.refs_2_.refs_8_ = bf16[256,256]{1,0:T(8,128)(2,1)S(1)} custom-call(s32[8]{0:T(128)S(1)} %copy-done.1, bf16[2,64,1024]{2,1,0:T(8,128)(2,1)S(1)} %get-tuple-element.42.after.refs_0_), custom_call_target="tpu_custom_call" | custom-call | tf_op jit(solution)/shard_map/place/pallas_call | solution.py:220
  25.9 1.1 %collective-permute-done.6.refs_1_ = bf16[2,64,1024]{2,1,0:T(8,128)(2,1)S(1)} collective-permute-done((bf16[2,64,1024]{2,1,0:T(8,128)(2,1)S(1)}, bf16[2,64,1024]{2,1,0:T(8,128)(2,1)S(1)}, u32[]{:S(2)}, u32[]{:S(2)}) %collective-permute-start.6) | collective-permute-done | bytes 262176 | tf_op jit(solution)/shard_map/ppermute | solution.py:277
  27.0 2.8 %collective-permute-start.11 = (bf16[1,64,1024]{2,1,0:T(8,128)(2,1)S(1)}, bf16[1,64,1024]{2,1,0:T(8,128)(2,1)S(1)}, u32[]{:S(2)}, u32[]{:S(2)}) collective-permute-start(bf16[1,64,1024]{2,1,0:T(8,128)(2,1)S(1)} %totals.10.refs_0_), channel_id=1, source_target_pairs={{0,2},{1,3},{2,0},{3,1},{4,6},{5,7},{6,4},{7,5},{8,10},{9,11},{10,... | collective-permute-start | bytes 393224 | tf_op jit(solution)/shard_map/ppermute | solution.py:277
  29.8 0.0 collective-permute-done.7.refs_1_
  29.8 0.0 collective-permute-done.8.refs_2_
  29.8 2.8 %product.8 = (bf16[2,32,1024]{2,1,0:T(8,128)(2,1)S(1)}, bf16[2,32,1024]{2,1,0:T(8,128)(2,1)S(1)}) custom-call(bf16[1,64,1024]{2,1,0:T(8,128)(2,1)S(1)} %totals.10.refs_0_, bf16[2,32,1024]{2,1,0:T(8,128)(2,1)S(1)} %collective-permute-done.7.refs_1_, bf16[2,32,1024]{2,1,0:T(8,128)(2,1)S(1)} %collective-permute-done.8.refs_2_, ...), custom_call_target="tpu_custom_call" | custom-call | flops 2147483648 | bytes 8388608 | tf_op jit(solution)/shard_map/product/pallas_call | solution.py:151
  32.6 1.6 %collective-permute-start.10 = (bf16[2,32,1024]{2,1,0:T(8,128)(2,1)S(1)}, bf16[2,32,1024]{2,1,0:T(8,128)(2,1)S(1)}, u32[]{:S(2)}, u32[]{:S(2)}) collective-permute-start(bf16[2,32,1024]{2,1,0:T(8,128)(2,1)S(1)} %get-tuple-element.48), channel_id=1, source_target_pairs={{0,1},{1,0},{2,3},{3,2},{4,5},{5,4},{6,7},{7,6},{8,9},{9,8},{10,11... | collective-permute-start | bytes 393224 | tf_op jit(solution)/shard_map/ppermute | solution.py:277
  34.2 0.4 collective-permute-start.9
  34.7 2.8 %product.9 = (bf16[2,32,1024]{2,1,0:T(8,128)(2,1)S(1)}, bf16[2,32,1024]{2,1,0:T(8,128)(2,1)S(1)}) custom-call(bf16[2,32,1024]{2,1,0:T(8,128)(2,1)S(1)} %get-tuple-element.45.refs_0_, bf16[2,32,1024]{2,1,0:T(8,128)(2,1)S(1)} %collective-permute-done.7.refs_1_, bf16[2,32,1024]{2,1,0:T(8,128)(2,1)S(1)} %collective-permute-done.8.refs_2_, ...), custom_call_target="tpu_custom_call" | custom-call | flops 2147483648 | bytes 8388608 | tf_op jit(solution)/shard_map/product/pallas_call | solution.py:151
  37.6 0.1 totals.12.refs_2_
  37.6 1.5 %collective-permute-start.16 = (bf16[2,32,1024]{2,1,0:T(8,128)(2,1)S(1)}, bf16[2,32,1024]{2,1,0:T(8,128)(2,1)S(1)}, u32[]{:S(2)}, u32[]{:S(2)}) collective-permute-start(bf16[2,32,1024]{2,1,0:T(8,128)(2,1)S(1)} %bitcast.10), channel_id=1, source_target_pairs={{0,8},{4,12},{8,0},{12,4},{16,24},{20,28},{24,16},{28,20},{1,9},{5... | collective-permute-start | bytes 393224 | tf_op jit(solution)/shard_map/ppermute | solution.py:274
  39.2 0.5 collective-permute-start.15
  39.7 2.5 %collective-permute-start.14 = (bf16[1,32,1024]{2,1,0:T(8,128)(2,1)S(1)}, bf16[1,32,1024]{2,1,0:T(8,128)(2,1)S(1)}, u32[]{:S(2)}, u32[]{:S(2)}) collective-permute-start(bf16[1,32,1024]{2,1,0:T(8,128)(2,1)S(1)} %totals.13.refs_2_), channel_id=1, source_target_pairs={{0,2},{1,3},{2,0},{3,1},{4,6},{5,7},{6,4},{7,5},{8,10},{9,11},{10,... | collective-permute-start | bytes 196616 | tf_op jit(solution)/shard_map/ppermute | solution.py:277
  42.2 1.7 %collective-permute-start.13 = (bf16[1,32,1024]{2,1,0:T(8,128)(2,1)S(1)}, bf16[1,32,1024]{2,1,0:T(8,128)(2,1)S(1)}, u32[]{:S(2)}, u32[]{:S(2)}) collective-permute-start(bf16[1,32,1024]{2,1,0:T(8,128)(2,1)S(1)} %totals.14.refs_3_), channel_id=1, source_target_pairs={{0,2},{1,3},{2,0},{3,1},{4,6},{5,7},{6,4},{7,5},{8,10},{9,11},{10,... | collective-permute-start | bytes 196616 | tf_op jit(solution)/shard_map/ppermute | solution.py:277
  43.9 6.9 %collective-permute-done.15.refs_2_ = bf16[1,64,1024]{2,1,0:T(8,128)(2,1)S(1)} collective-permute-done((bf16[1,64,1024]{2,1,0:T(8,128)(2,1)S(1)}, bf16[1,64,1024]{2,1,0:T(8,128)(2,1)S(1)}, u32[]{:S(2)}, u32[]{:S(2)}) %collective-permute-start.15) | collective-permute-done | bytes 131104 | tf_op jit(solution)/shard_map/ppermute | solution.py:277
  50.8 0.1 totals.15.refs_3_
  50.9 0.6 %collective-permute-done.14.refs_2_ = bf16[1,32,1024]{2,1,0:T(8,128)(2,1)S(1)} collective-permute-done((bf16[1,32,1024]{2,1,0:T(8,128)(2,1)S(1)}, bf16[1,32,1024]{2,1,0:T(8,128)(2,1)S(1)}, u32[]{:S(2)}, u32[]{:S(2)}) %collective-permute-start.14) | collective-permute-done | bytes 65568 | tf_op jit(solution)/shard_map/ppermute | solution.py:277
  51.5 0.1 collective-permute-start.18
  51.7 0.1 collective-permute-start.22
  51.7 1.6 %collective-permute-start.20 = (bf16[2,32,1024]{2,1,0:T(8,128)(2,1)S(1)}, bf16[2,32,1024]{2,1,0:T(8,128)(2,1)S(1)}, u32[]{:S(2)}, u32[]{:S(2)}) collective-permute-start(bf16[2,32,1024]{2,1,0:T(8,128)(2,1)S(1)} %bitcast.11), channel_id=1, source_target_pairs={{0,16},{4,20},{8,24},{12,28},{16,0},{20,4},{24,8},{28,12},{1,17},{... | collective-permute-start | bytes 393224 | tf_op jit(solution)/shard_map/ppermute | solution.py:274
  53.3 0.7 %collective-permute-start.19 = (bf16[32,1024]{1,0:T(8,128)(2,1)S(1)}, bf16[32,1024]{1,0:T(8,128)(2,1)S(1)}, u32[]{:S(2)}, u32[]{:S(2)}) collective-permute-start(bf16[32,1024]{1,0:T(8,128)(2,1)S(1)} %slice_bitcast_fusion.1), channel_id=1, source_target_pairs={{0,4},{4,0},{8,12},{12,8},{16,20},{20,16},{24,28},{28,24},{1,5},{5... | collective-permute-start | bytes 196616 | tf_op jit(solution)/shard_map/ppermute | solution.py:274
  54.1 2.1 %collective-permute-start.17 = (bf16[1,32,1024]{2,1,0:T(8,128)(2,1)S(1)}, bf16[1,32,1024]{2,1,0:T(8,128)(2,1)S(1)}, u32[]{:S(2)}, u32[]{:S(2)}) collective-permute-start(bf16[1,32,1024]{2,1,0:T(8,128)(2,1)S(1)} %totals.18.refs_3_), channel_id=1, source_target_pairs={{0,24},{4,28},{8,16},{12,20},{16,8},{20,12},{24,0},{28,4},{1,25},{... | collective-permute-start | bytes 196616 | tf_op jit(solution)/shard_map/ppermute | solution.py:274
  56.2 4.3 %collective-permute-done.22.refs_2_ = bf16[1,64,1024]{2,1,0:T(8,128)(2,1)S(1)} collective-permute-done((bf16[1,64,1024]{2,1,0:T(8,128)(2,1)S(1)}, bf16[1,64,1024]{2,1,0:T(8,128)(2,1)S(1)}, u32[]{:S(2)}, u32[]{:S(2)}) %collective-permute-start.22) | collective-permute-done | bytes 131104 | tf_op jit(solution)/shard_map/ppermute | solution.py:277
  60.4 0.1 totals.19
  60.5 0.2 collective-permute-start.23
  60.7 0.5 collective-permute-start.21
  61.2 0.7 %collective-permute-done.23.refs_7_ = bf16[32,1024]{1,0:T(8,128)(2,1)S(1)} collective-permute-done((bf16[32,1024]{1,0:T(8,128)(2,1)S(1)}, bf16[32,1024]{1,0:T(8,128)(2,1)S(1)}, u32[]{:S(2)}, u32[]{:S(2)}) %collective-permute-start.23) | collective-permute-done | bytes 65568 | tf_op jit(solution)/shard_map/ppermute | solution.py:274
  61.8 0.2 collective-permute-done.21.refs_5_
  62.1 1.0 %order.1 = bf16[256,1024]{1,0:T(8,128)(2,1)} custom-call(bf16[1,32,1024]{2,1,0:T(8,128)(2,1)S(1)} %collective-permute-done.17.refs_0_, bf16[1,32,1024]{2,1,0:T(8,128)(2,1)S(1)} %collective-permute-done.18.refs_1_, bf16[2,32,1024]{2,1,0:T(8,128)(2,1)S(1)} %collective-permute-done.16.refs_4_.refs_2_, bf16[32,1024]{1,0:T(8,128)(2,1)S(1)} %collective-permute-done.19.refs_3_, ...), custom_call_target="tpu_custom_call" | custom-call | tf_op jit(solution)/shard_map/order/pallas_call | solution.py:250
  (25 shorter events, 0.2 us)
Async XLA Ops:
  0.7 0.9 %copy-start = (bf16[32,4,1024]{2,1,0:T(4,128)(2,1)S(1)}, bf16[32,4,1024]{2,1,0:T(4,128)(2,1)}, u32[]{:S(2)}) copy-start(bf16[32,4,1024]{2,1,0:T(4,128)(2,1)} %amps.1) | copy-start | bytes 786436
  2.5 4.9 %collective-permute-start = (bf16[2,32,1024]{2,1,0:T(8,128)(2,1)S(1)}, bf16[2,32,1024]{2,1,0:T(8,128)(2,1)S(1)}, u32[]{:S(2)}, u32[]{:S(2)}) collective-permute-start(bf16[2,32,1024]{2,1,0:T(8,128)(2,1)S(1)} %get-tuple-element.30), channel_id=1, source_target_pairs={{0,4},{4,0},{8,12},{12,8},{16,20},{20,16},{24,28},{28,24},{1,5},{5... | collective-permute-start | bytes 393224 | tf_op jit(solution)/shard_map/ppermute | solution.py:274
  3.0 10.9 %collective-permute-start.2 = (bf16[2,32,1024]{2,1,0:T(8,128)(2,1)S(1)}, bf16[2,32,1024]{2,1,0:T(8,128)(2,1)S(1)}, u32[]{:S(2)}, u32[]{:S(2)}) collective-permute-start(bf16[2,32,1024]{2,1,0:T(8,128)(2,1)S(1)} %get-tuple-element.32), channel_id=1, source_target_pairs={{0,8},{4,12},{8,0},{12,4},{16,24},{20,28},{24,16},{28,20},{1,9},{5... | collective-permute-start | bytes 393224 | tf_op jit(solution)/shard_map/ppermute | solution.py:274
  5.6 8.3 %collective-permute-start.3 = (bf16[2,32,1024]{2,1,0:T(8,128)(2,1)S(1)}, bf16[2,32,1024]{2,1,0:T(8,128)(2,1)S(1)}, u32[]{:S(2)}, u32[]{:S(2)}) collective-permute-start(bf16[2,32,1024]{2,1,0:T(8,128)(2,1)S(1)} %get-tuple-element.33), channel_id=1, source_target_pairs={{0,12},{4,8},{8,4},{12,0},{16,28},{20,24},{24,20},{28,16},{1,13},{... | collective-permute-start | bytes 393224 | tf_op jit(solution)/shard_map/ppermute | solution.py:274
  5.7 8.3 %collective-permute-start.4 = (bf16[2,32,1024]{2,1,0:T(8,128)(2,1)S(1)}, bf16[2,32,1024]{2,1,0:T(8,128)(2,1)S(1)}, u32[]{:S(2)}, u32[]{:S(2)}) collective-permute-start(bf16[2,32,1024]{2,1,0:T(8,128)(2,1)S(1)} %get-tuple-element.34), channel_id=1, source_target_pairs={{0,16},{4,20},{8,24},{12,28},{16,0},{20,4},{24,8},{28,12},{1,17},{... | collective-permute-start | bytes 393224 | tf_op jit(solution)/shard_map/ppermute | solution.py:274
  7.4 6.5 %collective-permute-start.5 = (bf16[2,32,1024]{2,1,0:T(8,128)(2,1)S(1)}, bf16[2,32,1024]{2,1,0:T(8,128)(2,1)S(1)}, u32[]{:S(2)}, u32[]{:S(2)}) collective-permute-start(bf16[2,32,1024]{2,1,0:T(8,128)(2,1)S(1)} %get-tuple-element.35), channel_id=1, source_target_pairs={{0,20},{4,16},{8,28},{12,24},{16,4},{20,0},{24,12},{28,8},{1,21},{... | collective-permute-start | bytes 393224 | tf_op jit(solution)/shard_map/ppermute | solution.py:274
  12.1 9.9 %collective-permute-start.1 = (bf16[2,64,1024]{2,1,0:T(8,128)(2,1)S(1)}, bf16[2,64,1024]{2,1,0:T(8,128)(2,1)S(1)}, u32[]{:S(2)}, u32[]{:S(2)}) collective-permute-start(bf16[2,64,1024]{2,1,0:T(8,128)(2,1)S(1)} %get-tuple-element.31.refs_0_), channel_id=1, source_target_pairs={{0,1},{1,0},{2,3},{3,2},{4,5},{5,4},{6,7},{7,6},{8,9},{9,8},{10,11... | collective-permute-start | bytes 786440 | tf_op jit(solution)/shard_map/ppermute | solution.py:277
  17.4 7.7 %copy-start.1 = (s32[8]{0:T(128)S(1)}, s32[8]{0:T(128)}, u32[]{:S(2)}) copy-start(s32[8]{0:T(128)} %q_owner.1) | copy-start | bytes 100
  17.5 9.5 %collective-permute-start.6 = (bf16[2,64,1024]{2,1,0:T(8,128)(2,1)S(1)}, bf16[2,64,1024]{2,1,0:T(8,128)(2,1)S(1)}, u32[]{:S(2)}, u32[]{:S(2)}) collective-permute-start(bf16[2,64,1024]{2,1,0:T(8,128)(2,1)S(1)} %get-tuple-element.41), channel_id=1, source_target_pairs={{0,1},{1,0},{2,3},{3,2},{4,5},{5,4},{6,7},{7,6},{8,9},{9,8},{10,11... | collective-permute-start | bytes 786440 | tf_op jit(solution)/shard_map/ppermute | solution.py:277
  19.1 10.7 %collective-permute-start.7 = (bf16[2,32,1024]{2,1,0:T(8,128)(2,1)S(1)}, bf16[2,32,1024]{2,1,0:T(8,128)(2,1)S(1)}, u32[]{:S(2)}, u32[]{:S(2)}) collective-permute-start(bf16[2,32,1024]{2,1,0:T(8,128)(2,1)S(1)} %get-tuple-element.43), channel_id=1, source_target_pairs={{0,24},{4,28},{8,16},{12,20},{16,8},{20,12},{24,0},{28,4},{1,25},{... | collective-permute-start | bytes 393224 | tf_op jit(solution)/shard_map/ppermute | solution.py:274
  21.5 8.2 %collective-permute-start.8 = (bf16[2,32,1024]{2,1,0:T(8,128)(2,1)S(1)}, bf16[2,32,1024]{2,1,0:T(8,128)(2,1)S(1)}, u32[]{:S(2)}, u32[]{:S(2)}) collective-permute-start(bf16[2,32,1024]{2,1,0:T(8,128)(2,1)S(1)} %get-tuple-element.44), channel_id=1, source_target_pairs={{0,28},{4,24},{8,20},{12,16},{16,12},{20,8},{24,4},{28,0},{1,29},{... | collective-permute-start | bytes 393224 | tf_op jit(solution)/shard_map/ppermute | solution.py:274
  21.5 16.0 %collective-permute-start.12 = (bf16[2,64,1024]{2,1,0:T(8,128)(2,1)S(1)}, bf16[2,64,1024]{2,1,0:T(8,128)(2,1)S(1)}, u32[]{:S(2)}, u32[]{:S(2)}) collective-permute-start(bf16[2,64,1024]{2,1,0:T(8,128)(2,1)S(1)} %get-tuple-element.50), channel_id=1, source_target_pairs={{0,1},{1,0},{2,3},{3,2},{4,5},{5,4},{6,7},{7,6},{8,9},{9,8},{10,11... | collective-permute-start | bytes 786440 | tf_op jit(solution)/shard_map/ppermute | solution.py:277
  27.0 10.6 %collective-permute-start.11 = (bf16[1,64,1024]{2,1,0:T(8,128)(2,1)S(1)}, bf16[1,64,1024]{2,1,0:T(8,128)(2,1)S(1)}, u32[]{:S(2)}, u32[]{:S(2)}) collective-permute-start(bf16[1,64,1024]{2,1,0:T(8,128)(2,1)S(1)} %totals.10.refs_0_), channel_id=1, source_target_pairs={{0,2},{1,3},{2,0},{3,1},{4,6},{5,7},{6,4},{7,5},{8,10},{9,11},{10,... | collective-permute-start | bytes 393224 | tf_op jit(solution)/shard_map/ppermute | solution.py:277
  32.6 7.1 %collective-permute-start.10 = (bf16[2,32,1024]{2,1,0:T(8,128)(2,1)S(1)}, bf16[2,32,1024]{2,1,0:T(8,128)(2,1)S(1)}, u32[]{:S(2)}, u32[]{:S(2)}) collective-permute-start(bf16[2,32,1024]{2,1,0:T(8,128)(2,1)S(1)} %get-tuple-element.48), channel_id=1, source_target_pairs={{0,1},{1,0},{2,3},{3,2},{4,5},{5,4},{6,7},{7,6},{8,9},{9,8},{10,11... | collective-permute-start | bytes 393224 | tf_op jit(solution)/shard_map/ppermute | solution.py:277
  34.2 8.0 %collective-permute-start.9 = (bf16[2,32,1024]{2,1,0:T(8,128)(2,1)S(1)}, bf16[2,32,1024]{2,1,0:T(8,128)(2,1)S(1)}, u32[]{:S(2)}, u32[]{:S(2)}) collective-permute-start(bf16[2,32,1024]{2,1,0:T(8,128)(2,1)S(1)} %get-tuple-element.45.refs_0_), channel_id=1, source_target_pairs={{0,1},{1,0},{2,3},{3,2},{4,5},{5,4},{6,7},{7,6},{8,9},{9,8},{10,11... | collective-permute-start | bytes 393224 | tf_op jit(solution)/shard_map/ppermute | solution.py:277
  37.6 6.3 %collective-permute-start.16 = (bf16[2,32,1024]{2,1,0:T(8,128)(2,1)S(1)}, bf16[2,32,1024]{2,1,0:T(8,128)(2,1)S(1)}, u32[]{:S(2)}, u32[]{:S(2)}) collective-permute-start(bf16[2,32,1024]{2,1,0:T(8,128)(2,1)S(1)} %bitcast.10), channel_id=1, source_target_pairs={{0,8},{4,12},{8,0},{12,4},{16,24},{20,28},{24,16},{28,20},{1,9},{5... | collective-permute-start | bytes 393224 | tf_op jit(solution)/shard_map/ppermute | solution.py:274
  39.2 11.6 %collective-permute-start.15 = (bf16[1,64,1024]{2,1,0:T(8,128)(2,1)S(1)}, bf16[1,64,1024]{2,1,0:T(8,128)(2,1)S(1)}, u32[]{:S(2)}, u32[]{:S(2)}) collective-permute-start(bf16[1,64,1024]{2,1,0:T(8,128)(2,1)S(1)} %totals.11.refs_3_), channel_id=1, source_target_pairs={{0,2},{1,3},{2,0},{3,1},{4,6},{5,7},{6,4},{7,5},{8,10},{9,11},{10,... | collective-permute-start | bytes 393224 | tf_op jit(solution)/shard_map/ppermute | solution.py:277
  39.7 11.8 %collective-permute-start.14 = (bf16[1,32,1024]{2,1,0:T(8,128)(2,1)S(1)}, bf16[1,32,1024]{2,1,0:T(8,128)(2,1)S(1)}, u32[]{:S(2)}, u32[]{:S(2)}) collective-permute-start(bf16[1,32,1024]{2,1,0:T(8,128)(2,1)S(1)} %totals.13.refs_2_), channel_id=1, source_target_pairs={{0,2},{1,3},{2,0},{3,1},{4,6},{5,7},{6,4},{7,5},{8,10},{9,11},{10,... | collective-permute-start | bytes 196616 | tf_op jit(solution)/shard_map/ppermute | solution.py:277
  42.2 11.9 %collective-permute-start.13 = (bf16[1,32,1024]{2,1,0:T(8,128)(2,1)S(1)}, bf16[1,32,1024]{2,1,0:T(8,128)(2,1)S(1)}, u32[]{:S(2)}, u32[]{:S(2)}) collective-permute-start(bf16[1,32,1024]{2,1,0:T(8,128)(2,1)S(1)} %totals.14.refs_3_), channel_id=1, source_target_pairs={{0,2},{1,3},{2,0},{3,1},{4,6},{5,7},{6,4},{7,5},{8,10},{9,11},{10,... | collective-permute-start | bytes 196616 | tf_op jit(solution)/shard_map/ppermute | solution.py:277
  51.5 9.6 %collective-permute-start.18 = (bf16[1,32,1024]{2,1,0:T(8,128)(2,1)S(1)}, bf16[1,32,1024]{2,1,0:T(8,128)(2,1)S(1)}, u32[]{:S(2)}, u32[]{:S(2)}) collective-permute-start(bf16[1,32,1024]{2,1,0:T(8,128)(2,1)S(1)} %totals.16.refs_2_), channel_id=1, source_target_pairs={{0,28},{4,24},{8,20},{12,16},{16,12},{20,8},{24,4},{28,0},{1,29},{... | collective-permute-start | bytes 196616 | tf_op jit(solution)/shard_map/ppermute | solution.py:274
  51.7 8.8 %collective-permute-start.22 = (bf16[1,64,1024]{2,1,0:T(8,128)(2,1)S(1)}, bf16[1,64,1024]{2,1,0:T(8,128)(2,1)S(1)}, u32[]{:S(2)}, u32[]{:S(2)}) collective-permute-start(bf16[1,64,1024]{2,1,0:T(8,128)(2,1)S(1)} %totals.17.refs_3_), channel_id=1, source_target_pairs={{0,2},{1,3},{2,0},{3,1},{4,6},{5,7},{6,4},{7,5},{8,10},{9,11},{10,... | collective-permute-start | bytes 393224 | tf_op jit(solution)/shard_map/ppermute | solution.py:277
  51.7 8.9 %collective-permute-start.20 = (bf16[2,32,1024]{2,1,0:T(8,128)(2,1)S(1)}, bf16[2,32,1024]{2,1,0:T(8,128)(2,1)S(1)}, u32[]{:S(2)}, u32[]{:S(2)}) collective-permute-start(bf16[2,32,1024]{2,1,0:T(8,128)(2,1)S(1)} %bitcast.11), channel_id=1, source_target_pairs={{0,16},{4,20},{8,24},{12,28},{16,0},{20,4},{24,8},{28,12},{1,17},{... | collective-permute-start | bytes 393224 | tf_op jit(solution)/shard_map/ppermute | solution.py:274
  53.3 7.8 %collective-permute-start.19 = (bf16[32,1024]{1,0:T(8,128)(2,1)S(1)}, bf16[32,1024]{1,0:T(8,128)(2,1)S(1)}, u32[]{:S(2)}, u32[]{:S(2)}) collective-permute-start(bf16[32,1024]{1,0:T(8,128)(2,1)S(1)} %slice_bitcast_fusion.1), channel_id=1, source_target_pairs={{0,4},{4,0},{8,12},{12,8},{16,20},{20,16},{24,28},{28,24},{1,5},{5... | collective-permute-start | bytes 196616 | tf_op jit(solution)/shard_map/ppermute | solution.py:274
  54.1 7.1 %collective-permute-start.17 = (bf16[1,32,1024]{2,1,0:T(8,128)(2,1)S(1)}, bf16[1,32,1024]{2,1,0:T(8,128)(2,1)S(1)}, u32[]{:S(2)}, u32[]{:S(2)}) collective-permute-start(bf16[1,32,1024]{2,1,0:T(8,128)(2,1)S(1)} %totals.18.refs_3_), channel_id=1, source_target_pairs={{0,24},{4,28},{8,16},{12,20},{16,8},{20,12},{24,0},{28,4},{1,25},{... | collective-permute-start | bytes 196616 | tf_op jit(solution)/shard_map/ppermute | solution.py:274
  60.5 1.3 %collective-permute-start.23 = (bf16[32,1024]{1,0:T(8,128)(2,1)S(1)}, bf16[32,1024]{1,0:T(8,128)(2,1)S(1)}, u32[]{:S(2)}, u32[]{:S(2)}) collective-permute-start(bf16[32,1024]{1,0:T(8,128)(2,1)S(1)} %get-tuple-element.52), channel_id=1, source_target_pairs={{0,4},{4,0},{8,12},{12,8},{16,20},{20,16},{24,28},{28,24},{1,5},{5... | collective-permute-start | bytes 196616 | tf_op jit(solution)/shard_map/ppermute | solution.py:274
  60.7 1.4 %collective-permute-start.21 = (bf16[32,1024]{1,0:T(8,128)(2,1)S(1)}, bf16[32,1024]{1,0:T(8,128)(2,1)S(1)}, u32[]{:S(2)}, u32[]{:S(2)}) collective-permute-start(bf16[32,1024]{1,0:T(8,128)(2,1)S(1)} %slice_bitcast_fusion), channel_id=1, source_target_pairs={{0,4},{4,0},{8,12},{12,8},{16,20},{20,16},{24,28},{28,24},{1,5},{5... | collective-permute-start | bytes 196616 | tf_op jit(solution)/shard_map/ppermute | solution.py:274

commit v9 on v7

--- a/solution.py
+++ b/solution.py
@@ -320,7 +320,8 @@
     away.update(outs)
     come.update((u, first_step(away[u])) for u in near)
     kept, _ = multiply([mine] + near, all_even, even_ints, after=[come[mine]])
-    place = place_of(q_owner, peers * rows, kept[mine])
+    ready[mine], sums[mine] = later_steps(kept[mine], come[mine])
+    place = place_of(q_owner, peers * rows, ready[mine])
     ready[first], sums[first] = later_steps(kept[first], come[first], [place])
     outs, _ = multiply(far, all_odd, odd_ints, after=[ready[first]])
     away.update(outs)
@@ -329,7 +330,7 @@
     for u in others:
         ready[u], sums[u] = later_steps(kept[u], come[u], [last])
         last = ready[u]
-    outs, _ = multiply(far, all_even, even_ints, after=[last, sums[first][-1][0]])
+    outs, _ = multiply(far, all_even, even_ints, after=[last, sums[first][-1][0], sums[mine][-1][0]])
     kept.update(outs)
 
     shares = {}
@@ -352,12 +353,10 @@
     for u in far:
         ready[u], sums[u] = later_steps(kept[u], come[u], [last])
         last = ready[u]
+    last = close(mine, [last])
     for u in others:
         last = close(u, [last, shares[first[0]][0]])
-    last = close(far[0], [last])
-    ready[mine], sums[mine] = later_steps(kept[mine], come[mine], [last])
-    last = ready[mine]
-    for u in far[1:] + [mine]:
+    for u in far:
         last = close(u, [last])
     return order(place, [(j, *shares[j]) for u in far + near + [mine] for j in u]).reshape(rows, peers, -1)
 

time: 60.8 us -> 61.5 us (1.012)
  the two profiles are of different devices: /device:TPU:0 before, /device:TPU:31 now
where the time goes in v9:
time: 61.5 us; the launch traced here: 61.3 us
  starting transfers between devices  28.6 us (47%)
  Pallas kernels  19.8 us (32%)
  waiting for transfers between devices  11 us (18%)
  local copies, waits for them, and re-layouts  0.97 us (2%)
  other arithmetic  0.72 us (1%)
    ppermute x14, starting transfers between devices, swap(): return lax.ppermute(value, 'wide', [(w, w ^ j) for w in range(peers)])  19.1 us
    pallas_call x5, Pallas kernels, product(): pl.pallas_call(functools.partial(product_kernel, plan), out_shape=[jax.Sh...  16.9 us
    ppermute x10, starting transfers between devices, swap_line(): lax.ppermute(value, 'narrow', [(n, n ^ mask) for n in range(devices)])  9.47 us
    ppermute x10, waiting for transfers between devices, swap_line(): lax.ppermute(value, 'narrow', [(n, n ^ mask) for n in range(devices)])  8.82 us
    ppermute x14, waiting for transfers between devices, swap(): return lax.ppermute(value, 'wide', [(w, w ^ j) for w in range(peers)])  2.22 us
  transfers between devices with their start and end apart: 24, of which 5 were waited for; matrix products, arithmetic and copies ran while one was open for 0% of the time, Pallas kernels for 29%

profile of v9, /device:TPU:31, one launch (start us, length us, event | category | flops | bytes accessed | tf_op | source)
XLA Modules:
  0.0 61.3 jit_solution(16331445249084320666)
XLA Ops:
  0.0 0.7 %pad_add_fusion.tables_from = s32[7,8]{1,0:T(8,128)S(1)} fusion(s32[1,8]{1,0:T(1,128)} %bitcast.12, s32[2,8]{1,0:T(2,128)} %bitcast.14, s32[4,8]{1,0:T(4,128)} %bitcast.13), kind=kLoop, calls=%fused_computation.2 | loop fusion | flops 112 | bytes 448 | tf_op jit(solution)/shard_map/concatenate | solution.py:46
  0.7 0.9 %copy-done = bf16[32,4,1024]{2,1,0:T(4,128)(2,1)S(1)} copy-done((bf16[32,4,1024]{2,1,0:T(4,128)(2,1)S(1)}, bf16[32,4,1024]{2,1,0:T(4,128)(2,1)}, u32[]{:S(2)}) %copy-start) | copy-done | bytes 262168
  1.7 0.8 %pick.1 = (bf16[2,32,1024]{2,1,0:T(8,128)(2,1)S(1)}, bf16[2,32,1024]{2,1,0:T(8,128)(2,1)S(1)}, bf16[2,32,1024]{2,1,0:T(8,128)(2,1)S(1)}, bf16[2,32,1024]{2,1,0:T...) custom-call(s32[7,8]{1,0:T(8,128)S(1)} %pad_add_fusion.tables_from, ...), custom_call_target="tpu_custom_call" | custom-call | tf_op jit(solution)/shard_map/pick/pallas_call | solution.py:48
  2.5 0.7 %collective-permute-start = (bf16[2,32,1024]{2,1,0:T(8,128)(2,1)S(1)}, bf16[2,32,1024]{2,1,0:T(8,128)(2,1)S(1)}, u32[]{:S(2)}, u32[]{:S(2)}) collective-permute-start(bf16[2,32,1024]{2,1,0:T(8,128)(2,1)S(1)} %get-tuple-element.30), channel_id=1, source_target_pairs={{0,4},{4,0},{8,12},{12,8},{16,20},{20,16},{24,28},{28,24},{1,5},{5... | collective-permute-start | bytes 393224 | tf_op jit(solution)/shard_map/ppermute | solution.py:274
  3.2 0.3 collective-permute-start.2
  3.5 1.4 %collective-permute-start.3 = (bf16[2,32,1024]{2,1,0:T(8,128)(2,1)S(1)}, bf16[2,32,1024]{2,1,0:T(8,128)(2,1)S(1)}, u32[]{:S(2)}, u32[]{:S(2)}) collective-permute-start(bf16[2,32,1024]{2,1,0:T(8,128)(2,1)S(1)} %get-tuple-element.33), channel_id=1, source_target_pairs={{0,12},{4,8},{8,4},{12,0},{16,28},{20,24},{24,20},{28,16},{1,13},{... | collective-permute-start | bytes 393224 | tf_op jit(solution)/shard_map/ppermute | solution.py:274
  5.0 0.2 collective-permute-start.4
  5.2 1.6 %collective-permute-start.5 = (bf16[2,32,1024]{2,1,0:T(8,128)(2,1)S(1)}, bf16[2,32,1024]{2,1,0:T(8,128)(2,1)S(1)}, u32[]{:S(2)}, u32[]{:S(2)}) collective-permute-start(bf16[2,32,1024]{2,1,0:T(8,128)(2,1)S(1)} %get-tuple-element.35), channel_id=1, source_target_pairs={{0,20},{4,16},{8,28},{12,24},{16,4},{20,0},{24,12},{28,8},{1,21},{... | collective-permute-start | bytes 393224 | tf_op jit(solution)/shard_map/ppermute | solution.py:274
  6.8 0.0 collective-permute-done.refs_1_.refs_2_
  6.8 4.7 %product.5 = (bf16[2,64,1024]{2,1,0:T(8,128)(2,1)S(1)}, bf16[2,2,1024,1024]{3,2,1,0:T(8,128)(2,1)S(1)}) custom-call(bf16[2,32,1024]{2,1,0:T(8,128)(2,1)S(1)} %get-tuple-element.29.refs_0_.refs_1_, bf16[2,32,1024]{2,1,0:T(8,128)(2,1)S(1)} %collective-permute-done.refs_1_.refs_2_, bf16[1,2,4096,1024]{3,2,1,0:T(8,128)(2,1)} %refs_6_.1), custom_call_target="tpu_custom_call" | custom-call | flops 2147483648 | bytes 8388608 | tf_op jit(solution)/shard_map/product/pallas_call | solution.py:151
  11.4 0.2 collective-permute-start.1
  11.7 0.0 collective-permute-done.2.refs_1_.refs_3_
  11.7 0.0 collective-permute-done.3.refs_2_.refs_4_
  11.7 0.0 collective-permute-done.4.refs_3_.refs_5_
  11.7 1.3 %collective-permute-done.5.refs_4_.refs_6_ = bf16[2,32,1024]{2,1,0:T(8,128)(2,1)S(1)} collective-permute-done((bf16[2,32,1024]{2,1,0:T(8,128)(2,1)S(1)}, bf16[2,32,1024]{2,1,0:T(8,128)(2,1)S(1)}, u32[]{:S(2)}, u32[]{:S(2)}) %collective-permute-start.5) | collective-permute-done | bytes 131104 | tf_op jit(solution)/shard_map/ppermute | solution.py:274
  13.0 3.5 %product.6 = (bf16[2,64,1024]{2,1,0:T(8,128)(2,1)S(1)}, bf16[2,64,1024]{2,1,0:T(8,128)(2,1)S(1)}, bf16[2,2,1024,1024]{3,2,1,0:T(8,128)(2,1)S(1)}, bf16[2,32,1024...) custom-call(bf16[2,64,1024]{2,1,0:T(8,128)(2,1)S(1)} %get-tuple-element.31.refs_0_, ...), custom_call_target="tpu_custom_call", output_to_operand_aliasing={{3}: (7, {}), {4}: (8, {})} | custom-call | flops 2147483648 | bytes 8388608 | tf_op jit(solution)/shard_map/product/pallas_call | solution.py:151
  16.5 0.0 copy-start.1
  16.5 0.2 collective-permute-start.7
  16.7 0.2 collective-permute-start.8
  16.9 2.8 %collective-permute-start.9 = (bf16[2,32,1024]{2,1,0:T(8,128)(2,1)S(1)}, bf16[2,32,1024]{2,1,0:T(8,128)(2,1)S(1)}, u32[]{:S(2)}, u32[]{:S(2)}) collective-permute-start(bf16[2,32,1024]{2,1,0:T(8,128)(2,1)S(1)} %get-tuple-element.46), channel_id=1, source_target_pairs={{0,28},{4,24},{8,20},{12,16},{16,12},{20,8},{24,4},{28,0},{1,29},{... | collective-permute-start | bytes 393224 | tf_op jit(solution)/shard_map/ppermute | solution.py:274
  19.7 1.3 %collective-permute-start.6 = (bf16[2,64,1024]{2,1,0:T(8,128)(2,1)S(1)}, bf16[2,64,1024]{2,1,0:T(8,128)(2,1)S(1)}, u32[]{:S(2)}, u32[]{:S(2)}) collective-permute-start(bf16[2,64,1024]{2,1,0:T(8,128)(2,1)S(1)} %get-tuple-element.41), channel_id=1, source_target_pairs={{0,1},{1,0},{2,3},{3,2},{4,5},{5,4},{6,7},{7,6},{8,9},{9,8},{10,11... | collective-permute-start | bytes 786440 | tf_op jit(solution)/shard_map/ppermute | solution.py:277
  21.0 3.1 %product.7 = (bf16[2,64,1024]{2,1,0:T(8,128)(2,1)S(1)}, bf16[2,64,1024]{2,1,0:T(8,128)(2,1)S(1)}, bf16[2,64,1024]{2,1,0:T(8,128)(2,1)S(1)}) custom-call(bf16[2,64,1024]{2,1,0:T(8,128)(2,1)S(1)} %collective-permute-done.1.refs_0_.refs_1_, bf16[2,32,1024]{2,1,0:T(8,128)(2,1)S(1)} %get-tuple-element.29.refs_0_.refs_1_, ...), custom_call_target="tpu_custom_call" | custom-call | flops 2147483648 | bytes 8388608 | tf_op jit(solution)/shard_map/product/pallas_call | solution.py:151
  24.2 0.7 %place.1.refs_2_.refs_8_ = bf16[256,256]{1,0:T(8,128)(2,1)S(1)} custom-call(s32[8]{0:T(128)S(1)} %copy-done.1, bf16[1,64,1024]{2,1,0:T(8,128)(2,1)S(1)} %totals.10.after), custom_call_target="tpu_custom_call" | custom-call | tf_op jit(solution)/shard_map/place/pallas_call | solution.py:220
  24.9 0.1 collective-permute-start.11
  25.0 0.0 collective-permute-done.7.refs_1_
  25.1 2.4 %collective-permute-start.10 = (bf16[1,64,1024]{2,1,0:T(8,128)(2,1)S(1)}, bf16[1,64,1024]{2,1,0:T(8,128)(2,1)S(1)}, u32[]{:S(2)}, u32[]{:S(2)}) collective-permute-start(bf16[1,64,1024]{2,1,0:T(8,128)(2,1)S(1)} %totals.11.refs_0_), channel_id=1, source_target_pairs={{0,2},{1,3},{2,0},{3,1},{4,6},{5,7},{6,4},{7,5},{8,10},{9,11},{10,... | collective-permute-start | bytes 393224 | tf_op jit(solution)/shard_map/ppermute | solution.py:277
  27.4 2.8 %product.8 = (bf16[2,32,1024]{2,1,0:T(8,128)(2,1)S(1)}, bf16[2,32,1024]{2,1,0:T(8,128)(2,1)S(1)}) custom-call(bf16[1,64,1024]{2,1,0:T(8,128)(2,1)S(1)} %totals.11.refs_0_, bf16[2,32,1024]{2,1,0:T(8,128)(2,1)S(1)} %collective-permute-done.8.refs_1_.refs_3_, bf16[2,32,1024]{2,1,0:T(8,128)(2,1)S(1)} %collective-permute-done.9.refs_2_.refs_4_, ...), custom_call_target="tpu_custom_call" | custom-call | flops 2147483648 | bytes 8388608 | tf_op jit(solution)/shard_map/product/pallas_call | solution.py:151
  30.3 0.2 collective-permute-start.12
  30.5 2.4 %collective-permute-done.6.refs_1_ = bf16[2,64,1024]{2,1,0:T(8,128)(2,1)S(1)} collective-permute-done((bf16[2,64,1024]{2,1,0:T(8,128)(2,1)S(1)}, bf16[2,64,1024]{2,1,0:T(8,128)(2,1)S(1)}, u32[]{:S(2)}, u32[]{:S(2)}) %collective-permute-start.6) | collective-permute-done | bytes 262176 | tf_op jit(solution)/shard_map/ppermute | solution.py:277
  33.0 0.3 collective-permute-start.14
  33.3 2.2 %collective-permute-start.15 = (bf16[2,32,1024]{2,1,0:T(8,128)(2,1)S(1)}, bf16[2,32,1024]{2,1,0:T(8,128)(2,1)S(1)}, u32[]{:S(2)}, u32[]{:S(2)}) collective-permute-start(bf16[2,32,1024]{2,1,0:T(8,128)(2,1)S(1)} %get-tuple-element.50), channel_id=1, source_target_pairs={{0,1},{1,0},{2,3},{3,2},{4,5},{5,4},{6,7},{7,6},{8,9},{9,8},{10,11... | collective-permute-start | bytes 393224 | tf_op jit(solution)/shard_map/ppermute | solution.py:277
  35.5 0.7 %collective-permute-done.11.refs_2_ = bf16[1,64,1024]{2,1,0:T(8,128)(2,1)S(1)} collective-permute-done((bf16[1,64,1024]{2,1,0:T(8,128)(2,1)S(1)}, bf16[1,64,1024]{2,1,0:T(8,128)(2,1)S(1)}, u32[]{:S(2)}, u32[]{:S(2)}) %collective-permute-start.11) | collective-permute-done | bytes 131104 | tf_op jit(solution)/shard_map/ppermute | solution.py:277
  36.2 5.7 %collective-permute-done.10.refs_1_.refs_2_ = bf16[1,64,1024]{2,1,0:T(8,128)(2,1)S(1)} collective-permute-done((bf16[1,64,1024]{2,1,0:T(8,128)(2,1)S(1)}, bf16[1,64,1024]{2,1,0:T(8,128)(2,1)S(1)}, u32[]{:S(2)}, u32[]{:S(2)}) %collective-permute-start.10) | collective-permute-done | bytes 131104 | tf_op jit(solution)/shard_map/ppermute | solution.py:277
  41.9 2.8 %product.9 = (bf16[2,32,1024]{2,1,0:T(8,128)(2,1)S(1)}, bf16[2,32,1024]{2,1,0:T(8,128)(2,1)S(1)}) custom-call(bf16[1,64,1024]{2,1,0:T(8,128)(2,1)S(1)} %totals.12.refs_0_, bf16[1,64,1024]{2,1,0:T(8,128)(2,1)S(1)} %collective-permute-done.10.refs_1_.refs_2_, bf16[1,64,1024]{2,1,0:T(8,128)(2,1)S(1)} %collective-permute-done.11.refs_2_, ...), custom_call_target="tpu_custom_call" | custom-call | flops 2147483648 | bytes 8388608 | tf_op jit(solution)/shard_map/product/pallas_call | solution.py:151
  44.7 0.1 totals.13.refs_2_
  44.8 0.3 collective-permute-start.16
  45.1 0.1 collective-permute-start.13
  45.2 2.4 %collective-permute-start.18 = (bf16[1,32,1024]{2,1,0:T(8,128)(2,1)S(1)}, bf16[1,32,1024]{2,1,0:T(8,128)(2,1)S(1)}, u32[]{:S(2)}, u32[]{:S(2)}) collective-permute-start(bf16[1,32,1024]{2,1,0:T(8,128)(2,1)S(1)} %totals.15.refs_3_), channel_id=1, source_target_pairs={{0,2},{1,3},{2,0},{3,1},{4,6},{5,7},{6,4},{7,5},{8,10},{9,11},{10,... | collective-permute-start | bytes 196616 | tf_op jit(solution)/shard_map/ppermute | solution.py:277
  47.6 0.1 totals.16
  47.7 2.6 %collective-permute-start.23 = (bf16[32,1024]{1,0:T(8,128)(2,1)S(1)}, bf16[32,1024]{1,0:T(8,128)(2,1)S(1)}, u32[]{:S(2)}, u32[]{:S(2)}) collective-permute-start(bf16[32,1024]{1,0:T(8,128)(2,1)S(1)} %get-tuple-element.51.refs_3_), channel_id=1, source_target_pairs={{0,4},{4,0},{8,12},{12,8},{16,20},{20,16},{24,28},{28,24},{1,5},{5... | collective-permute-start | bytes 196616 | tf_op jit(solution)/shard_map/ppermute | solution.py:274
  50.3 0.1 totals.17.refs_3_
  50.3 0.4 collective-permute-start.21
  50.8 1.3 %collective-permute-start.20 = (bf16[32,1024]{1,0:T(8,128)(2,1)S(1)}, bf16[32,1024]{1,0:T(8,128)(2,1)S(1)}, u32[]{:S(2)}, u32[]{:S(2)}) collective-permute-start(bf16[32,1024]{1,0:T(8,128)(2,1)S(1)} %slice_bitcast_fusion.1), channel_id=1, source_target_pairs={{0,4},{4,0},{8,12},{12,8},{16,20},{20,16},{24,28},{28,24},{1,5},{5... | collective-permute-start | bytes 196616 | tf_op jit(solution)/shard_map/ppermute | solution.py:274
  52.2 1.3 %collective-permute-start.17 = (bf16[1,32,1024]{2,1,0:T(8,128)(2,1)S(1)}, bf16[1,32,1024]{2,1,0:T(8,128)(2,1)S(1)}, u32[]{:S(2)}, u32[]{:S(2)}) collective-permute-start(bf16[1,32,1024]{2,1,0:T(8,128)(2,1)S(1)} %totals.18.refs_3_), channel_id=1, source_target_pairs={{0,24},{4,28},{8,16},{12,20},{16,8},{20,12},{24,0},{28,4},{1,25},{... | collective-permute-start | bytes 196616 | tf_op jit(solution)/shard_map/ppermute | solution.py:274
  53.5 1.6 %collective-permute-start.19 = (bf16[1,32,1024]{2,1,0:T(8,128)(2,1)S(1)}, bf16[1,32,1024]{2,1,0:T(8,128)(2,1)S(1)}, u32[]{:S(2)}, u32[]{:S(2)}) collective-permute-start(bf16[1,32,1024]{2,1,0:T(8,128)(2,1)S(1)} %totals.19), channel_id=1, source_target_pairs={{0,28},{4,24},{8,20},{12,16},{16,12},{20,8},{24,4},{28,0},{1,29},{... | collective-permute-start | bytes 196616 | tf_op jit(solution)/shard_map/ppermute | solution.py:274
  55.1 4.3 %collective-permute-start.22 = (bf16[32,1024]{1,0:T(8,128)(2,1)S(1)}, bf16[32,1024]{1,0:T(8,128)(2,1)S(1)}, u32[]{:S(2)}, u32[]{:S(2)}) collective-permute-start(bf16[32,1024]{1,0:T(8,128)(2,1)S(1)} %slice_bitcast_fusion), channel_id=1, source_target_pairs={{0,4},{4,0},{8,12},{12,8},{16,20},{20,16},{24,28},{28,24},{1,5},{5... | collective-permute-start | bytes 196616 | tf_op jit(solution)/shard_map/ppermute | solution.py:274
  59.4 0.9 %collective-permute-done.22.refs_5_ = bf16[32,1024]{1,0:T(8,128)(2,1)S(1)} collective-permute-done((bf16[32,1024]{1,0:T(8,128)(2,1)S(1)}, bf16[32,1024]{1,0:T(8,128)(2,1)S(1)}, u32[]{:S(2)}, u32[]{:S(2)}) %collective-permute-start.22) | collective-permute-done | bytes 65568 | tf_op jit(solution)/shard_map/ppermute | solution.py:274
  60.3 1.0 %order.1 = bf16[256,1024]{1,0:T(8,128)(2,1)} custom-call(bf16[1,32,1024]{2,1,0:T(8,128)(2,1)S(1)} %collective-permute-done.17.refs_0_, bf16[1,32,1024]{2,1,0:T(8,128)(2,1)S(1)} %collective-permute-done.19.refs_1_, bf16[2,32,1024]{2,1,0:T(8,128)(2,1)S(1)} %collective-permute-done.16.refs_4_.refs_2_, bf16[32,1024]{1,0:T(8,128)(2,1)S(1)} %collective-permute-done.20.refs_3_, ...), custom_call_target="tpu_custom_call" | custom-call | tf_op jit(solution)/shard_map/order/pallas_call | solution.py:250
  (25 shorter events, 0.2 us)
Async XLA Ops:
  0.7 0.9 %copy-start = (bf16[32,4,1024]{2,1,0:T(4,128)(2,1)S(1)}, bf16[32,4,1024]{2,1,0:T(4,128)(2,1)}, u32[]{:S(2)}) copy-start(bf16[32,4,1024]{2,1,0:T(4,128)(2,1)} %amps.1) | copy-start | bytes 786436
  2.5 4.3 %collective-permute-start = (bf16[2,32,1024]{2,1,0:T(8,128)(2,1)S(1)}, bf16[2,32,1024]{2,1,0:T(8,128)(2,1)S(1)}, u32[]{:S(2)}, u32[]{:S(2)}) collective-permute-start(bf16[2,32,1024]{2,1,0:T(8,128)(2,1)S(1)} %get-tuple-element.30), channel_id=1, source_target_pairs={{0,4},{4,0},{8,12},{12,8},{16,20},{20,16},{24,28},{28,24},{1,5},{5... | collective-permute-start | bytes 393224 | tf_op jit(solution)/shard_map/ppermute | solution.py:274
  3.2 8.4 %collective-permute-start.2 = (bf16[2,32,1024]{2,1,0:T(8,128)(2,1)S(1)}, bf16[2,32,1024]{2,1,0:T(8,128)(2,1)S(1)}, u32[]{:S(2)}, u32[]{:S(2)}) collective-permute-start(bf16[2,32,1024]{2,1,0:T(8,128)(2,1)S(1)} %get-tuple-element.32), channel_id=1, source_target_pairs={{0,8},{4,12},{8,0},{12,4},{16,24},{20,28},{24,16},{28,20},{1,9},{5... | collective-permute-start | bytes 393224 | tf_op jit(solution)/shard_map/ppermute | solution.py:274
  3.5 8.2 %collective-permute-start.3 = (bf16[2,32,1024]{2,1,0:T(8,128)(2,1)S(1)}, bf16[2,32,1024]{2,1,0:T(8,128)(2,1)S(1)}, u32[]{:S(2)}, u32[]{:S(2)}) collective-permute-start(bf16[2,32,1024]{2,1,0:T(8,128)(2,1)S(1)} %get-tuple-element.33), channel_id=1, source_target_pairs={{0,12},{4,8},{8,4},{12,0},{16,28},{20,24},{24,20},{28,16},{1,13},{... | collective-permute-start | bytes 393224 | tf_op jit(solution)/shard_map/ppermute | solution.py:274
  5.0 6.7 %collective-permute-start.4 = (bf16[2,32,1024]{2,1,0:T(8,128)(2,1)S(1)}, bf16[2,32,1024]{2,1,0:T(8,128)(2,1)S(1)}, u32[]{:S(2)}, u32[]{:S(2)}) collective-permute-start(bf16[2,32,1024]{2,1,0:T(8,128)(2,1)S(1)} %get-tuple-element.34), channel_id=1, source_target_pairs={{0,16},{4,20},{8,24},{12,28},{16,0},{20,4},{24,8},{28,12},{1,17},{... | collective-permute-start | bytes 393224 | tf_op jit(solution)/shard_map/ppermute | solution.py:274
  5.2 7.8 %collective-permute-start.5 = (bf16[2,32,1024]{2,1,0:T(8,128)(2,1)S(1)}, bf16[2,32,1024]{2,1,0:T(8,128)(2,1)S(1)}, u32[]{:S(2)}, u32[]{:S(2)}) collective-permute-start(bf16[2,32,1024]{2,1,0:T(8,128)(2,1)S(1)} %get-tuple-element.35), channel_id=1, source_target_pairs={{0,20},{4,16},{8,28},{12,24},{16,4},{20,0},{24,12},{28,8},{1,21},{... | collective-permute-start | bytes 393224 | tf_op jit(solution)/shard_map/ppermute | solution.py:274
  11.4 9.6 %collective-permute-start.1 = (bf16[2,64,1024]{2,1,0:T(8,128)(2,1)S(1)}, bf16[2,64,1024]{2,1,0:T(8,128)(2,1)S(1)}, u32[]{:S(2)}, u32[]{:S(2)}) collective-permute-start(bf16[2,64,1024]{2,1,0:T(8,128)(2,1)S(1)} %get-tuple-element.31.refs_0_), channel_id=1, source_target_pairs={{0,1},{1,0},{2,3},{3,2},{4,5},{5,4},{6,7},{7,6},{8,9},{9,8},{10,11... | collective-permute-start | bytes 786440 | tf_op jit(solution)/shard_map/ppermute | solution.py:277
  16.5 7.7 %copy-start.1 = (s32[8]{0:T(128)S(1)}, s32[8]{0:T(128)}, u32[]{:S(2)}) copy-start(s32[8]{0:T(128)} %q_owner.1) | copy-start | bytes 100
  16.5 8.5 %collective-permute-start.7 = (bf16[2,64,1024]{2,1,0:T(8,128)(2,1)S(1)}, bf16[2,64,1024]{2,1,0:T(8,128)(2,1)S(1)}, u32[]{:S(2)}, u32[]{:S(2)}) collective-permute-start(bf16[2,64,1024]{2,1,0:T(8,128)(2,1)S(1)} %get-tuple-element.43), channel_id=1, source_target_pairs={{0,1},{1,0},{2,3},{3,2},{4,5},{5,4},{6,7},{7,6},{8,9},{9,8},{10,11... | collective-permute-start | bytes 786440 | tf_op jit(solution)/shard_map/ppermute | solution.py:277
  16.7 10.7 %collective-permute-start.8 = (bf16[2,32,1024]{2,1,0:T(8,128)(2,1)S(1)}, bf16[2,32,1024]{2,1,0:T(8,128)(2,1)S(1)}, u32[]{:S(2)}, u32[]{:S(2)}) collective-permute-start(bf16[2,32,1024]{2,1,0:T(8,128)(2,1)S(1)} %get-tuple-element.45), channel_id=1, source_target_pairs={{0,24},{4,28},{8,16},{12,20},{16,8},{20,12},{24,0},{28,4},{1,25},{... | collective-permute-start | bytes 393224 | tf_op jit(solution)/shard_map/ppermute | solution.py:274
  16.9 10.5 %collective-permute-start.9 = (bf16[2,32,1024]{2,1,0:T(8,128)(2,1)S(1)}, bf16[2,32,1024]{2,1,0:T(8,128)(2,1)S(1)}, u32[]{:S(2)}, u32[]{:S(2)}) collective-permute-start(bf16[2,32,1024]{2,1,0:T(8,128)(2,1)S(1)} %get-tuple-element.46), channel_id=1, source_target_pairs={{0,28},{4,24},{8,20},{12,16},{16,12},{20,8},{24,4},{28,0},{1,29},{... | collective-permute-start | bytes 393224 | tf_op jit(solution)/shard_map/ppermute | solution.py:274
  19.7 13.2 %collective-permute-start.6 = (bf16[2,64,1024]{2,1,0:T(8,128)(2,1)S(1)}, bf16[2,64,1024]{2,1,0:T(8,128)(2,1)S(1)}, u32[]{:S(2)}, u32[]{:S(2)}) collective-permute-start(bf16[2,64,1024]{2,1,0:T(8,128)(2,1)S(1)} %get-tuple-element.41), channel_id=1, source_target_pairs={{0,1},{1,0},{2,3},{3,2},{4,5},{5,4},{6,7},{7,6},{8,9},{9,8},{10,11... | collective-permute-start | bytes 786440 | tf_op jit(solution)/shard_map/ppermute | solution.py:277
  24.9 11.3 %collective-permute-start.11 = (bf16[1,64,1024]{2,1,0:T(8,128)(2,1)S(1)}, bf16[1,64,1024]{2,1,0:T(8,128)(2,1)S(1)}, u32[]{:S(2)}, u32[]{:S(2)}) collective-permute-start(bf16[1,64,1024]{2,1,0:T(8,128)(2,1)S(1)} %totals.10.after), channel_id=1, source_target_pairs={{0,2},{1,3},{2,0},{3,1},{4,6},{5,7},{6,4},{7,5},{8,10},{9,11},{10,... | collective-permute-start | bytes 393224 | tf_op jit(solution)/shard_map/ppermute | solution.py:277
  25.1 16.8 %collective-permute-start.10 = (bf16[1,64,1024]{2,1,0:T(8,128)(2,1)S(1)}, bf16[1,64,1024]{2,1,0:T(8,128)(2,1)S(1)}, u32[]{:S(2)}, u32[]{:S(2)}) collective-permute-start(bf16[1,64,1024]{2,1,0:T(8,128)(2,1)S(1)} %totals.11.refs_0_), channel_id=1, source_target_pairs={{0,2},{1,3},{2,0},{3,1},{4,6},{5,7},{6,4},{7,5},{8,10},{9,11},{10,... | collective-permute-start | bytes 393224 | tf_op jit(solution)/shard_map/ppermute | solution.py:277
  30.3 14.8 %collective-permute-start.12 = (bf16[2,32,1024]{2,1,0:T(8,128)(2,1)S(1)}, bf16[2,32,1024]{2,1,0:T(8,128)(2,1)S(1)}, u32[]{:S(2)}, u32[]{:S(2)}) collective-permute-start(bf16[2,32,1024]{2,1,0:T(8,128)(2,1)S(1)} %get-tuple-element.47.refs_2_), channel_id=1, source_target_pairs={{0,1},{1,0},{2,3},{3,2},{4,5},{5,4},{6,7},{7,6},{8,9},{9,8},{10,11... | collective-permute-start | bytes 393224 | tf_op jit(solution)/shard_map/ppermute | solution.py:277
  33.0 17.3 %collective-permute-start.14 = (bf16[1,64,1024]{2,1,0:T(8,128)(2,1)S(1)}, bf16[1,64,1024]{2,1,0:T(8,128)(2,1)S(1)}, u32[]{:S(2)}, u32[]{:S(2)}) collective-permute-start(bf16[1,64,1024]{2,1,0:T(8,128)(2,1)S(1)} %totals.12.refs_0_), channel_id=1, source_target_pairs={{0,2},{1,3},{2,0},{3,1},{4,6},{5,7},{6,4},{7,5},{8,10},{9,11},{10,... | collective-permute-start | bytes 393224 | tf_op jit(solution)/shard_map/ppermute | solution.py:277
  33.3 11.9 %collective-permute-start.15 = (bf16[2,32,1024]{2,1,0:T(8,128)(2,1)S(1)}, bf16[2,32,1024]{2,1,0:T(8,128)(2,1)S(1)}, u32[]{:S(2)}, u32[]{:S(2)}) collective-permute-start(bf16[2,32,1024]{2,1,0:T(8,128)(2,1)S(1)} %get-tuple-element.50), channel_id=1, source_target_pairs={{0,1},{1,0},{2,3},{3,2},{4,5},{5,4},{6,7},{7,6},{8,9},{9,8},{10,11... | collective-permute-start | bytes 393224 | tf_op jit(solution)/shard_map/ppermute | solution.py:277
  44.8 5.5 %collective-permute-start.16 = (bf16[2,32,1024]{2,1,0:T(8,128)(2,1)S(1)}, bf16[2,32,1024]{2,1,0:T(8,128)(2,1)S(1)}, u32[]{:S(2)}, u32[]{:S(2)}) collective-permute-start(bf16[2,32,1024]{2,1,0:T(8,128)(2,1)S(1)} %bitcast.10), channel_id=1, source_target_pairs={{0,8},{4,12},{8,0},{12,4},{16,24},{20,28},{24,16},{28,20},{1,9},{5... | collective-permute-start | bytes 393224 | tf_op jit(solution)/shard_map/ppermute | solution.py:274
  45.1 7.0 %collective-permute-start.13 = (bf16[1,32,1024]{2,1,0:T(8,128)(2,1)S(1)}, bf16[1,32,1024]{2,1,0:T(8,128)(2,1)S(1)}, u32[]{:S(2)}, u32[]{:S(2)}) collective-permute-start(bf16[1,32,1024]{2,1,0:T(8,128)(2,1)S(1)} %totals.14.refs_2_), channel_id=1, source_target_pairs={{0,2},{1,3},{2,0},{3,1},{4,6},{5,7},{6,4},{7,5},{8,10},{9,11},{10,... | collective-permute-start | bytes 196616 | tf_op jit(solution)/shard_map/ppermute | solution.py:277
  45.2 8.2 %collective-permute-start.18 = (bf16[1,32,1024]{2,1,0:T(8,128)(2,1)S(1)}, bf16[1,32,1024]{2,1,0:T(8,128)(2,1)S(1)}, u32[]{:S(2)}, u32[]{:S(2)}) collective-permute-start(bf16[1,32,1024]{2,1,0:T(8,128)(2,1)S(1)} %totals.15.refs_3_), channel_id=1, source_target_pairs={{0,2},{1,3},{2,0},{3,1},{4,6},{5,7},{6,4},{7,5},{8,10},{9,11},{10,... | collective-permute-start | bytes 196616 | tf_op jit(solution)/shard_map/ppermute | solution.py:277
  47.7 11.7 %collective-permute-start.23 = (bf16[32,1024]{1,0:T(8,128)(2,1)S(1)}, bf16[32,1024]{1,0:T(8,128)(2,1)S(1)}, u32[]{:S(2)}, u32[]{:S(2)}) collective-permute-start(bf16[32,1024]{1,0:T(8,128)(2,1)S(1)} %get-tuple-element.51.refs_3_), channel_id=1, source_target_pairs={{0,4},{4,0},{8,12},{12,8},{16,20},{20,16},{24,28},{28,24},{1,5},{5... | collective-permute-start | bytes 196616 | tf_op jit(solution)/shard_map/ppermute | solution.py:274
  50.3 4.7 %collective-permute-start.21 = (bf16[2,32,1024]{2,1,0:T(8,128)(2,1)S(1)}, bf16[2,32,1024]{2,1,0:T(8,128)(2,1)S(1)}, u32[]{:S(2)}, u32[]{:S(2)}) collective-permute-start(bf16[2,32,1024]{2,1,0:T(8,128)(2,1)S(1)} %bitcast.11), channel_id=1, source_target_pairs={{0,16},{4,20},{8,24},{12,28},{16,0},{20,4},{24,8},{28,12},{1,17},{... | collective-permute-start | bytes 393224 | tf_op jit(solution)/shard_map/ppermute | solution.py:274
  50.8 8.6 %collective-permute-start.20 = (bf16[32,1024]{1,0:T(8,128)(2,1)S(1)}, bf16[32,1024]{1,0:T(8,128)(2,1)S(1)}, u32[]{:S(2)}, u32[]{:S(2)}) collective-permute-start(bf16[32,1024]{1,0:T(8,128)(2,1)S(1)} %slice_bitcast_fusion.1), channel_id=1, source_target_pairs={{0,4},{4,0},{8,12},{12,8},{16,20},{20,16},{24,28},{28,24},{1,5},{5... | collective-permute-start | bytes 196616 | tf_op jit(solution)/shard_map/ppermute | solution.py:274
  52.2 7.2 %collective-permute-start.17 = (bf16[1,32,1024]{2,1,0:T(8,128)(2,1)S(1)}, bf16[1,32,1024]{2,1,0:T(8,128)(2,1)S(1)}, u32[]{:S(2)}, u32[]{:S(2)}) collective-permute-start(bf16[1,32,1024]{2,1,0:T(8,128)(2,1)S(1)} %totals.18.refs_3_), channel_id=1, source_target_pairs={{0,24},{4,28},{8,16},{12,20},{16,8},{20,12},{24,0},{28,4},{1,25},{... | collective-permute-start | bytes 196616 | tf_op jit(solution)/shard_map/ppermute | solution.py:274
  53.5 5.9 %collective-permute-start.19 = (bf16[1,32,1024]{2,1,0:T(8,128)(2,1)S(1)}, bf16[1,32,1024]{2,1,0:T(8,128)(2,1)S(1)}, u32[]{:S(2)}, u32[]{:S(2)}) collective-permute-start(bf16[1,32,1024]{2,1,0:T(8,128)(2,1)S(1)} %totals.19), channel_id=1, source_target_pairs={{0,28},{4,24},{8,20},{12,16},{16,12},{20,8},{24,4},{28,0},{1,29},{... | collective-permute-start | bytes 196616 | tf_op jit(solution)/shard_map/ppermute | solution.py:274
  55.1 5.2 %collective-permute-start.22 = (bf16[32,1024]{1,0:T(8,128)(2,1)S(1)}, bf16[32,1024]{1,0:T(8,128)(2,1)S(1)}, u32[]{:S(2)}, u32[]{:S(2)}) collective-permute-start(bf16[32,1024]{1,0:T(8,128)(2,1)S(1)} %slice_bitcast_fusion), channel_id=1, source_target_pairs={{0,4},{4,0},{8,12},{12,8},{16,20},{20,16},{24,28},{28,24},{1,5},{5... | collective-permute-start | bytes 196616 | tf_op jit(solution)/shard_map/ppermute | solution.py:274

commit v10 on v9

--- a/solution.py
+++ b/solution.py
@@ -330,7 +330,7 @@
     for u in others:
         ready[u], sums[u] = later_steps(kept[u], come[u], [last])
         last = ready[u]
-    outs, _ = multiply(far, all_even, even_ints, after=[last, sums[first][-1][0], sums[mine][-1][0]])
+    outs, _ = multiply(far, all_even, even_ints, after=[last, sums[mine][-1][0]])
     kept.update(outs)
 
     shares = {}

time: 61.5 us -> 59.8 us (0.972)
  the two profiles are of different devices: /device:TPU:31 before, /device:TPU:0 now
where the time goes in v10:
time: 59.8 us; the launch traced here: 59.2 us
  starting transfers between devices  29.1 us (49%)
  Pallas kernels  19.9 us (33%)
  waiting for transfers between devices  8.35 us (14%)
  local copies, waits for them, and re-layouts  0.97 us (2%)
  other arithmetic  0.72 us (1%)
    pallas_call x5, Pallas kernels, product(): pl.pallas_call(functools.partial(product_kernel, plan), out_shape=[jax.Sh...  16.9 us
    ppermute x10, starting transfers between devices, swap_line(): lax.ppermute(value, 'narrow', [(n, n ^ mask) for n in range(devices)])  15.7 us
    ppermute x14, starting transfers between devices, swap(): return lax.ppermute(value, 'wide', [(w, w ^ j) for w in range(peers)])  13.5 us
    ppermute x14, waiting for transfers between devices, swap(): return lax.ppermute(value, 'wide', [(w, w ^ j) for w in range(peers)])  4.39 us
    ppermute x10, waiting for transfers between devices, swap_line(): lax.ppermute(value, 'narrow', [(n, n ^ mask) for n in range(devices)])  3.96 us
  transfers between devices with their start and end apart: 24, of which 4 were waited for; matrix products, arithmetic and copies ran while one was open for 0% of the time, Pallas kernels for 30%

profile of v10, /device:TPU:0, one launch (start us, length us, event | category | flops | bytes accessed | tf_op | source)
XLA Modules:
  0.0 59.2 jit_solution(4969795830441650461)
XLA Ops:
  0.0 0.7 %pad_add_fusion.tables_from = s32[7,8]{1,0:T(8,128)S(1)} fusion(s32[1,8]{1,0:T(1,128)} %bitcast.12, s32[2,8]{1,0:T(2,128)} %bitcast.14, s32[4,8]{1,0:T(4,128)} %bitcast.13), kind=kLoop, calls=%fused_computation.2 | loop fusion | flops 112 | bytes 448 | tf_op jit(solution)/shard_map/concatenate | solution.py:46
  0.7 0.9 %copy-done = bf16[32,4,1024]{2,1,0:T(4,128)(2,1)S(1)} copy-done((bf16[32,4,1024]{2,1,0:T(4,128)(2,1)S(1)}, bf16[32,4,1024]{2,1,0:T(4,128)(2,1)}, u32[]{:S(2)}) %copy-start) | copy-done | bytes 262168
  1.7 0.8 %pick.1 = (bf16[2,32,1024]{2,1,0:T(8,128)(2,1)S(1)}, bf16[2,32,1024]{2,1,0:T(8,128)(2,1)S(1)}, bf16[2,32,1024]{2,1,0:T(8,128)(2,1)S(1)}, bf16[2,32,1024]{2,1,0:T...) custom-call(s32[7,8]{1,0:T(8,128)S(1)} %pad_add_fusion.tables_from, ...), custom_call_target="tpu_custom_call" | custom-call | tf_op jit(solution)/shard_map/pick/pallas_call | solution.py:48
  2.5 0.5 collective-permute-start
  3.0 2.6 %collective-permute-start.2 = (bf16[2,32,1024]{2,1,0:T(8,128)(2,1)S(1)}, bf16[2,32,1024]{2,1,0:T(8,128)(2,1)S(1)}, u32[]{:S(2)}, u32[]{:S(2)}) collective-permute-start(bf16[2,32,1024]{2,1,0:T(8,128)(2,1)S(1)} %get-tuple-element.32), channel_id=1, source_target_pairs={{0,8},{4,12},{8,0},{12,4},{16,24},{20,28},{24,16},{28,20},{1,9},{5... | collective-permute-start | bytes 393224 | tf_op jit(solution)/shard_map/ppermute | solution.py:274
  5.6 0.1 collective-permute-start.3
  5.7 1.8 %collective-permute-start.4 = (bf16[2,32,1024]{2,1,0:T(8,128)(2,1)S(1)}, bf16[2,32,1024]{2,1,0:T(8,128)(2,1)S(1)}, u32[]{:S(2)}, u32[]{:S(2)}) collective-permute-start(bf16[2,32,1024]{2,1,0:T(8,128)(2,1)S(1)} %get-tuple-element.34), channel_id=1, source_target_pairs={{0,16},{4,20},{8,24},{12,28},{16,0},{20,4},{24,8},{28,12},{1,17},{... | collective-permute-start | bytes 393224 | tf_op jit(solution)/shard_map/ppermute | solution.py:274
  7.4 0.0 collective-permute-start.5
  7.4 4.7 %product.5 = (bf16[2,64,1024]{2,1,0:T(8,128)(2,1)S(1)}, bf16[2,2,1024,1024]{3,2,1,0:T(8,128)(2,1)S(1)}) custom-call(bf16[2,32,1024]{2,1,0:T(8,128)(2,1)S(1)} %get-tuple-element.29.refs_0_.refs_1_, bf16[2,32,1024]{2,1,0:T(8,128)(2,1)S(1)} %collective-permute-done.refs_1_.refs_2_, bf16[1,2,4096,1024]{3,2,1,0:T(8,128)(2,1)} %refs_6_.1), custom_call_target="tpu_custom_call" | custom-call | flops 2147483648 | bytes 8388608 | tf_op jit(solution)/shard_map/product/pallas_call | solution.py:151
  12.1 1.8 %collective-permute-start.1 = (bf16[2,64,1024]{2,1,0:T(8,128)(2,1)S(1)}, bf16[2,64,1024]{2,1,0:T(8,128)(2,1)S(1)}, u32[]{:S(2)}, u32[]{:S(2)}) collective-permute-start(bf16[2,64,1024]{2,1,0:T(8,128)(2,1)S(1)} %get-tuple-element.31.refs_0_), channel_id=1, source_target_pairs={{0,1},{1,0},{2,3},{3,2},{4,5},{5,4},{6,7},{7,6},{8,9},{9,8},{10,11... | collective-permute-start | bytes 786440 | tf_op jit(solution)/shard_map/ppermute | solution.py:277
  13.9 0.0 collective-permute-done.5.refs_4_.refs_6_
  13.9 3.5 %product.6 = (bf16[2,64,1024]{2,1,0:T(8,128)(2,1)S(1)}, bf16[2,64,1024]{2,1,0:T(8,128)(2,1)S(1)}, bf16[2,2,1024,1024]{3,2,1,0:T(8,128)(2,1)S(1)}, bf16[2,32,1024...) custom-call(bf16[2,64,1024]{2,1,0:T(8,128)(2,1)S(1)} %get-tuple-element.31.refs_0_, ...), custom_call_target="tpu_custom_call", output_to_operand_aliasing={{3}: (7, {}), {4}: (8, {})} | custom-call | flops 2147483648 | bytes 8388608 | tf_op jit(solution)/shard_map/product/pallas_call | solution.py:151
  17.4 0.0 copy-start.1
  17.5 1.6 %collective-permute-start.7 = (bf16[2,64,1024]{2,1,0:T(8,128)(2,1)S(1)}, bf16[2,64,1024]{2,1,0:T(8,128)(2,1)S(1)}, u32[]{:S(2)}, u32[]{:S(2)}) collective-permute-start(bf16[2,64,1024]{2,1,0:T(8,128)(2,1)S(1)} %get-tuple-element.43), channel_id=1, source_target_pairs={{0,1},{1,0},{2,3},{3,2},{4,5},{5,4},{6,7},{7,6},{8,9},{9,8},{10,11... | collective-permute-start | bytes 786440 | tf_op jit(solution)/shard_map/ppermute | solution.py:277
  19.1 2.4 %collective-permute-start.8 = (bf16[2,32,1024]{2,1,0:T(8,128)(2,1)S(1)}, bf16[2,32,1024]{2,1,0:T(8,128)(2,1)S(1)}, u32[]{:S(2)}, u32[]{:S(2)}) collective-permute-start(bf16[2,32,1024]{2,1,0:T(8,128)(2,1)S(1)} %get-tuple-element.45), channel_id=1, source_target_pairs={{0,24},{4,28},{8,16},{12,20},{16,8},{20,12},{24,0},{28,4},{1,25},{... | collective-permute-start | bytes 393224 | tf_op jit(solution)/shard_map/ppermute | solution.py:274
  21.5 0.0 collective-permute-start.9
  21.5 0.5 collective-permute-start.6
  22.0 3.1 %product.7 = (bf16[2,64,1024]{2,1,0:T(8,128)(2,1)S(1)}, bf16[2,64,1024]{2,1,0:T(8,128)(2,1)S(1)}, bf16[2,64,1024]{2,1,0:T(8,128)(2,1)S(1)}) custom-call(bf16[2,64,1024]{2,1,0:T(8,128)(2,1)S(1)} %collective-permute-done.1.refs_0_.refs_1_, bf16[2,32,1024]{2,1,0:T(8,128)(2,1)S(1)} %get-tuple-element.29.refs_0_.refs_1_, ...), custom_call_target="tpu_custom_call" | custom-call | flops 2147483648 | bytes 8388608 | tf_op jit(solution)/shard_map/product/pallas_call | solution.py:151
  25.2 0.7 %place.1.refs_2_.refs_8_ = bf16[256,256]{1,0:T(8,128)(2,1)S(1)} custom-call(s32[8]{0:T(128)S(1)} %copy-done.1, bf16[1,64,1024]{2,1,0:T(8,128)(2,1)S(1)} %totals.10.after), custom_call_target="tpu_custom_call" | custom-call | tf_op jit(solution)/shard_map/place/pallas_call | solution.py:220
  25.9 2.6 %collective-permute-start.10 = (bf16[1,64,1024]{2,1,0:T(8,128)(2,1)S(1)}, bf16[1,64,1024]{2,1,0:T(8,128)(2,1)S(1)}, u32[]{:S(2)}, u32[]{:S(2)}) collective-permute-start(bf16[1,64,1024]{2,1,0:T(8,128)(2,1)S(1)} %totals.10.after), channel_id=1, source_target_pairs={{0,2},{1,3},{2,0},{3,1},{4,6},{5,7},{6,4},{7,5},{8,10},{9,11},{10,... | collective-permute-start | bytes 393224 | tf_op jit(solution)/shard_map/ppermute | solution.py:277
  28.5 0.0 collective-permute-done.7.refs_1_
  28.6 1.2 %collective-permute-start.12 = (bf16[1,64,1024]{2,1,0:T(8,128)(2,1)S(1)}, bf16[1,64,1024]{2,1,0:T(8,128)(2,1)S(1)}, u32[]{:S(2)}, u32[]{:S(2)}) collective-permute-start(bf16[1,64,1024]{2,1,0:T(8,128)(2,1)S(1)} %totals.11.refs_0_), channel_id=1, source_target_pairs={{0,2},{1,3},{2,0},{3,1},{4,6},{5,7},{6,4},{7,5},{8,10},{9,11},{10,... | collective-permute-start | bytes 393224 | tf_op jit(solution)/shard_map/ppermute | solution.py:277
  29.8 0.0 collective-permute-done.8.refs_1_.refs_2_
  29.8 0.0 collective-permute-done.9.refs_2_.refs_3_
  29.8 2.8 %product.8 = (bf16[2,32,1024]{2,1,0:T(8,128)(2,1)S(1)}, bf16[2,32,1024]{2,1,0:T(8,128)(2,1)S(1)}) custom-call(bf16[1,64,1024]{2,1,0:T(8,128)(2,1)S(1)} %totals.11.refs_0_, bf16[2,32,1024]{2,1,0:T(8,128)(2,1)S(1)} %collective-permute-done.8.refs_1_.refs_2_, bf16[2,32,1024]{2,1,0:T(8,128)(2,1)S(1)} %collective-permute-done.9.refs_2_.refs_3_, ...), custom_call_target="tpu_custom_call" | custom-call | flops 2147483648 | bytes 8388608 | tf_op jit(solution)/shard_map/product/pallas_call | solution.py:151
  32.6 1.6 %collective-permute-start.11 = (bf16[2,32,1024]{2,1,0:T(8,128)(2,1)S(1)}, bf16[2,32,1024]{2,1,0:T(8,128)(2,1)S(1)}, u32[]{:S(2)}, u32[]{:S(2)}) collective-permute-start(bf16[2,32,1024]{2,1,0:T(8,128)(2,1)S(1)} %get-tuple-element.47.refs_2_), channel_id=1, source_target_pairs={{0,1},{1,0},{2,3},{3,2},{4,5},{5,4},{6,7},{7,6},{8,9},{9,8},{10,11... | collective-permute-start | bytes 393224 | tf_op jit(solution)/shard_map/ppermute | solution.py:277
  34.2 2.9 %collective-permute-done.6.refs_1_ = bf16[2,64,1024]{2,1,0:T(8,128)(2,1)S(1)} collective-permute-done((bf16[2,64,1024]{2,1,0:T(8,128)(2,1)S(1)}, bf16[2,64,1024]{2,1,0:T(8,128)(2,1)S(1)}, u32[]{:S(2)}, u32[]{:S(2)}) %collective-permute-start.6) | collective-permute-done | bytes 262176 | tf_op jit(solution)/shard_map/ppermute | solution.py:277
  37.1 0.1 collective-permute-start.14
  37.2 1.9 %collective-permute-start.15 = (bf16[2,32,1024]{2,1,0:T(8,128)(2,1)S(1)}, bf16[2,32,1024]{2,1,0:T(8,128)(2,1)S(1)}, u32[]{:S(2)}, u32[]{:S(2)}) collective-permute-start(bf16[2,32,1024]{2,1,0:T(8,128)(2,1)S(1)} %get-tuple-element.50), channel_id=1, source_target_pairs={{0,1},{1,0},{2,3},{3,2},{4,5},{5,4},{6,7},{7,6},{8,9},{9,8},{10,11... | collective-permute-start | bytes 393224 | tf_op jit(solution)/shard_map/ppermute | solution.py:277
  39.1 2.8 %product.9 = (bf16[2,32,1024]{2,1,0:T(8,128)(2,1)S(1)}, bf16[2,32,1024]{2,1,0:T(8,128)(2,1)S(1)}) custom-call(bf16[1,64,1024]{2,1,0:T(8,128)(2,1)S(1)} %totals.12.refs_0_, bf16[1,64,1024]{2,1,0:T(8,128)(2,1)S(1)} %collective-permute-done.10.refs_1_.refs_2_, bf16[2,32,1024]{2,1,0:T(8,128)(2,1)S(1)} %collective-permute-done.8.refs_1_.refs_2_, ...), custom_call_target="tpu_custom_call" | custom-call | flops 2147483648 | bytes 8388608 | tf_op jit(solution)/shard_map/product/pallas_call | solution.py:151
  41.9 0.1 totals.13.refs_2_
  42.0 1.5 %collective-permute-start.16 = (bf16[2,32,1024]{2,1,0:T(8,128)(2,1)S(1)}, bf16[2,32,1024]{2,1,0:T(8,128)(2,1)S(1)}, u32[]{:S(2)}, u32[]{:S(2)}) collective-permute-start(bf16[2,32,1024]{2,1,0:T(8,128)(2,1)S(1)} %bitcast.10), channel_id=1, source_target_pairs={{0,8},{4,12},{8,0},{12,4},{16,24},{20,28},{24,16},{28,20},{1,9},{5... | collective-permute-start | bytes 393224 | tf_op jit(solution)/shard_map/ppermute | solution.py:274
  43.5 0.0 collective-permute-done.11.refs_1_
  43.5 1.3 %collective-permute-start.13 = (bf16[1,32,1024]{2,1,0:T(8,128)(2,1)S(1)}, bf16[1,32,1024]{2,1,0:T(8,128)(2,1)S(1)}, u32[]{:S(2)}, u32[]{:S(2)}) collective-permute-start(bf16[1,32,1024]{2,1,0:T(8,128)(2,1)S(1)} %totals.14.refs_2_), channel_id=1, source_target_pairs={{0,2},{1,3},{2,0},{3,1},{4,6},{5,7},{6,4},{7,5},{8,10},{9,11},{10,... | collective-permute-start | bytes 196616 | tf_op jit(solution)/shard_map/ppermute | solution.py:277
  44.8 1.1 %collective-permute-done.15.refs_1_ = bf16[2,32,1024]{2,1,0:T(8,128)(2,1)S(1)} collective-permute-done((bf16[2,32,1024]{2,1,0:T(8,128)(2,1)S(1)}, bf16[2,32,1024]{2,1,0:T(8,128)(2,1)S(1)}, u32[]{:S(2)}, u32[]{:S(2)}) %collective-permute-start.15) | collective-permute-done | bytes 131104 | tf_op jit(solution)/shard_map/ppermute | solution.py:277
  45.9 3.1 %collective-permute-start.18 = (bf16[1,32,1024]{2,1,0:T(8,128)(2,1)S(1)}, bf16[1,32,1024]{2,1,0:T(8,128)(2,1)S(1)}, u32[]{:S(2)}, u32[]{:S(2)}) collective-permute-start(bf16[1,32,1024]{2,1,0:T(8,128)(2,1)S(1)} %totals.15.refs_3_), channel_id=1, source_target_pairs={{0,2},{1,3},{2,0},{3,1},{4,6},{5,7},{6,4},{7,5},{8,10},{9,11},{10,... | collective-permute-start | bytes 196616 | tf_op jit(solution)/shard_map/ppermute | solution.py:277
  49.0 0.1 totals.16
  49.1 0.1 collective-permute-start.23
  49.2 0.0 collective-permute-done.14.refs_2_
  49.2 0.1 totals.17.refs_3_
  49.2 1.6 %collective-permute-start.21 = (bf16[2,32,1024]{2,1,0:T(8,128)(2,1)S(1)}, bf16[2,32,1024]{2,1,0:T(8,128)(2,1)S(1)}, u32[]{:S(2)}, u32[]{:S(2)}) collective-permute-start(bf16[2,32,1024]{2,1,0:T(8,128)(2,1)S(1)} %bitcast.11), channel_id=1, source_target_pairs={{0,16},{4,20},{8,24},{12,28},{16,0},{20,4},{24,8},{28,12},{1,17},{... | collective-permute-start | bytes 393224 | tf_op jit(solution)/shard_map/ppermute | solution.py:274
  50.8 0.2 collective-permute-start.20
  51.0 0.0 collective-permute-done.13.refs_2_
  51.1 1.9 %collective-permute-start.17 = (bf16[1,32,1024]{2,1,0:T(8,128)(2,1)S(1)}, bf16[1,32,1024]{2,1,0:T(8,128)(2,1)S(1)}, u32[]{:S(2)}, u32[]{:S(2)}) collective-permute-start(bf16[1,32,1024]{2,1,0:T(8,128)(2,1)S(1)} %totals.18.refs_3_), channel_id=1, source_target_pairs={{0,24},{4,28},{8,16},{12,20},{16,8},{20,12},{24,0},{28,4},{1,25},{... | collective-permute-start | bytes 196616 | tf_op jit(solution)/shard_map/ppermute | solution.py:274
  53.1 0.8 %collective-permute-start.19 = (bf16[1,32,1024]{2,1,0:T(8,128)(2,1)S(1)}, bf16[1,32,1024]{2,1,0:T(8,128)(2,1)S(1)}, u32[]{:S(2)}, u32[]{:S(2)}) collective-permute-start(bf16[1,32,1024]{2,1,0:T(8,128)(2,1)S(1)} %totals.19), channel_id=1, source_target_pairs={{0,28},{4,24},{8,20},{12,16},{16,12},{20,8},{24,4},{28,0},{1,29},{... | collective-permute-start | bytes 196616 | tf_op jit(solution)/shard_map/ppermute | solution.py:274
  53.8 2.8 %collective-permute-done.21.refs_4_ = bf16[2,32,1024]{2,1,0:T(8,128)(2,1)S(1)} collective-permute-done((bf16[2,32,1024]{2,1,0:T(8,128)(2,1)S(1)}, bf16[2,32,1024]{2,1,0:T(8,128)(2,1)S(1)}, u32[]{:S(2)}, u32[]{:S(2)}) %collective-permute-start.21) | collective-permute-done | bytes 131104 | tf_op jit(solution)/shard_map/ppermute | solution.py:274
  56.6 1.6 %collective-permute-done.19.refs_1_ = bf16[1,32,1024]{2,1,0:T(8,128)(2,1)S(1)} collective-permute-done((bf16[1,32,1024]{2,1,0:T(8,128)(2,1)S(1)}, bf16[1,32,1024]{2,1,0:T(8,128)(2,1)S(1)}, u32[]{:S(2)}, u32[]{:S(2)}) %collective-permute-start.19) | collective-permute-done | bytes 65568 | tf_op jit(solution)/shard_map/ppermute | solution.py:274
  58.2 1.0 %order.1 = bf16[256,1024]{1,0:T(8,128)(2,1)} custom-call(bf16[1,32,1024]{2,1,0:T(8,128)(2,1)S(1)} %collective-permute-done.17.refs_0_, bf16[1,32,1024]{2,1,0:T(8,128)(2,1)S(1)} %collective-permute-done.19.refs_1_, bf16[2,32,1024]{2,1,0:T(8,128)(2,1)S(1)} %collective-permute-done.16.refs_4_.refs_2_, bf16[32,1024]{1,0:T(8,128)(2,1)S(1)} %collective-permute-done.20.refs_3_, ...), custom_call_target="tpu_custom_call" | custom-call | tf_op jit(solution)/shard_map/order/pallas_call | solution.py:250
  (25 shorter events, 0.2 us)
Async XLA Ops:
  0.7 0.9 %copy-start = (bf16[32,4,1024]{2,1,0:T(4,128)(2,1)S(1)}, bf16[32,4,1024]{2,1,0:T(4,128)(2,1)}, u32[]{:S(2)}) copy-start(bf16[32,4,1024]{2,1,0:T(4,128)(2,1)} %amps.1) | copy-start | bytes 786436
  2.5 4.9 %collective-permute-start = (bf16[2,32,1024]{2,1,0:T(8,128)(2,1)S(1)}, bf16[2,32,1024]{2,1,0:T(8,128)(2,1)S(1)}, u32[]{:S(2)}, u32[]{:S(2)}) collective-permute-start(bf16[2,32,1024]{2,1,0:T(8,128)(2,1)S(1)} %get-tuple-element.30), channel_id=1, source_target_pairs={{0,4},{4,0},{8,12},{12,8},{16,20},{20,16},{24,28},{28,24},{1,5},{5... | collective-permute-start | bytes 393224 | tf_op jit(solution)/shard_map/ppermute | solution.py:274
  3.0 10.9 %collective-permute-start.2 = (bf16[2,32,1024]{2,1,0:T(8,128)(2,1)S(1)}, bf16[2,32,1024]{2,1,0:T(8,128)(2,1)S(1)}, u32[]{:S(2)}, u32[]{:S(2)}) collective-permute-start(bf16[2,32,1024]{2,1,0:T(8,128)(2,1)S(1)} %get-tuple-element.32), channel_id=1, source_target_pairs={{0,8},{4,12},{8,0},{12,4},{16,24},{20,28},{24,16},{28,20},{1,9},{5... | collective-permute-start | bytes 393224 | tf_op jit(solution)/shard_map/ppermute | solution.py:274
  5.6 8.3 %collective-permute-start.3 = (bf16[2,32,1024]{2,1,0:T(8,128)(2,1)S(1)}, bf16[2,32,1024]{2,1,0:T(8,128)(2,1)S(1)}, u32[]{:S(2)}, u32[]{:S(2)}) collective-permute-start(bf16[2,32,1024]{2,1,0:T(8,128)(2,1)S(1)} %get-tuple-element.33), channel_id=1, source_target_pairs={{0,12},{4,8},{8,4},{12,0},{16,28},{20,24},{24,20},{28,16},{1,13},{... | collective-permute-start | bytes 393224 | tf_op jit(solution)/shard_map/ppermute | solution.py:274
  5.7 8.3 %collective-permute-start.4 = (bf16[2,32,1024]{2,1,0:T(8,128)(2,1)S(1)}, bf16[2,32,1024]{2,1,0:T(8,128)(2,1)S(1)}, u32[]{:S(2)}, u32[]{:S(2)}) collective-permute-start(bf16[2,32,1024]{2,1,0:T(8,128)(2,1)S(1)} %get-tuple-element.34), channel_id=1, source_target_pairs={{0,16},{4,20},{8,24},{12,28},{16,0},{20,4},{24,8},{28,12},{1,17},{... | collective-permute-start | bytes 393224 | tf_op jit(solution)/shard_map/ppermute | solution.py:274
  7.4 6.5 %collective-permute-start.5 = (bf16[2,32,1024]{2,1,0:T(8,128)(2,1)S(1)}, bf16[2,32,1024]{2,1,0:T(8,128)(2,1)S(1)}, u32[]{:S(2)}, u32[]{:S(2)}) collective-permute-start(bf16[2,32,1024]{2,1,0:T(8,128)(2,1)S(1)} %get-tuple-element.35), channel_id=1, source_target_pairs={{0,20},{4,16},{8,28},{12,24},{16,4},{20,0},{24,12},{28,8},{1,21},{... | collective-permute-start | bytes 393224 | tf_op jit(solution)/shard_map/ppermute | solution.py:274
  12.1 9.9 %collective-permute-start.1 = (bf16[2,64,1024]{2,1,0:T(8,128)(2,1)S(1)}, bf16[2,64,1024]{2,1,0:T(8,128)(2,1)S(1)}, u32[]{:S(2)}, u32[]{:S(2)}) collective-permute-start(bf16[2,64,1024]{2,1,0:T(8,128)(2,1)S(1)} %get-tuple-element.31.refs_0_), channel_id=1, source_target_pairs={{0,1},{1,0},{2,3},{3,2},{4,5},{5,4},{6,7},{7,6},{8,9},{9,8},{10,11... | collective-permute-start | bytes 786440 | tf_op jit(solution)/shard_map/ppermute | solution.py:277
  17.4 7.8 %copy-start.1 = (s32[8]{0:T(128)S(1)}, s32[8]{0:T(128)}, u32[]{:S(2)}) copy-start(s32[8]{0:T(128)} %q_owner.1) | copy-start | bytes 100
  17.5 11.1 %collective-permute-start.7 = (bf16[2,64,1024]{2,1,0:T(8,128)(2,1)S(1)}, bf16[2,64,1024]{2,1,0:T(8,128)(2,1)S(1)}, u32[]{:S(2)}, u32[]{:S(2)}) collective-permute-start(bf16[2,64,1024]{2,1,0:T(8,128)(2,1)S(1)} %get-tuple-element.43), channel_id=1, source_target_pairs={{0,1},{1,0},{2,3},{3,2},{4,5},{5,4},{6,7},{7,6},{8,9},{9,8},{10,11... | collective-permute-start | bytes 786440 | tf_op jit(solution)/shard_map/ppermute | solution.py:277
  19.1 10.7 %collective-permute-start.8 = (bf16[2,32,1024]{2,1,0:T(8,128)(2,1)S(1)}, bf16[2,32,1024]{2,1,0:T(8,128)(2,1)S(1)}, u32[]{:S(2)}, u32[]{:S(2)}) collective-permute-start(bf16[2,32,1024]{2,1,0:T(8,128)(2,1)S(1)} %get-tuple-element.45), channel_id=1, source_target_pairs={{0,24},{4,28},{8,16},{12,20},{16,8},{20,12},{24,0},{28,4},{1,25},{... | collective-permute-start | bytes 393224 | tf_op jit(solution)/shard_map/ppermute | solution.py:274
  21.5 8.2 %collective-permute-start.9 = (bf16[2,32,1024]{2,1,0:T(8,128)(2,1)S(1)}, bf16[2,32,1024]{2,1,0:T(8,128)(2,1)S(1)}, u32[]{:S(2)}, u32[]{:S(2)}) collective-permute-start(bf16[2,32,1024]{2,1,0:T(8,128)(2,1)S(1)} %get-tuple-element.46), channel_id=1, source_target_pairs={{0,28},{4,24},{8,20},{12,16},{16,12},{20,8},{24,4},{28,0},{1,29},{... | collective-permute-start | bytes 393224 | tf_op jit(solution)/shard_map/ppermute | solution.py:274
  21.5 15.6 %collective-permute-start.6 = (bf16[2,64,1024]{2,1,0:T(8,128)(2,1)S(1)}, bf16[2,64,1024]{2,1,0:T(8,128)(2,1)S(1)}, u32[]{:S(2)}, u32[]{:S(2)}) collective-permute-start(bf16[2,64,1024]{2,1,0:T(8,128)(2,1)S(1)} %get-tuple-element.41), channel_id=1, source_target_pairs={{0,1},{1,0},{2,3},{3,2},{4,5},{5,4},{6,7},{7,6},{8,9},{9,8},{10,11... | collective-permute-start | bytes 786440 | tf_op jit(solution)/shard_map/ppermute | solution.py:277
  25.9 13.2 %collective-permute-start.10 = (bf16[1,64,1024]{2,1,0:T(8,128)(2,1)S(1)}, bf16[1,64,1024]{2,1,0:T(8,128)(2,1)S(1)}, u32[]{:S(2)}, u32[]{:S(2)}) collective-permute-start(bf16[1,64,1024]{2,1,0:T(8,128)(2,1)S(1)} %totals.10.after), channel_id=1, source_target_pairs={{0,2},{1,3},{2,0},{3,1},{4,6},{5,7},{6,4},{7,5},{8,10},{9,11},{10,... | collective-permute-start | bytes 393224 | tf_op jit(solution)/shard_map/ppermute | solution.py:277
  28.6 13.3 %collective-permute-start.12 = (bf16[1,64,1024]{2,1,0:T(8,128)(2,1)S(1)}, bf16[1,64,1024]{2,1,0:T(8,128)(2,1)S(1)}, u32[]{:S(2)}, u32[]{:S(2)}) collective-permute-start(bf16[1,64,1024]{2,1,0:T(8,128)(2,1)S(1)} %totals.11.refs_0_), channel_id=1, source_target_pairs={{0,2},{1,3},{2,0},{3,1},{4,6},{5,7},{6,4},{7,5},{8,10},{9,11},{10,... | collective-permute-start | bytes 393224 | tf_op jit(solution)/shard_map/ppermute | solution.py:277
  32.6 10.9 %collective-permute-start.11 = (bf16[2,32,1024]{2,1,0:T(8,128)(2,1)S(1)}, bf16[2,32,1024]{2,1,0:T(8,128)(2,1)S(1)}, u32[]{:S(2)}, u32[]{:S(2)}) collective-permute-start(bf16[2,32,1024]{2,1,0:T(8,128)(2,1)S(1)} %get-tuple-element.47.refs_2_), channel_id=1, source_target_pairs={{0,1},{1,0},{2,3},{3,2},{4,5},{5,4},{6,7},{7,6},{8,9},{9,8},{10,11... | collective-permute-start | bytes 393224 | tf_op jit(solution)/shard_map/ppermute | solution.py:277
  37.1 12.0 %collective-permute-start.14 = (bf16[1,64,1024]{2,1,0:T(8,128)(2,1)S(1)}, bf16[1,64,1024]{2,1,0:T(8,128)(2,1)S(1)}, u32[]{:S(2)}, u32[]{:S(2)}) collective-permute-start(bf16[1,64,1024]{2,1,0:T(8,128)(2,1)S(1)} %totals.12.refs_0_), channel_id=1, source_target_pairs={{0,2},{1,3},{2,0},{3,1},{4,6},{5,7},{6,4},{7,5},{8,10},{9,11},{10,... | collective-permute-start | bytes 393224 | tf_op jit(solution)/shard_map/ppermute | solution.py:277
  37.2 8.7 %collective-permute-start.15 = (bf16[2,32,1024]{2,1,0:T(8,128)(2,1)S(1)}, bf16[2,32,1024]{2,1,0:T(8,128)(2,1)S(1)}, u32[]{:S(2)}, u32[]{:S(2)}) collective-permute-start(bf16[2,32,1024]{2,1,0:T(8,128)(2,1)S(1)} %get-tuple-element.50), channel_id=1, source_target_pairs={{0,1},{1,0},{2,3},{3,2},{4,5},{5,4},{6,7},{7,6},{8,9},{9,8},{10,11... | collective-permute-start | bytes 393224 | tf_op jit(solution)/shard_map/ppermute | solution.py:277
  42.0 7.2 %collective-permute-start.16 = (bf16[2,32,1024]{2,1,0:T(8,128)(2,1)S(1)}, bf16[2,32,1024]{2,1,0:T(8,128)(2,1)S(1)}, u32[]{:S(2)}, u32[]{:S(2)}) collective-permute-start(bf16[2,32,1024]{2,1,0:T(8,128)(2,1)S(1)} %bitcast.10), channel_id=1, source_target_pairs={{0,8},{4,12},{8,0},{12,4},{16,24},{20,28},{24,16},{28,20},{1,9},{5... | collective-permute-start | bytes 393224 | tf_op jit(solution)/shard_map/ppermute | solution.py:274
  43.5 7.5 %collective-permute-start.13 = (bf16[1,32,1024]{2,1,0:T(8,128)(2,1)S(1)}, bf16[1,32,1024]{2,1,0:T(8,128)(2,1)S(1)}, u32[]{:S(2)}, u32[]{:S(2)}) collective-permute-start(bf16[1,32,1024]{2,1,0:T(8,128)(2,1)S(1)} %totals.14.refs_2_), channel_id=1, source_target_pairs={{0,2},{1,3},{2,0},{3,1},{4,6},{5,7},{6,4},{7,5},{8,10},{9,11},{10,... | collective-permute-start | bytes 196616 | tf_op jit(solution)/shard_map/ppermute | solution.py:277
  45.9 7.1 %collective-permute-start.18 = (bf16[1,32,1024]{2,1,0:T(8,128)(2,1)S(1)}, bf16[1,32,1024]{2,1,0:T(8,128)(2,1)S(1)}, u32[]{:S(2)}, u32[]{:S(2)}) collective-permute-start(bf16[1,32,1024]{2,1,0:T(8,128)(2,1)S(1)} %totals.15.refs_3_), channel_id=1, source_target_pairs={{0,2},{1,3},{2,0},{3,1},{4,6},{5,7},{6,4},{7,5},{8,10},{9,11},{10,... | collective-permute-start | bytes 196616 | tf_op jit(solution)/shard_map/ppermute | solution.py:277
  49.1 7.5 %collective-permute-start.23 = (bf16[32,1024]{1,0:T(8,128)(2,1)S(1)}, bf16[32,1024]{1,0:T(8,128)(2,1)S(1)}, u32[]{:S(2)}, u32[]{:S(2)}) collective-permute-start(bf16[32,1024]{1,0:T(8,128)(2,1)S(1)} %get-tuple-element.51.refs_3_), channel_id=1, source_target_pairs={{0,4},{4,0},{8,12},{12,8},{16,20},{20,16},{24,28},{28,24},{1,5},{5... | collective-permute-start | bytes 196616 | tf_op jit(solution)/shard_map/ppermute | solution.py:274
  49.2 7.3 %collective-permute-start.21 = (bf16[2,32,1024]{2,1,0:T(8,128)(2,1)S(1)}, bf16[2,32,1024]{2,1,0:T(8,128)(2,1)S(1)}, u32[]{:S(2)}, u32[]{:S(2)}) collective-permute-start(bf16[2,32,1024]{2,1,0:T(8,128)(2,1)S(1)} %bitcast.11), channel_id=1, source_target_pairs={{0,16},{4,20},{8,24},{12,28},{16,0},{20,4},{24,8},{28,12},{1,17},{... | collective-permute-start | bytes 393224 | tf_op jit(solution)/shard_map/ppermute | solution.py:274
  50.8 5.8 %collective-permute-start.20 = (bf16[32,1024]{1,0:T(8,128)(2,1)S(1)}, bf16[32,1024]{1,0:T(8,128)(2,1)S(1)}, u32[]{:S(2)}, u32[]{:S(2)}) collective-permute-start(bf16[32,1024]{1,0:T(8,128)(2,1)S(1)} %slice_bitcast_fusion.1), channel_id=1, source_target_pairs={{0,4},{4,0},{8,12},{12,8},{16,20},{20,16},{24,28},{28,24},{1,5},{5... | collective-permute-start | bytes 196616 | tf_op jit(solution)/shard_map/ppermute | solution.py:274
  51.1 7.1 %collective-permute-start.17 = (bf16[1,32,1024]{2,1,0:T(8,128)(2,1)S(1)}, bf16[1,32,1024]{2,1,0:T(8,128)(2,1)S(1)}, u32[]{:S(2)}, u32[]{:S(2)}) collective-permute-start(bf16[1,32,1024]{2,1,0:T(8,128)(2,1)S(1)} %totals.18.refs_3_), channel_id=1, source_target_pairs={{0,24},{4,28},{8,16},{12,20},{16,8},{20,12},{24,0},{28,4},{1,25},{... | collective-permute-start | bytes 196616 | tf_op jit(solution)/shard_map/ppermute | solution.py:274
  53.1 5.1 %collective-permute-start.19 = (bf16[1,32,1024]{2,1,0:T(8,128)(2,1)S(1)}, bf16[1,32,1024]{2,1,0:T(8,128)(2,1)S(1)}, u32[]{:S(2)}, u32[]{:S(2)}) collective-permute-start(bf16[1,32,1024]{2,1,0:T(8,128)(2,1)S(1)} %totals.19), channel_id=1, source_target_pairs={{0,28},{4,24},{8,20},{12,16},{16,12},{20,8},{24,4},{28,0},{1,29},{... | collective-permute-start | bytes 196616 | tf_op jit(solution)/shard_map/ppermute | solution.py:274
  56.6 1.6 %collective-permute-start.22 = (bf16[32,1024]{1,0:T(8,128)(2,1)S(1)}, bf16[32,1024]{1,0:T(8,128)(2,1)S(1)}, u32[]{:S(2)}, u32[]{:S(2)}) collective-permute-start(bf16[32,1024]{1,0:T(8,128)(2,1)S(1)} %slice_bitcast_fusion), channel_id=1, source_target_pairs={{0,4},{4,0},{8,12},{12,8},{16,20},{20,16},{24,28},{28,24},{1,5},{5... | collective-permute-start | bytes 196616 | tf_op jit(solution)/shard_map/ppermute | solution.py:274

commit v11 on v10

--- a/solution.py
+++ b/solution.py
@@ -8,7 +8,7 @@
 from jax.sharding import PartitionSpec as P
 
 PART = 512
-AHEAD = 3
+AHEAD = 4
 COST = 1
 LIMIT = 30 << 20
 FIRST = 40 << 20

time: 59.8 us -> 59.8 us (level)
  no operation moved by 1% of the time
where the time goes in v11:
time: 59.8 us; the launch traced here: 59.3 us
  starting transfers between devices  29.1 us (49%)
  Pallas kernels  19.8 us (33%)
  waiting for transfers between devices  8.39 us (14%)
  local copies, waits for them, and re-layouts  0.97 us (2%)
  other arithmetic  0.72 us (1%)
    pallas_call x5, Pallas kernels, product(): pl.pallas_call(functools.partial(product_kernel, plan), out_shape=[jax.Sh...  16.9 us
    ppermute x10, starting transfers between devices, swap_line(): lax.ppermute(value, 'narrow', [(n, n ^ mask) for n in range(devices)])  15.7 us
    ppermute x14, starting transfers between devices, swap(): return lax.ppermute(value, 'wide', [(w, w ^ j) for w in range(peers)])  13.4 us
    ppermute x14, waiting for transfers between devices, swap(): return lax.ppermute(value, 'wide', [(w, w ^ j) for w in range(peers)])  4.41 us
    ppermute x10, waiting for transfers between devices, swap_line(): lax.ppermute(value, 'narrow', [(n, n ^ mask) for n in range(devices)])  3.99 us
  transfers between devices with their start and end apart: 24, of which 4 were waited for; matrix products, arithmetic and copies ran while one was open for 0% of the time, Pallas kernels for 30%

profile of v11, /device:TPU:0, one launch (start us, length us, event | category | flops | bytes accessed | tf_op | source)
XLA Modules:
  0.0 59.3 jit_solution(310793852590795068)
XLA Ops:
  0.0 0.7 %pad_add_fusion.tables_from = s32[7,8]{1,0:T(8,128)S(1)} fusion(s32[1,8]{1,0:T(1,128)} %bitcast.12, s32[2,8]{1,0:T(2,128)} %bitcast.14, s32[4,8]{1,0:T(4,128)} %bitcast.13), kind=kLoop, calls=%fused_computation.2 | loop fusion | flops 112 | bytes 448 | tf_op jit(solution)/shard_map/concatenate | solution.py:46
  0.7 0.9 %copy-done = bf16[32,4,1024]{2,1,0:T(4,128)(2,1)S(1)} copy-done((bf16[32,4,1024]{2,1,0:T(4,128)(2,1)S(1)}, bf16[32,4,1024]{2,1,0:T(4,128)(2,1)}, u32[]{:S(2)}) %copy-start) | copy-done | bytes 262168
  1.7 0.8 %pick.1 = (bf16[2,32,1024]{2,1,0:T(8,128)(2,1)S(1)}, bf16[2,32,1024]{2,1,0:T(8,128)(2,1)S(1)}, bf16[2,32,1024]{2,1,0:T(8,128)(2,1)S(1)}, bf16[2,32,1024]{2,1,0:T...) custom-call(s32[7,8]{1,0:T(8,128)S(1)} %pad_add_fusion.tables_from, ...), custom_call_target="tpu_custom_call" | custom-call | tf_op jit(solution)/shard_map/pick/pallas_call | solution.py:48
  2.5 0.5 collective-permute-start
  3.0 2.6 %collective-permute-start.2 = (bf16[2,32,1024]{2,1,0:T(8,128)(2,1)S(1)}, bf16[2,32,1024]{2,1,0:T(8,128)(2,1)S(1)}, u32[]{:S(2)}, u32[]{:S(2)}) collective-permute-start(bf16[2,32,1024]{2,1,0:T(8,128)(2,1)S(1)} %get-tuple-element.32), channel_id=1, source_target_pairs={{0,8},{4,12},{8,0},{12,4},{16,24},{20,28},{24,16},{28,20},{1,9},{5... | collective-permute-start | bytes 393224 | tf_op jit(solution)/shard_map/ppermute | solution.py:274
  5.6 0.1 collective-permute-start.3
  5.7 1.8 %collective-permute-start.4 = (bf16[2,32,1024]{2,1,0:T(8,128)(2,1)S(1)}, bf16[2,32,1024]{2,1,0:T(8,128)(2,1)S(1)}, u32[]{:S(2)}, u32[]{:S(2)}) collective-permute-start(bf16[2,32,1024]{2,1,0:T(8,128)(2,1)S(1)} %get-tuple-element.34), channel_id=1, source_target_pairs={{0,16},{4,20},{8,24},{12,28},{16,0},{20,4},{24,8},{28,12},{1,17},{... | collective-permute-start | bytes 393224 | tf_op jit(solution)/shard_map/ppermute | solution.py:274
  7.4 0.0 collective-permute-start.5
  7.4 4.7 %product.5 = (bf16[2,64,1024]{2,1,0:T(8,128)(2,1)S(1)}, bf16[2,2,1024,1024]{3,2,1,0:T(8,128)(2,1)S(1)}) custom-call(bf16[2,32,1024]{2,1,0:T(8,128)(2,1)S(1)} %get-tuple-element.29.refs_0_.refs_1_, bf16[2,32,1024]{2,1,0:T(8,128)(2,1)S(1)} %collective-permute-done.refs_1_.refs_2_, bf16[1,2,4096,1024]{3,2,1,0:T(8,128)(2,1)} %refs_6_.1), custom_call_target="tpu_custom_call" | custom-call | flops 2147483648 | bytes 8388608 | tf_op jit(solution)/shard_map/product/pallas_call | solution.py:151
  12.1 1.8 %collective-permute-start.1 = (bf16[2,64,1024]{2,1,0:T(8,128)(2,1)S(1)}, bf16[2,64,1024]{2,1,0:T(8,128)(2,1)S(1)}, u32[]{:S(2)}, u32[]{:S(2)}) collective-permute-start(bf16[2,64,1024]{2,1,0:T(8,128)(2,1)S(1)} %get-tuple-element.31.refs_0_), channel_id=1, source_target_pairs={{0,1},{1,0},{2,3},{3,2},{4,5},{5,4},{6,7},{7,6},{8,9},{9,8},{10,11... | collective-permute-start | bytes 786440 | tf_op jit(solution)/shard_map/ppermute | solution.py:277
  13.9 0.0 collective-permute-done.5.refs_4_.refs_6_
  13.9 3.5 %product.6 = (bf16[2,64,1024]{2,1,0:T(8,128)(2,1)S(1)}, bf16[2,64,1024]{2,1,0:T(8,128)(2,1)S(1)}, bf16[2,2,1024,1024]{3,2,1,0:T(8,128)(2,1)S(1)}, bf16[2,32,1024...) custom-call(bf16[2,64,1024]{2,1,0:T(8,128)(2,1)S(1)} %get-tuple-element.31.refs_0_, ...), custom_call_target="tpu_custom_call", output_to_operand_aliasing={{3}: (7, {}), {4}: (8, {})} | custom-call | flops 2147483648 | bytes 8388608 | tf_op jit(solution)/shard_map/product/pallas_call | solution.py:151
  17.4 0.0 copy-start.1
  17.5 1.6 %collective-permute-start.7 = (bf16[2,64,1024]{2,1,0:T(8,128)(2,1)S(1)}, bf16[2,64,1024]{2,1,0:T(8,128)(2,1)S(1)}, u32[]{:S(2)}, u32[]{:S(2)}) collective-permute-start(bf16[2,64,1024]{2,1,0:T(8,128)(2,1)S(1)} %get-tuple-element.43), channel_id=1, source_target_pairs={{0,1},{1,0},{2,3},{3,2},{4,5},{5,4},{6,7},{7,6},{8,9},{9,8},{10,11... | collective-permute-start | bytes 786440 | tf_op jit(solution)/shard_map/ppermute | solution.py:277
  19.1 2.4 %collective-permute-start.8 = (bf16[2,32,1024]{2,1,0:T(8,128)(2,1)S(1)}, bf16[2,32,1024]{2,1,0:T(8,128)(2,1)S(1)}, u32[]{:S(2)}, u32[]{:S(2)}) collective-permute-start(bf16[2,32,1024]{2,1,0:T(8,128)(2,1)S(1)} %get-tuple-element.45), channel_id=1, source_target_pairs={{0,24},{4,28},{8,16},{12,20},{16,8},{20,12},{24,0},{28,4},{1,25},{... | collective-permute-start | bytes 393224 | tf_op jit(solution)/shard_map/ppermute | solution.py:274
  21.5 0.0 collective-permute-start.9
  21.5 0.5 collective-permute-start.6
  22.0 3.1 %product.7 = (bf16[2,64,1024]{2,1,0:T(8,128)(2,1)S(1)}, bf16[2,64,1024]{2,1,0:T(8,128)(2,1)S(1)}, bf16[2,64,1024]{2,1,0:T(8,128)(2,1)S(1)}) custom-call(bf16[2,64,1024]{2,1,0:T(8,128)(2,1)S(1)} %collective-permute-done.1.refs_0_.refs_1_, bf16[2,32,1024]{2,1,0:T(8,128)(2,1)S(1)} %get-tuple-element.29.refs_0_.refs_1_, ...), custom_call_target="tpu_custom_call" | custom-call | flops 2147483648 | bytes 8388608 | tf_op jit(solution)/shard_map/product/pallas_call | solution.py:151
  25.2 0.7 %place.1.refs_2_.refs_8_ = bf16[256,256]{1,0:T(8,128)(2,1)S(1)} custom-call(s32[8]{0:T(128)S(1)} %copy-done.1, bf16[1,64,1024]{2,1,0:T(8,128)(2,1)S(1)} %totals.10.after), custom_call_target="tpu_custom_call" | custom-call | tf_op jit(solution)/shard_map/place/pallas_call | solution.py:220
  25.9 2.7 %collective-permute-start.10 = (bf16[1,64,1024]{2,1,0:T(8,128)(2,1)S(1)}, bf16[1,64,1024]{2,1,0:T(8,128)(2,1)S(1)}, u32[]{:S(2)}, u32[]{:S(2)}) collective-permute-start(bf16[1,64,1024]{2,1,0:T(8,128)(2,1)S(1)} %totals.10.after), channel_id=1, source_target_pairs={{0,2},{1,3},{2,0},{3,1},{4,6},{5,7},{6,4},{7,5},{8,10},{9,11},{10,... | collective-permute-start | bytes 393224 | tf_op jit(solution)/shard_map/ppermute | solution.py:277
  28.5 0.0 collective-permute-done.7.refs_1_
  28.6 1.2 %collective-permute-start.12 = (bf16[1,64,1024]{2,1,0:T(8,128)(2,1)S(1)}, bf16[1,64,1024]{2,1,0:T(8,128)(2,1)S(1)}, u32[]{:S(2)}, u32[]{:S(2)}) collective-permute-start(bf16[1,64,1024]{2,1,0:T(8,128)(2,1)S(1)} %totals.11.refs_0_), channel_id=1, source_target_pairs={{0,2},{1,3},{2,0},{3,1},{4,6},{5,7},{6,4},{7,5},{8,10},{9,11},{10,... | collective-permute-start | bytes 393224 | tf_op jit(solution)/shard_map/ppermute | solution.py:277
  29.8 0.0 collective-permute-done.8.refs_1_.refs_2_
  29.8 0.0 collective-permute-done.9.refs_2_.refs_3_
  29.8 2.8 %product.8 = (bf16[2,32,1024]{2,1,0:T(8,128)(2,1)S(1)}, bf16[2,32,1024]{2,1,0:T(8,128)(2,1)S(1)}) custom-call(bf16[1,64,1024]{2,1,0:T(8,128)(2,1)S(1)} %totals.11.refs_0_, bf16[2,32,1024]{2,1,0:T(8,128)(2,1)S(1)} %collective-permute-done.8.refs_1_.refs_2_, bf16[2,32,1024]{2,1,0:T(8,128)(2,1)S(1)} %collective-permute-done.9.refs_2_.refs_3_, ...), custom_call_target="tpu_custom_call" | custom-call | flops 2147483648 | bytes 8388608 | tf_op jit(solution)/shard_map/product/pallas_call | solution.py:151
  32.6 1.6 %collective-permute-start.11 = (bf16[2,32,1024]{2,1,0:T(8,128)(2,1)S(1)}, bf16[2,32,1024]{2,1,0:T(8,128)(2,1)S(1)}, u32[]{:S(2)}, u32[]{:S(2)}) collective-permute-start(bf16[2,32,1024]{2,1,0:T(8,128)(2,1)S(1)} %get-tuple-element.47.refs_2_), channel_id=1, source_target_pairs={{0,1},{1,0},{2,3},{3,2},{4,5},{5,4},{6,7},{7,6},{8,9},{9,8},{10,11... | collective-permute-start | bytes 393224 | tf_op jit(solution)/shard_map/ppermute | solution.py:277
  34.2 2.8 %collective-permute-done.6.refs_1_ = bf16[2,64,1024]{2,1,0:T(8,128)(2,1)S(1)} collective-permute-done((bf16[2,64,1024]{2,1,0:T(8,128)(2,1)S(1)}, bf16[2,64,1024]{2,1,0:T(8,128)(2,1)S(1)}, u32[]{:S(2)}, u32[]{:S(2)}) %collective-permute-start.6) | collective-permute-done | bytes 262176 | tf_op jit(solution)/shard_map/ppermute | solution.py:277
  37.1 0.1 collective-permute-start.14
  37.2 1.9 %collective-permute-start.15 = (bf16[2,32,1024]{2,1,0:T(8,128)(2,1)S(1)}, bf16[2,32,1024]{2,1,0:T(8,128)(2,1)S(1)}, u32[]{:S(2)}, u32[]{:S(2)}) collective-permute-start(bf16[2,32,1024]{2,1,0:T(8,128)(2,1)S(1)} %get-tuple-element.50), channel_id=1, source_target_pairs={{0,1},{1,0},{2,3},{3,2},{4,5},{5,4},{6,7},{7,6},{8,9},{9,8},{10,11... | collective-permute-start | bytes 393224 | tf_op jit(solution)/shard_map/ppermute | solution.py:277
  39.1 0.0 collective-permute-done.10.refs_1_.refs_2_
  39.1 2.8 %product.9 = (bf16[2,32,1024]{2,1,0:T(8,128)(2,1)S(1)}, bf16[2,32,1024]{2,1,0:T(8,128)(2,1)S(1)}) custom-call(bf16[1,64,1024]{2,1,0:T(8,128)(2,1)S(1)} %totals.12.refs_0_, bf16[1,64,1024]{2,1,0:T(8,128)(2,1)S(1)} %collective-permute-done.10.refs_1_.refs_2_, bf16[2,32,1024]{2,1,0:T(8,128)(2,1)S(1)} %collective-permute-done.8.refs_1_.refs_2_, ...), custom_call_target="tpu_custom_call" | custom-call | flops 2147483648 | bytes 8388608 | tf_op jit(solution)/shard_map/product/pallas_call | solution.py:151
  41.9 0.1 totals.13.refs_2_
  42.0 1.5 %collective-permute-start.16 = (bf16[2,32,1024]{2,1,0:T(8,128)(2,1)S(1)}, bf16[2,32,1024]{2,1,0:T(8,128)(2,1)S(1)}, u32[]{:S(2)}, u32[]{:S(2)}) collective-permute-start(bf16[2,32,1024]{2,1,0:T(8,128)(2,1)S(1)} %bitcast.10), channel_id=1, source_target_pairs={{0,8},{4,12},{8,0},{12,4},{16,24},{20,28},{24,16},{28,20},{1,9},{5... | collective-permute-start | bytes 393224 | tf_op jit(solution)/shard_map/ppermute | solution.py:274
  43.5 1.3 %collective-permute-start.13 = (bf16[1,32,1024]{2,1,0:T(8,128)(2,1)S(1)}, bf16[1,32,1024]{2,1,0:T(8,128)(2,1)S(1)}, u32[]{:S(2)}, u32[]{:S(2)}) collective-permute-start(bf16[1,32,1024]{2,1,0:T(8,128)(2,1)S(1)} %totals.14.refs_2_), channel_id=1, source_target_pairs={{0,2},{1,3},{2,0},{3,1},{4,6},{5,7},{6,4},{7,5},{8,10},{9,11},{10,... | collective-permute-start | bytes 196616 | tf_op jit(solution)/shard_map/ppermute | solution.py:277
  44.8 1.1 %collective-permute-done.15.refs_1_ = bf16[2,32,1024]{2,1,0:T(8,128)(2,1)S(1)} collective-permute-done((bf16[2,32,1024]{2,1,0:T(8,128)(2,1)S(1)}, bf16[2,32,1024]{2,1,0:T(8,128)(2,1)S(1)}, u32[]{:S(2)}, u32[]{:S(2)}) %collective-permute-start.15) | collective-permute-done | bytes 131104 | tf_op jit(solution)/shard_map/ppermute | solution.py:277
  45.9 3.1 %collective-permute-start.18 = (bf16[1,32,1024]{2,1,0:T(8,128)(2,1)S(1)}, bf16[1,32,1024]{2,1,0:T(8,128)(2,1)S(1)}, u32[]{:S(2)}, u32[]{:S(2)}) collective-permute-start(bf16[1,32,1024]{2,1,0:T(8,128)(2,1)S(1)} %totals.15.refs_3_), channel_id=1, source_target_pairs={{0,2},{1,3},{2,0},{3,1},{4,6},{5,7},{6,4},{7,5},{8,10},{9,11},{10,... | collective-permute-start | bytes 196616 | tf_op jit(solution)/shard_map/ppermute | solution.py:277
  49.0 0.1 totals.16
  49.1 0.1 collective-permute-start.23
  49.2 0.0 collective-permute-done.16.refs_4_.refs_2_
  49.2 0.1 totals.17.refs_3_
  49.2 1.6 %collective-permute-start.21 = (bf16[2,32,1024]{2,1,0:T(8,128)(2,1)S(1)}, bf16[2,32,1024]{2,1,0:T(8,128)(2,1)S(1)}, u32[]{:S(2)}, u32[]{:S(2)}) collective-permute-start(bf16[2,32,1024]{2,1,0:T(8,128)(2,1)S(1)} %bitcast.11), channel_id=1, source_target_pairs={{0,16},{4,20},{8,24},{12,28},{16,0},{20,4},{24,8},{28,12},{1,17},{... | collective-permute-start | bytes 393224 | tf_op jit(solution)/shard_map/ppermute | solution.py:274
  50.8 0.2 collective-permute-start.20
  51.0 0.0 collective-permute-done.13.refs_2_
  51.1 2.0 %collective-permute-start.17 = (bf16[1,32,1024]{2,1,0:T(8,128)(2,1)S(1)}, bf16[1,32,1024]{2,1,0:T(8,128)(2,1)S(1)}, u32[]{:S(2)}, u32[]{:S(2)}) collective-permute-start(bf16[1,32,1024]{2,1,0:T(8,128)(2,1)S(1)} %totals.18.refs_3_), channel_id=1, source_target_pairs={{0,24},{4,28},{8,16},{12,20},{16,8},{20,12},{24,0},{28,4},{1,25},{... | collective-permute-start | bytes 196616 | tf_op jit(solution)/shard_map/ppermute | solution.py:274
  53.1 0.7 %collective-permute-start.19 = (bf16[1,32,1024]{2,1,0:T(8,128)(2,1)S(1)}, bf16[1,32,1024]{2,1,0:T(8,128)(2,1)S(1)}, u32[]{:S(2)}, u32[]{:S(2)}) collective-permute-start(bf16[1,32,1024]{2,1,0:T(8,128)(2,1)S(1)} %totals.19), channel_id=1, source_target_pairs={{0,28},{4,24},{8,20},{12,16},{16,12},{20,8},{24,4},{28,0},{1,29},{... | collective-permute-start | bytes 196616 | tf_op jit(solution)/shard_map/ppermute | solution.py:274
  53.8 2.8 %collective-permute-done.21.refs_4_ = bf16[2,32,1024]{2,1,0:T(8,128)(2,1)S(1)} collective-permute-done((bf16[2,32,1024]{2,1,0:T(8,128)(2,1)S(1)}, bf16[2,32,1024]{2,1,0:T(8,128)(2,1)S(1)}, u32[]{:S(2)}, u32[]{:S(2)}) %collective-permute-start.21) | collective-permute-done | bytes 131104 | tf_op jit(solution)/shard_map/ppermute | solution.py:274
  56.6 1.6 %collective-permute-done.19.refs_1_ = bf16[1,32,1024]{2,1,0:T(8,128)(2,1)S(1)} collective-permute-done((bf16[1,32,1024]{2,1,0:T(8,128)(2,1)S(1)}, bf16[1,32,1024]{2,1,0:T(8,128)(2,1)S(1)}, u32[]{:S(2)}, u32[]{:S(2)}) %collective-permute-start.19) | collective-permute-done | bytes 65568 | tf_op jit(solution)/shard_map/ppermute | solution.py:274
  58.2 1.0 %order.1 = bf16[256,1024]{1,0:T(8,128)(2,1)} custom-call(bf16[1,32,1024]{2,1,0:T(8,128)(2,1)S(1)} %collective-permute-done.17.refs_0_, bf16[1,32,1024]{2,1,0:T(8,128)(2,1)S(1)} %collective-permute-done.19.refs_1_, bf16[2,32,1024]{2,1,0:T(8,128)(2,1)S(1)} %collective-permute-done.16.refs_4_.refs_2_, bf16[32,1024]{1,0:T(8,128)(2,1)S(1)} %collective-permute-done.20.refs_3_, ...), custom_call_target="tpu_custom_call" | custom-call | tf_op jit(solution)/shard_map/order/pallas_call | solution.py:250
  (25 shorter events, 0.2 us)
Async XLA Ops:
  0.7 0.9 %copy-start = (bf16[32,4,1024]{2,1,0:T(4,128)(2,1)S(1)}, bf16[32,4,1024]{2,1,0:T(4,128)(2,1)}, u32[]{:S(2)}) copy-start(bf16[32,4,1024]{2,1,0:T(4,128)(2,1)} %amps.1) | copy-start | bytes 786436
  2.5 4.9 %collective-permute-start = (bf16[2,32,1024]{2,1,0:T(8,128)(2,1)S(1)}, bf16[2,32,1024]{2,1,0:T(8,128)(2,1)S(1)}, u32[]{:S(2)}, u32[]{:S(2)}) collective-permute-start(bf16[2,32,1024]{2,1,0:T(8,128)(2,1)S(1)} %get-tuple-element.30), channel_id=1, source_target_pairs={{0,4},{4,0},{8,12},{12,8},{16,20},{20,16},{24,28},{28,24},{1,5},{5... | collective-permute-start | bytes 393224 | tf_op jit(solution)/shard_map/ppermute | solution.py:274
  3.0 10.9 %collective-permute-start.2 = (bf16[2,32,1024]{2,1,0:T(8,128)(2,1)S(1)}, bf16[2,32,1024]{2,1,0:T(8,128)(2,1)S(1)}, u32[]{:S(2)}, u32[]{:S(2)}) collective-permute-start(bf16[2,32,1024]{2,1,0:T(8,128)(2,1)S(1)} %get-tuple-element.32), channel_id=1, source_target_pairs={{0,8},{4,12},{8,0},{12,4},{16,24},{20,28},{24,16},{28,20},{1,9},{5... | collective-permute-start | bytes 393224 | tf_op jit(solution)/shard_map/ppermute | solution.py:274
  5.6 8.3 %collective-permute-start.3 = (bf16[2,32,1024]{2,1,0:T(8,128)(2,1)S(1)}, bf16[2,32,1024]{2,1,0:T(8,128)(2,1)S(1)}, u32[]{:S(2)}, u32[]{:S(2)}) collective-permute-start(bf16[2,32,1024]{2,1,0:T(8,128)(2,1)S(1)} %get-tuple-element.33), channel_id=1, source_target_pairs={{0,12},{4,8},{8,4},{12,0},{16,28},{20,24},{24,20},{28,16},{1,13},{... | collective-permute-start | bytes 393224 | tf_op jit(solution)/shard_map/ppermute | solution.py:274
  5.7 8.3 %collective-permute-start.4 = (bf16[2,32,1024]{2,1,0:T(8,128)(2,1)S(1)}, bf16[2,32,1024]{2,1,0:T(8,128)(2,1)S(1)}, u32[]{:S(2)}, u32[]{:S(2)}) collective-permute-start(bf16[2,32,1024]{2,1,0:T(8,128)(2,1)S(1)} %get-tuple-element.34), channel_id=1, source_target_pairs={{0,16},{4,20},{8,24},{12,28},{16,0},{20,4},{24,8},{28,12},{1,17},{... | collective-permute-start | bytes 393224 | tf_op jit(solution)/shard_map/ppermute | solution.py:274
  7.4 6.5 %collective-permute-start.5 = (bf16[2,32,1024]{2,1,0:T(8,128)(2,1)S(1)}, bf16[2,32,1024]{2,1,0:T(8,128)(2,1)S(1)}, u32[]{:S(2)}, u32[]{:S(2)}) collective-permute-start(bf16[2,32,1024]{2,1,0:T(8,128)(2,1)S(1)} %get-tuple-element.35), channel_id=1, source_target_pairs={{0,20},{4,16},{8,28},{12,24},{16,4},{20,0},{24,12},{28,8},{1,21},{... | collective-permute-start | bytes 393224 | tf_op jit(solution)/shard_map/ppermute | solution.py:274
  12.1 9.9 %collective-permute-start.1 = (bf16[2,64,1024]{2,1,0:T(8,128)(2,1)S(1)}, bf16[2,64,1024]{2,1,0:T(8,128)(2,1)S(1)}, u32[]{:S(2)}, u32[]{:S(2)}) collective-permute-start(bf16[2,64,1024]{2,1,0:T(8,128)(2,1)S(1)} %get-tuple-element.31.refs_0_), channel_id=1, source_target_pairs={{0,1},{1,0},{2,3},{3,2},{4,5},{5,4},{6,7},{7,6},{8,9},{9,8},{10,11... | collective-permute-start | bytes 786440 | tf_op jit(solution)/shard_map/ppermute | solution.py:277
  17.4 7.7 %copy-start.1 = (s32[8]{0:T(128)S(1)}, s32[8]{0:T(128)}, u32[]{:S(2)}) copy-start(s32[8]{0:T(128)} %q_owner.1) | copy-start | bytes 100
  17.5 11.1 %collective-permute-start.7 = (bf16[2,64,1024]{2,1,0:T(8,128)(2,1)S(1)}, bf16[2,64,1024]{2,1,0:T(8,128)(2,1)S(1)}, u32[]{:S(2)}, u32[]{:S(2)}) collective-permute-start(bf16[2,64,1024]{2,1,0:T(8,128)(2,1)S(1)} %get-tuple-element.43), channel_id=1, source_target_pairs={{0,1},{1,0},{2,3},{3,2},{4,5},{5,4},{6,7},{7,6},{8,9},{9,8},{10,11... | collective-permute-start | bytes 786440 | tf_op jit(solution)/shard_map/ppermute | solution.py:277
  19.1 10.7 %collective-permute-start.8 = (bf16[2,32,1024]{2,1,0:T(8,128)(2,1)S(1)}, bf16[2,32,1024]{2,1,0:T(8,128)(2,1)S(1)}, u32[]{:S(2)}, u32[]{:S(2)}) collective-permute-start(bf16[2,32,1024]{2,1,0:T(8,128)(2,1)S(1)} %get-tuple-element.45), channel_id=1, source_target_pairs={{0,24},{4,28},{8,16},{12,20},{16,8},{20,12},{24,0},{28,4},{1,25},{... | collective-permute-start | bytes 393224 | tf_op jit(solution)/shard_map/ppermute | solution.py:274
  21.5 8.2 %collective-permute-start.9 = (bf16[2,32,1024]{2,1,0:T(8,128)(2,1)S(1)}, bf16[2,32,1024]{2,1,0:T(8,128)(2,1)S(1)}, u32[]{:S(2)}, u32[]{:S(2)}) collective-permute-start(bf16[2,32,1024]{2,1,0:T(8,128)(2,1)S(1)} %get-tuple-element.46), channel_id=1, source_target_pairs={{0,28},{4,24},{8,20},{12,16},{16,12},{20,8},{24,4},{28,0},{1,29},{... | collective-permute-start | bytes 393224 | tf_op jit(solution)/shard_map/ppermute | solution.py:274
  21.5 15.6 %collective-permute-start.6 = (bf16[2,64,1024]{2,1,0:T(8,128)(2,1)S(1)}, bf16[2,64,1024]{2,1,0:T(8,128)(2,1)S(1)}, u32[]{:S(2)}, u32[]{:S(2)}) collective-permute-start(bf16[2,64,1024]{2,1,0:T(8,128)(2,1)S(1)} %get-tuple-element.41), channel_id=1, source_target_pairs={{0,1},{1,0},{2,3},{3,2},{4,5},{5,4},{6,7},{7,6},{8,9},{9,8},{10,11... | collective-permute-start | bytes 786440 | tf_op jit(solution)/shard_map/ppermute | solution.py:277
  25.9 13.2 %collective-permute-start.10 = (bf16[1,64,1024]{2,1,0:T(8,128)(2,1)S(1)}, bf16[1,64,1024]{2,1,0:T(8,128)(2,1)S(1)}, u32[]{:S(2)}, u32[]{:S(2)}) collective-permute-start(bf16[1,64,1024]{2,1,0:T(8,128)(2,1)S(1)} %totals.10.after), channel_id=1, source_target_pairs={{0,2},{1,3},{2,0},{3,1},{4,6},{5,7},{6,4},{7,5},{8,10},{9,11},{10,... | collective-permute-start | bytes 393224 | tf_op jit(solution)/shard_map/ppermute | solution.py:277
  28.6 13.3 %collective-permute-start.12 = (bf16[1,64,1024]{2,1,0:T(8,128)(2,1)S(1)}, bf16[1,64,1024]{2,1,0:T(8,128)(2,1)S(1)}, u32[]{:S(2)}, u32[]{:S(2)}) collective-permute-start(bf16[1,64,1024]{2,1,0:T(8,128)(2,1)S(1)} %totals.11.refs_0_), channel_id=1, source_target_pairs={{0,2},{1,3},{2,0},{3,1},{4,6},{5,7},{6,4},{7,5},{8,10},{9,11},{10,... | collective-permute-start | bytes 393224 | tf_op jit(solution)/shard_map/ppermute | solution.py:277
  32.6 10.9 %collective-permute-start.11 = (bf16[2,32,1024]{2,1,0:T(8,128)(2,1)S(1)}, bf16[2,32,1024]{2,1,0:T(8,128)(2,1)S(1)}, u32[]{:S(2)}, u32[]{:S(2)}) collective-permute-start(bf16[2,32,1024]{2,1,0:T(8,128)(2,1)S(1)} %get-tuple-element.47.refs_2_), channel_id=1, source_target_pairs={{0,1},{1,0},{2,3},{3,2},{4,5},{5,4},{6,7},{7,6},{8,9},{9,8},{10,11... | collective-permute-start | bytes 393224 | tf_op jit(solution)/shard_map/ppermute | solution.py:277
  37.1 12.0 %collective-permute-start.14 = (bf16[1,64,1024]{2,1,0:T(8,128)(2,1)S(1)}, bf16[1,64,1024]{2,1,0:T(8,128)(2,1)S(1)}, u32[]{:S(2)}, u32[]{:S(2)}) collective-permute-start(bf16[1,64,1024]{2,1,0:T(8,128)(2,1)S(1)} %totals.12.refs_0_), channel_id=1, source_target_pairs={{0,2},{1,3},{2,0},{3,1},{4,6},{5,7},{6,4},{7,5},{8,10},{9,11},{10,... | collective-permute-start | bytes 393224 | tf_op jit(solution)/shard_map/ppermute | solution.py:277
  37.2 8.7 %collective-permute-start.15 = (bf16[2,32,1024]{2,1,0:T(8,128)(2,1)S(1)}, bf16[2,32,1024]{2,1,0:T(8,128)(2,1)S(1)}, u32[]{:S(2)}, u32[]{:S(2)}) collective-permute-start(bf16[2,32,1024]{2,1,0:T(8,128)(2,1)S(1)} %get-tuple-element.50), channel_id=1, source_target_pairs={{0,1},{1,0},{2,3},{3,2},{4,5},{5,4},{6,7},{7,6},{8,9},{9,8},{10,11... | collective-permute-start | bytes 393224 | tf_op jit(solution)/shard_map/ppermute | solution.py:277
  42.0 7.2 %collective-permute-start.16 = (bf16[2,32,1024]{2,1,0:T(8,128)(2,1)S(1)}, bf16[2,32,1024]{2,1,0:T(8,128)(2,1)S(1)}, u32[]{:S(2)}, u32[]{:S(2)}) collective-permute-start(bf16[2,32,1024]{2,1,0:T(8,128)(2,1)S(1)} %bitcast.10), channel_id=1, source_target_pairs={{0,8},{4,12},{8,0},{12,4},{16,24},{20,28},{24,16},{28,20},{1,9},{5... | collective-permute-start | bytes 393224 | tf_op jit(solution)/shard_map/ppermute | solution.py:274
  43.5 7.5 %collective-permute-start.13 = (bf16[1,32,1024]{2,1,0:T(8,128)(2,1)S(1)}, bf16[1,32,1024]{2,1,0:T(8,128)(2,1)S(1)}, u32[]{:S(2)}, u32[]{:S(2)}) collective-permute-start(bf16[1,32,1024]{2,1,0:T(8,128)(2,1)S(1)} %totals.14.refs_2_), channel_id=1, source_target_pairs={{0,2},{1,3},{2,0},{3,1},{4,6},{5,7},{6,4},{7,5},{8,10},{9,11},{10,... | collective-permute-start | bytes 196616 | tf_op jit(solution)/shard_map/ppermute | solution.py:277
  45.9 7.1 %collective-permute-start.18 = (bf16[1,32,1024]{2,1,0:T(8,128)(2,1)S(1)}, bf16[1,32,1024]{2,1,0:T(8,128)(2,1)S(1)}, u32[]{:S(2)}, u32[]{:S(2)}) collective-permute-start(bf16[1,32,1024]{2,1,0:T(8,128)(2,1)S(1)} %totals.15.refs_3_), channel_id=1, source_target_pairs={{0,2},{1,3},{2,0},{3,1},{4,6},{5,7},{6,4},{7,5},{8,10},{9,11},{10,... | collective-permute-start | bytes 196616 | tf_op jit(solution)/shard_map/ppermute | solution.py:277
  49.1 7.5 %collective-permute-start.23 = (bf16[32,1024]{1,0:T(8,128)(2,1)S(1)}, bf16[32,1024]{1,0:T(8,128)(2,1)S(1)}, u32[]{:S(2)}, u32[]{:S(2)}) collective-permute-start(bf16[32,1024]{1,0:T(8,128)(2,1)S(1)} %get-tuple-element.51.refs_3_), channel_id=1, source_target_pairs={{0,4},{4,0},{8,12},{12,8},{16,20},{20,16},{24,28},{28,24},{1,5},{5... | collective-permute-start | bytes 196616 | tf_op jit(solution)/shard_map/ppermute | solution.py:274
  49.2 7.3 %collective-permute-start.21 = (bf16[2,32,1024]{2,1,0:T(8,128)(2,1)S(1)}, bf16[2,32,1024]{2,1,0:T(8,128)(2,1)S(1)}, u32[]{:S(2)}, u32[]{:S(2)}) collective-permute-start(bf16[2,32,1024]{2,1,0:T(8,128)(2,1)S(1)} %bitcast.11), channel_id=1, source_target_pairs={{0,16},{4,20},{8,24},{12,28},{16,0},{20,4},{24,8},{28,12},{1,17},{... | collective-permute-start | bytes 393224 | tf_op jit(solution)/shard_map/ppermute | solution.py:274
  50.8 5.8 %collective-permute-start.20 = (bf16[32,1024]{1,0:T(8,128)(2,1)S(1)}, bf16[32,1024]{1,0:T(8,128)(2,1)S(1)}, u32[]{:S(2)}, u32[]{:S(2)}) collective-permute-start(bf16[32,1024]{1,0:T(8,128)(2,1)S(1)} %slice_bitcast_fusion.1), channel_id=1, source_target_pairs={{0,4},{4,0},{8,12},{12,8},{16,20},{20,16},{24,28},{28,24},{1,5},{5... | collective-permute-start | bytes 196616 | tf_op jit(solution)/shard_map/ppermute | solution.py:274
  51.1 7.1 %collective-permute-start.17 = (bf16[1,32,1024]{2,1,0:T(8,128)(2,1)S(1)}, bf16[1,32,1024]{2,1,0:T(8,128)(2,1)S(1)}, u32[]{:S(2)}, u32[]{:S(2)}) collective-permute-start(bf16[1,32,1024]{2,1,0:T(8,128)(2,1)S(1)} %totals.18.refs_3_), channel_id=1, source_target_pairs={{0,24},{4,28},{8,16},{12,20},{16,8},{20,12},{24,0},{28,4},{1,25},{... | collective-permute-start | bytes 196616 | tf_op jit(solution)/shard_map/ppermute | solution.py:274
  53.1 5.1 %collective-permute-start.19 = (bf16[1,32,1024]{2,1,0:T(8,128)(2,1)S(1)}, bf16[1,32,1024]{2,1,0:T(8,128)(2,1)S(1)}, u32[]{:S(2)}, u32[]{:S(2)}) collective-permute-start(bf16[1,32,1024]{2,1,0:T(8,128)(2,1)S(1)} %totals.19), channel_id=1, source_target_pairs={{0,28},{4,24},{8,20},{12,16},{16,12},{20,8},{24,4},{28,0},{1,29},{... | collective-permute-start | bytes 196616 | tf_op jit(solution)/shard_map/ppermute | solution.py:274
  56.6 1.6 %collective-permute-start.22 = (bf16[32,1024]{1,0:T(8,128)(2,1)S(1)}, bf16[32,1024]{1,0:T(8,128)(2,1)S(1)}, u32[]{:S(2)}, u32[]{:S(2)}) collective-permute-start(bf16[32,1024]{1,0:T(8,128)(2,1)S(1)} %slice_bitcast_fusion), channel_id=1, source_target_pairs={{0,4},{4,0},{8,12},{12,8},{16,20},{20,16},{24,28},{28,24},{1,5},{5... | collective-permute-start | bytes 196616 | tf_op jit(solution)/shard_map/ppermute | solution.py:274
